TPU v7x, 32 devices: a whole 2x2x4 slice. The times are simulated.
32 devices in a mesh: band: 4 (over y, core), dom: 8 (over z, x).
Axes of the slice: x: 2, y: 2, z: 4, core: 2. Of those that a mesh axis runs over, the one named last changes fastest.
Arguments:
- trial_waves: float32 [64, 16, 16, 512], P('dom', None, None, 'band'), may hold values from -10 to 10
- potential: float32 [64, 16, 16], P('dom'), may hold values from -2 to 1
- proj_weights: float32 [16, 8, 256], P('dom'), may hold values from -0.5 to 0.5
- kb_energy: float32 [8], replicated, may hold values from 1 to 4
- atom_cell: int32 [16, 3], P('dom'), may hold values from 0 to 63, as said below
- point_codes: int32 [16, 256], P('dom'), may hold values from 0 to 728, as said below
Outputs:
- filtered: float32 [64, 16, 16, 512], P('dom', None, None, 'band')
- correlation: float32 [512, 512], P('band')
Inputs may be any that keep to these rules, and one draw needn't show every extreme that they name: `atom_cell`: atom k's centre lies in the first-dimension planes k // 2 * 8 to (k // 2 + 1) * 8 - 1. `point_codes`: the 256 codes of one atom are distinct cells of the cube of side 2 * 4 + 1 around its centre.
All inputs are finite; a program needn't handle non-finite values.
Results may differ from a plain program's by a relative error of at most 0.0001.
Values sent between devices are 32-bit elements; how exact they have to be, the bound alone decides.
No kernel may reach another device: no remote copies, remote signals or barrier semaphores. Data moves between devices by JAX's collectives and lax.ppermute only.
A program may use at most 128 MiB of HBM per device.

v0:
```python
import jax
import jax.numpy as jnp
from jax import lax
from jax.sharding import PartitionSpec as P

HALO = 6
REACH = 4


COEFFS = (
    -5369.0 / 1800.0,
    12.0 / 7.0,
    -15.0 / 56.0,
    10.0 / 189.0,
    -1.0 / 112.0,
    2.0 / 1925.0,
    -1.0 / 16632.0,
)
FILTER_LOWER = 5.0
FILTER_UPPER = 24.0
SPECTRUM_BOTTOM = 0.0
EPSILON = 1e-06


def extended_2(cells, sides, width):
    for axis, dim in sides:
        count = lax.axis_size(axis)
        head = lax.slice_in_dim(cells, 0, width, axis=dim)
        tail = lax.slice_in_dim(cells, cells.shape[dim] - width, cells.shape[dim], axis=dim)
        cells = jnp.concatenate(
            [
                lax.ppermute(tail, axis, [(i, (i + 1) % count) for i in range(count)]),
                cells,
                lax.ppermute(head, axis, [((i + 1) % count, i) for i in range(count)]),
            ],
            axis=dim,
        )
    return cells


def from_behind(value, axis, steps):
    count = lax.axis_size(axis)
    pairs = [(source, (source + steps) % count) for source in range(count)]
    return lax.ppermute(value, axis, pairs)


def support_places(atom_cell, point_codes, planes, rows_y, rows_z):
    cube_side = 2 * REACH + 1
    off_x = point_codes // (cube_side * cube_side)
    off_y = point_codes // cube_side % cube_side
    off_z = point_codes % cube_side
    planes_at = atom_cell[:, 0:1] % planes + off_x - REACH
    cell_y = (atom_cell[:, 1:2] + off_y - REACH) % rows_y
    cell_z = (atom_cell[:, 2:3] + off_z - REACH) % rows_z
    return (planes_at, cell_y * rows_z + cell_z)


def kinetic(wavefield, extended):
    planes = wavefield.shape[0]
    summed = 3.0 * COEFFS[0] * wavefield
    for k in range(1, HALO + 1):
        summed = summed + COEFFS[k] * (
            extended[HALO - k : HALO - k + planes] + extended[HALO + k : HALO + k + planes]
        )
        summed = summed + COEFFS[k] * (jnp.roll(wavefield, k, 1) + jnp.roll(wavefield, -k, 1))
        summed = summed + COEFFS[k] * (jnp.roll(wavefield, k, 2) + jnp.roll(wavefield, -k, 2))
    return -0.5 * summed


def on_device(trial_waves, potential, proj_weights, kb_energy, atom_cell, point_codes):
    planes, rows_y, rows_z, band_count = trial_waves.shape
    lat_size = rows_y * rows_z
    atom_count = atom_cell.shape[0]
    planes_at, lateral = support_places(atom_cell, point_codes, planes, rows_y, rows_z)
    own_index = ((planes_at + HALO) * lat_size + lateral).reshape(-1)
    scaled = proj_weights * kb_energy[None, :, None]
    push_index = ((planes_at + REACH) * lat_size + lateral).reshape(-1)

    def hamiltonian(wavefield):
        extended = extended_2(wavefield, (("dom", 0),), HALO)
        ext_rows = extended.reshape(-1, band_count)
        cell_rows = jnp.take(ext_rows, own_index, axis=0).reshape(
            atom_count, planes_at.shape[1], band_count
        )
        projections = jnp.einsum(
            "ajp,apb->ajb", proj_weights, cell_rows, precision=lax.Precision.HIGHEST
        )
        contrib = jnp.einsum("ajp,ajb->apb", scaled, projections, precision=lax.Precision.HIGHEST)
        spread = (
            jnp.zeros(((planes + 2 * REACH) * lat_size, band_count), jnp.float32)
            .at[push_index]
            .add(contrib.reshape(-1, band_count))
        )
        spread = spread.reshape(planes + 2 * REACH, rows_y, rows_z, band_count)
        from_above = from_behind(spread[:REACH], "dom", -1)
        from_below = from_behind(spread[planes + REACH :], "dom", 1)
        nonlocal_term = spread[REACH : REACH + planes]
        nonlocal_term = (
            nonlocal_term.at[:REACH].add(from_below).at[planes - REACH :].add(from_above)
        )
        return kinetic(wavefield, extended) + potential[..., None] * wavefield + nonlocal_term

    half_width = (FILTER_UPPER - FILTER_LOWER) / 2.0
    centre = (FILTER_UPPER + FILTER_LOWER) / 2.0
    sigma_first = half_width / (SPECTRUM_BOTTOM - centre)
    older = trial_waves
    applied = hamiltonian(trial_waves)
    newer = sigma_first / half_width * (applied - centre * trial_waves)
    sigma_next = 1.0 / (2.0 / sigma_first - sigma_first)
    applied = hamiltonian(newer)
    newer, older = (
        2.0 * sigma_next / half_width * (applied - centre * newer)
        - sigma_first * sigma_next * older,
        newer,
    )
    cell_total = planes * lat_size * lax.axis_size("dom")
    own_start = lax.axis_index("band") * band_count
    flat_rows = newer.reshape(-1, band_count)
    sq_own = lax.psum(jnp.sum(flat_rows * flat_rows, axis=0), "dom")
    rms_own = jnp.sqrt(sq_own / cell_total + EPSILON)
    source = newer / rms_own
    swapped = lax.all_to_all(source, "band", split_axis=1, concat_axis=3, tiled=True)
    swap_rows = swapped.reshape(-1, swapped.shape[3])
    full_gram = lax.dot_general(
        swap_rows,
        swap_rows,
        (((0,), (0,)), ((), ())),
        precision=lax.Precision.HIGHEST,
        preferred_element_type=jnp.float32,
    )
    gram_sum = lax.psum(full_gram, ("band", "dom"))
    gram_part = lax.dynamic_slice_in_dim(gram_sum, own_start, band_count, 0)
    correlation = gram_part / cell_total
    return (source, correlation)


def solution(mesh):
    return jax.shard_map(
        on_device,
        mesh=mesh,
        in_specs=(
            P("dom", None, None, "band"),
            P("dom", None, None),
            P("dom", None, None),
            P(),
            P("dom", None),
            P("dom", None),
        ),
        out_specs=(P("dom", None, None, "band"), P("band", None)),
        check_vma=False,
    )
```

profile of v0, /device:TPU:0, one launch (start us, length us, event | category | flops | bytes accessed | tf_op | source)
XLA Modules:
  0.0 379.8 jit_solution(3349953583725822948)
XLA Ops:
  8.8 3.0 collective-permute-start
  11.8 3.1 collective-permute-start.1
  17.9 1.6 fusion.165
  40.4 1.6 fusion.173
  43.5 1.9 collective-permute-done
  45.4 2.2 collective-permute-done.1
  47.6 1.7 pad_maximum_fusion
  49.3 2.8 gather_fusion
  53.9 3.1 scatter_custom_fusion
  57.8 2.5 broadcast_multiply_fusion.1
  60.3 3.5 collective-permute-start.3
  66.8 12.5 %collective-permute-done.2 = f32[4,16,16,128]{3,2,1,0:T(8,128)S(1)} collective-permute-done((f32[4,16,16,128]{3,2,1,0:T(8,128)S(1)}, f32[4,16,16,128]{3,2,1,0:T(8,128)S(1)}, u32[]{:S(2)}, u32[]{:S(2)}) %collective-permute-start.2) | collective-permute-done | bytes 524320 | tf_op jit(solution)/shard_map/ppermute | solution.py:44
  79.4 4.3 %collective-permute-done.3 = f32[4,16,16,128]{3,2,1,0:T(8,128)S(1)} collective-permute-done((f32[4,16,16,128]{3,2,1,0:T(8,128)S(1)}, f32[4,16,16,128]{3,2,1,0:T(8,128)S(1)}, u32[]{:S(2)}, u32[]{:S(2)}) %collective-permute-start.3) | collective-permute-done | bytes 524320 | tf_op jit(solution)/shard_map/ppermute | solution.py:44
  84.0 8.3 %broadcast_multiply_fusion = (f32[8,16,16,128]{3,2,1,0:T(8,128)S(1)}, f32[8,16,16,128]{3,2,1,0:T(8,128)S(1)}) fusion(f32[8,16,16,128]{3,2,1,0:T(8,128)S(1)} %copy-done, f32[8,16,16,128]{3,2,1,0:T(8,128)S(1)} %fusion.106, f32[8,16,16]{2,1,0:T(8,128)} %param.17, f32[8,16,6,128]{3,2,1,0:T(8,128)} %get-tuple-element.166, f32[8,16,10,128]{3,2,1,0:T(8,128)S(1)} %copy-done.25, ...), kind=kLoop, calls=%fused_computation.170 | loop fusion | flops 22544384 | bytes 41951232 | tf_op jit(solution)/shard_map/mul | solution.py:108
  95.5 1.6 fusion.152
  114.1 4.7 %collective-permute-start.5 = (f32[6,16,16,128]{3,2,1,0:T(8,128)S(1)}, f32[6,16,16,128]{3,2,1,0:T(8,128)S(1)}, u32[]{:S(2)}, u32[]{:S(2)}) collective-permute-start(f32[6,16,16,128]{3,2,1,0:T(8,128)S(1)} %get-tuple-element.118), channel_id=1, source_target_pairs={{1,0},{2,1},{3,2},{4,3},{5,4},{6,5},{7,6},{0,7},{9,8},{10,9},{11,1... | collective-permute-start | bytes 2359304 | tf_op jit(solution)/shard_map/ppermute | solution.py:34
  122.5 25.7 %collective-permute-done.4 = f32[6,16,16,128]{3,2,1,0:T(8,128)S(1)} collective-permute-done((f32[6,16,16,128]{3,2,1,0:T(8,128)S(1)}, f32[6,16,16,128]{3,2,1,0:T(8,128)S(1)}, u32[]{:S(2)}, u32[]{:S(2)}) %collective-permute-start.4) | collective-permute-done | bytes 786464 | tf_op jit(solution)/shard_map/ppermute | solution.py:32
  148.3 2.5 collective-permute-done.5
  150.7 1.7 pad_maximum_fusion.1
  152.4 3.5 gather_fusion.1
  157.3 2.0 fusion.107
  159.3 4.0 %scatter_custom_fusion.1 = f32[4096,128]{1,0:T(8,128)} fusion(s32[512]{0:T(512)} %bitcast.56, f32[512,128]{1,0:T(8,128)} %bitcast.50, f32[]{:T(128)} %constant.200.clone.1), kind=kCustom, calls=%fused_computation.160 | custom fusion | flops 65536 | bytes 2097664 | tf_op jit(solution)/shard_map/scatter-add | solution.py:92
  163.4 1.6 fusion.127
  165.4 4.5 %collective-permute-start.7 = (f32[4,16,16,128]{3,2,1,0:T(8,128)S(1)}, f32[4,16,16,128]{3,2,1,0:T(8,128)S(1)}, u32[]{:S(2)}, u32[]{:S(2)}) collective-permute-start(f32[4,16,16,128]{3,2,1,0:T(8,128)S(1)} %bitcast.47), channel_id=1, source_target_pairs={{0,7},{1,0},{2,1},{3,2},{4,3},{5,4},{6,5},{7,6},{8,15},{9,8},{10,9... | collective-permute-start | bytes 1572872 | tf_op jit(solution)/shard_map/ppermute | solution.py:44
  170.1 17.2 %collective-permute-done.6 = f32[4,16,16,128]{3,2,1,0:T(8,128)S(1)} collective-permute-done((f32[4,16,16,128]{3,2,1,0:T(8,128)S(1)}, f32[4,16,16,128]{3,2,1,0:T(8,128)S(1)}, u32[]{:S(2)}, u32[]{:S(2)}) %collective-permute-start.6) | collective-permute-done | bytes 524320 | tf_op jit(solution)/shard_map/ppermute | solution.py:44
  187.4 3.8 collective-permute-done.7
  191.4 12.9 %multiply_reduce_fusion = (f32[128]{0:T(128)S(1)}, f32[8,16,16,128]{3,2,1,0:T(8,128)}) fusion(f32[8,16,16,128]{3,2,1,0:T(8,128)S(1)} %copy-done, f32[8,16,16,128]{3,2,1,0:T(8,128)S(1)} %get-tuple-element.59, f32[8,16,16,128]{3,2,1,0:T(8,128)S(1)} %fusion.105, f32[8,16,16]{2,1,0:T(8,128)S(1)} %copy-done.32, f32[8,16,6,128]{3,2,1,0:T(8,128)S(1)} %get-tuple-element.114, ...), kind=kLoop, calls=%fused_computation.159 | loop fusion | flops 26738560 | bytes 31990272 | tf_op jit(solution)/shard_map/reduce_sum | solution.py:119
  204.3 18.3 %psum.14 = f32[128]{0:T(128)S(1)} all-reduce(f32[128]{0:T(128)S(1)} %get-tuple-element.56), channel_id=1, replica_groups=mesh['band'=4,'dom'=8] {'dom'}, use_global_device_ids=true, to_apply=%region_3.5 | all-reduce | flops 128 | bytes 1024 | tf_op jit(solution)/shard_map/psum | solution.py:119
  224.1 17.1 %all_to_all.15 = f32[8,16,16,128]{3,2,0,1:T(8,128)S(1)} all-to-all(f32[8,16,16,128]{3,2,0,1:T(8,128)S(1)} %copy.72), channel_id=1, replica_groups=mesh['band'=4,'dom'=8] {'band'}, dimensions={1} | all-to-all | bytes 2097152 | tf_op jit(solution)/shard_map/all_to_all | solution.py:122
  241.8 2.9 fusion.44
  244.7 126.5 %all-reduce.2.cloned.1.call-done = f32[512,512]{1,0:T(8,128)} async-done(((f32[512,512]{1,0:T(8,128)}), f32[512,512]{1,0:T(8,128)}) %all-reduce.2.cloned.1.call-update) | async-done | bytes 1048592 | tf_op jit(solution)/shard_map/psum | solution.py:131
  371.2 1.7 dynamic-slice_multiply_fusion
  (160 shorter events, 60.7 us)
Async XLA Ops:
  7.2 364.1 %all-reduce.2.cloned.1.call-start = ((), (), s32[]{:S(2)}) async-start(), calls=%async_computation.1 | async-start | bytes 2097152 | tf_op jit(solution)/shard_map/psum | solution.py:131
  8.8 36.6 %collective-permute-start = (f32[6,16,16,128]{3,2,1,0:T(8,128)S(1)}, f32[6,16,16,128]{3,2,1,0:T(8,128)S(1)}, u32[]{:S(2)}, u32[]{:S(2)}) collective-permute-start(f32[6,16,16,128]{3,2,1,0:T(8,128)S(1)} %get-tuple-element.169), channel_id=1, source_target_pairs={{0,1},{1,2},{2,3},{3,4},{4,5},{5,6},{6,7},{7,0},{8,9},{9,10},{10,1... | collective-permute-start | bytes 2359304 | tf_op jit(solution)/shard_map/ppermute | solution.py:32
  11.8 35.9 %collective-permute-start.1 = (f32[6,16,16,128]{3,2,1,0:T(8,128)S(1)}, f32[6,16,16,128]{3,2,1,0:T(8,128)S(1)}, u32[]{:S(2)}, u32[]{:S(2)}) collective-permute-start(f32[6,16,16,128]{3,2,1,0:T(8,128)S(1)} %get-tuple-element.170), channel_id=1, source_target_pairs={{1,0},{2,1},{3,2},{4,3},{5,4},{6,5},{7,6},{0,7},{9,8},{10,9},{11,1... | collective-permute-start | bytes 2359304 | tf_op jit(solution)/shard_map/ppermute | solution.py:34
  57.1 26.7 %copy-start.24 = (f32[8,16,10,128]{3,2,1,0:T(8,128)S(1)}, f32[8,16,10,128]{3,2,1,0:T(8,128)}, u32[]{:S(2)}) copy-start(f32[8,16,10,128]{3,2,1,0:T(8,128)} %get-tuple-element.167) | copy-start | bytes 1966084
  57.1 26.7 %copy-start.25 = (f32[8,16,10,128]{3,2,1,0:T(8,128)S(1)}, f32[8,16,10,128]{3,2,1,0:T(8,128)}, u32[]{:S(2)}) copy-start(f32[8,16,10,128]{3,2,1,0:T(8,128)} %get-tuple-element.168) | copy-start | bytes 1966084
  57.1 26.7 %copy-start.26 = (f32[8,15,16,128]{3,2,1,0:T(8,128)S(1)}, f32[8,15,16,128]{3,2,1,0:T(8,128)}, u32[]{:S(2)}) copy-start(f32[8,15,16,128]{3,2,1,0:T(8,128)} %get-tuple-element.121) | copy-start | bytes 2949124
  57.1 26.7 %copy-start.31 = (f32[8,16,3,128]{3,2,1,0:T(4,128)S(1)}, f32[8,16,3,128]{3,2,1,0:T(4,128)}, u32[]{:S(2)}) copy-start(f32[8,16,3,128]{3,2,1,0:T(4,128)} %get-tuple-element.139) | copy-start | bytes 589828
  57.2 22.1 %collective-permute-start.2 = (f32[4,16,16,128]{3,2,1,0:T(8,128)S(1)}, f32[4,16,16,128]{3,2,1,0:T(8,128)S(1)}, u32[]{:S(2)}, u32[]{:S(2)}) collective-permute-start(f32[4,16,16,128]{3,2,1,0:T(8,128)S(1)} %bitcast.48), channel_id=1, source_target_pairs={{0,1},{1,2},{2,3},{3,4},{4,5},{5,6},{6,7},{7,0},{8,9},{9,10},{10,1... | collective-permute-start | bytes 1572872 | tf_op jit(solution)/shard_map/ppermute | solution.py:44
  60.3 23.6 %copy-start.21 = (f32[8,16,11,128]{3,2,1,0:T(8,128)S(1)}, f32[8,16,11,128]{3,2,1,0:T(8,128)}, u32[]{:S(2)}) copy-start(f32[8,16,11,128]{3,2,1,0:T(8,128)} %get-tuple-element.157) | copy-start | bytes 2162692
  60.3 23.6 %copy-start.22 = (f32[8,16,11,128]{3,2,1,0:T(8,128)S(1)}, f32[8,16,11,128]{3,2,1,0:T(8,128)}, u32[]{:S(2)}) copy-start(f32[8,16,11,128]{3,2,1,0:T(8,128)} %get-tuple-element.158) | copy-start | bytes 2162692
  60.3 23.4 %collective-permute-start.3 = (f32[4,16,16,128]{3,2,1,0:T(8,128)S(1)}, f32[4,16,16,128]{3,2,1,0:T(8,128)S(1)}, u32[]{:S(2)}, u32[]{:S(2)}) collective-permute-start(f32[4,16,16,128]{3,2,1,0:T(8,128)S(1)} %bitcast.46), channel_id=1, source_target_pairs={{0,7},{1,0},{2,1},{3,2},{4,3},{5,4},{6,5},{7,6},{8,15},{9,8},{10,9... | collective-permute-start | bytes 1572872 | tf_op jit(solution)/shard_map/ppermute | solution.py:44
  63.9 20.0 %copy-start.9 = (f32[8,16,12,128]{3,2,1,0:T(8,128)S(1)}, f32[8,16,12,128]{3,2,1,0:T(8,128)}, u32[]{:S(2)}) copy-start(f32[8,16,12,128]{3,2,1,0:T(8,128)} %get-tuple-element.149) | copy-start | bytes 2359300
  63.9 20.0 %copy-start.10 = (f32[8,16,12,128]{3,2,1,0:T(8,128)S(1)}, f32[8,16,12,128]{3,2,1,0:T(8,128)}, u32[]{:S(2)}) copy-start(f32[8,16,12,128]{3,2,1,0:T(8,128)} %get-tuple-element.150) | copy-start | bytes 2359300
  65.2 18.7 %copy-start.7 = (f32[8,16,13,128]{3,2,1,0:T(8,128)S(1)}, f32[8,16,13,128]{3,2,1,0:T(8,128)}, u32[]{:S(2)}) copy-start(f32[8,16,13,128]{3,2,1,0:T(8,128)} %get-tuple-element.141) | copy-start | bytes 2555908
  65.2 18.7 %copy-start.8 = (f32[8,16,13,128]{3,2,1,0:T(8,128)S(1)}, f32[8,16,13,128]{3,2,1,0:T(8,128)}, u32[]{:S(2)}) copy-start(f32[8,16,13,128]{3,2,1,0:T(8,128)} %get-tuple-element.142) | copy-start | bytes 2555908
  114.1 34.1 %collective-permute-start.4 = (f32[6,16,16,128]{3,2,1,0:T(8,128)S(1)}, f32[6,16,16,128]{3,2,1,0:T(8,128)S(1)}, u32[]{:S(2)}, u32[]{:S(2)}) collective-permute-start(f32[6,16,16,128]{3,2,1,0:T(8,128)S(1)} %get-tuple-element.117), channel_id=1, source_target_pairs={{0,1},{1,2},{2,3},{3,4},{4,5},{5,6},{6,7},{7,0},{8,9},{9,10},{10,1... | collective-permute-start | bytes 2359304 | tf_op jit(solution)/shard_map/ppermute | solution.py:32
  114.1 36.6 %collective-permute-start.5 = (f32[6,16,16,128]{3,2,1,0:T(8,128)S(1)}, f32[6,16,16,128]{3,2,1,0:T(8,128)S(1)}, u32[]{:S(2)}, u32[]{:S(2)}) collective-permute-start(f32[6,16,16,128]{3,2,1,0:T(8,128)S(1)} %get-tuple-element.118), channel_id=1, source_target_pairs={{1,0},{2,1},{3,2},{4,3},{5,4},{6,5},{7,6},{0,7},{9,8},{10,9},{11,1... | collective-permute-start | bytes 2359304 | tf_op jit(solution)/shard_map/ppermute | solution.py:34
  163.4 28.0 %copy-start.19 = (f32[8,16,14,128]{3,2,1,0:T(8,128)S(1)}, f32[8,16,14,128]{3,2,1,0:T(8,128)}, u32[]{:S(2)}) copy-start(f32[8,16,14,128]{3,2,1,0:T(8,128)} %get-tuple-element.83) | copy-start | bytes 2752516
  163.4 28.0 %copy-start.20 = (f32[8,16,14,128]{3,2,1,0:T(8,128)S(1)}, f32[8,16,14,128]{3,2,1,0:T(8,128)}, u32[]{:S(2)}) copy-start(f32[8,16,14,128]{3,2,1,0:T(8,128)} %get-tuple-element.84) | copy-start | bytes 2752516
  163.4 28.0 %copy-start.23 = (f32[8,16,13,128]{3,2,1,0:T(8,128)S(1)}, f32[8,16,13,128]{3,2,1,0:T(8,128)}, u32[]{:S(2)}) copy-start(f32[8,16,13,128]{3,2,1,0:T(8,128)} %get-tuple-element.91) | copy-start | bytes 2555908
  165.0 22.4 %collective-permute-start.6 = (f32[4,16,16,128]{3,2,1,0:T(8,128)S(1)}, f32[4,16,16,128]{3,2,1,0:T(8,128)S(1)}, u32[]{:S(2)}, u32[]{:S(2)}) collective-permute-start(f32[4,16,16,128]{3,2,1,0:T(8,128)S(1)} %bitcast.49), channel_id=1, source_target_pairs={{0,1},{1,2},{2,3},{3,4},{4,5},{5,6},{6,7},{7,0},{8,9},{9,10},{10,1... | collective-permute-start | bytes 1572872 | tf_op jit(solution)/shard_map/ppermute | solution.py:44
  165.3 26.1 %copy-start.17 = (f32[8,16,15,128]{3,2,1,0:T(8,128)S(1)}, f32[8,16,15,128]{3,2,1,0:T(8,128)}, u32[]{:S(2)}) copy-start(f32[8,16,15,128]{3,2,1,0:T(8,128)} %get-tuple-element.75) | copy-start | bytes 2949124
  165.3 26.1 %copy-start.18 = (f32[8,16,15,128]{3,2,1,0:T(8,128)S(1)}, f32[8,16,15,128]{3,2,1,0:T(8,128)}, u32[]{:S(2)}) copy-start(f32[8,16,15,128]{3,2,1,0:T(8,128)} %get-tuple-element.76) | copy-start | bytes 2949124
  165.4 22.0 %slice-start = ((f32[4096,128]{1,0:T(8,128)}), f32[2048,128]{1,0:T(8,128)S(1)}, s32[]{:S(2)}) async-start(f32[4096,128]{1,0:T(8,128)} %scatter_custom_fusion.1), calls=%async_computation.2 | async-start | bytes 2097152 | tf_op jit(solution)/shard_map/slice | solution.py:97
  165.4 25.8 %collective-permute-start.7 = (f32[4,16,16,128]{3,2,1,0:T(8,128)S(1)}, f32[4,16,16,128]{3,2,1,0:T(8,128)S(1)}, u32[]{:S(2)}, u32[]{:S(2)}) collective-permute-start(f32[4,16,16,128]{3,2,1,0:T(8,128)S(1)} %bitcast.47), channel_id=1, source_target_pairs={{0,7},{1,0},{2,1},{3,2},{4,3},{5,4},{6,5},{7,6},{8,15},{9,8},{10,9... | collective-permute-start | bytes 1572872 | tf_op jit(solution)/shard_map/ppermute | solution.py:44
  169.9 21.4 %copy-start.16 = (f32[8,16,10,128]{3,2,1,0:T(8,128)S(1)}, f32[8,16,10,128]{3,2,1,0:T(8,128)}, u32[]{:S(2)}) copy-start(f32[8,16,10,128]{3,2,1,0:T(8,128)} %get-tuple-element.116) | copy-start | bytes 1966084
  170.0 21.3 %copy-start.14 = (f32[8,16,11,128]{3,2,1,0:T(8,128)S(1)}, f32[8,16,11,128]{3,2,1,0:T(8,128)}, u32[]{:S(2)}) copy-start(f32[8,16,11,128]{3,2,1,0:T(8,128)} %get-tuple-element.108) | copy-start | bytes 2162692
  170.0 21.3 %copy-start.15 = (f32[8,16,10,128]{3,2,1,0:T(8,128)S(1)}, f32[8,16,10,128]{3,2,1,0:T(8,128)}, u32[]{:S(2)}) copy-start(f32[8,16,10,128]{3,2,1,0:T(8,128)} %get-tuple-element.115) | copy-start | bytes 1966084
  170.1 21.3 %copy-start.11 = (f32[8,16,12,128]{3,2,1,0:T(8,128)S(1)}, f32[8,16,12,128]{3,2,1,0:T(8,128)}, u32[]{:S(2)}) copy-start(f32[8,16,12,128]{3,2,1,0:T(8,128)} %get-tuple-element.99) | copy-start | bytes 2359300
  170.1 21.3 %copy-start.12 = (f32[8,16,12,128]{3,2,1,0:T(8,128)S(1)}, f32[8,16,12,128]{3,2,1,0:T(8,128)}, u32[]{:S(2)}) copy-start(f32[8,16,12,128]{3,2,1,0:T(8,128)} %get-tuple-element.100) | copy-start | bytes 2359300
  170.1 21.3 %copy-start.13 = (f32[8,16,11,128]{3,2,1,0:T(8,128)S(1)}, f32[8,16,11,128]{3,2,1,0:T(8,128)}, u32[]{:S(2)}) copy-start(f32[8,16,11,128]{3,2,1,0:T(8,128)} %get-tuple-element.107) | copy-start | bytes 2162692
  170.1 21.3 %copy-start.32 = (f32[8,16,16]{2,1,0:T(8,128)S(1)}, f32[8,16,16]{2,1,0:T(8,128)}, u32[]{:S(2)}) copy-start(f32[8,16,16]{2,1,0:T(8,128)} %broadcast_multiply_fusion.1) | copy-start | bytes 24580
  (18 other events, 166.5 us)
Sparse Core Ops, SparseCore 0:
  244.8 126.3 all-reduce.1
where the time goes:
time: 380 us
  waiting for transfers between devices  197 us (52%)
  local copies, waits for them, and re-layouts  66.8 us (18%)
  other arithmetic  39.7 us (10%)
  blocking collectives  35.4 us (9%)
  starting transfers between devices  19.8 us (5%)
  between operations  14.7 us (4%)
  matrix products  6.76 us (2%)
    psum x1, waiting for transfers between devices, on_device(): gram_sum = lax.psum(full_gram, ('band', 'dom'))  127 us
    ppermute x4, waiting for transfers between devices, from_behind(): return lax.ppermute(value, axis, pairs)  37.8 us
    ppermute x2, waiting for transfers between devices, extended_2(): lax.ppermute(tail, axis, [(i, (i + 1) % count) for i in range(count)])  27.7 us
    slice x24, local copies, waits for them, and re-layouts, kinetic(): jnp.roll(wavefield, k, 2) + jnp.roll(wavefield, -k, 2)  27.6 us
    slice x24, local copies, waits for them, and re-layouts, kinetic(): jnp.roll(wavefield, k, 1) + jnp.roll(wavefield, -k, 1)  25.7 us
    psum x1, blocking collectives, on_device(): sq_own = lax.psum(jnp.sum(flat_rows * flat_rows, axis=0), 'dom')  18.3 us
    all_to_all x1, blocking collectives, on_device(): lax.all_to_all(source, 'band', split_axis=1, concat_axis=3, tiled=True)  17.1 us
    reduce_sum x1, other arithmetic, on_device(): sq_own = lax.psum(jnp.sum(flat_rows * flat_rows, axis=0), 'dom')  12.9 us
  transfers between devices with their start and end apart: 9, of which 9 were waited for; matrix products, arithmetic and copies ran while one was open for 10% of the time, Pallas kernels for 0%

commit v1 on v0

v1 whole, which is shorter than its diff:
```python
import functools

import jax
import jax.numpy as jnp
import numpy as np
from jax import lax
from jax.experimental import pallas as pl
from jax.experimental.pallas import tpu as pltpu
from jax.sharding import PartitionSpec as P

HALO = 6
REACH = 4
SLAB = 8
SIDE = 16
LAT = SIDE * SIDE
CHUNKS = 1

COEFFS = (
    -5369.0 / 1800.0,
    12.0 / 7.0,
    -15.0 / 56.0,
    10.0 / 189.0,
    -1.0 / 112.0,
    2.0 / 1925.0,
    -1.0 / 16632.0,
)
FILTER_LOWER = 5.0
FILTER_UPPER = 24.0
SPECTRUM_BOTTOM = 0.0
EPSILON = 1e-06

HALF_WIDTH = (FILTER_UPPER - FILTER_LOWER) / 2.0
CENTRE = (FILTER_UPPER + FILTER_LOWER) / 2.0
SIGMA_1 = HALF_WIDTH / (SPECTRUM_BOTTOM - CENTRE)
SIGMA_2 = 1.0 / (2.0 / SIGMA_1 - SIGMA_1)

VMEM_LIMIT = 48 * 1024 * 1024
BF16 = jnp.bfloat16
F32 = jnp.float32
NN = (((1,), (0,)), ((), ()))
NT = (((1,), (1,)), ((), ()))


def dot(a, b, dims=NN):
    return lax.dot_general(a, b, dims, preferred_element_type=F32)


def halves(x):
    hi = x.astype(BF16)
    return hi, (x - hi.astype(F32)).astype(BF16)


def dot3(ah, al, bh, bl, dims=NN):
    return dot(ah, bh, dims) + dot(al, bh, dims) + dot(ah, bl, dims)


def lateral_matrix():
    line = np.zeros((SIDE, SIDE))
    at = np.arange(SIDE)
    for k in range(1, HALO + 1):
        for sign in (1, -1):
            np.add.at(line, ((at + sign * k) % SIDE, at), -0.5 * COEFFS[k])
    eye = np.eye(SIDE)
    return np.kron(line, eye) + np.kron(eye, line)


def relation():
    return [[-1, 0] if q < REACH else [0, 1] for q in range(SLAB)]


def fold_matrix():
    out = np.zeros((256, 384), np.float32)
    for q, pair in enumerate(relation()):
        for half, rel in enumerate(pair):
            for r in range(16):
                out[q * 32 + half * 16 + r, (rel + 1) * 128 + r] = 1.0
    return out


def split_const(matrix):
    matrix = np.asarray(matrix, np.float32)
    hi = jnp.asarray(matrix, F32).astype(BF16)
    lo = (jnp.asarray(matrix, F32) - hi.astype(F32)).astype(BF16)
    return hi, lo


def split_kernel(nd, nb, chunks, pos_ref, x_ref, *refs):
    outs, scratch = refs[:-1], refs[-1]
    i = pos_ref[0]
    for q in range(SLAB):
        scratch[q] = x_ref[q].T
    real = scratch.shape[1] // (nd * chunks)
    for c in range(chunks):
        for j in range(nd):
            start = c * nd * real + (i ^ j) * real
            for q in range(SLAB):
                outs[c * nd + j][q * nb : (q + 1) * nb] = scratch[q, pl.ds(pl.multiple_of(start, nb), nb)]


def weights_kernel(nd, pos_ref, *refs):
    parts, (wh_ref, wl_ref, v_ref, scratch) = refs[:4], refs[4:]
    i, b = pos_ref[0], pos_ref[1]
    for jb in range(4):
        rows = pl.ds(pl.multiple_of((b ^ jb) * 8, 8), 8)
        for j in range(nd):
            scratch[i ^ j, rows] = parts[jb][j]
    lat = lax.broadcasted_iota(jnp.int32, (LAT, 256), 0).astype(F32)
    plane = lax.broadcasted_iota(jnp.int32, (16, 1, 1), 0).astype(F32)
    diagonal = -1.5 * COEFFS[0] - CENTRE

    def body(s, carry):
        his, los = [], []
        for a in range(2):
            w = scratch[s, a * 8 : a * 8 + 8]
            px = scratch[s, 16 + a : 17 + a]
            place = scratch[s, 18 + a : 19 + a]
            hot = jnp.where(lat == place, 1.0, 0.0).astype(BF16)
            masked = jnp.where(px[None] == plane, w[None], 0.0).reshape(128, 256)
            mh, ml = halves(masked)
            his.append(dot(mh, hot, NT).reshape(16, 8, LAT))
            los.append(dot(ml, hot, NT).reshape(16, 8, LAT))
        hi = jnp.concatenate(his, axis=1).astype(BF16)
        lo = jnp.concatenate(los, axis=1).astype(BF16)
        for t in range(16):
            p = (s * SLAB - REACH + t + nd * SLAB) % (nd * SLAB) if isinstance(s, int) else lax.rem(
                s * SLAB - REACH + t + nd * SLAB, nd * SLAB
            )
            row = pl.ds(pl.multiple_of(p * 32 + (16 if t < SLAB else 0), 16), 16)
            wh_ref[row] = hi[t]
            wl_ref[row] = lo[t]
        v_ref[pl.ds(pl.multiple_of(s * SLAB, SLAB), SLAB)] = scratch[s, 24:32] + diagonal
        return carry

    if nd <= 8:
        for s in range(nd):
            body(s, 0)
    else:
        lax.fori_loop(0, nd, body, 0)


def filter_kernel(nd, nb, total, pos_ref, kb_ref, v_ref, wh_ref, wl_ref, lh_ref, ll_ref, fold_ref, spread_ref, *refs):
    pieces, outs = refs[:nd], refs[nd : 2 * nd]
    f0_ref, f1_ref, fold_out, spread_out = refs[2 * nd :]
    i = pos_ref[0]
    R = SLAB * nb
    rows_q = lax.broadcasted_iota(jnp.int32, (SLAB, nb, 256), 0)
    lanes_q = lax.broadcasted_iota(jnp.int32, (SLAB, nb, 256), 2) // 32
    same = rows_q == lanes_q

    def slab_rows(s, k=0):
        return pl.ds(pl.multiple_of((s * SLAB + HALO + k) * nb, nb), R)

    def wrap(ref):
        ref[0 : HALO * nb] = ref[nd * R : nd * R + HALO * nb]
        ref[HALO * nb + nd * R : 2 * HALO * nb + nd * R] = ref[HALO * nb : 2 * HALO * nb]

    def each(body):
        if nd <= 8:
            for s in range(nd):
                body(s)
        else:
            lax.fori_loop(0, nd, lambda s, c: (body(s), c)[1], 0)

    for j in range(nd):
        f0_ref[slab_rows(i ^ j)] = pieces[j][...]
    wrap(f0_ref)

    def apply(ref, finish):
        def project(s):
            fh, fl = halves(ref[slab_rows(s)])
            w = pl.ds(pl.multiple_of(s * 256, 256), 256)
            g = dot3(fh, fl, wh_ref[w], wl_ref[w], NT).reshape(SLAB, nb, 256)
            fold_out[pl.ds(pl.multiple_of(s * nb, nb), nb)] = jnp.sum(jnp.where(same, g, 0.0), axis=0)

        each(project)
        gh, gl = halves(fold_out[...])
        h = dot(gh, fold_ref[...]) + dot(gl, fold_ref[...])
        below, at, above = h[:, :128], h[:, 128:256], h[:, 256:]

        def next_slab(x):
            return jnp.concatenate([x[-nb:], x[:-nb]], axis=0)

        def previous_slab(x):
            return jnp.concatenate([x[nb:], x[:nb]], axis=0)

        p = (at + next_slab(above) + previous_slab(below)) * kb_ref[...]
        wide = jnp.concatenate([next_slab(p), p, previous_slab(p)], axis=1)
        ph, plo = halves(wide)
        spread_out[...] = dot(ph, spread_ref[...], NT) + dot(plo, spread_ref[...], NT)

        def step(s):
            f = ref[slab_rows(s)]
            fh, fl = halves(f)
            x = jnp.where(same, spread_out[pl.ds(pl.multiple_of(s * nb, nb), nb)][None], 0.0).reshape(R, 256)
            xh, xl = halves(x)
            w = pl.ds(pl.multiple_of(s * 256, 256), 256)
            acc = dot3(xh, xl, wh_ref[w], wl_ref[w]) + dot3(fh, fl, lh_ref[...], ll_ref[...])
            v = v_ref[pl.ds(pl.multiple_of(s * SLAB, SLAB), SLAB)]
            acc = acc + (f.reshape(SLAB, nb, LAT) * v[:, None, :]).reshape(R, LAT)
            for k in range(1, HALO + 1):
                acc = acc + (-0.5 * COEFFS[k]) * (ref[slab_rows(s, k)] + ref[slab_rows(s, -k)])
            finish(s, acc)

        each(step)

    def first(s, acc):
        f1_ref[slab_rows(s)] = (SIGMA_1 / HALF_WIDTH) * acc

    apply(f0_ref, first)
    wrap(f1_ref)

    def second(s, acc):
        f0_ref_new = (2.0 * SIGMA_2 / HALF_WIDTH) * acc - (SIGMA_1 * SIGMA_2) * f0_ref[slab_rows(s)]
        y2_store(s, f0_ref_new)

    def y2_store(s, value):
        f0_ref[slab_rows(s)] = value

    apply(f1_ref, second)
    square = jnp.zeros((nb, LAT), F32)
    if nd <= 8:
        for s in range(nd):
            y = f0_ref[slab_rows(s)].reshape(SLAB, nb, LAT)
            square = square + jnp.sum(y * y, axis=0)
    else:

        def add(s, total_square):
            y = f0_ref[slab_rows(s)].reshape(SLAB, nb, LAT)
            return total_square + jnp.sum(y * y, axis=0)

        square = lax.fori_loop(0, nd, add, square)
    scale = 1.0 / jnp.sqrt(jnp.sum(square, axis=1, keepdims=True) / total + EPSILON)
    for j in range(nd):
        y = f0_ref[slab_rows(i ^ j)].reshape(SLAB, nb, LAT)
        outs[j][...] = (y * scale[None]).reshape(R, LAT)


def join_kernel(nd, nb, real, pos_ref, *refs):
    pieces, (z_ref, send_ref) = refs[:nd], refs[nd:]
    i, y = pos_ref[0], pos_ref[2]
    for j in range(nd):
        rows = pl.ds(pl.multiple_of((i ^ j) * real, real), real)
        for q in range(SLAB):
            z_ref[q, rows] = pieces[j][q * nb : q * nb + real]
    half = SLAB // 2
    for q in range(half):
        send_ref[q] = z_ref[(1 - y) * half + q]


def gram_kernel(chunks, pos_ref, *refs):
    own, core, far, far_core = (refs[k * chunks : (k + 1) * chunks] for k in range(4))
    g_ref, far_ref = refs[4 * chunks :]
    b, y = pos_ref[1], pos_ref[2]
    half = SLAB // 2

    def load(group, q):
        return halves(jnp.concatenate([r[q] for r in group], axis=0))

    def add(totals, place, value):
        totals[place] = value if totals.get(place) is None else totals[place] + value

    totals = {}
    for q in range(half):
        for mine in (True, False):
            at = q + y * half if mine else q + (1 - y) * half
            zh, zl = load(own, at)
            ch, cl = load(core, at)
            add(totals, "own", dot3(zh, zl, zh, zl, NT))
            add(totals, "core", dot3(zh, zl, ch, cl, NT))
            if mine:
                fh, fl = load(far, q)
                gh, gl = load(far_core, q)
                add(totals, "far", dot3(zh, zl, fh, fl, NT))
                add(totals, "far_core", dot3(zh, zl, gh, gl, NT))
                add(totals, "back", dot3(fh, fl, zh, zl, NT))
                add(totals, "back_core", dot3(fh, fl, ch, cl, NT))
    g_ref[b] = totals["own"]
    g_ref[b ^ 1] = totals["core"]
    g_ref[b ^ 2] = totals["far"]
    g_ref[b ^ 3] = totals["far_core"]
    far_ref[b & 1] = totals["back"]
    far_ref[(b & 1) ^ 1] = totals["back_core"]


def output_kernel(chunks, *refs):
    zs, out_ref = refs[:chunks], refs[chunks]
    for q in range(SLAB):
        out_ref[q] = jnp.concatenate([z[q] for z in zs], axis=0).T


def part_kernel(nd, pos_ref, g_ref, far_ref, *outs):
    i, y = pos_ref[0], pos_ref[2]
    size = outs[0].shape[1]
    for j in range(nd):
        rows = pl.ds(pl.multiple_of((i ^ j) * size, size), size)
        for c in range(2):
            outs[j][y * 2 + c] = g_ref[y * 2 + c, rows]
            outs[j][(1 - y) * 2 + c] = g_ref[(1 - y) * 2 + c, rows] + far_ref[c, rows]


def sum_kernel(total, *refs):
    acc = refs[0][...]
    for r in refs[1:-1]:
        acc = acc + r[...]
    refs[-1][...] = acc * (1.0 / total)


def place_kernel(nd, pos_ref, *refs):
    pieces, out_ref = refs[:nd], refs[nd]
    i = pos_ref[0]
    size = pieces[0].shape[1]
    for j in range(nd):
        rows = pl.ds(pl.multiple_of((i ^ j) * size, size), size)
        for k in range(4):
            out_ref[rows, k * 128 : (k + 1) * 128] = pieces[j][k]


def call(kernel, out_shape, operands, scratch=(), name=None):
    specs = [
        pl.BlockSpec(memory_space=pltpu.SMEM) if o.dtype == jnp.int32 else pl.BlockSpec(memory_space=pltpu.VMEM)
        for o in operands
    ]
    single = not isinstance(out_shape, (list, tuple))
    return pl.pallas_call(
        kernel,
        out_shape=out_shape,
        in_specs=specs,
        out_specs=(
            pl.BlockSpec(memory_space=pltpu.VMEM)
            if single
            else [pl.BlockSpec(memory_space=pltpu.VMEM) for _ in out_shape]
        ),
        scratch_shapes=list(scratch),
        compiler_params=pltpu.CompilerParams(vmem_limit_bytes=VMEM_LIMIT),
        name=name,
    )(*operands)


def shape(*dims, dtype=F32):
    return jax.ShapeDtypeStruct(dims, dtype)


def xor_permute(value, axis, step):
    count = lax.axis_size(axis)
    return lax.ppermute(value, axis, [(k, k ^ step) for k in range(count)])


def swap_all(pieces, direct):
    if direct:
        return [pieces[0]] + [xor_permute(p, "dom", j) for j, p in enumerate(pieces) if j]
    stacked = lax.all_to_all(jnp.stack(pieces), "dom", 0, 0, tiled=True)
    return [stacked[j] for j in range(len(pieces))]


def packed_atoms(potential, proj_weights, atom_cell, point_codes):
    cube = 2 * REACH + 1
    off_x = point_codes // (cube * cube)
    off_y = point_codes // cube % cube
    off_z = point_codes % cube
    plane = atom_cell[:, 0:1] % SLAB + off_x
    cell_y = (atom_cell[:, 1:2] + off_y - REACH) % SIDE
    cell_z = (atom_cell[:, 2:3] + off_z - REACH) % SIDE
    lateral = cell_y * SIDE + cell_z
    return jnp.concatenate(
        [
            proj_weights.reshape(-1, 256),
            plane.astype(F32),
            lateral.astype(F32),
            jnp.zeros((4, 256), F32),
            potential.reshape(SLAB, LAT),
        ],
        axis=0,
    )


def on_device(trial_waves, potential, proj_weights, kb_energy, atom_cell, point_codes):
    nd = lax.axis_size("dom")
    bands = trial_waves.shape[-1]
    direct = nd == 8
    chunks = CHUNKS if direct else 1
    real = bands // (nd * chunks)
    nb = max(real, 8)
    total = nd * SLAB * LAT
    dom = lax.axis_index("dom") if direct else jnp.int32(0)
    band = lax.axis_index("band")
    pos = jnp.stack([dom, band if direct else jnp.int32(0), band // 2]).astype(jnp.int32)
    pos_band = jnp.stack([dom, band, band // 2]).astype(jnp.int32)
    R = SLAB * nb

    packed = packed_atoms(potential, proj_weights, atom_cell, point_codes)
    if direct:
        mine = lax.dynamic_slice_in_dim(packed, band * 8, 8, 0)
        gathered = jnp.stack([mine] + [xor_permute(mine, "dom", j) for j in range(1, nd)])
        parts = [gathered] + [xor_permute(gathered, "band", j) for j in range(1, 4)]
    else:
        gathered = lax.all_gather(packed, "dom", axis=0)
        parts = [gathered[:, k * 8 : k * 8 + 8] for k in range(4)]

    waves = trial_waves.reshape(SLAB, LAT, bands)
    if direct:
        cut = call(
            functools.partial(split_kernel, nd, nb, chunks),
            [shape(R, LAT)] * (nd * chunks),
            [pos, waves],
            [pltpu.VMEM((SLAB, bands, LAT), F32)],
            "split",
        )
    else:
        turned = waves.transpose(0, 2, 1).reshape(SLAB, nd, real, LAT).transpose(1, 0, 2, 3)
        cut = [turned[j] for j in range(nd)]

    wh, wl, shifted = call(
        functools.partial(weights_kernel, nd),
        [shape(nd * 256, 256, dtype=BF16), shape(nd * 256, 256, dtype=BF16), shape(nd * SLAB, LAT)],
        [pos] + parts,
        [pltpu.VMEM((nd, 32, 256), F32)],
        "weights",
    )
    lh, ll = split_const(lateral_matrix())
    fold = jnp.asarray(fold_matrix()).astype(BF16)
    kb_row = jnp.concatenate([kb_energy, kb_energy, jnp.zeros((112,), F32)])[None]
    spread = fold
    arrived = [swap_all(cut[c * nd : (c + 1) * nd], direct) for c in range(chunks)]
    joined, sends = [], []
    for c in range(chunks):
        pieces = arrived[c]
        if not direct:
            pieces = [jnp.pad(p, ((0, 0), (0, nb - real), (0, 0))).reshape(R, LAT) for p in pieces]
        ready = call(
            functools.partial(filter_kernel, nd, nb, float(total)),
            [shape(R, LAT)] * nd,
            [pos, kb_row, shifted, wh, wl, lh, ll, fold, spread] + pieces,
            [
                pltpu.VMEM(((nd * SLAB + 2 * HALO) * nb, LAT), F32),
                pltpu.VMEM(((nd * SLAB + 2 * HALO) * nb, LAT), F32),
                pltpu.VMEM((nd * nb, 256), F32),
                pltpu.VMEM((nd * nb, 256), F32),
            ],
            "filter",
        )
        if not direct:
            ready = [p.reshape(SLAB, nb, LAT)[:, :real] for p in ready]
        back = swap_all(ready, direct)
        if direct:
            z, send = call(
                functools.partial(join_kernel, nd, nb, real),
                [shape(SLAB, nd * real, LAT), shape(SLAB // 2, nd * real, LAT)],
                [pos_band] + back,
                (),
                "join",
            )
        else:
            z = jnp.concatenate(back, axis=1)
            send = lax.dynamic_slice_in_dim(z, (1 - band // 2) * (SLAB // 2), SLAB // 2, 0)
        joined.append(z)
        sends.append(send)

    core = [xor_permute(z, "band", 1) for z in joined]
    far = [xor_permute(s, "band", 2) for s in sends]
    far_core = [xor_permute(s, "band", 1) for s in far]
    gram, gram_far = call(
        functools.partial(gram_kernel, chunks),
        [shape(4, bands, bands), shape(2, bands, bands)],
        [pos_band] + joined + core + far + far_core,
        (),
        "gram",
    )
    far_share = xor_permute(gram_far, "band", 2)
    filtered = call(functools.partial(output_kernel, chunks), shape(SLAB, LAT, bands), joined, (), "output")
    if direct:
        size = bands // nd
        cut_gram = call(
            functools.partial(part_kernel, nd),
            [shape(4, size, bands)] * nd,
            [pos_band, gram, far_share],
            (),
            "part",
        )
        summed = call(
            functools.partial(sum_kernel, float(total)), shape(4, size, bands), swap_all(cut_gram, direct), (), "sum"
        )
        everyone = [summed] + [xor_permute(summed, "dom", j) for j in range(1, nd)]
        correlation = call(
            functools.partial(place_kernel, nd), shape(bands, 4 * bands), [pos_band] + everyone, (), "place"
        )
    else:
        start = (1 - band // 2) * 2
        cross = lax.dynamic_slice_in_dim(gram, start, 2, 0) + far_share
        gram = lax.dynamic_update_slice_in_dim(gram, cross, start, 0)
        wide = gram.transpose(1, 0, 2).reshape(bands, 4 * bands)
        correlation = lax.psum(wide, "dom") / total
    return filtered.reshape(trial_waves.shape), correlation


def solution(mesh):
    return jax.shard_map(
        on_device,
        mesh=mesh,
        in_specs=(
            P("dom", None, None, "band"),
            P("dom", None, None),
            P("dom", None, None),
            P(),
            P("dom", None),
            P("dom", None),
        ),
        out_specs=(P("dom", None, None, "band"), P("band", None)),
        check_vma=False,
    )
```

time: 380 us -> 145 us (0.38)
  waiting for transfers between devices: 197 us -> 54.8 us
  local copies, waits for them, and re-layouts: 66.8 us -> 3.51 us
  starting transfers between devices: 19.8 us -> 67.7 us
  other arithmetic: 39.7 us -> 0.45 us
  blocking collectives: 35.4 us -> 0 us
  Pallas kernels: 0 us -> 17.1 us
  between operations: 14.7 us -> 0.88 us
  matrix products: 6.76 us -> 0 us
    psum x1 -> x0, waiting for transfers between devices: 127 us -> none  [on_device(): gram_sum = lax.psum(full_gram, ('band', 'dom'))]
    slice x56 -> x0, local copies, waits for them, and re-layouts: 56.7 us -> none  [the longest x24 27.6 us: kinetic(): jnp.roll(wavefield, k, 2) + jnp.roll(wavefield, -k, 2)]
    ppermute x8 -> x42, starting transfers between devices: 19.7 us -> 67.7 us  [xor_permute(): return lax.ppermute(value, axis, [(k, k ^ step) for k in range(count)])]
    psum x1 -> x0, blocking collectives: 18.3 us -> none  [on_device(): sq_own = lax.psum(jnp.sum(flat_rows * flat_rows, axis=0), 'dom')]
    all_to_all x1 -> x0, blocking collectives: 17.1 us -> none  [on_device(): lax.all_to_all(source, 'band', split_axis=1, concat_axis=3, tiled=True)]
    pallas_call x0 -> x9, Pallas kernels: none -> 17.1 us  [call(): pl.pallas_call(kernel, out_shape=out_shape, in_specs=specs, out_specs=pl....]
    ppermute x8 -> x42, waiting for transfers between devices: 70.2 us -> 54.8 us  [xor_permute(): return lax.ppermute(value, axis, [(k, k ^ step) for k in range(count)])]
    reduce_sum x1 -> x0, other arithmetic: 12.9 us -> none  [on_device(): sq_own = lax.psum(jnp.sum(flat_rows * flat_rows, axis=0), 'dom')]
  transfers between devices with their start and end apart: 9 -> 42, of which waited for: 9 -> 15; matrix products, arithmetic and copies ran while one was open for 10% -> 0% of each run, Pallas kernels for 0% -> 3%
where the time goes in v1:
time: 145 us; the launch traced here: 144 us
  starting transfers between devices  67.7 us (47%)
  waiting for transfers between devices  54.8 us (38%)
  Pallas kernels  17.1 us (12%)
  local copies, waits for them, and re-layouts  3.51 us (2%)
    ppermute x42, starting transfers between devices, xor_permute(): return lax.ppermute(value, axis, [(k, k ^ step) for k in range(count)])  67.7 us
    ppermute x42, waiting for transfers between devices, xor_permute(): return lax.ppermute(value, axis, [(k, k ^ step) for k in range(count)])  54.8 us
    pallas_call x9, Pallas kernels, call(): pl.pallas_call(kernel, out_shape=out_shape, in_specs=specs, out_specs=pl....  17.1 us
  transfers between devices with their start and end apart: 42, of which 15 were waited for; matrix products, arithmetic and copies ran while one was open for 0% of the time, Pallas kernels for 3%

profile of v1, /device:TPU:0, one launch (start us, length us, event | category | flops | bytes accessed | tf_op | source)
XLA Modules:
  0.0 144.4 jit_solution(13992084865012243257)
XLA Ops:
  3.2 3.0 %collective-permute-start = (f32[8,256]{1,0:T(8,128)S(1)}, f32[8,256]{1,0:T(8,128)S(1)}, u32[]{:S(2)}, u32[]{:S(2)}) collective-permute-start(f32[8,256]{1,0:T(8,128)S(1)} %get-tuple-element.68), channel_id=1, source_target_pairs={{0,1},{1,0},{2,3},{3,2},{4,5},{5,4},{6,7},{7,6},{8,9},{9,8},{10,11... | collective-permute-start | bytes 24584 | tf_op jit(solution)/shard_map/ppermute | solution.py:345
  6.2 1.6 %collective-permute-start.1 = (f32[8,256]{1,0:T(8,128)S(1)}, f32[8,256]{1,0:T(8,128)S(1)}, u32[]{:S(2)}, u32[]{:S(2)}) collective-permute-start(f32[8,256]{1,0:T(8,128)S(1)} %get-tuple-element.68), channel_id=1, source_target_pairs={{0,2},{1,3},{2,0},{3,1},{4,6},{5,7},{6,4},{7,5},{8,10},{9,11},{10,... | collective-permute-start | bytes 24584 | tf_op jit(solution)/shard_map/ppermute | solution.py:345
  7.8 3.0 %collective-permute-start.3 = (f32[8,256]{1,0:T(8,128)S(1)}, f32[8,256]{1,0:T(8,128)S(1)}, u32[]{:S(2)}, u32[]{:S(2)}) collective-permute-start(f32[8,256]{1,0:T(8,128)S(1)} %get-tuple-element.68), channel_id=1, source_target_pairs={{0,4},{1,5},{2,6},{3,7},{4,0},{5,1},{6,2},{7,3},{8,12},{9,13},{10,... | collective-permute-start | bytes 24584 | tf_op jit(solution)/shard_map/ppermute | solution.py:345
  14.4 3.7 %collective-permute-start.5 = (f32[8,256]{1,0:T(8,128)S(1)}, f32[8,256]{1,0:T(8,128)S(1)}, u32[]{:S(2)}, u32[]{:S(2)}) collective-permute-start(f32[8,256]{1,0:T(8,128)S(1)} %get-tuple-element.68), channel_id=1, source_target_pairs={{0,6},{1,7},{2,4},{3,5},{4,2},{5,3},{6,0},{7,1},{8,14},{9,15},{10,... | collective-permute-start | bytes 24584 | tf_op jit(solution)/shard_map/ppermute | solution.py:345
  18.1 1.7 %collective-permute-start.10 = (f32[128,256]{1,0:T(8,128)S(1)}, f32[128,256]{1,0:T(8,128)S(1)}, u32[]{:S(2)}, u32[]{:S(2)}) collective-permute-start(f32[128,256]{1,0:T(8,128)S(1)} %get-tuple-element.37), channel_id=1, source_target_pairs={{0,1},{1,0},{2,3},{3,2},{4,5},{5,4},{6,7},{7,6},{8,9},{9,8},{10,11... | collective-permute-start | bytes 393224 | tf_op jit(solution)/shard_map/ppermute | solution.py:345
  19.9 4.7 %collective-permute-done.6 = f32[8,256]{1,0:T(8,128)S(1)} collective-permute-done((f32[8,256]{1,0:T(8,128)S(1)}, f32[8,256]{1,0:T(8,128)S(1)}, u32[]{:S(2)}, u32[]{:S(2)}) %collective-permute-start.6) | collective-permute-done | bytes 8224 | tf_op jit(solution)/shard_map/ppermute | solution.py:345
  26.4 2.6 %collective-permute-done.8.refs_2_ = f32[8,8,256]{2,1,0:T(8,128)S(1)} collective-permute-done((f32[8,8,256]{2,1,0:T(8,128)S(1)}, f32[8,8,256]{2,1,0:T(8,128)S(1)}, u32[]{:S(2)}, u32[]{:S(2)}) %collective-permute-start.8) | collective-permute-done | bytes 65568 | tf_op jit(solution)/shard_map/ppermute | solution.py:345
  30.1 1.8 %collective-permute-start.14 = (f32[128,256]{1,0:T(8,128)S(1)}, f32[128,256]{1,0:T(8,128)S(1)}, u32[]{:S(2)}, u32[]{:S(2)}) collective-permute-start(f32[128,256]{1,0:T(8,128)S(1)} %get-tuple-element.41), channel_id=1, source_target_pairs={{0,5},{1,4},{2,7},{3,6},{4,1},{5,0},{6,3},{7,2},{8,13},{9,12},{10,... | collective-permute-start | bytes 393224 | tf_op jit(solution)/shard_map/ppermute | solution.py:345
  32.1 4.6 %collective-permute-start.16 = (f32[128,256]{1,0:T(8,128)S(1)}, f32[128,256]{1,0:T(8,128)S(1)}, u32[]{:S(2)}, u32[]{:S(2)}) collective-permute-start(f32[128,256]{1,0:T(8,128)S(1)} %get-tuple-element.43), channel_id=1, source_target_pairs={{0,7},{1,6},{2,5},{3,4},{4,3},{5,2},{6,1},{7,0},{8,15},{9,14},{10,... | collective-permute-start | bytes 393224 | tf_op jit(solution)/shard_map/ppermute | solution.py:345
  36.8 2.1 %weights.1 = (bf16[2048,256]{1,0:T(8,128)(2,1)S(1)}, bf16[2048,256]{1,0:T(8,128)(2,1)S(1)}, f32[64,256]{1,0:T(8,128)S(1)}) custom-call(s32[3]{0:T(128)S(1)} %pad_add_fusion.pos_ref, f32[8,8,256]{2,1,0:T(8,128)S(1)} %constant_dynamic-update-slice_fusion.refs_0_, f32[8,8,256]{2,1,0:T(8,128)S(1)} %collective-permute-done.7.refs_1_, ...), custom_call_target="tpu_custom_call" | custom-call | tf_op jit(solution)/shard_map/weights/pallas_call | solution.py:324
  39.0 6.5 %collective-permute-done.13.refs_4_ = f32[128,256]{1,0:T(8,128)S(1)} collective-permute-done((f32[128,256]{1,0:T(8,128)S(1)}, f32[128,256]{1,0:T(8,128)S(1)}, u32[]{:S(2)}, u32[]{:S(2)}) %collective-permute-start.13) | collective-permute-done | bytes 131104 | tf_op jit(solution)/shard_map/ppermute | solution.py:345
  45.5 3.7 %collective-permute-done.14.refs_5_ = f32[128,256]{1,0:T(8,128)S(1)} collective-permute-done((f32[128,256]{1,0:T(8,128)S(1)}, f32[128,256]{1,0:T(8,128)S(1)}, u32[]{:S(2)}, u32[]{:S(2)}) %collective-permute-start.14) | collective-permute-done | bytes 131104 | tf_op jit(solution)/shard_map/ppermute | solution.py:345
  49.3 7.8 %filter.1 = (f32[128,256]{1,0:T(8,128)S(1)}, f32[128,256]{1,0:T(8,128)S(1)}, f32[128,256]{1,0:T(8,128)S(1)}, f32[128,256]{1,0:T(8,128)S(1)}, f32[128,256]{1,0:T(...) custom-call(s32[3]{0:T(128)S(1)} %pad_add_fusion.pos_ref, ...), custom_call_target="tpu_custom_call" | custom-call | tf_op jit(solution)/shard_map/filter/pallas_call | solution.py:324
  57.7 6.1 %collective-permute-start.18 = (f32[128,256]{1,0:T(8,128)S(1)}, f32[128,256]{1,0:T(8,128)S(1)}, u32[]{:S(2)}, u32[]{:S(2)}) collective-permute-start(f32[128,256]{1,0:T(8,128)S(1)} %get-tuple-element.46), channel_id=1, source_target_pairs={{0,2},{1,3},{2,0},{3,1},{4,6},{5,7},{6,4},{7,5},{8,10},{9,11},{10,... | collective-permute-start | bytes 393224 | tf_op jit(solution)/shard_map/ppermute | solution.py:345
  65.6 2.0 %collective-permute-start.21 = (f32[128,256]{1,0:T(8,128)S(1)}, f32[128,256]{1,0:T(8,128)S(1)}, u32[]{:S(2)}, u32[]{:S(2)}) collective-permute-start(f32[128,256]{1,0:T(8,128)S(1)} %get-tuple-element.49), channel_id=1, source_target_pairs={{0,5},{1,4},{2,7},{3,6},{4,1},{5,0},{6,3},{7,2},{8,13},{9,12},{10,... | collective-permute-start | bytes 393224 | tf_op jit(solution)/shard_map/ppermute | solution.py:345
  69.1 3.3 %collective-permute-start.23 = (f32[128,256]{1,0:T(8,128)S(1)}, f32[128,256]{1,0:T(8,128)S(1)}, u32[]{:S(2)}, u32[]{:S(2)}) collective-permute-start(f32[128,256]{1,0:T(8,128)S(1)} %get-tuple-element.51), channel_id=1, source_target_pairs={{0,7},{1,6},{2,5},{3,4},{4,3},{5,2},{6,1},{7,0},{8,15},{9,14},{10,... | collective-permute-start | bytes 393224 | tf_op jit(solution)/shard_map/ppermute | solution.py:345
  73.4 9.7 %collective-permute-done.20.refs_4_ = f32[128,256]{1,0:T(8,128)S(1)} collective-permute-done((f32[128,256]{1,0:T(8,128)S(1)}, f32[128,256]{1,0:T(8,128)S(1)}, u32[]{:S(2)}, u32[]{:S(2)}) %collective-permute-start.20) | collective-permute-done | bytes 131104 | tf_op jit(solution)/shard_map/ppermute | solution.py:345
  83.1 2.8 %collective-permute-done.21.refs_5_ = f32[128,256]{1,0:T(8,128)S(1)} collective-permute-done((f32[128,256]{1,0:T(8,128)S(1)}, f32[128,256]{1,0:T(8,128)S(1)}, u32[]{:S(2)}, u32[]{:S(2)}) %collective-permute-start.21) | collective-permute-done | bytes 131104 | tf_op jit(solution)/shard_map/ppermute | solution.py:345
  86.6 1.6 %collective-permute-start.25 = (f32[4,128,256]{2,1,0:T(8,128)S(1)}, f32[4,128,256]{2,1,0:T(8,128)S(1)}, u32[]{:S(2)}, u32[]{:S(2)}) collective-permute-start(f32[4,128,256]{2,1,0:T(8,128)S(1)} %get-tuple-element.53), channel_id=1, source_target_pairs={{0,16},{8,24},{16,0},{24,8},{1,17},{9,25},{17,1},{25,9},{2,18},{10... | collective-permute-start | bytes 1572872 | tf_op jit(solution)/shard_map/ppermute | solution.py:345
  88.2 9.3 %collective-permute-done.25.refs_2_ = f32[4,128,256]{2,1,0:T(8,128)S(1)} collective-permute-done((f32[4,128,256]{2,1,0:T(8,128)S(1)}, f32[4,128,256]{2,1,0:T(8,128)S(1)}, u32[]{:S(2)}, u32[]{:S(2)}) %collective-permute-start.25) | collective-permute-done | bytes 524320 | tf_op jit(solution)/shard_map/ppermute | solution.py:345
  97.5 1.9 %collective-permute-done.26.refs_3_ = f32[4,128,256]{2,1,0:T(8,128)S(1)} collective-permute-done((f32[4,128,256]{2,1,0:T(8,128)S(1)}, f32[4,128,256]{2,1,0:T(8,128)S(1)}, u32[]{:S(2)}, u32[]{:S(2)}) %collective-permute-start.26) | collective-permute-done | bytes 524320 | tf_op jit(solution)/shard_map/ppermute | solution.py:345
  99.4 2.4 %gram.1 = (f32[4,128,128]{2,1,0:T(8,128)S(1)}, f32[2,128,128]{2,1,0:T(8,128)S(1)}) custom-call(s32[3]{0:T(128)S(1)} %pad_add_fusion.pos_ref, f32[8,128,256]{2,1,0:T(8,128)S(1)} %get-tuple-element.52.refs_0_, f32[8,128,256]{2,1,0:T(8,128)S(1)} %collective-permute-done.24.refs_1_, f32[4,128,256]{2,1,0:T(8,128)S(1)} %collective-permute-done.25.refs_2_, ...), custom_call_target="tpu_custom_call" | custom-call | tf_op jit(solution)/shard_map/gram/pallas_call | solution.py:324
  101.8 1.6 %collective-permute-start.27 = (f32[2,128,128]{2,1,0:T(8,128)S(1)}, f32[2,128,128]{2,1,0:T(8,128)S(1)}, u32[]{:S(2)}, u32[]{:S(2)}) collective-permute-start(f32[2,128,128]{2,1,0:T(8,128)S(1)} %get-tuple-element.55), channel_id=1, source_target_pairs={{0,16},{8,24},{16,0},{24,8},{1,17},{9,25},{17,1},{25,9},{2,18},{10... | collective-permute-start | bytes 393224 | tf_op jit(solution)/shard_map/ppermute | solution.py:345
  103.4 4.0 %collective-permute-done.27.far_ref = f32[2,128,128]{2,1,0:T(8,128)S(1)} collective-permute-done((f32[2,128,128]{2,1,0:T(8,128)S(1)}, f32[2,128,128]{2,1,0:T(8,128)S(1)}, u32[]{:S(2)}, u32[]{:S(2)}) %collective-permute-start.27) | collective-permute-done | bytes 131104 | tf_op jit(solution)/shard_map/ppermute | solution.py:345
  109.5 6.2 %collective-permute-start.29 = (f32[4,16,128]{2,1,0:T(8,128)S(1)}, f32[4,16,128]{2,1,0:T(8,128)S(1)}, u32[]{:S(2)}, u32[]{:S(2)}) collective-permute-start(f32[4,16,128]{2,1,0:T(8,128)S(1)} %get-tuple-element.58), channel_id=1, source_target_pairs={{0,2},{1,3},{2,0},{3,1},{4,6},{5,7},{6,4},{7,5},{8,10},{9,11},{10,... | collective-permute-start | bytes 98312 | tf_op jit(solution)/shard_map/ppermute | solution.py:345
  115.7 2.4 %collective-permute-start.31 = (f32[4,16,128]{2,1,0:T(8,128)S(1)}, f32[4,16,128]{2,1,0:T(8,128)S(1)}, u32[]{:S(2)}, u32[]{:S(2)}) collective-permute-start(f32[4,16,128]{2,1,0:T(8,128)S(1)} %get-tuple-element.60), channel_id=1, source_target_pairs={{0,4},{1,5},{2,6},{3,7},{4,0},{5,1},{6,2},{7,3},{8,12},{9,13},{10,... | collective-permute-start | bytes 98312 | tf_op jit(solution)/shard_map/ppermute | solution.py:345
  119.5 2.3 %collective-permute-start.33 = (f32[4,16,128]{2,1,0:T(8,128)S(1)}, f32[4,16,128]{2,1,0:T(8,128)S(1)}, u32[]{:S(2)}, u32[]{:S(2)}) collective-permute-start(f32[4,16,128]{2,1,0:T(8,128)S(1)} %get-tuple-element.62), channel_id=1, source_target_pairs={{0,6},{1,7},{2,4},{3,5},{4,2},{5,3},{6,0},{7,1},{8,14},{9,15},{10,... | collective-permute-start | bytes 98312 | tf_op jit(solution)/shard_map/ppermute | solution.py:345
  125.2 3.3 %collective-permute-done.34.refs_7_ = f32[4,16,128]{2,1,0:T(8,128)S(1)} collective-permute-done((f32[4,16,128]{2,1,0:T(8,128)S(1)}, f32[4,16,128]{2,1,0:T(8,128)S(1)}, u32[]{:S(2)}, u32[]{:S(2)}) %collective-permute-start.34) | collective-permute-done | bytes 32800 | tf_op jit(solution)/shard_map/ppermute | solution.py:345
  129.2 2.9 %collective-permute-start.37 = (f32[4,16,128]{2,1,0:T(8,128)S(1)}, f32[4,16,128]{2,1,0:T(8,128)S(1)}, u32[]{:S(2)}, u32[]{:S(2)}) collective-permute-start(f32[4,16,128]{2,1,0:T(8,128)S(1)} %sum.1.refs_0_), channel_id=1, source_target_pairs={{0,3},{1,2},{2,1},{3,0},{4,7},{5,6},{6,5},{7,4},{8,11},{9,10},{10,... | collective-permute-start | bytes 98312 | tf_op jit(solution)/shard_map/ppermute | solution.py:345
  132.1 2.9 %collective-permute-start.39 = (f32[4,16,128]{2,1,0:T(8,128)S(1)}, f32[4,16,128]{2,1,0:T(8,128)S(1)}, u32[]{:S(2)}, u32[]{:S(2)}) collective-permute-start(f32[4,16,128]{2,1,0:T(8,128)S(1)} %sum.1.refs_0_), channel_id=1, source_target_pairs={{0,5},{1,4},{2,7},{3,6},{4,1},{5,0},{6,3},{7,2},{8,13},{9,12},{10,... | collective-permute-start | bytes 98312 | tf_op jit(solution)/shard_map/ppermute | solution.py:345
  136.5 3.2 %collective-permute-start.41 = (f32[4,16,128]{2,1,0:T(8,128)S(1)}, f32[4,16,128]{2,1,0:T(8,128)S(1)}, u32[]{:S(2)}, u32[]{:S(2)}) collective-permute-start(f32[4,16,128]{2,1,0:T(8,128)S(1)} %sum.1.refs_0_), channel_id=1, source_target_pairs={{0,7},{1,6},{2,5},{3,4},{4,3},{5,2},{6,1},{7,0},{8,15},{9,14},{10,... | collective-permute-start | bytes 98312 | tf_op jit(solution)/shard_map/ppermute | solution.py:345
  141.1 2.1 %collective-permute-done.41.refs_7_ = f32[4,16,128]{2,1,0:T(8,128)S(1)} collective-permute-done((f32[4,16,128]{2,1,0:T(8,128)S(1)}, f32[4,16,128]{2,1,0:T(8,128)S(1)}, u32[]{:S(2)}, u32[]{:S(2)}) %collective-permute-start.41) | collective-permute-done | bytes 32800 | tf_op jit(solution)/shard_map/ppermute | solution.py:345
  (93 shorter events, 26.7 us)
Async XLA Ops:
  3.2 11.1 %collective-permute-start = (f32[8,256]{1,0:T(8,128)S(1)}, f32[8,256]{1,0:T(8,128)S(1)}, u32[]{:S(2)}, u32[]{:S(2)}) collective-permute-start(f32[8,256]{1,0:T(8,128)S(1)} %get-tuple-element.68), channel_id=1, source_target_pairs={{0,1},{1,0},{2,3},{3,2},{4,5},{5,4},{6,7},{7,6},{8,9},{9,8},{10,11... | collective-permute-start | bytes 24584 | tf_op jit(solution)/shard_map/ppermute | solution.py:345
  6.2 11.8 %collective-permute-start.1 = (f32[8,256]{1,0:T(8,128)S(1)}, f32[8,256]{1,0:T(8,128)S(1)}, u32[]{:S(2)}, u32[]{:S(2)}) collective-permute-start(f32[8,256]{1,0:T(8,128)S(1)} %get-tuple-element.68), channel_id=1, source_target_pairs={{0,2},{1,3},{2,0},{3,1},{4,6},{5,7},{6,4},{7,5},{8,10},{9,11},{10,... | collective-permute-start | bytes 24584 | tf_op jit(solution)/shard_map/ppermute | solution.py:345
  7.8 10.3 %collective-permute-start.2 = (f32[8,256]{1,0:T(8,128)S(1)}, f32[8,256]{1,0:T(8,128)S(1)}, u32[]{:S(2)}, u32[]{:S(2)}) collective-permute-start(f32[8,256]{1,0:T(8,128)S(1)} %get-tuple-element.68), channel_id=1, source_target_pairs={{0,3},{1,2},{2,1},{3,0},{4,7},{5,6},{6,5},{7,4},{8,11},{9,10},{10,... | collective-permute-start | bytes 24584 | tf_op jit(solution)/shard_map/ppermute | solution.py:345
  7.8 12.0 %collective-permute-start.3 = (f32[8,256]{1,0:T(8,128)S(1)}, f32[8,256]{1,0:T(8,128)S(1)}, u32[]{:S(2)}, u32[]{:S(2)}) collective-permute-start(f32[8,256]{1,0:T(8,128)S(1)} %get-tuple-element.68), channel_id=1, source_target_pairs={{0,4},{1,5},{2,6},{3,7},{4,0},{5,1},{6,2},{7,3},{8,12},{9,13},{10,... | collective-permute-start | bytes 24584 | tf_op jit(solution)/shard_map/ppermute | solution.py:345
  10.8 9.0 %collective-permute-start.4 = (f32[8,256]{1,0:T(8,128)S(1)}, f32[8,256]{1,0:T(8,128)S(1)}, u32[]{:S(2)}, u32[]{:S(2)}) collective-permute-start(f32[8,256]{1,0:T(8,128)S(1)} %get-tuple-element.68), channel_id=1, source_target_pairs={{0,5},{1,4},{2,7},{3,6},{4,1},{5,0},{6,3},{7,2},{8,13},{9,12},{10,... | collective-permute-start | bytes 24584 | tf_op jit(solution)/shard_map/ppermute | solution.py:345
  18.0 6.5 %collective-permute-start.6 = (f32[8,256]{1,0:T(8,128)S(1)}, f32[8,256]{1,0:T(8,128)S(1)}, u32[]{:S(2)}, u32[]{:S(2)}) collective-permute-start(f32[8,256]{1,0:T(8,128)S(1)} %get-tuple-element.68), channel_id=1, source_target_pairs={{0,7},{1,6},{2,5},{3,4},{4,3},{5,2},{6,1},{7,0},{8,15},{9,14},{10,... | collective-permute-start | bytes 24584 | tf_op jit(solution)/shard_map/ppermute | solution.py:345
  18.1 13.8 %collective-permute-start.10 = (f32[128,256]{1,0:T(8,128)S(1)}, f32[128,256]{1,0:T(8,128)S(1)}, u32[]{:S(2)}, u32[]{:S(2)}) collective-permute-start(f32[128,256]{1,0:T(8,128)S(1)} %get-tuple-element.37), channel_id=1, source_target_pairs={{0,1},{1,0},{2,3},{3,2},{4,5},{5,4},{6,7},{7,6},{8,9},{9,8},{10,11... | collective-permute-start | bytes 393224 | tf_op jit(solution)/shard_map/ppermute | solution.py:345
  19.8 12.3 %collective-permute-start.11 = (f32[128,256]{1,0:T(8,128)S(1)}, f32[128,256]{1,0:T(8,128)S(1)}, u32[]{:S(2)}, u32[]{:S(2)}) collective-permute-start(f32[128,256]{1,0:T(8,128)S(1)} %get-tuple-element.38), channel_id=1, source_target_pairs={{0,2},{1,3},{2,0},{3,1},{4,6},{5,7},{6,4},{7,5},{8,10},{9,11},{10,... | collective-permute-start | bytes 393224 | tf_op jit(solution)/shard_map/ppermute | solution.py:345
  26.4 12.5 %collective-permute-start.12 = (f32[128,256]{1,0:T(8,128)S(1)}, f32[128,256]{1,0:T(8,128)S(1)}, u32[]{:S(2)}, u32[]{:S(2)}) collective-permute-start(f32[128,256]{1,0:T(8,128)S(1)} %get-tuple-element.39), channel_id=1, source_target_pairs={{0,3},{1,2},{2,1},{3,0},{4,7},{5,6},{6,5},{7,4},{8,11},{9,10},{10,... | collective-permute-start | bytes 393224 | tf_op jit(solution)/shard_map/ppermute | solution.py:345
  29.1 16.4 %collective-permute-start.13 = (f32[128,256]{1,0:T(8,128)S(1)}, f32[128,256]{1,0:T(8,128)S(1)}, u32[]{:S(2)}, u32[]{:S(2)}) collective-permute-start(f32[128,256]{1,0:T(8,128)S(1)} %get-tuple-element.40), channel_id=1, source_target_pairs={{0,4},{1,5},{2,6},{3,7},{4,0},{5,1},{6,2},{7,3},{8,12},{9,13},{10,... | collective-permute-start | bytes 393224 | tf_op jit(solution)/shard_map/ppermute | solution.py:345
  30.1 19.1 %collective-permute-start.14 = (f32[128,256]{1,0:T(8,128)S(1)}, f32[128,256]{1,0:T(8,128)S(1)}, u32[]{:S(2)}, u32[]{:S(2)}) collective-permute-start(f32[128,256]{1,0:T(8,128)S(1)} %get-tuple-element.41), channel_id=1, source_target_pairs={{0,5},{1,4},{2,7},{3,6},{4,1},{5,0},{6,3},{7,2},{8,13},{9,12},{10,... | collective-permute-start | bytes 393224 | tf_op jit(solution)/shard_map/ppermute | solution.py:345
  32.0 17.3 %collective-permute-start.15 = (f32[128,256]{1,0:T(8,128)S(1)}, f32[128,256]{1,0:T(8,128)S(1)}, u32[]{:S(2)}, u32[]{:S(2)}) collective-permute-start(f32[128,256]{1,0:T(8,128)S(1)} %get-tuple-element.42), channel_id=1, source_target_pairs={{0,6},{1,7},{2,4},{3,5},{4,2},{5,3},{6,0},{7,1},{8,14},{9,15},{10,... | collective-permute-start | bytes 393224 | tf_op jit(solution)/shard_map/ppermute | solution.py:345
  32.1 17.1 %collective-permute-start.16 = (f32[128,256]{1,0:T(8,128)S(1)}, f32[128,256]{1,0:T(8,128)S(1)}, u32[]{:S(2)}, u32[]{:S(2)}) collective-permute-start(f32[128,256]{1,0:T(8,128)S(1)} %get-tuple-element.43), channel_id=1, source_target_pairs={{0,7},{1,6},{2,5},{3,4},{4,3},{5,2},{6,1},{7,0},{8,15},{9,14},{10,... | collective-permute-start | bytes 393224 | tf_op jit(solution)/shard_map/ppermute | solution.py:345
  57.1 10.5 %collective-permute-start.17 = (f32[128,256]{1,0:T(8,128)S(1)}, f32[128,256]{1,0:T(8,128)S(1)}, u32[]{:S(2)}, u32[]{:S(2)}) collective-permute-start(f32[128,256]{1,0:T(8,128)S(1)} %get-tuple-element.45), channel_id=1, source_target_pairs={{0,1},{1,0},{2,3},{3,2},{4,5},{5,4},{6,7},{7,6},{8,9},{9,8},{10,11... | collective-permute-start | bytes 393224 | tf_op jit(solution)/shard_map/ppermute | solution.py:345
  57.7 11.4 %collective-permute-start.18 = (f32[128,256]{1,0:T(8,128)S(1)}, f32[128,256]{1,0:T(8,128)S(1)}, u32[]{:S(2)}, u32[]{:S(2)}) collective-permute-start(f32[128,256]{1,0:T(8,128)S(1)} %get-tuple-element.46), channel_id=1, source_target_pairs={{0,2},{1,3},{2,0},{3,1},{4,6},{5,7},{6,4},{7,5},{8,10},{9,11},{10,... | collective-permute-start | bytes 393224 | tf_op jit(solution)/shard_map/ppermute | solution.py:345
  63.8 9.6 %collective-permute-start.19 = (f32[128,256]{1,0:T(8,128)S(1)}, f32[128,256]{1,0:T(8,128)S(1)}, u32[]{:S(2)}, u32[]{:S(2)}) collective-permute-start(f32[128,256]{1,0:T(8,128)S(1)} %get-tuple-element.47), channel_id=1, source_target_pairs={{0,3},{1,2},{2,1},{3,0},{4,7},{5,6},{6,5},{7,4},{8,11},{9,10},{10,... | collective-permute-start | bytes 393224 | tf_op jit(solution)/shard_map/ppermute | solution.py:345
  64.7 18.4 %collective-permute-start.20 = (f32[128,256]{1,0:T(8,128)S(1)}, f32[128,256]{1,0:T(8,128)S(1)}, u32[]{:S(2)}, u32[]{:S(2)}) collective-permute-start(f32[128,256]{1,0:T(8,128)S(1)} %get-tuple-element.48), channel_id=1, source_target_pairs={{0,4},{1,5},{2,6},{3,7},{4,0},{5,1},{6,2},{7,3},{8,12},{9,13},{10,... | collective-permute-start | bytes 393224 | tf_op jit(solution)/shard_map/ppermute | solution.py:345
  65.6 20.3 %collective-permute-start.21 = (f32[128,256]{1,0:T(8,128)S(1)}, f32[128,256]{1,0:T(8,128)S(1)}, u32[]{:S(2)}, u32[]{:S(2)}) collective-permute-start(f32[128,256]{1,0:T(8,128)S(1)} %get-tuple-element.49), channel_id=1, source_target_pairs={{0,5},{1,4},{2,7},{3,6},{4,1},{5,0},{6,3},{7,2},{8,13},{9,12},{10,... | collective-permute-start | bytes 393224 | tf_op jit(solution)/shard_map/ppermute | solution.py:345
  67.6 18.3 %collective-permute-start.22 = (f32[128,256]{1,0:T(8,128)S(1)}, f32[128,256]{1,0:T(8,128)S(1)}, u32[]{:S(2)}, u32[]{:S(2)}) collective-permute-start(f32[128,256]{1,0:T(8,128)S(1)} %get-tuple-element.50), channel_id=1, source_target_pairs={{0,6},{1,7},{2,4},{3,5},{4,2},{5,3},{6,0},{7,1},{8,14},{9,15},{10,... | collective-permute-start | bytes 393224 | tf_op jit(solution)/shard_map/ppermute | solution.py:345
  69.1 16.8 %collective-permute-start.23 = (f32[128,256]{1,0:T(8,128)S(1)}, f32[128,256]{1,0:T(8,128)S(1)}, u32[]{:S(2)}, u32[]{:S(2)}) collective-permute-start(f32[128,256]{1,0:T(8,128)S(1)} %get-tuple-element.51), channel_id=1, source_target_pairs={{0,7},{1,6},{2,5},{3,4},{4,3},{5,2},{6,1},{7,0},{8,15},{9,14},{10,... | collective-permute-start | bytes 393224 | tf_op jit(solution)/shard_map/ppermute | solution.py:345
  86.6 10.9 %collective-permute-start.25 = (f32[4,128,256]{2,1,0:T(8,128)S(1)}, f32[4,128,256]{2,1,0:T(8,128)S(1)}, u32[]{:S(2)}, u32[]{:S(2)}) collective-permute-start(f32[4,128,256]{2,1,0:T(8,128)S(1)} %get-tuple-element.53), channel_id=1, source_target_pairs={{0,16},{8,24},{16,0},{24,8},{1,17},{9,25},{17,1},{25,9},{2,18},{10... | collective-permute-start | bytes 1572872 | tf_op jit(solution)/shard_map/ppermute | solution.py:345
  88.2 11.2 %collective-permute-start.24 = (f32[8,128,256]{2,1,0:T(8,128)S(1)}, f32[8,128,256]{2,1,0:T(8,128)S(1)}, u32[]{:S(2)}, u32[]{:S(2)}) collective-permute-start(f32[8,128,256]{2,1,0:T(8,128)S(1)} %get-tuple-element.52.refs_0_), channel_id=1, source_target_pairs={{0,8},{8,0},{16,24},{24,16},{1,9},{9,1},{17,25},{25,17},{2,10},{10... | collective-permute-start | bytes 3145736 | tf_op jit(solution)/shard_map/ppermute | solution.py:345
  108.0 11.5 %collective-permute-start.28 = (f32[4,16,128]{2,1,0:T(8,128)S(1)}, f32[4,16,128]{2,1,0:T(8,128)S(1)}, u32[]{:S(2)}, u32[]{:S(2)}) collective-permute-start(f32[4,16,128]{2,1,0:T(8,128)S(1)} %get-tuple-element.57), channel_id=1, source_target_pairs={{0,1},{1,0},{2,3},{3,2},{4,5},{5,4},{6,7},{7,6},{8,9},{9,8},{10,11... | collective-permute-start | bytes 98312 | tf_op jit(solution)/shard_map/ppermute | solution.py:345
  109.5 12.3 %collective-permute-start.29 = (f32[4,16,128]{2,1,0:T(8,128)S(1)}, f32[4,16,128]{2,1,0:T(8,128)S(1)}, u32[]{:S(2)}, u32[]{:S(2)}) collective-permute-start(f32[4,16,128]{2,1,0:T(8,128)S(1)} %get-tuple-element.58), channel_id=1, source_target_pairs={{0,2},{1,3},{2,0},{3,1},{4,6},{5,7},{6,4},{7,5},{8,10},{9,11},{10,... | collective-permute-start | bytes 98312 | tf_op jit(solution)/shard_map/ppermute | solution.py:345
  115.6 7.7 %collective-permute-start.30 = (f32[4,16,128]{2,1,0:T(8,128)S(1)}, f32[4,16,128]{2,1,0:T(8,128)S(1)}, u32[]{:S(2)}, u32[]{:S(2)}) collective-permute-start(f32[4,16,128]{2,1,0:T(8,128)S(1)} %get-tuple-element.59), channel_id=1, source_target_pairs={{0,3},{1,2},{2,1},{3,0},{4,7},{5,6},{6,5},{7,4},{8,11},{9,10},{10,... | collective-permute-start | bytes 98312 | tf_op jit(solution)/shard_map/ppermute | solution.py:345
  115.7 7.7 %collective-permute-start.31 = (f32[4,16,128]{2,1,0:T(8,128)S(1)}, f32[4,16,128]{2,1,0:T(8,128)S(1)}, u32[]{:S(2)}, u32[]{:S(2)}) collective-permute-start(f32[4,16,128]{2,1,0:T(8,128)S(1)} %get-tuple-element.60), channel_id=1, source_target_pairs={{0,4},{1,5},{2,6},{3,7},{4,0},{5,1},{6,2},{7,3},{8,12},{9,13},{10,... | collective-permute-start | bytes 98312 | tf_op jit(solution)/shard_map/ppermute | solution.py:345
  121.8 6.7 %collective-permute-start.34 = (f32[4,16,128]{2,1,0:T(8,128)S(1)}, f32[4,16,128]{2,1,0:T(8,128)S(1)}, u32[]{:S(2)}, u32[]{:S(2)}) collective-permute-start(f32[4,16,128]{2,1,0:T(8,128)S(1)} %get-tuple-element.63), channel_id=1, source_target_pairs={{0,7},{1,6},{2,5},{3,4},{4,3},{5,2},{6,1},{7,0},{8,15},{9,14},{10,... | collective-permute-start | bytes 98312 | tf_op jit(solution)/shard_map/ppermute | solution.py:345
  129.2 7.4 %collective-permute-start.36 = (f32[4,16,128]{2,1,0:T(8,128)S(1)}, f32[4,16,128]{2,1,0:T(8,128)S(1)}, u32[]{:S(2)}, u32[]{:S(2)}) collective-permute-start(f32[4,16,128]{2,1,0:T(8,128)S(1)} %sum.1.refs_0_), channel_id=1, source_target_pairs={{0,2},{1,3},{2,0},{3,1},{4,6},{5,7},{6,4},{7,5},{8,10},{9,11},{10,... | collective-permute-start | bytes 98312 | tf_op jit(solution)/shard_map/ppermute | solution.py:345
  129.2 11.9 %collective-permute-start.37 = (f32[4,16,128]{2,1,0:T(8,128)S(1)}, f32[4,16,128]{2,1,0:T(8,128)S(1)}, u32[]{:S(2)}, u32[]{:S(2)}) collective-permute-start(f32[4,16,128]{2,1,0:T(8,128)S(1)} %sum.1.refs_0_), channel_id=1, source_target_pairs={{0,3},{1,2},{2,1},{3,0},{4,7},{5,6},{6,5},{7,4},{8,11},{9,10},{10,... | collective-permute-start | bytes 98312 | tf_op jit(solution)/shard_map/ppermute | solution.py:345
  132.1 9.0 %collective-permute-start.38 = (f32[4,16,128]{2,1,0:T(8,128)S(1)}, f32[4,16,128]{2,1,0:T(8,128)S(1)}, u32[]{:S(2)}, u32[]{:S(2)}) collective-permute-start(f32[4,16,128]{2,1,0:T(8,128)S(1)} %sum.1.refs_0_), channel_id=1, source_target_pairs={{0,4},{1,5},{2,6},{3,7},{4,0},{5,1},{6,2},{7,3},{8,12},{9,13},{10,... | collective-permute-start | bytes 98312 | tf_op jit(solution)/shard_map/ppermute | solution.py:345
  132.1 8.9 %collective-permute-start.39 = (f32[4,16,128]{2,1,0:T(8,128)S(1)}, f32[4,16,128]{2,1,0:T(8,128)S(1)}, u32[]{:S(2)}, u32[]{:S(2)}) collective-permute-start(f32[4,16,128]{2,1,0:T(8,128)S(1)} %sum.1.refs_0_), channel_id=1, source_target_pairs={{0,5},{1,4},{2,7},{3,6},{4,1},{5,0},{6,3},{7,2},{8,13},{9,12},{10,... | collective-permute-start | bytes 98312 | tf_op jit(solution)/shard_map/ppermute | solution.py:345
  136.5 6.6 %collective-permute-start.41 = (f32[4,16,128]{2,1,0:T(8,128)S(1)}, f32[4,16,128]{2,1,0:T(8,128)S(1)}, u32[]{:S(2)}, u32[]{:S(2)}) collective-permute-start(f32[4,16,128]{2,1,0:T(8,128)S(1)} %sum.1.refs_0_), channel_id=1, source_target_pairs={{0,7},{1,6},{2,5},{3,4},{4,3},{5,2},{6,1},{7,0},{8,15},{9,14},{10,... | collective-permute-start | bytes 98312 | tf_op jit(solution)/shard_map/ppermute | solution.py:345
  (18 other events, 149.9 us)

commit v2 on v1

--- a/solution.py
+++ b/solution.py
@@ -98,10 +98,10 @@
 
 
 def weights_kernel(nd, pos_ref, *refs):
-    parts, (wh_ref, wl_ref, v_ref, scratch) = refs[:4], refs[4:]
-    i, b = pos_ref[0], pos_ref[1]
-    for jb in range(4):
-        rows = pl.ds(pl.multiple_of((b ^ jb) * 8, 8), 8)
+    parts, (wh_ref, wl_ref, v_ref, scratch) = refs[:2], refs[2:]
+    i, core = pos_ref[0], pos_ref[1] & 1
+    for jb in range(2):
+        rows = pl.ds(pl.multiple_of((core ^ jb) * 16, 16), 16)
         for j in range(nd):
             scratch[i ^ j, rows] = parts[jb][j]
     lat = lax.broadcasted_iota(jnp.int32, (LAT, 256), 0).astype(F32)
@@ -235,26 +235,92 @@
         outs[j][...] = (y * scale[None]).reshape(R, LAT)
 
 
-def join_kernel(nd, nb, real, pos_ref, *refs):
-    pieces, (z_ref, send_ref) = refs[:nd], refs[nd:]
+def join_kernel(count, nb, pos_ref, *refs):
+    pieces, (z_ref, send_ref) = refs[:count], refs[count:]
     i, y = pos_ref[0], pos_ref[2]
-    for j in range(nd):
-        rows = pl.ds(pl.multiple_of((i ^ j) * real, real), real)
+    for j in range(count):
+        rows = pl.ds(pl.multiple_of(((i ^ j) & (count - 1)) * nb, nb), nb)
         for q in range(SLAB):
-            z_ref[q, rows] = pieces[j][q * nb : q * nb + real]
+            z_ref[q, rows] = pieces[j][q * nb : (q + 1) * nb]
     half = SLAB // 2
     for q in range(half):
         send_ref[q] = z_ref[(1 - y) * half + q]
 
 
-def gram_kernel(chunks, pos_ref, *refs):
-    own, core, far, far_core = (refs[k * chunks : (k + 1) * chunks] for k in range(4))
-    g_ref, far_ref = refs[4 * chunks :]
+def place_halves(pos_ref, near, far, out):
+    h = pos_ref[0] // 4
+    for q in range(out.shape[0]):
+        out[q, pl.ds(pl.multiple_of(h * 64, 64), 64)] = near[q]
+        out[q, pl.ds(pl.multiple_of((1 - h) * 64, 64), 64)] = far[q]
+
+
+def own_kernel(pos_ref, near, far, core_near, core_far, z_ref, zc_ref, keep_ref, send_ref, g_ref):
+    i, b = pos_ref[0], pos_ref[1]
+    place_halves(pos_ref, near, far, z_ref)
+    place_halves(pos_ref, core_near, core_far, zc_ref)
+    own = core = None
+    for q in range(SLAB):
+        zh, zl = halves(z_ref[q])
+        ch, cl = halves(zc_ref[q])
+        mine, other = dot3(zh, zl, zh, zl, NT), dot3(zh, zl, ch, cl, NT)
+        own, core = (mine, other) if own is None else (own + mine, core + other)
+    g_ref[b & 1] = own
+    g_ref[(b & 1) ^ 1] = core
+    cut_rows(i, g_ref, keep_ref, send_ref)
+
+
+def cut_rows(i, g_ref, keep_ref, send_ref):
+    x = i & 1
+    for c in range(2):
+        keep_ref[c] = g_ref[c, pl.ds(pl.multiple_of(x * 64, 64), 64)]
+        send_ref[c] = g_ref[c, pl.ds(pl.multiple_of((1 - x) * 64, 64), 64)]
+
+
+def cross_kernel(pos_ref, z_ref, zc_ref, near, far, core_near, core_far, g_ref, back_ref, f_ref, fc_ref):
     b, y = pos_ref[1], pos_ref[2]
     half = SLAB // 2
-
-    def load(group, q):
-        return halves(jnp.concatenate([r[q] for r in group], axis=0))
+    place_halves(pos_ref, near, far, f_ref)
+    place_halves(pos_ref, core_near, core_far, fc_ref)
+    totals = None
+    for q in range(half):
+        zh, zl = halves(z_ref[y * half + q])
+        ch, cl = halves(zc_ref[y * half + q])
+        fh, fl = halves(f_ref[q])
+        gh, gl = halves(fc_ref[q])
+        now = (
+            dot3(zh, zl, fh, fl, NT),
+            dot3(zh, zl, gh, gl, NT),
+            dot3(fh, fl, zh, zl, NT),
+            dot3(fh, fl, ch, cl, NT),
+        )
+        totals = now if totals is None else tuple(t + n for t, n in zip(totals, now))
+    c = b & 1
+    g_ref[c], g_ref[c ^ 1], back_ref[c], back_ref[c ^ 1] = totals
+
+
+def part_kernel(pos_ref, g_ref, share_ref, keep_ref, send_ref, sum_ref):
+    sum_ref[...] = g_ref[...] + share_ref[...]
+    cut_rows(pos_ref[0], sum_ref, keep_ref, send_ref)
+
+
+def output_kernel(z_ref, out_ref):
+    for q in range(SLAB):
+        out_ref[q] = z_ref[q].T
+
+
+def place_kernel(total, pos_ref, own, own_other, cross, cross_other, out_ref):
+    i, y = pos_ref[0], pos_ref[2]
+    x = i & 1
+    for c in range(2):
+        for mine, other, chip in ((own, own_other, y), (cross, cross_other, 1 - y)):
+            lanes = pl.ds(pl.multiple_of((chip * 2 + c) * 128, 128), 128)
+            out_ref[pl.ds(pl.multiple_of(x * 64, 64), 64), lanes] = mine[c] * (1.0 / total)
+            out_ref[pl.ds(pl.multiple_of((1 - x) * 64, 64), 64), lanes] = other[c] * (1.0 / total)
+
+
+def gram_kernel(pos_ref, own, core, far, far_core, g_ref, far_ref):
+    b, y = pos_ref[1], pos_ref[2]
+    half = SLAB // 2
 
     def add(totals, place, value):
         totals[place] = value if totals.get(place) is None else totals[place] + value
@@ -263,13 +329,13 @@
     for q in range(half):
         for mine in (True, False):
             at = q + y * half if mine else q + (1 - y) * half
-            zh, zl = load(own, at)
-            ch, cl = load(core, at)
+            zh, zl = halves(own[at])
+            ch, cl = halves(core[at])
             add(totals, "own", dot3(zh, zl, zh, zl, NT))
             add(totals, "core", dot3(zh, zl, ch, cl, NT))
             if mine:
-                fh, fl = load(far, q)
-                gh, gl = load(far_core, q)
+                fh, fl = halves(far[q])
+                gh, gl = halves(far_core[q])
                 add(totals, "far", dot3(zh, zl, fh, fl, NT))
                 add(totals, "far_core", dot3(zh, zl, gh, gl, NT))
                 add(totals, "back", dot3(fh, fl, zh, zl, NT))
@@ -280,39 +346,6 @@
     g_ref[b ^ 3] = totals["far_core"]
     far_ref[b & 1] = totals["back"]
     far_ref[(b & 1) ^ 1] = totals["back_core"]
-
-
-def output_kernel(chunks, *refs):
-    zs, out_ref = refs[:chunks], refs[chunks]
-    for q in range(SLAB):
-        out_ref[q] = jnp.concatenate([z[q] for z in zs], axis=0).T
-
-
-def part_kernel(nd, pos_ref, g_ref, far_ref, *outs):
-    i, y = pos_ref[0], pos_ref[2]
-    size = outs[0].shape[1]
-    for j in range(nd):
-        rows = pl.ds(pl.multiple_of((i ^ j) * size, size), size)
-        for c in range(2):
-            outs[j][y * 2 + c] = g_ref[y * 2 + c, rows]
-            outs[j][(1 - y) * 2 + c] = g_ref[(1 - y) * 2 + c, rows] + far_ref[c, rows]
-
-
-def sum_kernel(total, *refs):
-    acc = refs[0][...]
-    for r in refs[1:-1]:
-        acc = acc + r[...]
-    refs[-1][...] = acc * (1.0 / total)
-
-
-def place_kernel(nd, pos_ref, *refs):
-    pieces, out_ref = refs[:nd], refs[nd]
-    i = pos_ref[0]
-    size = pieces[0].shape[1]
-    for j in range(nd):
-        rows = pl.ds(pl.multiple_of((i ^ j) * size, size), size)
-        for k in range(4):
-            out_ref[rows, k * 128 : (k + 1) * 128] = pieces[j][k]
 
 
 def call(kernel, out_shape, operands, scratch=(), name=None):
@@ -389,12 +422,13 @@
 
     packed = packed_atoms(potential, proj_weights, atom_cell, point_codes)
     if direct:
-        mine = lax.dynamic_slice_in_dim(packed, band * 8, 8, 0)
-        gathered = jnp.stack([mine] + [xor_permute(mine, "dom", j) for j in range(1, nd)])
-        parts = [gathered] + [xor_permute(gathered, "band", j) for j in range(1, 4)]
+        gathered = lax.dynamic_slice_in_dim(packed, band % 2 * 16, 16, 0)[None]
+        for step in (1, 2, 4):
+            gathered = jnp.concatenate([gathered, xor_permute(gathered, "dom", step)])
+        parts = [gathered, xor_permute(gathered, "band", 1)]
     else:
         gathered = lax.all_gather(packed, "dom", axis=0)
-        parts = [gathered[:, k * 8 : k * 8 + 8] for k in range(4)]
+        parts = [gathered[:, :16], gathered[:, 16:]]
 
     waves = trial_waves.reshape(SLAB, LAT, bands)
     if direct:
@@ -421,7 +455,6 @@
     kb_row = jnp.concatenate([kb_energy, kb_energy, jnp.zeros((112,), F32)])[None]
     spread = fold
     arrived = [swap_all(cut[c * nd : (c + 1) * nd], direct) for c in range(chunks)]
-    joined, sends = [], []
     for c in range(chunks):
         pieces = arrived[c]
         if not direct:
@@ -441,55 +474,78 @@
         if not direct:
             ready = [p.reshape(SLAB, nb, LAT)[:, :real] for p in ready]
         back = swap_all(ready, direct)
-        if direct:
-            z, send = call(
-                functools.partial(join_kernel, nd, nb, real),
-                [shape(SLAB, nd * real, LAT), shape(SLAB // 2, nd * real, LAT)],
-                [pos_band] + back,
-                (),
-                "join",
-            )
-        else:
-            z = jnp.concatenate(back, axis=1)
-            send = lax.dynamic_slice_in_dim(z, (1 - band // 2) * (SLAB // 2), SLAB // 2, 0)
-        joined.append(z)
-        sends.append(send)
-
-    core = [xor_permute(z, "band", 1) for z in joined]
-    far = [xor_permute(s, "band", 2) for s in sends]
-    far_core = [xor_permute(s, "band", 1) for s in far]
+    if direct:
+        filtered, correlation = finish_direct(back, pos, nb, bands, float(total))
+    else:
+        filtered, correlation = finish_plain(jnp.concatenate(back, axis=1), pos_band, band, bands, float(total))
+    return filtered.reshape(trial_waves.shape), correlation
+
+
+def finish_direct(back, pos, nb, bands, total):
+    group = len(back) // 2
+    half = SLAB // 2
+
+    def exchanged(pieces):
+        z, send = call(
+            functools.partial(join_kernel, group, nb),
+            [shape(SLAB, group * nb, LAT), shape(half, group * nb, LAT)],
+            [pos] + pieces,
+            (),
+            "join",
+        )
+        far = xor_permute(send, "band", 2)
+        return z, xor_permute(z, "band", 1), far, xor_permute(far, "band", 1)
+
+    z_near, core_near, far_near, far_core_near = exchanged(back[:group])
+    z_far, core_far, far_far, far_core_far = exchanged(back[group:])
+    part = shape(2, bands // 2, bands)
+    block = pltpu.VMEM((2, bands, bands), F32)
+    z, z_core, own_keep, own_send = call(
+        own_kernel,
+        [shape(SLAB, bands, LAT), shape(SLAB, bands, LAT), part, part],
+        [pos, z_near, z_far, core_near, core_far],
+        [block],
+        "own",
+    )
+    gram, share = call(
+        cross_kernel,
+        [shape(2, bands, bands), shape(2, bands, bands)],
+        [pos, z, z_core, far_near, far_far, far_core_near, far_core_far],
+        [pltpu.VMEM((half, bands, LAT), F32), pltpu.VMEM((half, bands, LAT), F32)],
+        "cross",
+    )
+    cross_keep, cross_send = call(
+        part_kernel, [part, part], [pos, gram, xor_permute(share, "band", 2)], [block], "part"
+    )
+
+    def summed(keep, send):
+        rows = keep + xor_permute(send, "dom", 1)
+        rows = rows + xor_permute(rows, "dom", 2)
+        rows = rows + xor_permute(rows, "dom", 4)
+        return [rows, xor_permute(rows, "dom", 1)]
+
+    rows = summed(own_keep, own_send) + summed(cross_keep, cross_send)
+    filtered = call(output_kernel, shape(SLAB, LAT, bands), [z], (), "output")
+    correlation = call(functools.partial(place_kernel, total), shape(bands, 4 * bands), [pos] + rows, (), "place")
+    return filtered, correlation
+
+
+def finish_plain(z, pos, band, bands, total):
+    send = lax.dynamic_slice_in_dim(z, (1 - band // 2) * (SLAB // 2), SLAB // 2, 0)
+    far = xor_permute(send, "band", 2)
     gram, gram_far = call(
-        functools.partial(gram_kernel, chunks),
+        gram_kernel,
         [shape(4, bands, bands), shape(2, bands, bands)],
-        [pos_band] + joined + core + far + far_core,
+        [pos, z, xor_permute(z, "band", 1), far, xor_permute(far, "band", 1)],
         (),
         "gram",
     )
-    far_share = xor_permute(gram_far, "band", 2)
-    filtered = call(functools.partial(output_kernel, chunks), shape(SLAB, LAT, bands), joined, (), "output")
-    if direct:
-        size = bands // nd
-        cut_gram = call(
-            functools.partial(part_kernel, nd),
-            [shape(4, size, bands)] * nd,
-            [pos_band, gram, far_share],
-            (),
-            "part",
-        )
-        summed = call(
-            functools.partial(sum_kernel, float(total)), shape(4, size, bands), swap_all(cut_gram, direct), (), "sum"
-        )
-        everyone = [summed] + [xor_permute(summed, "dom", j) for j in range(1, nd)]
-        correlation = call(
-            functools.partial(place_kernel, nd), shape(bands, 4 * bands), [pos_band] + everyone, (), "place"
-        )
-    else:
-        start = (1 - band // 2) * 2
-        cross = lax.dynamic_slice_in_dim(gram, start, 2, 0) + far_share
-        gram = lax.dynamic_update_slice_in_dim(gram, cross, start, 0)
-        wide = gram.transpose(1, 0, 2).reshape(bands, 4 * bands)
-        correlation = lax.psum(wide, "dom") / total
-    return filtered.reshape(trial_waves.shape), correlation
+    filtered = call(output_kernel, shape(SLAB, LAT, bands), [z], (), "output")
+    start = (1 - band // 2) * 2
+    cross = lax.dynamic_slice_in_dim(gram, start, 2, 0) + xor_permute(gram_far, "band", 2)
+    gram = lax.dynamic_update_slice_in_dim(gram, cross, start, 0)
+    wide = gram.transpose(1, 0, 2).reshape(bands, 4 * bands)
+    return filtered, lax.psum(wide, "dom") / total
 
 
 def solution(mesh):

time: 145 us -> 122 us (0.84)
  starting transfers between devices: 67.7 us -> 50.3 us
  waiting for transfers between devices: 54.8 us -> 48.3 us
    ppermute x42 -> x33, starting transfers between devices: 67.7 us -> 50.3 us  [xor_permute(): return lax.ppermute(value, axis, [(k, k ^ step) for k in range(count)])]
    ppermute x42 -> x33, waiting for transfers between devices: 54.8 us -> 48.3 us  [xor_permute(): return lax.ppermute(value, axis, [(k, k ^ step) for k in range(count)])]
    pallas_call x9 -> x10, Pallas kernels: 17.1 us -> 18.5 us  [call(): pl.pallas_call(kernel, out_shape=out_shape, in_specs=specs, out_specs=pl....]
  transfers between devices with their start and end apart: 42 -> 33, of which waited for: 15 -> 17; matrix products, arithmetic and copies ran while one was open for 0% -> 0% of each run, Pallas kernels for 3% -> 6%
where the time goes in v2:
time: 122 us
  starting transfers between devices  50.3 us (41%)
  waiting for transfers between devices  48.3 us (40%)
  Pallas kernels  18.5 us (15%)
  local copies, waits for them, and re-layouts  3.49 us (3%)
    ppermute x33, starting transfers between devices, xor_permute(): return lax.ppermute(value, axis, [(k, k ^ step) for k in range(count)])  50.3 us
    ppermute x33, waiting for transfers between devices, xor_permute(): return lax.ppermute(value, axis, [(k, k ^ step) for k in range(count)])  48.3 us
    pallas_call x10, Pallas kernels, call(): pl.pallas_call(kernel, out_shape=out_shape, in_specs=specs, out_specs=pl....  18.5 us
    unnamed x16, local copies, waits for them, and re-layouts  2.52 us
  transfers between devices with their start and end apart: 33, of which 17 were waited for; matrix products, arithmetic and copies ran while one was open for 0% of the time, Pallas kernels for 6%

profile of v2, /device:TPU:0, one launch (start us, length us, event | category | flops | bytes accessed | tf_op | source)
XLA Modules:
  0.0 122.0 jit_solution(5645229957840249857)
XLA Ops:
  3.2 3.0 %collective-permute-start = (f32[1,16,256]{2,1,0:T(8,128)S(1)}, f32[1,16,256]{2,1,0:T(8,128)S(1)}, u32[]{:S(2)}, u32[]{:S(2)}) collective-permute-start(f32[1,16,256]{2,1,0:T(8,128)S(1)} %dynamic-slice_bitcast_fusion), channel_id=1, source_target_pairs={{0,1},{1,0},{2,3},{3,2},{4,5},{5,4},{6,7},{7,6},{8,9},{9,8},{10,11... | collective-permute-start | bytes 49160 | tf_op jit(solution)/shard_map/ppermute | solution.py:378
  6.2 1.7 %collective-permute-done = f32[1,16,256]{2,1,0:T(8,128)S(1)} collective-permute-done((f32[1,16,256]{2,1,0:T(8,128)S(1)}, f32[1,16,256]{2,1,0:T(8,128)S(1)}, u32[]{:S(2)}, u32[]{:S(2)}) %collective-permute-start) | collective-permute-done | bytes 16416 | tf_op jit(solution)/shard_map/ppermute | solution.py:378
  8.0 2.1 %collective-permute-start.1 = (f32[2,16,256]{2,1,0:T(8,128)S(1)}, f32[2,16,256]{2,1,0:T(8,128)S(1)}, u32[]{:S(2)}, u32[]{:S(2)}) collective-permute-start(f32[2,16,256]{2,1,0:T(8,128)S(1)} %pad_maximum_fusion.2), channel_id=1, source_target_pairs={{0,2},{1,3},{2,0},{3,1},{4,6},{5,7},{6,4},{7,5},{8,10},{9,11},{10,... | collective-permute-start | bytes 98312 | tf_op jit(solution)/shard_map/ppermute | solution.py:378
  10.1 1.9 %collective-permute-done.1 = f32[2,16,256]{2,1,0:T(8,128)S(1)} collective-permute-done((f32[2,16,256]{2,1,0:T(8,128)S(1)}, f32[2,16,256]{2,1,0:T(8,128)S(1)}, u32[]{:S(2)}, u32[]{:S(2)}) %collective-permute-start.1) | collective-permute-done | bytes 32800 | tf_op jit(solution)/shard_map/ppermute | solution.py:378
  12.0 3.0 %collective-permute-start.2 = (f32[4,16,256]{2,1,0:T(8,128)S(1)}, f32[4,16,256]{2,1,0:T(8,128)S(1)}, u32[]{:S(2)}, u32[]{:S(2)}) collective-permute-start(f32[4,16,256]{2,1,0:T(8,128)S(1)} %pad_maximum_fusion.1), channel_id=1, source_target_pairs={{0,4},{1,5},{2,6},{3,7},{4,0},{5,1},{6,2},{7,3},{8,12},{9,13},{10,... | collective-permute-start | bytes 196616 | tf_op jit(solution)/shard_map/ppermute | solution.py:378
  17.3 2.3 %collective-permute-start.10 = (f32[128,256]{1,0:T(8,128)S(1)}, f32[128,256]{1,0:T(8,128)S(1)}, u32[]{:S(2)}, u32[]{:S(2)}) collective-permute-start(f32[128,256]{1,0:T(8,128)S(1)} %get-tuple-element.43), channel_id=1, source_target_pairs={{0,7},{1,6},{2,5},{3,4},{4,3},{5,2},{6,1},{7,0},{8,15},{9,14},{10,... | collective-permute-start | bytes 393224 | tf_op jit(solution)/shard_map/ppermute | solution.py:378
  20.9 2.3 %collective-permute-start.6 = (f32[128,256]{1,0:T(8,128)S(1)}, f32[128,256]{1,0:T(8,128)S(1)}, u32[]{:S(2)}, u32[]{:S(2)}) collective-permute-start(f32[128,256]{1,0:T(8,128)S(1)} %get-tuple-element.39), channel_id=1, source_target_pairs={{0,3},{1,2},{2,1},{3,0},{4,7},{5,6},{6,5},{7,4},{8,11},{9,10},{10,... | collective-permute-start | bytes 393224 | tf_op jit(solution)/shard_map/ppermute | solution.py:378
  23.3 2.0 %collective-permute-done.10.refs_7_ = f32[128,256]{1,0:T(8,128)S(1)} collective-permute-done((f32[128,256]{1,0:T(8,128)S(1)}, f32[128,256]{1,0:T(8,128)S(1)}, u32[]{:S(2)}, u32[]{:S(2)}) %collective-permute-start.10) | collective-permute-done | bytes 131104 | tf_op jit(solution)/shard_map/ppermute | solution.py:378
  26.5 2.5 %collective-permute-start.8 = (f32[128,256]{1,0:T(8,128)S(1)}, f32[128,256]{1,0:T(8,128)S(1)}, u32[]{:S(2)}, u32[]{:S(2)}) collective-permute-start(f32[128,256]{1,0:T(8,128)S(1)} %get-tuple-element.41), channel_id=1, source_target_pairs={{0,5},{1,4},{2,7},{3,6},{4,1},{5,0},{6,3},{7,2},{8,13},{9,12},{10,... | collective-permute-start | bytes 393224 | tf_op jit(solution)/shard_map/ppermute | solution.py:378
  29.0 1.8 %collective-permute-start.9 = (f32[128,256]{1,0:T(8,128)S(1)}, f32[128,256]{1,0:T(8,128)S(1)}, u32[]{:S(2)}, u32[]{:S(2)}) collective-permute-start(f32[128,256]{1,0:T(8,128)S(1)} %get-tuple-element.42), channel_id=1, source_target_pairs={{0,6},{1,7},{2,4},{3,5},{4,2},{5,3},{6,0},{7,1},{8,14},{9,15},{10,... | collective-permute-start | bytes 393224 | tf_op jit(solution)/shard_map/ppermute | solution.py:378
  30.9 2.1 %weights.1 = (bf16[2048,256]{1,0:T(8,128)(2,1)S(1)}, bf16[2048,256]{1,0:T(8,128)(2,1)S(1)}, f32[64,256]{1,0:T(8,128)S(1)}) custom-call(s32[3]{0:T(128)S(1)} %pad_add_fusion.pos_ref, f32[8,16,256]{2,1,0:T(8,128)S(1)} %pad_maximum_fusion.refs_0_, f32[8,16,256]{2,1,0:T(8,128)S(1)} %collective-permute-done.3.refs_1_), custom_call_target="tpu_custom_call" | custom-call | tf_op jit(solution)/shard_map/weights/pallas_call | solution.py:357
  34.1 6.8 %collective-permute-done.7.refs_4_ = f32[128,256]{1,0:T(8,128)S(1)} collective-permute-done((f32[128,256]{1,0:T(8,128)S(1)}, f32[128,256]{1,0:T(8,128)S(1)}, u32[]{:S(2)}, u32[]{:S(2)}) %collective-permute-start.7) | collective-permute-done | bytes 131104 | tf_op jit(solution)/shard_map/ppermute | solution.py:378
  40.9 2.7 %collective-permute-done.8.refs_5_ = f32[128,256]{1,0:T(8,128)S(1)} collective-permute-done((f32[128,256]{1,0:T(8,128)S(1)}, f32[128,256]{1,0:T(8,128)S(1)}, u32[]{:S(2)}, u32[]{:S(2)}) %collective-permute-start.8) | collective-permute-done | bytes 131104 | tf_op jit(solution)/shard_map/ppermute | solution.py:378
  43.6 7.8 %filter.1 = (f32[128,256]{1,0:T(8,128)S(1)}, f32[128,256]{1,0:T(8,128)S(1)}, f32[128,256]{1,0:T(8,128)S(1)}, f32[128,256]{1,0:T(8,128)S(1)}, f32[128,256]{1,0:T(...) custom-call(s32[3]{0:T(128)S(1)} %pad_add_fusion.pos_ref, ...), custom_call_target="tpu_custom_call" | custom-call | tf_op jit(solution)/shard_map/filter/pallas_call | solution.py:357
  51.5 2.5 %collective-permute-start.14 = (f32[128,256]{1,0:T(8,128)S(1)}, f32[128,256]{1,0:T(8,128)S(1)}, u32[]{:S(2)}, u32[]{:S(2)}) collective-permute-start(f32[128,256]{1,0:T(8,128)S(1)} %get-tuple-element.49), channel_id=1, source_target_pairs={{0,4},{1,5},{2,6},{3,7},{4,0},{5,1},{6,2},{7,3},{8,12},{9,13},{10,... | collective-permute-start | bytes 393224 | tf_op jit(solution)/shard_map/ppermute | solution.py:378
  54.5 2.5 %collective-permute-start.16 = (f32[128,256]{1,0:T(8,128)S(1)}, f32[128,256]{1,0:T(8,128)S(1)}, u32[]{:S(2)}, u32[]{:S(2)}) collective-permute-start(f32[128,256]{1,0:T(8,128)S(1)} %get-tuple-element.51), channel_id=1, source_target_pairs={{0,6},{1,7},{2,4},{3,5},{4,2},{5,3},{6,0},{7,1},{8,14},{9,15},{10,... | collective-permute-start | bytes 393224 | tf_op jit(solution)/shard_map/ppermute | solution.py:378
  57.0 2.2 %collective-permute-start.17 = (f32[128,256]{1,0:T(8,128)S(1)}, f32[128,256]{1,0:T(8,128)S(1)}, u32[]{:S(2)}, u32[]{:S(2)}) collective-permute-start(f32[128,256]{1,0:T(8,128)S(1)} %get-tuple-element.52), channel_id=1, source_target_pairs={{0,7},{1,6},{2,5},{3,4},{4,3},{5,2},{6,1},{7,0},{8,15},{9,14},{10,... | collective-permute-start | bytes 393224 | tf_op jit(solution)/shard_map/ppermute | solution.py:378
  59.8 8.4 %collective-permute-done.14.refs_0_ = f32[128,256]{1,0:T(8,128)S(1)} collective-permute-done((f32[128,256]{1,0:T(8,128)S(1)}, f32[128,256]{1,0:T(8,128)S(1)}, u32[]{:S(2)}, u32[]{:S(2)}) %collective-permute-start.14) | collective-permute-done | bytes 131104 | tf_op jit(solution)/shard_map/ppermute | solution.py:378
  68.8 1.7 %collective-permute-done.15.refs_1_ = f32[128,256]{1,0:T(8,128)S(1)} collective-permute-done((f32[128,256]{1,0:T(8,128)S(1)}, f32[128,256]{1,0:T(8,128)S(1)}, u32[]{:S(2)}, u32[]{:S(2)}) %collective-permute-start.15) | collective-permute-done | bytes 131104 | tf_op jit(solution)/shard_map/ppermute | solution.py:378
  73.6 2.8 %collective-permute-done.13.refs_3_ = f32[128,256]{1,0:T(8,128)S(1)} collective-permute-done((f32[128,256]{1,0:T(8,128)S(1)}, f32[128,256]{1,0:T(8,128)S(1)}, u32[]{:S(2)}, u32[]{:S(2)}) %collective-permute-start.13) | collective-permute-done | bytes 131104 | tf_op jit(solution)/shard_map/ppermute | solution.py:378
  79.2 7.1 %collective-permute-done.25.far = f32[4,64,256]{2,1,0:T(8,128)S(1)} collective-permute-done((f32[4,64,256]{2,1,0:T(8,128)S(1)}, f32[4,64,256]{2,1,0:T(8,128)S(1)}, u32[]{:S(2)}, u32[]{:S(2)}) %collective-permute-start.25) | collective-permute-done | bytes 262176 | tf_op jit(solution)/shard_map/ppermute | solution.py:378
  86.3 5.2 %collective-permute-done.24.near = f32[4,64,256]{2,1,0:T(8,128)S(1)} collective-permute-done((f32[4,64,256]{2,1,0:T(8,128)S(1)}, f32[4,64,256]{2,1,0:T(8,128)S(1)}, u32[]{:S(2)}, u32[]{:S(2)}) %collective-permute-start.24) | collective-permute-done | bytes 262176 | tf_op jit(solution)/shard_map/ppermute | solution.py:378
  91.4 1.7 %own.1 = (f32[8,128,256]{2,1,0:T(8,128)S(1)}, f32[8,128,256]{2,1,0:T(8,128)S(1)}, f32[2,64,128]{2,1,0:T(8,128)S(1)}, f32[2,64,128]{2,1,0:T(8,128)S(1)}) custom-call(s32[3]{0:T(128)S(1)} %pad_add_fusion.pos_ref, f32[8,64,256]{2,1,0:T(8,128)S(1)} %get-tuple-element.48.near, f32[8,64,256]{2,1,0:T(8,128)S(1)} %get-tuple-element.53.far, ...), custom_call_target="tpu_custom_call" | custom-call | tf_op jit(solution)/shard_map/own/pallas_call | solution.py:357
  96.3 2.1 %collective-permute-start.20 = (f32[2,64,128]{2,1,0:T(8,128)S(1)}, f32[2,64,128]{2,1,0:T(8,128)S(1)}, u32[]{:S(2)}, u32[]{:S(2)}) collective-permute-start(f32[2,64,128]{2,1,0:T(8,128)S(1)} %get-tuple-element.56), channel_id=1, source_target_pairs={{0,1},{1,0},{2,3},{3,2},{4,5},{5,4},{6,7},{7,6},{8,9},{9,8},{10,11... | collective-permute-start | bytes 196616 | tf_op jit(solution)/shard_map/ppermute | solution.py:378
  98.4 2.3 %collective-permute-done.28.share_ref = f32[2,128,128]{2,1,0:T(8,128)S(1)} collective-permute-done((f32[2,128,128]{2,1,0:T(8,128)S(1)}, f32[2,128,128]{2,1,0:T(8,128)S(1)}, u32[]{:S(2)}, u32[]{:S(2)}) %collective-permute-start.28) | collective-permute-done | bytes 131104 | tf_op jit(solution)/shard_map/ppermute | solution.py:378
  101.3 2.1 %collective-permute-start.29 = (f32[2,64,128]{2,1,0:T(8,128)S(1)}, f32[2,64,128]{2,1,0:T(8,128)S(1)}, u32[]{:S(2)}, u32[]{:S(2)}) collective-permute-start(f32[2,64,128]{2,1,0:T(8,128)S(1)} %get-tuple-element.63), channel_id=1, source_target_pairs={{0,1},{1,0},{2,3},{3,2},{4,5},{5,4},{6,7},{7,6},{8,9},{9,8},{10,11... | collective-permute-start | bytes 196616 | tf_op jit(solution)/shard_map/ppermute | solution.py:378
  103.4 2.3 %collective-permute-start.21 = (f32[2,64,128]{2,1,0:T(8,128)S(1)}, f32[2,64,128]{2,1,0:T(8,128)S(1)}, u32[]{:S(2)}, u32[]{:S(2)}) collective-permute-start(f32[2,64,128]{2,1,0:T(8,128)S(1)} %add.104), channel_id=1, source_target_pairs={{0,2},{1,3},{2,0},{3,1},{4,6},{5,7},{6,4},{7,5},{8,10},{9,11},{10,... | collective-permute-start | bytes 196616 | tf_op jit(solution)/shard_map/ppermute | solution.py:378
  105.7 2.2 %collective-permute-start.30 = (f32[2,64,128]{2,1,0:T(8,128)S(1)}, f32[2,64,128]{2,1,0:T(8,128)S(1)}, u32[]{:S(2)}, u32[]{:S(2)}) collective-permute-start(f32[2,64,128]{2,1,0:T(8,128)S(1)} %add.107), channel_id=1, source_target_pairs={{0,2},{1,3},{2,0},{3,1},{4,6},{5,7},{6,4},{7,5},{8,10},{9,11},{10,... | collective-permute-start | bytes 196616 | tf_op jit(solution)/shard_map/ppermute | solution.py:378
  108.4 1.8 %collective-permute-start.22 = (f32[2,64,128]{2,1,0:T(8,128)S(1)}, f32[2,64,128]{2,1,0:T(8,128)S(1)}, u32[]{:S(2)}, u32[]{:S(2)}) collective-permute-start(f32[2,64,128]{2,1,0:T(8,128)S(1)} %add.105), channel_id=1, source_target_pairs={{0,4},{1,5},{2,6},{3,7},{4,0},{5,1},{6,2},{7,3},{8,12},{9,13},{10,... | collective-permute-start | bytes 196616 | tf_op jit(solution)/shard_map/ppermute | solution.py:378
  110.2 2.9 %collective-permute-start.31 = (f32[2,64,128]{2,1,0:T(8,128)S(1)}, f32[2,64,128]{2,1,0:T(8,128)S(1)}, u32[]{:S(2)}, u32[]{:S(2)}) collective-permute-start(f32[2,64,128]{2,1,0:T(8,128)S(1)} %add.108), channel_id=1, source_target_pairs={{0,4},{1,5},{2,6},{3,7},{4,0},{5,1},{6,2},{7,3},{8,12},{9,13},{10,... | collective-permute-start | bytes 196616 | tf_op jit(solution)/shard_map/ppermute | solution.py:378
  113.8 2.6 %collective-permute-start.23 = (f32[2,64,128]{2,1,0:T(8,128)S(1)}, f32[2,64,128]{2,1,0:T(8,128)S(1)}, u32[]{:S(2)}, u32[]{:S(2)}) collective-permute-start(f32[2,64,128]{2,1,0:T(8,128)S(1)} %add.106.own), channel_id=1, source_target_pairs={{0,1},{1,0},{2,3},{3,2},{4,5},{5,4},{6,7},{7,6},{8,9},{9,8},{10,11... | collective-permute-start | bytes 196616 | tf_op jit(solution)/shard_map/ppermute | solution.py:378
  118.9 1.8 %collective-permute-done.32.cross_other = f32[2,64,128]{2,1,0:T(8,128)S(1)} collective-permute-done((f32[2,64,128]{2,1,0:T(8,128)S(1)}, f32[2,64,128]{2,1,0:T(8,128)S(1)}, u32[]{:S(2)}, u32[]{:S(2)}) %collective-permute-start.32) | collective-permute-done | bytes 65568 | tf_op jit(solution)/shard_map/ppermute | solution.py:378
  (78 shorter events, 24.8 us)
Async XLA Ops:
  3.2 4.7 %collective-permute-start = (f32[1,16,256]{2,1,0:T(8,128)S(1)}, f32[1,16,256]{2,1,0:T(8,128)S(1)}, u32[]{:S(2)}, u32[]{:S(2)}) collective-permute-start(f32[1,16,256]{2,1,0:T(8,128)S(1)} %dynamic-slice_bitcast_fusion), channel_id=1, source_target_pairs={{0,1},{1,0},{2,3},{3,2},{4,5},{5,4},{6,7},{7,6},{8,9},{9,8},{10,11... | collective-permute-start | bytes 49160 | tf_op jit(solution)/shard_map/ppermute | solution.py:378
  8.0 4.0 %collective-permute-start.1 = (f32[2,16,256]{2,1,0:T(8,128)S(1)}, f32[2,16,256]{2,1,0:T(8,128)S(1)}, u32[]{:S(2)}, u32[]{:S(2)}) collective-permute-start(f32[2,16,256]{2,1,0:T(8,128)S(1)} %pad_maximum_fusion.2), channel_id=1, source_target_pairs={{0,2},{1,3},{2,0},{3,1},{4,6},{5,7},{6,4},{7,5},{8,10},{9,11},{10,... | collective-permute-start | bytes 98312 | tf_op jit(solution)/shard_map/ppermute | solution.py:378
  12.0 8.2 %collective-permute-start.2 = (f32[4,16,256]{2,1,0:T(8,128)S(1)}, f32[4,16,256]{2,1,0:T(8,128)S(1)}, u32[]{:S(2)}, u32[]{:S(2)}) collective-permute-start(f32[4,16,256]{2,1,0:T(8,128)S(1)} %pad_maximum_fusion.1), channel_id=1, source_target_pairs={{0,4},{1,5},{2,6},{3,7},{4,0},{5,1},{6,2},{7,3},{8,12},{9,13},{10,... | collective-permute-start | bytes 196616 | tf_op jit(solution)/shard_map/ppermute | solution.py:378
  17.3 8.0 %collective-permute-start.10 = (f32[128,256]{1,0:T(8,128)S(1)}, f32[128,256]{1,0:T(8,128)S(1)}, u32[]{:S(2)}, u32[]{:S(2)}) collective-permute-start(f32[128,256]{1,0:T(8,128)S(1)} %get-tuple-element.43), channel_id=1, source_target_pairs={{0,7},{1,6},{2,5},{3,4},{4,3},{5,2},{6,1},{7,0},{8,15},{9,14},{10,... | collective-permute-start | bytes 393224 | tf_op jit(solution)/shard_map/ppermute | solution.py:378
  19.6 6.9 %collective-permute-start.4 = (f32[128,256]{1,0:T(8,128)S(1)}, f32[128,256]{1,0:T(8,128)S(1)}, u32[]{:S(2)}, u32[]{:S(2)}) collective-permute-start(f32[128,256]{1,0:T(8,128)S(1)} %get-tuple-element.37), channel_id=1, source_target_pairs={{0,1},{1,0},{2,3},{3,2},{4,5},{5,4},{6,7},{7,6},{8,9},{9,8},{10,11... | collective-permute-start | bytes 393224 | tf_op jit(solution)/shard_map/ppermute | solution.py:378
  20.2 8.8 %collective-permute-start.3 = (f32[8,16,256]{2,1,0:T(8,128)S(1)}, f32[8,16,256]{2,1,0:T(8,128)S(1)}, u32[]{:S(2)}, u32[]{:S(2)}) collective-permute-start(f32[8,16,256]{2,1,0:T(8,128)S(1)} %pad_maximum_fusion.refs_0_), channel_id=1, source_target_pairs={{0,8},{8,0},{16,24},{24,16},{1,9},{9,1},{17,25},{25,17},{2,10},{10... | collective-permute-start | bytes 393224 | tf_op jit(solution)/shard_map/ppermute | solution.py:378
  20.3 12.7 %collective-permute-start.5 = (f32[128,256]{1,0:T(8,128)S(1)}, f32[128,256]{1,0:T(8,128)S(1)}, u32[]{:S(2)}, u32[]{:S(2)}) collective-permute-start(f32[128,256]{1,0:T(8,128)S(1)} %get-tuple-element.38), channel_id=1, source_target_pairs={{0,2},{1,3},{2,0},{3,1},{4,6},{5,7},{6,4},{7,5},{8,10},{9,11},{10,... | collective-permute-start | bytes 393224 | tf_op jit(solution)/shard_map/ppermute | solution.py:378
  20.9 13.2 %collective-permute-start.6 = (f32[128,256]{1,0:T(8,128)S(1)}, f32[128,256]{1,0:T(8,128)S(1)}, u32[]{:S(2)}, u32[]{:S(2)}) collective-permute-start(f32[128,256]{1,0:T(8,128)S(1)} %get-tuple-element.39), channel_id=1, source_target_pairs={{0,3},{1,2},{2,1},{3,0},{4,7},{5,6},{6,5},{7,4},{8,11},{9,10},{10,... | collective-permute-start | bytes 393224 | tf_op jit(solution)/shard_map/ppermute | solution.py:378
  25.2 15.7 %collective-permute-start.7 = (f32[128,256]{1,0:T(8,128)S(1)}, f32[128,256]{1,0:T(8,128)S(1)}, u32[]{:S(2)}, u32[]{:S(2)}) collective-permute-start(f32[128,256]{1,0:T(8,128)S(1)} %get-tuple-element.40), channel_id=1, source_target_pairs={{0,4},{1,5},{2,6},{3,7},{4,0},{5,1},{6,2},{7,3},{8,12},{9,13},{10,... | collective-permute-start | bytes 393224 | tf_op jit(solution)/shard_map/ppermute | solution.py:378
  26.5 17.1 %collective-permute-start.8 = (f32[128,256]{1,0:T(8,128)S(1)}, f32[128,256]{1,0:T(8,128)S(1)}, u32[]{:S(2)}, u32[]{:S(2)}) collective-permute-start(f32[128,256]{1,0:T(8,128)S(1)} %get-tuple-element.41), channel_id=1, source_target_pairs={{0,5},{1,4},{2,7},{3,6},{4,1},{5,0},{6,3},{7,2},{8,13},{9,12},{10,... | collective-permute-start | bytes 393224 | tf_op jit(solution)/shard_map/ppermute | solution.py:378
  29.0 14.6 %collective-permute-start.9 = (f32[128,256]{1,0:T(8,128)S(1)}, f32[128,256]{1,0:T(8,128)S(1)}, u32[]{:S(2)}, u32[]{:S(2)}) collective-permute-start(f32[128,256]{1,0:T(8,128)S(1)} %get-tuple-element.42), channel_id=1, source_target_pairs={{0,6},{1,7},{2,4},{3,5},{4,2},{5,3},{6,0},{7,1},{8,14},{9,15},{10,... | collective-permute-start | bytes 393224 | tf_op jit(solution)/shard_map/ppermute | solution.py:378
  51.5 16.7 %collective-permute-start.14 = (f32[128,256]{1,0:T(8,128)S(1)}, f32[128,256]{1,0:T(8,128)S(1)}, u32[]{:S(2)}, u32[]{:S(2)}) collective-permute-start(f32[128,256]{1,0:T(8,128)S(1)} %get-tuple-element.49), channel_id=1, source_target_pairs={{0,4},{1,5},{2,6},{3,7},{4,0},{5,1},{6,2},{7,3},{8,12},{9,13},{10,... | collective-permute-start | bytes 393224 | tf_op jit(solution)/shard_map/ppermute | solution.py:378
  54.0 16.5 %collective-permute-start.15 = (f32[128,256]{1,0:T(8,128)S(1)}, f32[128,256]{1,0:T(8,128)S(1)}, u32[]{:S(2)}, u32[]{:S(2)}) collective-permute-start(f32[128,256]{1,0:T(8,128)S(1)} %get-tuple-element.50), channel_id=1, source_target_pairs={{0,5},{1,4},{2,7},{3,6},{4,1},{5,0},{6,3},{7,2},{8,13},{9,12},{10,... | collective-permute-start | bytes 393224 | tf_op jit(solution)/shard_map/ppermute | solution.py:378
  54.5 16.7 %collective-permute-start.16 = (f32[128,256]{1,0:T(8,128)S(1)}, f32[128,256]{1,0:T(8,128)S(1)}, u32[]{:S(2)}, u32[]{:S(2)}) collective-permute-start(f32[128,256]{1,0:T(8,128)S(1)} %get-tuple-element.51), channel_id=1, source_target_pairs={{0,6},{1,7},{2,4},{3,5},{4,2},{5,3},{6,0},{7,1},{8,14},{9,15},{10,... | collective-permute-start | bytes 393224 | tf_op jit(solution)/shard_map/ppermute | solution.py:378
  57.0 14.2 %collective-permute-start.17 = (f32[128,256]{1,0:T(8,128)S(1)}, f32[128,256]{1,0:T(8,128)S(1)}, u32[]{:S(2)}, u32[]{:S(2)}) collective-permute-start(f32[128,256]{1,0:T(8,128)S(1)} %get-tuple-element.52), channel_id=1, source_target_pairs={{0,7},{1,6},{2,5},{3,4},{4,3},{5,2},{6,1},{7,0},{8,15},{9,14},{10,... | collective-permute-start | bytes 393224 | tf_op jit(solution)/shard_map/ppermute | solution.py:378
  59.2 12.7 %collective-permute-start.11 = (f32[128,256]{1,0:T(8,128)S(1)}, f32[128,256]{1,0:T(8,128)S(1)}, u32[]{:S(2)}, u32[]{:S(2)}) collective-permute-start(f32[128,256]{1,0:T(8,128)S(1)} %get-tuple-element.45), channel_id=1, source_target_pairs={{0,1},{1,0},{2,3},{3,2},{4,5},{5,4},{6,7},{7,6},{8,9},{9,8},{10,11... | collective-permute-start | bytes 393224 | tf_op jit(solution)/shard_map/ppermute | solution.py:378
  68.2 5.4 %collective-permute-start.12 = (f32[128,256]{1,0:T(8,128)S(1)}, f32[128,256]{1,0:T(8,128)S(1)}, u32[]{:S(2)}, u32[]{:S(2)}) collective-permute-start(f32[128,256]{1,0:T(8,128)S(1)} %get-tuple-element.46), channel_id=1, source_target_pairs={{0,2},{1,3},{2,0},{3,1},{4,6},{5,7},{6,4},{7,5},{8,10},{9,11},{10,... | collective-permute-start | bytes 393224 | tf_op jit(solution)/shard_map/ppermute | solution.py:378
  70.5 5.9 %collective-permute-start.13 = (f32[128,256]{1,0:T(8,128)S(1)}, f32[128,256]{1,0:T(8,128)S(1)}, u32[]{:S(2)}, u32[]{:S(2)}) collective-permute-start(f32[128,256]{1,0:T(8,128)S(1)} %get-tuple-element.47), channel_id=1, source_target_pairs={{0,3},{1,2},{2,1},{3,0},{4,7},{5,6},{6,5},{7,4},{8,11},{9,10},{10,... | collective-permute-start | bytes 393224 | tf_op jit(solution)/shard_map/ppermute | solution.py:378
  71.8 19.6 %collective-permute-start.19 = (f32[8,64,256]{2,1,0:T(8,128)S(1)}, f32[8,64,256]{2,1,0:T(8,128)S(1)}, u32[]{:S(2)}, u32[]{:S(2)}) collective-permute-start(f32[8,64,256]{2,1,0:T(8,128)S(1)} %get-tuple-element.53.far), channel_id=1, source_target_pairs={{0,8},{8,0},{16,24},{24,16},{1,9},{9,1},{17,25},{25,17},{2,10},{10... | collective-permute-start | bytes 1572872 | tf_op jit(solution)/shard_map/ppermute | solution.py:378
  77.0 14.4 %collective-permute-start.18 = (f32[8,64,256]{2,1,0:T(8,128)S(1)}, f32[8,64,256]{2,1,0:T(8,128)S(1)}, u32[]{:S(2)}, u32[]{:S(2)}) collective-permute-start(f32[8,64,256]{2,1,0:T(8,128)S(1)} %get-tuple-element.48.near), channel_id=1, source_target_pairs={{0,8},{8,0},{16,24},{24,16},{1,9},{9,1},{17,25},{25,17},{2,10},{10... | collective-permute-start | bytes 1572872 | tf_op jit(solution)/shard_map/ppermute | solution.py:378
  77.1 9.2 %collective-permute-start.25 = (f32[4,64,256]{2,1,0:T(8,128)S(1)}, f32[4,64,256]{2,1,0:T(8,128)S(1)}, u32[]{:S(2)}, u32[]{:S(2)}) collective-permute-start(f32[4,64,256]{2,1,0:T(8,128)S(1)} %get-tuple-element.59), channel_id=1, source_target_pairs={{0,16},{8,24},{16,0},{24,8},{1,17},{9,25},{17,1},{25,9},{2,18},{10... | collective-permute-start | bytes 786440 | tf_op jit(solution)/shard_map/ppermute | solution.py:378
  78.6 12.8 %collective-permute-start.24 = (f32[4,64,256]{2,1,0:T(8,128)S(1)}, f32[4,64,256]{2,1,0:T(8,128)S(1)}, u32[]{:S(2)}, u32[]{:S(2)}) collective-permute-start(f32[4,64,256]{2,1,0:T(8,128)S(1)} %get-tuple-element.58), channel_id=1, source_target_pairs={{0,16},{8,24},{16,0},{24,8},{1,17},{9,25},{17,1},{25,9},{2,18},{10... | collective-permute-start | bytes 786440 | tf_op jit(solution)/shard_map/ppermute | solution.py:378
  86.3 6.9 %collective-permute-start.27 = (f32[4,64,256]{2,1,0:T(8,128)S(1)}, f32[4,64,256]{2,1,0:T(8,128)S(1)}, u32[]{:S(2)}, u32[]{:S(2)}) collective-permute-start(f32[4,64,256]{2,1,0:T(8,128)S(1)} %collective-permute-done.25.far), channel_id=1, source_target_pairs={{0,8},{8,0},{16,24},{24,16},{1,9},{9,1},{17,25},{25,17},{2,10},{10... | collective-permute-start | bytes 786440 | tf_op jit(solution)/shard_map/ppermute | solution.py:378
  94.8 6.0 %collective-permute-start.28 = (f32[2,128,128]{2,1,0:T(8,128)S(1)}, f32[2,128,128]{2,1,0:T(8,128)S(1)}, u32[]{:S(2)}, u32[]{:S(2)}) collective-permute-start(f32[2,128,128]{2,1,0:T(8,128)S(1)} %get-tuple-element.61), channel_id=1, source_target_pairs={{0,16},{8,24},{16,0},{24,8},{1,17},{9,25},{17,1},{25,9},{2,18},{10... | collective-permute-start | bytes 393224 | tf_op jit(solution)/shard_map/ppermute | solution.py:378
  96.3 7.1 %collective-permute-start.20 = (f32[2,64,128]{2,1,0:T(8,128)S(1)}, f32[2,64,128]{2,1,0:T(8,128)S(1)}, u32[]{:S(2)}, u32[]{:S(2)}) collective-permute-start(f32[2,64,128]{2,1,0:T(8,128)S(1)} %get-tuple-element.56), channel_id=1, source_target_pairs={{0,1},{1,0},{2,3},{3,2},{4,5},{5,4},{6,7},{7,6},{8,9},{9,8},{10,11... | collective-permute-start | bytes 196616 | tf_op jit(solution)/shard_map/ppermute | solution.py:378
  101.3 4.4 %collective-permute-start.29 = (f32[2,64,128]{2,1,0:T(8,128)S(1)}, f32[2,64,128]{2,1,0:T(8,128)S(1)}, u32[]{:S(2)}, u32[]{:S(2)}) collective-permute-start(f32[2,64,128]{2,1,0:T(8,128)S(1)} %get-tuple-element.63), channel_id=1, source_target_pairs={{0,1},{1,0},{2,3},{3,2},{4,5},{5,4},{6,7},{7,6},{8,9},{9,8},{10,11... | collective-permute-start | bytes 196616 | tf_op jit(solution)/shard_map/ppermute | solution.py:378
  103.4 5.0 %collective-permute-start.21 = (f32[2,64,128]{2,1,0:T(8,128)S(1)}, f32[2,64,128]{2,1,0:T(8,128)S(1)}, u32[]{:S(2)}, u32[]{:S(2)}) collective-permute-start(f32[2,64,128]{2,1,0:T(8,128)S(1)} %add.104), channel_id=1, source_target_pairs={{0,2},{1,3},{2,0},{3,1},{4,6},{5,7},{6,4},{7,5},{8,10},{9,11},{10,... | collective-permute-start | bytes 196616 | tf_op jit(solution)/shard_map/ppermute | solution.py:378
  105.7 4.5 %collective-permute-start.30 = (f32[2,64,128]{2,1,0:T(8,128)S(1)}, f32[2,64,128]{2,1,0:T(8,128)S(1)}, u32[]{:S(2)}, u32[]{:S(2)}) collective-permute-start(f32[2,64,128]{2,1,0:T(8,128)S(1)} %add.107), channel_id=1, source_target_pairs={{0,2},{1,3},{2,0},{3,1},{4,6},{5,7},{6,4},{7,5},{8,10},{9,11},{10,... | collective-permute-start | bytes 196616 | tf_op jit(solution)/shard_map/ppermute | solution.py:378
  108.4 5.4 %collective-permute-start.22 = (f32[2,64,128]{2,1,0:T(8,128)S(1)}, f32[2,64,128]{2,1,0:T(8,128)S(1)}, u32[]{:S(2)}, u32[]{:S(2)}) collective-permute-start(f32[2,64,128]{2,1,0:T(8,128)S(1)} %add.105), channel_id=1, source_target_pairs={{0,4},{1,5},{2,6},{3,7},{4,0},{5,1},{6,2},{7,3},{8,12},{9,13},{10,... | collective-permute-start | bytes 196616 | tf_op jit(solution)/shard_map/ppermute | solution.py:378
  110.2 6.2 %collective-permute-start.31 = (f32[2,64,128]{2,1,0:T(8,128)S(1)}, f32[2,64,128]{2,1,0:T(8,128)S(1)}, u32[]{:S(2)}, u32[]{:S(2)}) collective-permute-start(f32[2,64,128]{2,1,0:T(8,128)S(1)} %add.108), channel_id=1, source_target_pairs={{0,4},{1,5},{2,6},{3,7},{4,0},{5,1},{6,2},{7,3},{8,12},{9,13},{10,... | collective-permute-start | bytes 196616 | tf_op jit(solution)/shard_map/ppermute | solution.py:378
  113.8 5.1 %collective-permute-start.23 = (f32[2,64,128]{2,1,0:T(8,128)S(1)}, f32[2,64,128]{2,1,0:T(8,128)S(1)}, u32[]{:S(2)}, u32[]{:S(2)}) collective-permute-start(f32[2,64,128]{2,1,0:T(8,128)S(1)} %add.106.own), channel_id=1, source_target_pairs={{0,1},{1,0},{2,3},{3,2},{4,5},{5,4},{6,7},{7,6},{8,9},{9,8},{10,11... | collective-permute-start | bytes 196616 | tf_op jit(solution)/shard_map/ppermute | solution.py:378
  116.4 4.3 %collective-permute-start.32 = (f32[2,64,128]{2,1,0:T(8,128)S(1)}, f32[2,64,128]{2,1,0:T(8,128)S(1)}, u32[]{:S(2)}, u32[]{:S(2)}) collective-permute-start(f32[2,64,128]{2,1,0:T(8,128)S(1)} %add.109.cross), channel_id=1, source_target_pairs={{0,1},{1,0},{2,3},{3,2},{4,5},{5,4},{6,7},{7,6},{8,9},{9,8},{10,11... | collective-permute-start | bytes 196616 | tf_op jit(solution)/shard_map/ppermute | solution.py:378
  (9 other events, 86.4 us)

commit v3 on v2

--- a/solution.py
+++ b/solution.py
@@ -13,7 +13,7 @@
 SLAB = 8
 SIDE = 16
 LAT = SIDE * SIDE
-CHUNKS = 1
+ORDER = (5, 6, 7, 1, 2, 3, 4)
 
 COEFFS = (
     -5369.0 / 1800.0,
@@ -84,17 +84,35 @@
     return hi, lo
 
 
-def split_kernel(nd, nb, chunks, pos_ref, x_ref, *refs):
-    outs, scratch = refs[:-1], refs[-1]
-    i = pos_ref[0]
+def split_kernel(nd, nb, pos_ref, cell_ref, x_ref, v_ref, w_ref, code_ref, mine_ref, *refs):
+    outs, (scratch, packed) = refs[:-2], refs[-2:]
+    i, core = pos_ref[0], pos_ref[1] & 1
+    cube = 2 * REACH + 1
+    code = code_ref[...].astype(F32)
+    off_x = jnp.floor((code + 0.5) * (1.0 / (cube * cube)))
+    rest = code - off_x * (cube * cube)
+    off_y = jnp.floor((rest + 0.5) * (1.0 / cube))
+    off_z = rest - off_y * cube
+    for a in range(2):
+        packed[a * 8 : a * 8 + 8] = w_ref[a]
+        cell_x, cell_y, cell_z = (
+            lax.rem(cell_ref[a, k], n).astype(F32) for k, n in enumerate((SLAB, SIDE, SIDE))
+        )
+        y = off_y[a : a + 1] + (cell_y + float(SIDE - REACH))
+        z = off_z[a : a + 1] + (cell_z + float(SIDE - REACH))
+        y = y - SIDE * jnp.floor(y * (1.0 / SIDE))
+        z = z - SIDE * jnp.floor(z * (1.0 / SIDE))
+        packed[16 + a : 17 + a] = off_x[a : a + 1] + cell_x
+        packed[18 + a : 19 + a] = y * SIDE + z
+    packed[20:24] = jnp.zeros((4, LAT), F32)
+    packed[24:32] = jnp.concatenate([v_ref[:, y, :] for y in range(SIDE)], axis=1)
+    mine_ref[0] = packed[pl.ds(pl.multiple_of(core * 16, 16), 16)]
     for q in range(SLAB):
         scratch[q] = x_ref[q].T
-    real = scratch.shape[1] // (nd * chunks)
-    for c in range(chunks):
-        for j in range(nd):
-            start = c * nd * real + (i ^ j) * real
-            for q in range(SLAB):
-                outs[c * nd + j][q * nb : (q + 1) * nb] = scratch[q, pl.ds(pl.multiple_of(start, nb), nb)]
+    for j in range(nd):
+        start = (i ^ j) * nb
+        for q in range(SLAB):
+            outs[j][q * nb : (q + 1) * nb] = scratch[q, pl.ds(pl.multiple_of(start, nb), nb)]
 
 
 def weights_kernel(nd, pos_ref, *refs):
@@ -235,8 +253,8 @@
         outs[j][...] = (y * scale[None]).reshape(R, LAT)
 
 
-def join_kernel(count, nb, pos_ref, *refs):
-    pieces, (z_ref, send_ref) = refs[:count], refs[count:]
+def join_kernel(count, nb, ties, pos_ref, *refs):
+    pieces, (z_ref, send_ref) = refs[:count], refs[count + ties :]
     i, y = pos_ref[0], pos_ref[2]
     for j in range(count):
         rows = pl.ds(pl.multiple_of(((i ^ j) & (count - 1)) * nb, nb), nb)
@@ -276,8 +294,10 @@
         send_ref[c] = g_ref[c, pl.ds(pl.multiple_of((1 - x) * 64, 64), 64)]
 
 
-def cross_kernel(pos_ref, z_ref, zc_ref, near, far, core_near, core_far, g_ref, back_ref, f_ref, fc_ref):
-    b, y = pos_ref[1], pos_ref[2]
+def cross_kernel(
+    pos_ref, z_ref, zc_ref, near, far, core_near, core_far, tie, keep, send, back, back_send, g_ref, back_ref, f_ref, fc_ref
+):
+    i, b, y = pos_ref[0], pos_ref[1], pos_ref[2]
     half = SLAB // 2
     place_halves(pos_ref, near, far, f_ref)
     place_halves(pos_ref, core_near, core_far, fc_ref)
@@ -296,11 +316,19 @@
         totals = now if totals is None else tuple(t + n for t, n in zip(totals, now))
     c = b & 1
     g_ref[c], g_ref[c ^ 1], back_ref[c], back_ref[c ^ 1] = totals
-
-
-def part_kernel(pos_ref, g_ref, share_ref, keep_ref, send_ref, sum_ref):
-    sum_ref[...] = g_ref[...] + share_ref[...]
-    cut_rows(pos_ref[0], sum_ref, keep_ref, send_ref)
+    cut_rows(i, g_ref, keep, send)
+    cut_rows(i, back_ref, back, back_send)
+
+
+def sum_kernel(a_ref, b_ref, c_ref, d_ref, tie, out_ref):
+    out_ref[...] = (a_ref[...] + b_ref[...]) + (c_ref[...] + d_ref[...])
+
+
+def pair_kernel(total, pos_ref, own, cross, cross_other, out_ref):
+    y = pos_ref[2]
+    for c in range(2):
+        out_ref[y * 2 + c] = own[c] * (1.0 / total)
+        out_ref[(1 - y) * 2 + c] = (cross[c] + cross_other[c]) * (1.0 / total)
 
 
 def output_kernel(z_ref, out_ref):
@@ -308,14 +336,12 @@
         out_ref[q] = z_ref[q].T
 
 
-def place_kernel(total, pos_ref, own, own_other, cross, cross_other, out_ref):
-    i, y = pos_ref[0], pos_ref[2]
-    x = i & 1
-    for c in range(2):
-        for mine, other, chip in ((own, own_other, y), (cross, cross_other, 1 - y)):
-            lanes = pl.ds(pl.multiple_of((chip * 2 + c) * 128, 128), 128)
-            out_ref[pl.ds(pl.multiple_of(x * 64, 64), 64), lanes] = mine[c] * (1.0 / total)
-            out_ref[pl.ds(pl.multiple_of((1 - x) * 64, 64), 64), lanes] = other[c] * (1.0 / total)
+def place_kernel(pos_ref, mine, other, out_ref):
+    x = pos_ref[0] & 1
+    for k in range(4):
+        lanes = slice(k * 128, (k + 1) * 128)
+        out_ref[pl.ds(pl.multiple_of(x * 64, 64), 64), lanes] = mine[k]
+        out_ref[pl.ds(pl.multiple_of((1 - x) * 64, 64), 64), lanes] = other[k]
 
 
 def gram_kernel(pos_ref, own, core, far, far_core, g_ref, far_ref):
@@ -348,11 +374,10 @@
     far_ref[(b & 1) ^ 1] = totals["back_core"]
 
 
-def call(kernel, out_shape, operands, scratch=(), name=None):
+def call(kernel, out_shape, operands, scratch=(), name=None, ties=()):
     specs = [
-        pl.BlockSpec(memory_space=pltpu.SMEM) if o.dtype == jnp.int32 else pl.BlockSpec(memory_space=pltpu.VMEM)
-        for o in operands
-    ]
+        pl.BlockSpec(memory_space=pltpu.SMEM if o.dtype == jnp.int32 and o.size < 128 else pltpu.VMEM) for o in operands
+    ] + [pl.BlockSpec(memory_space=pl.ANY) for _ in ties]
     single = not isinstance(out_shape, (list, tuple))
     return pl.pallas_call(
         kernel,
@@ -366,7 +391,7 @@
         scratch_shapes=list(scratch),
         compiler_params=pltpu.CompilerParams(vmem_limit_bytes=VMEM_LIMIT),
         name=name,
-    )(*operands)
+    )(*operands, *ties)
 
 
 def shape(*dims, dtype=F32):
@@ -378,9 +403,18 @@
     return lax.ppermute(value, axis, [(k, k ^ step) for k in range(count)])
 
 
+def both_permute(value):
+    nd, ng = lax.axis_size("dom"), lax.axis_size("band")
+    pairs = [(b * nd + d, (b ^ 2) * nd + (d ^ 1)) for b in range(ng) for d in range(nd)]
+    return lax.ppermute(value, ("band", "dom"), pairs)
+
+
 def swap_all(pieces, direct):
     if direct:
-        return [pieces[0]] + [xor_permute(p, "dom", j) for j, p in enumerate(pieces) if j]
+        got = {0: pieces[0]}
+        for j in ORDER:
+            got[j] = xor_permute(pieces[j], "dom", j)
+        return [got[j] for j in range(len(pieces))]
     stacked = lax.all_to_all(jnp.stack(pieces), "dom", 0, 0, tiled=True)
     return [stacked[j] for j in range(len(pieces))]
 
@@ -410,8 +444,7 @@
     nd = lax.axis_size("dom")
     bands = trial_waves.shape[-1]
     direct = nd == 8
-    chunks = CHUNKS if direct else 1
-    real = bands // (nd * chunks)
+    real = bands // nd
     nb = max(real, 8)
     total = nd * SLAB * LAT
     dom = lax.axis_index("dom") if direct else jnp.int32(0)
@@ -420,26 +453,22 @@
     pos_band = jnp.stack([dom, band, band // 2]).astype(jnp.int32)
     R = SLAB * nb
 
-    packed = packed_atoms(potential, proj_weights, atom_cell, point_codes)
+    waves = trial_waves.reshape(SLAB, LAT, bands)
     if direct:
-        gathered = lax.dynamic_slice_in_dim(packed, band % 2 * 16, 16, 0)[None]
+        gathered, *cut = call(
+            functools.partial(split_kernel, nd, nb),
+            [shape(1, 16, 256)] + [shape(R, LAT)] * nd,
+            [pos, atom_cell, waves, potential, proj_weights, point_codes],
+            [pltpu.VMEM((SLAB, bands, LAT), F32), pltpu.VMEM((32, 256), F32)],
+            "split",
+        )
         for step in (1, 2, 4):
             gathered = jnp.concatenate([gathered, xor_permute(gathered, "dom", step)])
         parts = [gathered, xor_permute(gathered, "band", 1)]
     else:
+        packed = packed_atoms(potential, proj_weights, atom_cell, point_codes)
         gathered = lax.all_gather(packed, "dom", axis=0)
         parts = [gathered[:, :16], gathered[:, 16:]]
-
-    waves = trial_waves.reshape(SLAB, LAT, bands)
-    if direct:
-        cut = call(
-            functools.partial(split_kernel, nd, nb, chunks),
-            [shape(R, LAT)] * (nd * chunks),
-            [pos, waves],
-            [pltpu.VMEM((SLAB, bands, LAT), F32)],
-            "split",
-        )
-    else:
         turned = waves.transpose(0, 2, 1).reshape(SLAB, nd, real, LAT).transpose(1, 0, 2, 3)
         cut = [turned[j] for j in range(nd)]
 
@@ -454,26 +483,24 @@
     fold = jnp.asarray(fold_matrix()).astype(BF16)
     kb_row = jnp.concatenate([kb_energy, kb_energy, jnp.zeros((112,), F32)])[None]
     spread = fold
-    arrived = [swap_all(cut[c * nd : (c + 1) * nd], direct) for c in range(chunks)]
-    for c in range(chunks):
-        pieces = arrived[c]
-        if not direct:
-            pieces = [jnp.pad(p, ((0, 0), (0, nb - real), (0, 0))).reshape(R, LAT) for p in pieces]
-        ready = call(
-            functools.partial(filter_kernel, nd, nb, float(total)),
-            [shape(R, LAT)] * nd,
-            [pos, kb_row, shifted, wh, wl, lh, ll, fold, spread] + pieces,
-            [
-                pltpu.VMEM(((nd * SLAB + 2 * HALO) * nb, LAT), F32),
-                pltpu.VMEM(((nd * SLAB + 2 * HALO) * nb, LAT), F32),
-                pltpu.VMEM((nd * nb, 256), F32),
-                pltpu.VMEM((nd * nb, 256), F32),
-            ],
-            "filter",
-        )
-        if not direct:
-            ready = [p.reshape(SLAB, nb, LAT)[:, :real] for p in ready]
-        back = swap_all(ready, direct)
+    pieces = swap_all(cut, direct)
+    if not direct:
+        pieces = [jnp.pad(p, ((0, 0), (0, nb - real), (0, 0))).reshape(R, LAT) for p in pieces]
+    ready = call(
+        functools.partial(filter_kernel, nd, nb, float(total)),
+        [shape(R, LAT)] * nd,
+        [pos, kb_row, shifted, wh, wl, lh, ll, fold, spread] + pieces,
+        [
+            pltpu.VMEM(((nd * SLAB + 2 * HALO) * nb, LAT), F32),
+            pltpu.VMEM(((nd * SLAB + 2 * HALO) * nb, LAT), F32),
+            pltpu.VMEM((nd * nb, 256), F32),
+            pltpu.VMEM((nd * nb, 256), F32),
+        ],
+        "filter",
+    )
+    if not direct:
+        ready = [p.reshape(SLAB, nb, LAT)[:, :real] for p in ready]
+    back = swap_all(ready, direct)
     if direct:
         filtered, correlation = finish_direct(back, pos, nb, bands, float(total))
     else:
@@ -485,19 +512,20 @@
     group = len(back) // 2
     half = SLAB // 2
 
-    def exchanged(pieces):
+    def exchanged(pieces, ties):
         z, send = call(
-            functools.partial(join_kernel, group, nb),
+            functools.partial(join_kernel, group, nb, len(ties)),
             [shape(SLAB, group * nb, LAT), shape(half, group * nb, LAT)],
             [pos] + pieces,
             (),
             "join",
+            ties,
         )
         far = xor_permute(send, "band", 2)
         return z, xor_permute(z, "band", 1), far, xor_permute(far, "band", 1)
 
-    z_near, core_near, far_near, far_core_near = exchanged(back[:group])
-    z_far, core_far, far_far, far_core_far = exchanged(back[group:])
+    z_near, core_near, far_near, far_core_near = exchanged(back[:group], [])
+    z_far, core_far, far_far, far_core_far = exchanged(back[group:], [far_near])
     part = shape(2, bands // 2, bands)
     block = pltpu.VMEM((2, bands, bands), F32)
     z, z_core, own_keep, own_send = call(
@@ -507,26 +535,41 @@
         [block],
         "own",
     )
-    gram, share = call(
+    own = own_keep + xor_permute(own_send, "dom", 1)
+    own_tie = own
+    own = own + xor_permute(own, "dom", 2)
+    own = own + xor_permute(own, "dom", 4)
+    keep, send, back_keep, back_send = call(
         cross_kernel,
-        [shape(2, bands, bands), shape(2, bands, bands)],
+        [part] * 4,
         [pos, z, z_core, far_near, far_far, far_core_near, far_core_far],
-        [pltpu.VMEM((half, bands, LAT), F32), pltpu.VMEM((half, bands, LAT), F32)],
+        [block, block, pltpu.VMEM((half, bands, LAT), F32), pltpu.VMEM((half, bands, LAT), F32)],
         "cross",
-    )
-    cross_keep, cross_send = call(
-        part_kernel, [part, part], [pos, gram, xor_permute(share, "band", 2)], [block], "part"
-    )
-
-    def summed(keep, send):
-        rows = keep + xor_permute(send, "dom", 1)
-        rows = rows + xor_permute(rows, "dom", 2)
-        rows = rows + xor_permute(rows, "dom", 4)
-        return [rows, xor_permute(rows, "dom", 1)]
-
-    rows = summed(own_keep, own_send) + summed(cross_keep, cross_send)
+        [own_tie],
+    )
+    cross = call(
+        sum_kernel,
+        part,
+        [
+            keep,
+            xor_permute(send, "dom", 1),
+            xor_permute(back_keep, "band", 2),
+            both_permute(back_send),
+        ],
+        (),
+        "sum",
+        [own],
+    )
+    cross = cross + xor_permute(cross, "dom", 2)
+    rows = call(
+        functools.partial(pair_kernel, total),
+        shape(4, bands // 2, bands),
+        [pos, own, cross, xor_permute(cross, "dom", 4)],
+        (),
+        "pair",
+    )
     filtered = call(output_kernel, shape(SLAB, LAT, bands), [z], (), "output")
-    correlation = call(functools.partial(place_kernel, total), shape(bands, 4 * bands), [pos] + rows, (), "place")
+    correlation = call(place_kernel, shape(bands, 4 * bands), [pos, rows, xor_permute(rows, "dom", 1)], (), "place")
     return filtered, correlation
 
 

time: 122 us -> 132 us (1.082)
  waiting for transfers between devices: 48.3 us -> 65.9 us
  starting transfers between devices: 50.3 us -> 43.4 us
    ppermute x33 -> x32, waiting for transfers between devices: 48.3 us -> 64.5 us  [xor_permute(): return lax.ppermute(value, axis, [(k, k ^ step) for k in range(count)])]
    ppermute x33 -> x32, starting transfers between devices: 50.3 us -> 41.9 us  [xor_permute(): return lax.ppermute(value, axis, [(k, k ^ step) for k in range(count)])]
    ppermute x0 -> x1, starting transfers between devices: none -> 1.44 us  [both_permute(): return lax.ppermute(value, ('band', 'dom'), pairs)]
    ppermute x0 -> x1, waiting for transfers between devices: none -> 1.41 us  [both_permute(): return lax.ppermute(value, ('band', 'dom'), pairs)]
    unnamed x16 -> x21, local copies, waits for them, and re-layouts: 2.52 us -> 2.78 us
    pallas_call x10 -> x11, Pallas kernels: 18.5 us -> 18.6 us  [call(): pl.pallas_call(kernel, out_shape=out_shape, in_specs=specs, out_specs=pl....]
  transfers between devices with their start and end apart: 33 -> 33, of which waited for: 17 -> 18; matrix products, arithmetic and copies ran while one was open for 0% -> 0% of each run, Pallas kernels for 6% -> 6%
where the time goes in v3:
time: 132 us
  waiting for transfers between devices  65.9 us (50%)
  starting transfers between devices  43.4 us (33%)
  Pallas kernels  18.6 us (14%)
  local copies, waits for them, and re-layouts  2.79 us (2%)
    ppermute x32, waiting for transfers between devices, xor_permute(): return lax.ppermute(value, axis, [(k, k ^ step) for k in range(count)])  64.5 us
    ppermute x32, starting transfers between devices, xor_permute(): return lax.ppermute(value, axis, [(k, k ^ step) for k in range(count)])  41.9 us
    pallas_call x11, Pallas kernels, call(): pl.pallas_call(kernel, out_shape=out_shape, in_specs=specs, out_specs=pl....  18.6 us
    unnamed x21, local copies, waits for them, and re-layouts  2.78 us
  transfers between devices with their start and end apart: 33, of which 18 were waited for; matrix products, arithmetic and copies ran while one was open for 0% of the time, Pallas kernels for 6%

profile of v3, /device:TPU:0, one launch (start us, length us, event | category | flops | bytes accessed | tf_op | source)
XLA Modules:
  0.0 131.7 jit_solution(1063390617203446452)
XLA Ops:
  4.5 3.0 %collective-permute-start = (f32[1,16,256]{2,1,0:T(8,128)S(1)}, f32[1,16,256]{2,1,0:T(8,128)S(1)}, u32[]{:S(2)}, u32[]{:S(2)}) collective-permute-start(f32[1,16,256]{2,1,0:T(8,128)S(1)} %get-tuple-element.34), channel_id=1, source_target_pairs={{0,1},{1,0},{2,3},{3,2},{4,5},{5,4},{6,7},{7,6},{8,9},{9,8},{10,11... | collective-permute-start | bytes 49160 | tf_op jit(solution)/shard_map/ppermute | solution.py:403
  7.5 3.6 %collective-permute-start.10 = (f32[128,256]{1,0:T(8,128)S(1)}, f32[128,256]{1,0:T(8,128)S(1)}, u32[]{:S(2)}, u32[]{:S(2)}) collective-permute-start(f32[128,256]{1,0:T(8,128)S(1)} %get-tuple-element.45), channel_id=1, source_target_pairs={{0,7},{1,6},{2,5},{3,4},{4,3},{5,2},{6,1},{7,0},{8,15},{9,14},{10,... | collective-permute-start | bytes 393224 | tf_op jit(solution)/shard_map/ppermute | solution.py:403
  11.1 1.5 %collective-permute-start.4 = (f32[128,256]{1,0:T(8,128)S(1)}, f32[128,256]{1,0:T(8,128)S(1)}, u32[]{:S(2)}, u32[]{:S(2)}) collective-permute-start(f32[128,256]{1,0:T(8,128)S(1)} %get-tuple-element.39), channel_id=1, source_target_pairs={{0,1},{1,0},{2,3},{3,2},{4,5},{5,4},{6,7},{7,6},{8,9},{9,8},{10,11... | collective-permute-start | bytes 393224 | tf_op jit(solution)/shard_map/ppermute | solution.py:403
  12.7 3.9 %collective-permute-done.1 = f32[2,16,256]{2,1,0:T(8,128)S(1)} collective-permute-done((f32[2,16,256]{2,1,0:T(8,128)S(1)}, f32[2,16,256]{2,1,0:T(8,128)S(1)}, u32[]{:S(2)}, u32[]{:S(2)}) %collective-permute-start.1) | collective-permute-done | bytes 32800 | tf_op jit(solution)/shard_map/ppermute | solution.py:403
  16.6 5.5 %collective-permute-done.2 = f32[4,16,256]{2,1,0:T(8,128)S(1)} collective-permute-done((f32[4,16,256]{2,1,0:T(8,128)S(1)}, f32[4,16,256]{2,1,0:T(8,128)S(1)}, u32[]{:S(2)}, u32[]{:S(2)}) %collective-permute-start.2) | collective-permute-done | bytes 65568 | tf_op jit(solution)/shard_map/ppermute | solution.py:403
  22.2 1.6 %collective-permute-start.6 = (f32[128,256]{1,0:T(8,128)S(1)}, f32[128,256]{1,0:T(8,128)S(1)}, u32[]{:S(2)}, u32[]{:S(2)}) collective-permute-start(f32[128,256]{1,0:T(8,128)S(1)} %get-tuple-element.41), channel_id=1, source_target_pairs={{0,3},{1,2},{2,1},{3,0},{4,7},{5,6},{6,5},{7,4},{8,11},{9,10},{10,... | collective-permute-start | bytes 393224 | tf_op jit(solution)/shard_map/ppermute | solution.py:403
  23.8 2.8 %collective-permute-start.7 = (f32[128,256]{1,0:T(8,128)S(1)}, f32[128,256]{1,0:T(8,128)S(1)}, u32[]{:S(2)}, u32[]{:S(2)}) collective-permute-start(f32[128,256]{1,0:T(8,128)S(1)} %get-tuple-element.42), channel_id=1, source_target_pairs={{0,4},{1,5},{2,6},{3,7},{4,0},{5,1},{6,2},{7,3},{8,12},{9,13},{10,... | collective-permute-start | bytes 393224 | tf_op jit(solution)/shard_map/ppermute | solution.py:403
  28.0 1.6 %collective-permute-start.9 = (f32[128,256]{1,0:T(8,128)S(1)}, f32[128,256]{1,0:T(8,128)S(1)}, u32[]{:S(2)}, u32[]{:S(2)}) collective-permute-start(f32[128,256]{1,0:T(8,128)S(1)} %get-tuple-element.44), channel_id=1, source_target_pairs={{0,6},{1,7},{2,4},{3,5},{4,2},{5,3},{6,0},{7,1},{8,14},{9,15},{10,... | collective-permute-start | bytes 393224 | tf_op jit(solution)/shard_map/ppermute | solution.py:403
  29.7 2.1 %weights.1 = (bf16[2048,256]{1,0:T(8,128)(2,1)S(1)}, bf16[2048,256]{1,0:T(8,128)(2,1)S(1)}, f32[64,256]{1,0:T(8,128)S(1)}) custom-call(s32[3]{0:T(128)S(1)} %pad_add_fusion.pos_ref, f32[8,16,256]{2,1,0:T(8,128)S(1)} %constant_dynamic-update-slice_fusion.refs_0_, f32[8,16,256]{2,1,0:T(8,128)S(1)} %collective-permute-done.3.refs_1_), custom_call_target="tpu_custom_call" | custom-call | tf_op jit(solution)/shard_map/weights/pallas_call | solution.py:382
  32.2 2.4 %collective-permute-done.6.refs_3_ = f32[128,256]{1,0:T(8,128)S(1)} collective-permute-done((f32[128,256]{1,0:T(8,128)S(1)}, f32[128,256]{1,0:T(8,128)S(1)}, u32[]{:S(2)}, u32[]{:S(2)}) %collective-permute-start.6) | collective-permute-done | bytes 131104 | tf_op jit(solution)/shard_map/ppermute | solution.py:403
  34.7 8.6 %collective-permute-done.8.refs_5_ = f32[128,256]{1,0:T(8,128)S(1)} collective-permute-done((f32[128,256]{1,0:T(8,128)S(1)}, f32[128,256]{1,0:T(8,128)S(1)}, u32[]{:S(2)}, u32[]{:S(2)}) %collective-permute-start.8) | collective-permute-done | bytes 131104 | tf_op jit(solution)/shard_map/ppermute | solution.py:403
  43.3 7.8 %filter.1 = (f32[128,256]{1,0:T(8,128)S(1)}, f32[128,256]{1,0:T(8,128)S(1)}, f32[128,256]{1,0:T(8,128)S(1)}, f32[128,256]{1,0:T(8,128)S(1)}, f32[128,256]{1,0:T(...) custom-call(s32[3]{0:T(128)S(1)} %pad_add_fusion.pos_ref, ...), custom_call_target="tpu_custom_call" | custom-call | tf_op jit(solution)/shard_map/filter/pallas_call | solution.py:382
  51.5 2.8 %collective-permute-start.12 = (f32[128,256]{1,0:T(8,128)S(1)}, f32[128,256]{1,0:T(8,128)S(1)}, u32[]{:S(2)}, u32[]{:S(2)}) collective-permute-start(f32[128,256]{1,0:T(8,128)S(1)} %get-tuple-element.48), channel_id=1, source_target_pairs={{0,2},{1,3},{2,0},{3,1},{4,6},{5,7},{6,4},{7,5},{8,10},{9,11},{10,... | collective-permute-start | bytes 393224 | tf_op jit(solution)/shard_map/ppermute | solution.py:403
  54.7 1.5 %collective-permute-done.11.refs_1_ = f32[128,256]{1,0:T(8,128)S(1)} collective-permute-done((f32[128,256]{1,0:T(8,128)S(1)}, f32[128,256]{1,0:T(8,128)S(1)}, u32[]{:S(2)}, u32[]{:S(2)}) %collective-permute-start.11) | collective-permute-done | bytes 131104 | tf_op jit(solution)/shard_map/ppermute | solution.py:403
  56.2 2.4 %collective-permute-done.12.refs_2_ = f32[128,256]{1,0:T(8,128)S(1)} collective-permute-done((f32[128,256]{1,0:T(8,128)S(1)}, f32[128,256]{1,0:T(8,128)S(1)}, u32[]{:S(2)}, u32[]{:S(2)}) %collective-permute-start.12) | collective-permute-done | bytes 131104 | tf_op jit(solution)/shard_map/ppermute | solution.py:403
  58.6 1.9 %collective-permute-done.13.refs_3_ = f32[128,256]{1,0:T(8,128)S(1)} collective-permute-done((f32[128,256]{1,0:T(8,128)S(1)}, f32[128,256]{1,0:T(8,128)S(1)}, u32[]{:S(2)}, u32[]{:S(2)}) %collective-permute-start.13) | collective-permute-done | bytes 131104 | tf_op jit(solution)/shard_map/ppermute | solution.py:403
  61.1 1.6 %collective-permute-start.18 = (f32[4,64,256]{2,1,0:T(8,128)S(1)}, f32[4,64,256]{2,1,0:T(8,128)S(1)}, u32[]{:S(2)}, u32[]{:S(2)}) collective-permute-start(f32[4,64,256]{2,1,0:T(8,128)S(1)} %get-tuple-element.55), channel_id=1, source_target_pairs={{0,16},{8,24},{16,0},{24,8},{1,17},{9,25},{17,1},{25,9},{2,18},{10... | collective-permute-start | bytes 786440 | tf_op jit(solution)/shard_map/ppermute | solution.py:403
  62.7 2.8 %collective-permute-start.14 = (f32[128,256]{1,0:T(8,128)S(1)}, f32[128,256]{1,0:T(8,128)S(1)}, u32[]{:S(2)}, u32[]{:S(2)}) collective-permute-start(f32[128,256]{1,0:T(8,128)S(1)} %get-tuple-element.51), channel_id=1, source_target_pairs={{0,4},{1,5},{2,6},{3,7},{4,0},{5,1},{6,2},{7,3},{8,12},{9,13},{10,... | collective-permute-start | bytes 393224 | tf_op jit(solution)/shard_map/ppermute | solution.py:403
  66.0 3.1 %collective-permute-start.16 = (f32[128,256]{1,0:T(8,128)S(1)}, f32[128,256]{1,0:T(8,128)S(1)}, u32[]{:S(2)}, u32[]{:S(2)}) collective-permute-start(f32[128,256]{1,0:T(8,128)S(1)} %get-tuple-element.53), channel_id=1, source_target_pairs={{0,6},{1,7},{2,4},{3,5},{4,2},{5,3},{6,0},{7,1},{8,14},{9,15},{10,... | collective-permute-start | bytes 393224 | tf_op jit(solution)/shard_map/ppermute | solution.py:403
  70.3 9.5 %collective-permute-done.14.refs_0_ = f32[128,256]{1,0:T(8,128)S(1)} collective-permute-done((f32[128,256]{1,0:T(8,128)S(1)}, f32[128,256]{1,0:T(8,128)S(1)}, u32[]{:S(2)}, u32[]{:S(2)}) %collective-permute-start.14) | collective-permute-done | bytes 131104 | tf_op jit(solution)/shard_map/ppermute | solution.py:403
  79.8 2.5 %collective-permute-done.15.refs_1_ = f32[128,256]{1,0:T(8,128)S(1)} collective-permute-done((f32[128,256]{1,0:T(8,128)S(1)}, f32[128,256]{1,0:T(8,128)S(1)}, u32[]{:S(2)}, u32[]{:S(2)}) %collective-permute-start.15) | collective-permute-done | bytes 131104 | tf_op jit(solution)/shard_map/ppermute | solution.py:403
  83.8 8.0 %collective-permute-done.24.far = f32[4,64,256]{2,1,0:T(8,128)S(1)} collective-permute-done((f32[4,64,256]{2,1,0:T(8,128)S(1)}, f32[4,64,256]{2,1,0:T(8,128)S(1)}, u32[]{:S(2)}, u32[]{:S(2)}) %collective-permute-start.24) | collective-permute-done | bytes 262176 | tf_op jit(solution)/shard_map/ppermute | solution.py:403
  91.8 1.7 %own.1 = (f32[8,128,256]{2,1,0:T(8,128)S(1)}, f32[8,128,256]{2,1,0:T(8,128)S(1)}, f32[2,64,128]{2,1,0:T(8,128)S(1)}, f32[2,64,128]{2,1,0:T(8,128)S(1)}) custom-call(s32[3]{0:T(128)S(1)} %pad_add_fusion.pos_ref, f32[8,64,256]{2,1,0:T(8,128)S(1)} %get-tuple-element.50.near, f32[8,64,256]{2,1,0:T(8,128)S(1)} %get-tuple-element.56.far, ...), custom_call_target="tpu_custom_call" | custom-call | tf_op jit(solution)/shard_map/own/pallas_call | solution.py:382
  93.5 1.8 %collective-permute-start.21 = (f32[2,64,128]{2,1,0:T(8,128)S(1)}, f32[2,64,128]{2,1,0:T(8,128)S(1)}, u32[]{:S(2)}, u32[]{:S(2)}) collective-permute-start(f32[2,64,128]{2,1,0:T(8,128)S(1)} %get-tuple-element.59), channel_id=1, source_target_pairs={{0,1},{1,0},{2,3},{3,2},{4,5},{5,4},{6,7},{7,6},{8,9},{9,8},{10,11... | collective-permute-start | bytes 196616 | tf_op jit(solution)/shard_map/ppermute | solution.py:403
  95.3 2.8 %collective-permute-done.21 = f32[2,64,128]{2,1,0:T(8,128)S(1)} collective-permute-done((f32[2,64,128]{2,1,0:T(8,128)S(1)}, f32[2,64,128]{2,1,0:T(8,128)S(1)}, u32[]{:S(2)}, u32[]{:S(2)}) %collective-permute-start.21) | collective-permute-done | bytes 65568 | tf_op jit(solution)/shard_map/ppermute | solution.py:403
  98.1 5.1 %collective-permute-start.22 = (f32[2,64,128]{2,1,0:T(8,128)S(1)}, f32[2,64,128]{2,1,0:T(8,128)S(1)}, u32[]{:S(2)}, u32[]{:S(2)}) collective-permute-start(f32[2,64,128]{2,1,0:T(8,128)S(1)} %add.13.tie), channel_id=1, source_target_pairs={{0,2},{1,3},{2,0},{3,1},{4,6},{5,7},{6,4},{7,5},{8,10},{9,11},{10,... | collective-permute-start | bytes 196616 | tf_op jit(solution)/shard_map/ppermute | solution.py:403
  103.2 1.6 %cross.1 = (f32[2,64,128]{2,1,0:T(8,128)S(1)}, f32[2,64,128]{2,1,0:T(8,128)S(1)}, f32[2,64,128]{2,1,0:T(8,128)S(1)}, f32[2,64,128]{2,1,0:T(8,128)S(1)}) custom-call(s32[3]{0:T(128)S(1)} %pad_add_fusion.pos_ref, f32[8,128,256]{2,1,0:T(8,128)S(1)} %get-tuple-element.57.z_ref, f32[8,128,256]{2,1,0:T(8,128)S(1)} %get-tuple-element.60.zc_ref, ...), custom_call_target="tpu_custom_call" | custom-call | tf_op jit(solution)/shard_map/cross/pallas_call | solution.py:382
  106.0 2.8 %collective-permute-start.23 = (f32[2,64,128]{2,1,0:T(8,128)S(1)}, f32[2,64,128]{2,1,0:T(8,128)S(1)}, u32[]{:S(2)}, u32[]{:S(2)}) collective-permute-start(f32[2,64,128]{2,1,0:T(8,128)S(1)} %add.14), channel_id=1, source_target_pairs={{0,4},{1,5},{2,6},{3,7},{4,0},{5,1},{6,2},{7,3},{8,12},{9,13},{10,... | collective-permute-start | bytes 196616 | tf_op jit(solution)/shard_map/ppermute | solution.py:403
  111.3 1.8 %collective-permute-done.28.c_ref = f32[2,64,128]{2,1,0:T(8,128)S(1)} collective-permute-done((f32[2,64,128]{2,1,0:T(8,128)S(1)}, f32[2,64,128]{2,1,0:T(8,128)S(1)}, u32[]{:S(2)}, u32[]{:S(2)}) %collective-permute-start.28) | collective-permute-done | bytes 65568 | tf_op jit(solution)/shard_map/ppermute | solution.py:403
  114.6 4.6 %collective-permute-done.30 = f32[2,64,128]{2,1,0:T(8,128)S(1)} collective-permute-done((f32[2,64,128]{2,1,0:T(8,128)S(1)}, f32[2,64,128]{2,1,0:T(8,128)S(1)}, u32[]{:S(2)}, u32[]{:S(2)}) %collective-permute-start.30) | collective-permute-done | bytes 65568 | tf_op jit(solution)/shard_map/ppermute | solution.py:403
  119.3 5.5 %collective-permute-done.31.cross_other = f32[2,64,128]{2,1,0:T(8,128)S(1)} collective-permute-done((f32[2,64,128]{2,1,0:T(8,128)S(1)}, f32[2,64,128]{2,1,0:T(8,128)S(1)}, u32[]{:S(2)}, u32[]{:S(2)}) %collective-permute-start.31) | collective-permute-done | bytes 65568 | tf_op jit(solution)/shard_map/ppermute | solution.py:403
  127.7 2.8 %collective-permute-done.32.other = f32[4,64,128]{2,1,0:T(8,128)S(1)} collective-permute-done((f32[4,64,128]{2,1,0:T(8,128)S(1)}, f32[4,64,128]{2,1,0:T(8,128)S(1)}, u32[]{:S(2)}, u32[]{:S(2)}) %collective-permute-start.32) | collective-permute-done | bytes 131104 | tf_op jit(solution)/shard_map/ppermute | solution.py:403
  (76 shorter events, 20.0 us)
Async XLA Ops:
  4.5 8.1 %collective-permute-start = (f32[1,16,256]{2,1,0:T(8,128)S(1)}, f32[1,16,256]{2,1,0:T(8,128)S(1)}, u32[]{:S(2)}, u32[]{:S(2)}) collective-permute-start(f32[1,16,256]{2,1,0:T(8,128)S(1)} %get-tuple-element.34), channel_id=1, source_target_pairs={{0,1},{1,0},{2,3},{3,2},{4,5},{5,4},{6,7},{7,6},{8,9},{9,8},{10,11... | collective-permute-start | bytes 49160 | tf_op jit(solution)/shard_map/ppermute | solution.py:403
  7.5 16.3 %collective-permute-start.10 = (f32[128,256]{1,0:T(8,128)S(1)}, f32[128,256]{1,0:T(8,128)S(1)}, u32[]{:S(2)}, u32[]{:S(2)}) collective-permute-start(f32[128,256]{1,0:T(8,128)S(1)} %get-tuple-element.45), channel_id=1, source_target_pairs={{0,7},{1,6},{2,5},{3,4},{4,3},{5,2},{6,1},{7,0},{8,15},{9,14},{10,... | collective-permute-start | bytes 393224 | tf_op jit(solution)/shard_map/ppermute | solution.py:403
  11.1 15.5 %collective-permute-start.4 = (f32[128,256]{1,0:T(8,128)S(1)}, f32[128,256]{1,0:T(8,128)S(1)}, u32[]{:S(2)}, u32[]{:S(2)}) collective-permute-start(f32[128,256]{1,0:T(8,128)S(1)} %get-tuple-element.39), channel_id=1, source_target_pairs={{0,1},{1,0},{2,3},{3,2},{4,5},{5,4},{6,7},{7,6},{8,9},{9,8},{10,11... | collective-permute-start | bytes 393224 | tf_op jit(solution)/shard_map/ppermute | solution.py:403
  16.6 5.5 %collective-permute-start.2 = (f32[4,16,256]{2,1,0:T(8,128)S(1)}, f32[4,16,256]{2,1,0:T(8,128)S(1)}, u32[]{:S(2)}, u32[]{:S(2)}) collective-permute-start(f32[4,16,256]{2,1,0:T(8,128)S(1)} %pad_maximum_fusion), channel_id=1, source_target_pairs={{0,4},{1,5},{2,6},{3,7},{4,0},{5,1},{6,2},{7,3},{8,12},{9,13},{10,... | collective-permute-start | bytes 196616 | tf_op jit(solution)/shard_map/ppermute | solution.py:403
  22.1 5.9 %collective-permute-start.3 = (f32[8,16,256]{2,1,0:T(8,128)S(1)}, f32[8,16,256]{2,1,0:T(8,128)S(1)}, u32[]{:S(2)}, u32[]{:S(2)}) collective-permute-start(f32[8,16,256]{2,1,0:T(8,128)S(1)} %constant_dynamic-update-slice_fusion.refs_0_), channel_id=1, source_target_pairs={{0,8},{8,0},{16,24},{24,16},{1,9},{9,1},{17,25},{25,17},{2,10},{10... | collective-permute-start | bytes 393224 | tf_op jit(solution)/shard_map/ppermute | solution.py:403
  22.1 10.1 %collective-permute-start.5 = (f32[128,256]{1,0:T(8,128)S(1)}, f32[128,256]{1,0:T(8,128)S(1)}, u32[]{:S(2)}, u32[]{:S(2)}) collective-permute-start(f32[128,256]{1,0:T(8,128)S(1)} %get-tuple-element.40), channel_id=1, source_target_pairs={{0,2},{1,3},{2,0},{3,1},{4,6},{5,7},{6,4},{7,5},{8,10},{9,11},{10,... | collective-permute-start | bytes 393224 | tf_op jit(solution)/shard_map/ppermute | solution.py:403
  22.2 12.5 %collective-permute-start.6 = (f32[128,256]{1,0:T(8,128)S(1)}, f32[128,256]{1,0:T(8,128)S(1)}, u32[]{:S(2)}, u32[]{:S(2)}) collective-permute-start(f32[128,256]{1,0:T(8,128)S(1)} %get-tuple-element.41), channel_id=1, source_target_pairs={{0,3},{1,2},{2,1},{3,0},{4,7},{5,6},{6,5},{7,4},{8,11},{9,10},{10,... | collective-permute-start | bytes 393224 | tf_op jit(solution)/shard_map/ppermute | solution.py:403
  23.8 10.8 %collective-permute-start.7 = (f32[128,256]{1,0:T(8,128)S(1)}, f32[128,256]{1,0:T(8,128)S(1)}, u32[]{:S(2)}, u32[]{:S(2)}) collective-permute-start(f32[128,256]{1,0:T(8,128)S(1)} %get-tuple-element.42), channel_id=1, source_target_pairs={{0,4},{1,5},{2,6},{3,7},{4,0},{5,1},{6,2},{7,3},{8,12},{9,13},{10,... | collective-permute-start | bytes 393224 | tf_op jit(solution)/shard_map/ppermute | solution.py:403
  26.6 16.7 %collective-permute-start.8 = (f32[128,256]{1,0:T(8,128)S(1)}, f32[128,256]{1,0:T(8,128)S(1)}, u32[]{:S(2)}, u32[]{:S(2)}) collective-permute-start(f32[128,256]{1,0:T(8,128)S(1)} %get-tuple-element.43), channel_id=1, source_target_pairs={{0,5},{1,4},{2,7},{3,6},{4,1},{5,0},{6,3},{7,2},{8,13},{9,12},{10,... | collective-permute-start | bytes 393224 | tf_op jit(solution)/shard_map/ppermute | solution.py:403
  28.0 15.3 %collective-permute-start.9 = (f32[128,256]{1,0:T(8,128)S(1)}, f32[128,256]{1,0:T(8,128)S(1)}, u32[]{:S(2)}, u32[]{:S(2)}) collective-permute-start(f32[128,256]{1,0:T(8,128)S(1)} %get-tuple-element.44), channel_id=1, source_target_pairs={{0,6},{1,7},{2,4},{3,5},{4,2},{5,3},{6,0},{7,1},{8,14},{9,15},{10,... | collective-permute-start | bytes 393224 | tf_op jit(solution)/shard_map/ppermute | solution.py:403
  51.1 5.0 %collective-permute-start.11 = (f32[128,256]{1,0:T(8,128)S(1)}, f32[128,256]{1,0:T(8,128)S(1)}, u32[]{:S(2)}, u32[]{:S(2)}) collective-permute-start(f32[128,256]{1,0:T(8,128)S(1)} %get-tuple-element.47), channel_id=1, source_target_pairs={{0,1},{1,0},{2,3},{3,2},{4,5},{5,4},{6,7},{7,6},{8,9},{9,8},{10,11... | collective-permute-start | bytes 393224 | tf_op jit(solution)/shard_map/ppermute | solution.py:403
  51.5 7.0 %collective-permute-start.12 = (f32[128,256]{1,0:T(8,128)S(1)}, f32[128,256]{1,0:T(8,128)S(1)}, u32[]{:S(2)}, u32[]{:S(2)}) collective-permute-start(f32[128,256]{1,0:T(8,128)S(1)} %get-tuple-element.48), channel_id=1, source_target_pairs={{0,2},{1,3},{2,0},{3,1},{4,6},{5,7},{6,4},{7,5},{8,10},{9,11},{10,... | collective-permute-start | bytes 393224 | tf_op jit(solution)/shard_map/ppermute | solution.py:403
  54.4 6.1 %collective-permute-start.13 = (f32[128,256]{1,0:T(8,128)S(1)}, f32[128,256]{1,0:T(8,128)S(1)}, u32[]{:S(2)}, u32[]{:S(2)}) collective-permute-start(f32[128,256]{1,0:T(8,128)S(1)} %get-tuple-element.49), channel_id=1, source_target_pairs={{0,3},{1,2},{2,1},{3,0},{4,7},{5,6},{6,5},{7,4},{8,11},{9,10},{10,... | collective-permute-start | bytes 393224 | tf_op jit(solution)/shard_map/ppermute | solution.py:403
  61.1 21.3 %collective-permute-start.18 = (f32[4,64,256]{2,1,0:T(8,128)S(1)}, f32[4,64,256]{2,1,0:T(8,128)S(1)}, u32[]{:S(2)}, u32[]{:S(2)}) collective-permute-start(f32[4,64,256]{2,1,0:T(8,128)S(1)} %get-tuple-element.55), channel_id=1, source_target_pairs={{0,16},{8,24},{16,0},{24,8},{1,17},{9,25},{17,1},{25,9},{2,18},{10... | collective-permute-start | bytes 786440 | tf_op jit(solution)/shard_map/ppermute | solution.py:403
  62.7 17.2 %collective-permute-start.14 = (f32[128,256]{1,0:T(8,128)S(1)}, f32[128,256]{1,0:T(8,128)S(1)}, u32[]{:S(2)}, u32[]{:S(2)}) collective-permute-start(f32[128,256]{1,0:T(8,128)S(1)} %get-tuple-element.51), channel_id=1, source_target_pairs={{0,4},{1,5},{2,6},{3,7},{4,0},{5,1},{6,2},{7,3},{8,12},{9,13},{10,... | collective-permute-start | bytes 393224 | tf_op jit(solution)/shard_map/ppermute | solution.py:403
  65.4 16.9 %collective-permute-start.15 = (f32[128,256]{1,0:T(8,128)S(1)}, f32[128,256]{1,0:T(8,128)S(1)}, u32[]{:S(2)}, u32[]{:S(2)}) collective-permute-start(f32[128,256]{1,0:T(8,128)S(1)} %get-tuple-element.52), channel_id=1, source_target_pairs={{0,5},{1,4},{2,7},{3,6},{4,1},{5,0},{6,3},{7,2},{8,13},{9,12},{10,... | collective-permute-start | bytes 393224 | tf_op jit(solution)/shard_map/ppermute | solution.py:403
  66.0 16.4 %collective-permute-start.16 = (f32[128,256]{1,0:T(8,128)S(1)}, f32[128,256]{1,0:T(8,128)S(1)}, u32[]{:S(2)}, u32[]{:S(2)}) collective-permute-start(f32[128,256]{1,0:T(8,128)S(1)} %get-tuple-element.53), channel_id=1, source_target_pairs={{0,6},{1,7},{2,4},{3,5},{4,2},{5,3},{6,0},{7,1},{8,14},{9,15},{10,... | collective-permute-start | bytes 393224 | tf_op jit(solution)/shard_map/ppermute | solution.py:403
  69.0 13.3 %collective-permute-start.17 = (f32[128,256]{1,0:T(8,128)S(1)}, f32[128,256]{1,0:T(8,128)S(1)}, u32[]{:S(2)}, u32[]{:S(2)}) collective-permute-start(f32[128,256]{1,0:T(8,128)S(1)} %get-tuple-element.54), channel_id=1, source_target_pairs={{0,7},{1,6},{2,5},{3,4},{4,3},{5,2},{6,1},{7,0},{8,15},{9,14},{10,... | collective-permute-start | bytes 393224 | tf_op jit(solution)/shard_map/ppermute | solution.py:403
  79.8 11.9 %collective-permute-start.19 = (f32[8,64,256]{2,1,0:T(8,128)S(1)}, f32[8,64,256]{2,1,0:T(8,128)S(1)}, u32[]{:S(2)}, u32[]{:S(2)}) collective-permute-start(f32[8,64,256]{2,1,0:T(8,128)S(1)} %get-tuple-element.50.near), channel_id=1, source_target_pairs={{0,8},{8,0},{16,24},{24,16},{1,9},{9,1},{17,25},{25,17},{2,10},{10... | collective-permute-start | bytes 1572872 | tf_op jit(solution)/shard_map/ppermute | solution.py:403
  83.0 8.8 %collective-permute-start.20 = (f32[8,64,256]{2,1,0:T(8,128)S(1)}, f32[8,64,256]{2,1,0:T(8,128)S(1)}, u32[]{:S(2)}, u32[]{:S(2)}) collective-permute-start(f32[8,64,256]{2,1,0:T(8,128)S(1)} %get-tuple-element.56.far), channel_id=1, source_target_pairs={{0,8},{8,0},{16,24},{24,16},{1,9},{9,1},{17,25},{25,17},{2,10},{10... | collective-permute-start | bytes 1572872 | tf_op jit(solution)/shard_map/ppermute | solution.py:403
  83.0 8.7 %collective-permute-start.24 = (f32[4,64,256]{2,1,0:T(8,128)S(1)}, f32[4,64,256]{2,1,0:T(8,128)S(1)}, u32[]{:S(2)}, u32[]{:S(2)}) collective-permute-start(f32[4,64,256]{2,1,0:T(8,128)S(1)} %get-tuple-element.61), channel_id=1, source_target_pairs={{0,16},{8,24},{16,0},{24,8},{1,17},{9,25},{17,1},{25,9},{2,18},{10... | collective-permute-start | bytes 786440 | tf_op jit(solution)/shard_map/ppermute | solution.py:403
  83.6 19.6 %collective-permute-start.25 = (f32[4,64,256]{2,1,0:T(8,128)S(1)}, f32[4,64,256]{2,1,0:T(8,128)S(1)}, u32[]{:S(2)}, u32[]{:S(2)}) collective-permute-start(f32[4,64,256]{2,1,0:T(8,128)S(1)} %collective-permute-done.18.refs_4_.near), channel_id=1, source_target_pairs={{0,8},{8,0},{16,24},{24,16},{1,9},{9,1},{17,25},{25,17},{2,10},{10... | collective-permute-start | bytes 786440 | tf_op jit(solution)/shard_map/ppermute | solution.py:403
  91.8 11.4 %collective-permute-start.26 = (f32[4,64,256]{2,1,0:T(8,128)S(1)}, f32[4,64,256]{2,1,0:T(8,128)S(1)}, u32[]{:S(2)}, u32[]{:S(2)}) collective-permute-start(f32[4,64,256]{2,1,0:T(8,128)S(1)} %collective-permute-done.24.far), channel_id=1, source_target_pairs={{0,8},{8,0},{16,24},{24,16},{1,9},{9,1},{17,25},{25,17},{2,10},{10... | collective-permute-start | bytes 786440 | tf_op jit(solution)/shard_map/ppermute | solution.py:403
  93.5 4.6 %collective-permute-start.21 = (f32[2,64,128]{2,1,0:T(8,128)S(1)}, f32[2,64,128]{2,1,0:T(8,128)S(1)}, u32[]{:S(2)}, u32[]{:S(2)}) collective-permute-start(f32[2,64,128]{2,1,0:T(8,128)S(1)} %get-tuple-element.59), channel_id=1, source_target_pairs={{0,1},{1,0},{2,3},{3,2},{4,5},{5,4},{6,7},{7,6},{8,9},{9,8},{10,11... | collective-permute-start | bytes 196616 | tf_op jit(solution)/shard_map/ppermute | solution.py:403
  98.1 8.0 %collective-permute-start.22 = (f32[2,64,128]{2,1,0:T(8,128)S(1)}, f32[2,64,128]{2,1,0:T(8,128)S(1)}, u32[]{:S(2)}, u32[]{:S(2)}) collective-permute-start(f32[2,64,128]{2,1,0:T(8,128)S(1)} %add.13.tie), channel_id=1, source_target_pairs={{0,2},{1,3},{2,0},{3,1},{4,6},{5,7},{6,4},{7,5},{8,10},{9,11},{10,... | collective-permute-start | bytes 196616 | tf_op jit(solution)/shard_map/ppermute | solution.py:403
  104.8 6.5 %collective-permute-start.27 = (f32[2,64,128]{2,1,0:T(8,128)S(1)}, f32[2,64,128]{2,1,0:T(8,128)S(1)}, u32[]{:S(2)}, u32[]{:S(2)}) collective-permute-start(f32[2,64,128]{2,1,0:T(8,128)S(1)} %get-tuple-element.63), channel_id=1, source_target_pairs={{0,1},{1,0},{2,3},{3,2},{4,5},{5,4},{6,7},{7,6},{8,9},{9,8},{10,11... | collective-permute-start | bytes 196616 | tf_op jit(solution)/shard_map/ppermute | solution.py:403
  106.0 5.2 %collective-permute-start.23 = (f32[2,64,128]{2,1,0:T(8,128)S(1)}, f32[2,64,128]{2,1,0:T(8,128)S(1)}, u32[]{:S(2)}, u32[]{:S(2)}) collective-permute-start(f32[2,64,128]{2,1,0:T(8,128)S(1)} %add.14), channel_id=1, source_target_pairs={{0,4},{1,5},{2,6},{3,7},{4,0},{5,1},{6,2},{7,3},{8,12},{9,13},{10,... | collective-permute-start | bytes 196616 | tf_op jit(solution)/shard_map/ppermute | solution.py:403
  108.8 4.3 %collective-permute-start.28 = (f32[2,64,128]{2,1,0:T(8,128)S(1)}, f32[2,64,128]{2,1,0:T(8,128)S(1)}, u32[]{:S(2)}, u32[]{:S(2)}) collective-permute-start(f32[2,64,128]{2,1,0:T(8,128)S(1)} %get-tuple-element.64), channel_id=1, source_target_pairs={{0,16},{8,24},{16,0},{24,8},{1,17},{9,25},{17,1},{25,9},{2,18},{10... | collective-permute-start | bytes 196616 | tf_op jit(solution)/shard_map/ppermute | solution.py:403
  109.4 5.2 %collective-permute-start.29 = (f32[2,64,128]{2,1,0:T(8,128)S(1)}, f32[2,64,128]{2,1,0:T(8,128)S(1)}, u32[]{:S(2)}, u32[]{:S(2)}) collective-permute-start(f32[2,64,128]{2,1,0:T(8,128)S(1)} %get-tuple-element.65), channel_id=1, source_target_pairs={{0,17},{1,16},{2,19},{3,18},{4,21},{5,20},{6,23},{7,22},{8,25},{9,... | collective-permute-start | bytes 196616 | tf_op jit(solution)/shard_map/ppermute | solution.py:409
  114.5 4.7 %collective-permute-start.30 = (f32[2,64,128]{2,1,0:T(8,128)S(1)}, f32[2,64,128]{2,1,0:T(8,128)S(1)}, u32[]{:S(2)}, u32[]{:S(2)}) collective-permute-start(f32[2,64,128]{2,1,0:T(8,128)S(1)} %sum.1), channel_id=1, source_target_pairs={{0,2},{1,3},{2,0},{3,1},{4,6},{5,7},{6,4},{7,5},{8,10},{9,11},{10,... | collective-permute-start | bytes 196616 | tf_op jit(solution)/shard_map/ppermute | solution.py:403
  119.2 5.6 %collective-permute-start.31 = (f32[2,64,128]{2,1,0:T(8,128)S(1)}, f32[2,64,128]{2,1,0:T(8,128)S(1)}, u32[]{:S(2)}, u32[]{:S(2)}) collective-permute-start(f32[2,64,128]{2,1,0:T(8,128)S(1)} %add.16.cross), channel_id=1, source_target_pairs={{0,4},{1,5},{2,6},{3,7},{4,0},{5,1},{6,2},{7,3},{8,12},{9,13},{10,... | collective-permute-start | bytes 196616 | tf_op jit(solution)/shard_map/ppermute | solution.py:403
  125.4 5.0 %collective-permute-start.32 = (f32[4,64,128]{2,1,0:T(8,128)S(1)}, f32[4,64,128]{2,1,0:T(8,128)S(1)}, u32[]{:S(2)}, u32[]{:S(2)}) collective-permute-start(f32[4,64,128]{2,1,0:T(8,128)S(1)} %pair.1.mine), channel_id=1, source_target_pairs={{0,1},{1,0},{2,3},{3,2},{4,5},{5,4},{6,7},{7,6},{8,9},{9,8},{10,11... | collective-permute-start | bytes 393224 | tf_op jit(solution)/shard_map/ppermute | solution.py:403
  (10 other events, 88.2 us)

commit v4 on v3

--- a/solution.py
+++ b/solution.py
@@ -13,7 +13,6 @@
 SLAB = 8
 SIDE = 16
 LAT = SIDE * SIDE
-ORDER = (5, 6, 7, 1, 2, 3, 4)
 
 COEFFS = (
     -5369.0 / 1800.0,
@@ -84,9 +83,9 @@
     return hi, lo
 
 
-def split_kernel(nd, nb, pos_ref, cell_ref, x_ref, v_ref, w_ref, code_ref, mine_ref, *refs):
+def split_kernel(nd, nb, pos_ref, cell_ref, x_ref, v_ref, w_ref, code_ref, *refs):
     outs, (scratch, packed) = refs[:-2], refs[-2:]
-    i, core = pos_ref[0], pos_ref[1] & 1
+    i = pos_ref[0]
     cube = 2 * REACH + 1
     code = code_ref[...].astype(F32)
     off_x = jnp.floor((code + 0.5) * (1.0 / (cube * cube)))
@@ -106,22 +105,16 @@
         packed[18 + a : 19 + a] = y * SIDE + z
     packed[20:24] = jnp.zeros((4, LAT), F32)
     packed[24:32] = jnp.concatenate([v_ref[:, y, :] for y in range(SIDE)], axis=1)
-    mine_ref[0] = packed[pl.ds(pl.multiple_of(core * 16, 16), 16)]
     for q in range(SLAB):
         scratch[q] = x_ref[q].T
     for j in range(nd):
         start = (i ^ j) * nb
         for q in range(SLAB):
             outs[j][q * nb : (q + 1) * nb] = scratch[q, pl.ds(pl.multiple_of(start, nb), nb)]
-
-
-def weights_kernel(nd, pos_ref, *refs):
-    parts, (wh_ref, wl_ref, v_ref, scratch) = refs[:2], refs[2:]
-    i, core = pos_ref[0], pos_ref[1] & 1
-    for jb in range(2):
-        rows = pl.ds(pl.multiple_of((core ^ jb) * 16, 16), 16)
-        for j in range(nd):
-            scratch[i ^ j, rows] = parts[jb][j]
+        outs[j][SLAB * nb :] = packed[...]
+
+
+def build_projectors(nd, scratch, wh_ref, wl_ref, v_ref):
     lat = lax.broadcasted_iota(jnp.int32, (LAT, 256), 0).astype(F32)
     plane = lax.broadcasted_iota(jnp.int32, (16, 1, 1), 0).astype(F32)
     diagonal = -1.5 * COEFFS[0] - CENTRE
@@ -156,9 +149,9 @@
         lax.fori_loop(0, nd, body, 0)
 
 
-def filter_kernel(nd, nb, total, pos_ref, kb_ref, v_ref, wh_ref, wl_ref, lh_ref, ll_ref, fold_ref, spread_ref, *refs):
+def filter_kernel(nd, nb, total, pos_ref, kb_ref, lh_ref, ll_ref, fold_ref, *refs):
     pieces, outs = refs[:nd], refs[nd : 2 * nd]
-    f0_ref, f1_ref, fold_out, spread_out = refs[2 * nd :]
+    f0_ref, f1_ref, fold_out, spread_out, wh_ref, wl_ref, v_ref, packed = refs[2 * nd :]
     i = pos_ref[0]
     R = SLAB * nb
     rows_q = lax.broadcasted_iota(jnp.int32, (SLAB, nb, 256), 0)
@@ -180,8 +173,10 @@
             lax.fori_loop(0, nd, lambda s, c: (body(s), c)[1], 0)
 
     for j in range(nd):
-        f0_ref[slab_rows(i ^ j)] = pieces[j][...]
+        f0_ref[slab_rows(i ^ j)] = pieces[j][:R]
+        packed[i ^ j] = pieces[j][R:]
     wrap(f0_ref)
+    build_projectors(nd, packed, wh_ref, wl_ref, v_ref)
 
     def apply(ref, finish):
         def project(s):
@@ -204,7 +199,7 @@
         p = (at + next_slab(above) + previous_slab(below)) * kb_ref[...]
         wide = jnp.concatenate([next_slab(p), p, previous_slab(p)], axis=1)
         ph, plo = halves(wide)
-        spread_out[...] = dot(ph, spread_ref[...], NT) + dot(plo, spread_ref[...], NT)
+        spread_out[...] = dot(ph, fold_ref[...], NT) + dot(plo, fold_ref[...], NT)
 
         def step(s):
             f = ref[slab_rows(s)]
@@ -253,29 +248,21 @@
         outs[j][...] = (y * scale[None]).reshape(R, LAT)
 
 
-def join_kernel(count, nb, ties, pos_ref, *refs):
-    pieces, (z_ref, send_ref) = refs[:count], refs[count + ties :]
+def join_kernel(nd, nb, pos_ref, *refs):
+    pieces, (z_ref, first_ref, second_ref) = refs[:nd], refs[nd:]
     i, y = pos_ref[0], pos_ref[2]
-    for j in range(count):
-        rows = pl.ds(pl.multiple_of(((i ^ j) & (count - 1)) * nb, nb), nb)
+    for j in range(nd):
+        rows = pl.ds(pl.multiple_of((i ^ j) * nb, nb), nb)
         for q in range(SLAB):
             z_ref[q, rows] = pieces[j][q * nb : (q + 1) * nb]
     half = SLAB // 2
-    for q in range(half):
-        send_ref[q] = z_ref[(1 - y) * half + q]
-
-
-def place_halves(pos_ref, near, far, out):
-    h = pos_ref[0] // 4
-    for q in range(out.shape[0]):
-        out[q, pl.ds(pl.multiple_of(h * 64, 64), 64)] = near[q]
-        out[q, pl.ds(pl.multiple_of((1 - h) * 64, 64), 64)] = far[q]
-
-
-def own_kernel(pos_ref, near, far, core_near, core_far, z_ref, zc_ref, keep_ref, send_ref, g_ref):
+    for q in range(half // 2):
+        first_ref[q] = z_ref[(1 - y) * half + q]
+        second_ref[q] = z_ref[(1 - y) * half + half // 2 + q]
+
+
+def own_kernel(pos_ref, z_ref, zc_ref, keep_ref, send_ref, g_ref):
     i, b = pos_ref[0], pos_ref[1]
-    place_halves(pos_ref, near, far, z_ref)
-    place_halves(pos_ref, core_near, core_far, zc_ref)
     own = core = None
     for q in range(SLAB):
         zh, zl = halves(z_ref[q])
@@ -295,18 +282,16 @@
 
 
 def cross_kernel(
-    pos_ref, z_ref, zc_ref, near, far, core_near, core_far, tie, keep, send, back, back_send, g_ref, back_ref, f_ref, fc_ref
+    pos_ref, z_ref, zc_ref, first, second, core_first, core_second, tie, keep, send, back, back_send, g_ref, back_ref
 ):
     i, b, y = pos_ref[0], pos_ref[1], pos_ref[2]
     half = SLAB // 2
-    place_halves(pos_ref, near, far, f_ref)
-    place_halves(pos_ref, core_near, core_far, fc_ref)
     totals = None
     for q in range(half):
         zh, zl = halves(z_ref[y * half + q])
         ch, cl = halves(zc_ref[y * half + q])
-        fh, fl = halves(f_ref[q])
-        gh, gl = halves(fc_ref[q])
+        fh, fl = halves((first, second)[q // (half // 2)][q % (half // 2)])
+        gh, gl = halves((core_first, core_second)[q // (half // 2)][q % (half // 2)])
         now = (
             dot3(zh, zl, fh, fl, NT),
             dot3(zh, zl, gh, gl, NT),
@@ -412,7 +397,7 @@
 def swap_all(pieces, direct):
     if direct:
         got = {0: pieces[0]}
-        for j in ORDER:
+        for j in range(1, len(pieces)):
             got[j] = xor_permute(pieces[j], "dom", j)
         return [got[j] for j in range(len(pieces))]
     stacked = lax.all_to_all(jnp.stack(pieces), "dom", 0, 0, tiled=True)
@@ -455,46 +440,41 @@
 
     waves = trial_waves.reshape(SLAB, LAT, bands)
     if direct:
-        gathered, *cut = call(
+        cut = call(
             functools.partial(split_kernel, nd, nb),
-            [shape(1, 16, 256)] + [shape(R, LAT)] * nd,
+            [shape(R + 32, LAT)] * nd,
             [pos, atom_cell, waves, potential, proj_weights, point_codes],
             [pltpu.VMEM((SLAB, bands, LAT), F32), pltpu.VMEM((32, 256), F32)],
             "split",
         )
-        for step in (1, 2, 4):
-            gathered = jnp.concatenate([gathered, xor_permute(gathered, "dom", step)])
-        parts = [gathered, xor_permute(gathered, "band", 1)]
     else:
         packed = packed_atoms(potential, proj_weights, atom_cell, point_codes)
         gathered = lax.all_gather(packed, "dom", axis=0)
-        parts = [gathered[:, :16], gathered[:, 16:]]
         turned = waves.transpose(0, 2, 1).reshape(SLAB, nd, real, LAT).transpose(1, 0, 2, 3)
         cut = [turned[j] for j in range(nd)]
 
-    wh, wl, shifted = call(
-        functools.partial(weights_kernel, nd),
-        [shape(nd * 256, 256, dtype=BF16), shape(nd * 256, 256, dtype=BF16), shape(nd * SLAB, LAT)],
-        [pos] + parts,
-        [pltpu.VMEM((nd, 32, 256), F32)],
-        "weights",
-    )
     lh, ll = split_const(lateral_matrix())
     fold = jnp.asarray(fold_matrix()).astype(BF16)
     kb_row = jnp.concatenate([kb_energy, kb_energy, jnp.zeros((112,), F32)])[None]
-    spread = fold
     pieces = swap_all(cut, direct)
     if not direct:
-        pieces = [jnp.pad(p, ((0, 0), (0, nb - real), (0, 0))).reshape(R, LAT) for p in pieces]
+        pieces = [
+            jnp.concatenate([jnp.pad(p, ((0, 0), (0, nb - real), (0, 0))).reshape(R, LAT), gathered[j]])
+            for j, p in enumerate(pieces)
+        ]
     ready = call(
         functools.partial(filter_kernel, nd, nb, float(total)),
         [shape(R, LAT)] * nd,
-        [pos, kb_row, shifted, wh, wl, lh, ll, fold, spread] + pieces,
+        [pos, kb_row, lh, ll, fold] + pieces,
         [
             pltpu.VMEM(((nd * SLAB + 2 * HALO) * nb, LAT), F32),
             pltpu.VMEM(((nd * SLAB + 2 * HALO) * nb, LAT), F32),
             pltpu.VMEM((nd * nb, 256), F32),
             pltpu.VMEM((nd * nb, 256), F32),
+            pltpu.VMEM((nd * 256, 256), BF16),
+            pltpu.VMEM((nd * 256, 256), BF16),
+            pltpu.VMEM((nd * SLAB, LAT), F32),
+            pltpu.VMEM((nd, 32, 256), F32),
         ],
         "filter",
     )
@@ -509,43 +489,31 @@
 
 
 def finish_direct(back, pos, nb, bands, total):
-    group = len(back) // 2
-    half = SLAB // 2
-
-    def exchanged(pieces, ties):
-        z, send = call(
-            functools.partial(join_kernel, group, nb, len(ties)),
-            [shape(SLAB, group * nb, LAT), shape(half, group * nb, LAT)],
-            [pos] + pieces,
-            (),
-            "join",
-            ties,
-        )
-        far = xor_permute(send, "band", 2)
-        return z, xor_permute(z, "band", 1), far, xor_permute(far, "band", 1)
-
-    z_near, core_near, far_near, far_core_near = exchanged(back[:group], [])
-    z_far, core_far, far_far, far_core_far = exchanged(back[group:], [far_near])
+    nd, half = len(back), SLAB // 2
+    z, first, second = call(
+        functools.partial(join_kernel, nd, nb),
+        [shape(SLAB, bands, LAT), shape(half // 2, bands, LAT), shape(half // 2, bands, LAT)],
+        [pos] + back,
+        (),
+        "join",
+    )
+    far_first = xor_permute(first, "band", 2)
+    z_core = xor_permute(z, "band", 1)
+    far_second = xor_permute(second, "band", 2)
     part = shape(2, bands // 2, bands)
     block = pltpu.VMEM((2, bands, bands), F32)
-    z, z_core, own_keep, own_send = call(
-        own_kernel,
-        [shape(SLAB, bands, LAT), shape(SLAB, bands, LAT), part, part],
-        [pos, z_near, z_far, core_near, core_far],
-        [block],
-        "own",
-    )
-    own = own_keep + xor_permute(own_send, "dom", 1)
-    own_tie = own
-    own = own + xor_permute(own, "dom", 2)
-    own = own + xor_permute(own, "dom", 4)
+    own_keep, own_send = call(own_kernel, [part, part], [pos, z, z_core], [block], "own")
+    own_1 = own_keep + xor_permute(own_send, "dom", 1)
+    far_second, own_1 = lax.optimization_barrier((far_second, own_1))
+    own_2 = own_1 + xor_permute(own_1, "dom", 2)
+    own = own_2 + xor_permute(own_2, "dom", 4)
     keep, send, back_keep, back_send = call(
         cross_kernel,
         [part] * 4,
-        [pos, z, z_core, far_near, far_far, far_core_near, far_core_far],
-        [block, block, pltpu.VMEM((half, bands, LAT), F32), pltpu.VMEM((half, bands, LAT), F32)],
+        [pos, z, z_core, far_first, far_second, xor_permute(far_first, "band", 1), xor_permute(far_second, "band", 1)],
+        [block, block],
         "cross",
-        [own_tie],
+        [own_2],
     )
     cross = call(
         sum_kernel,

time: 132 us -> 123 us (0.932)
  waiting for transfers between devices: 65.9 us -> 57.8 us
  Pallas kernels: 18.6 us -> 17.2 us
    ppermute x32 -> x27, waiting for transfers between devices: 64.5 us -> 55.9 us  [xor_permute(): return lax.ppermute(value, axis, [(k, k ^ step) for k in range(count)])]
    pallas_call x11 -> x9, Pallas kernels: 18.6 us -> 17.2 us  [call(): pl.pallas_call(kernel, out_shape=out_shape, in_specs=specs, out_specs=pl....]
    ppermute x32 -> x27, starting transfers between devices: 41.9 us -> 43.2 us  [xor_permute(): return lax.ppermute(value, axis, [(k, k ^ step) for k in range(count)])]
    unnamed x21 -> x18, local copies, waits for them, and re-layouts: 2.78 us -> 2.76 us
  transfers between devices with their start and end apart: 33 -> 28, of which waited for: 18 -> 17; matrix products, arithmetic and copies ran while one was open for 0% -> 0% of each run, Pallas kernels for 6% -> 4%
where the time goes in v4:
time: 123 us
  waiting for transfers between devices  57.8 us (47%)
  starting transfers between devices  43.9 us (36%)
  Pallas kernels  17.2 us (14%)
  local copies, waits for them, and re-layouts  2.76 us (2%)
    ppermute x27, waiting for transfers between devices, xor_permute(): return lax.ppermute(value, axis, [(k, k ^ step) for k in range(count)])  55.9 us
    ppermute x27, starting transfers between devices, xor_permute(): return lax.ppermute(value, axis, [(k, k ^ step) for k in range(count)])  43.2 us
    pallas_call x9, Pallas kernels, call(): pl.pallas_call(kernel, out_shape=out_shape, in_specs=specs, out_specs=pl....  17.2 us
    unnamed x18, local copies, waits for them, and re-layouts  2.76 us
  transfers between devices with their start and end apart: 28, of which 17 were waited for; matrix products, arithmetic and copies ran while one was open for 0% of the time, Pallas kernels for 4%

profile of v4, /device:TPU:0, one launch (start us, length us, event | category | flops | bytes accessed | tf_op | source)
XLA Modules:
  0.0 122.7 jit_solution(2544176209307357365)
XLA Ops:
  4.5 3.0 %collective-permute-start = (f32[160,256]{1,0:T(8,128)S(1)}, f32[160,256]{1,0:T(8,128)S(1)}, u32[]{:S(2)}, u32[]{:S(2)}) collective-permute-start(f32[160,256]{1,0:T(8,128)S(1)} %get-tuple-element.30), channel_id=1, source_target_pairs={{0,1},{1,0},{2,3},{3,2},{4,5},{5,4},{6,7},{7,6},{8,9},{9,8},{10,11... | collective-permute-start | bytes 491528 | tf_op jit(solution)/shard_map/ppermute | solution.py:388
  7.5 1.6 %collective-permute-start.1 = (f32[160,256]{1,0:T(8,128)S(1)}, f32[160,256]{1,0:T(8,128)S(1)}, u32[]{:S(2)}, u32[]{:S(2)}) collective-permute-start(f32[160,256]{1,0:T(8,128)S(1)} %get-tuple-element.31), channel_id=1, source_target_pairs={{0,2},{1,3},{2,0},{3,1},{4,6},{5,7},{6,4},{7,5},{8,10},{9,11},{10,... | collective-permute-start | bytes 491528 | tf_op jit(solution)/shard_map/ppermute | solution.py:388
  9.1 3.0 %collective-permute-start.3 = (f32[160,256]{1,0:T(8,128)S(1)}, f32[160,256]{1,0:T(8,128)S(1)}, u32[]{:S(2)}, u32[]{:S(2)}) collective-permute-start(f32[160,256]{1,0:T(8,128)S(1)} %get-tuple-element.33), channel_id=1, source_target_pairs={{0,4},{1,5},{2,6},{3,7},{4,0},{5,1},{6,2},{7,3},{8,12},{9,13},{10,... | collective-permute-start | bytes 491528 | tf_op jit(solution)/shard_map/ppermute | solution.py:388
  13.4 3.6 %collective-permute-start.5 = (f32[160,256]{1,0:T(8,128)S(1)}, f32[160,256]{1,0:T(8,128)S(1)}, u32[]{:S(2)}, u32[]{:S(2)}) collective-permute-start(f32[160,256]{1,0:T(8,128)S(1)} %get-tuple-element.35), channel_id=1, source_target_pairs={{0,6},{1,7},{2,4},{3,5},{4,2},{5,3},{6,0},{7,1},{8,14},{9,15},{10,... | collective-permute-start | bytes 491528 | tf_op jit(solution)/shard_map/ppermute | solution.py:388
  17.0 3.6 %collective-permute-done.1.refs_2_ = f32[160,256]{1,0:T(8,128)S(1)} collective-permute-done((f32[160,256]{1,0:T(8,128)S(1)}, f32[160,256]{1,0:T(8,128)S(1)}, u32[]{:S(2)}, u32[]{:S(2)}) %collective-permute-start.1) | collective-permute-done | bytes 163872 | tf_op jit(solution)/shard_map/ppermute | solution.py:388
  22.1 13.6 %collective-permute-done.4.refs_5_ = f32[160,256]{1,0:T(8,128)S(1)} collective-permute-done((f32[160,256]{1,0:T(8,128)S(1)}, f32[160,256]{1,0:T(8,128)S(1)}, u32[]{:S(2)}, u32[]{:S(2)}) %collective-permute-start.4) | collective-permute-done | bytes 163872 | tf_op jit(solution)/shard_map/ppermute | solution.py:388
  35.7 9.4 %filter.1 = (f32[128,256]{1,0:T(8,128)S(1)}, f32[128,256]{1,0:T(8,128)S(1)}, f32[128,256]{1,0:T(8,128)S(1)}, f32[128,256]{1,0:T(8,128)S(1)}, f32[128,256]{1,0:T(...) custom-call(s32[3]{0:T(128)S(1)} %pad_add_fusion.pos_ref, ...), custom_call_target="tpu_custom_call" | custom-call | tf_op jit(solution)/shard_map/filter/pallas_call | solution.py:367
  45.1 8.1 %collective-permute-start.10 = (f32[128,256]{1,0:T(8,128)S(1)}, f32[128,256]{1,0:T(8,128)S(1)}, u32[]{:S(2)}, u32[]{:S(2)}) collective-permute-start(f32[128,256]{1,0:T(8,128)S(1)} %get-tuple-element.41), channel_id=1, source_target_pairs={{0,4},{1,5},{2,6},{3,7},{4,0},{5,1},{6,2},{7,3},{8,12},{9,13},{10,... | collective-permute-start | bytes 393224 | tf_op jit(solution)/shard_map/ppermute | solution.py:388
  53.7 4.3 %collective-permute-start.13 = (f32[128,256]{1,0:T(8,128)S(1)}, f32[128,256]{1,0:T(8,128)S(1)}, u32[]{:S(2)}, u32[]{:S(2)}) collective-permute-start(f32[128,256]{1,0:T(8,128)S(1)} %get-tuple-element.44), channel_id=1, source_target_pairs={{0,7},{1,6},{2,5},{3,4},{4,3},{5,2},{6,1},{7,0},{8,15},{9,14},{10,... | collective-permute-start | bytes 393224 | tf_op jit(solution)/shard_map/ppermute | solution.py:388
  58.5 8.5 %collective-permute-done.10.refs_4_ = f32[128,256]{1,0:T(8,128)S(1)} collective-permute-done((f32[128,256]{1,0:T(8,128)S(1)}, f32[128,256]{1,0:T(8,128)S(1)}, u32[]{:S(2)}, u32[]{:S(2)}) %collective-permute-start.10) | collective-permute-done | bytes 131104 | tf_op jit(solution)/shard_map/ppermute | solution.py:388
  67.0 2.3 %collective-permute-done.11.refs_5_ = f32[128,256]{1,0:T(8,128)S(1)} collective-permute-done((f32[128,256]{1,0:T(8,128)S(1)}, f32[128,256]{1,0:T(8,128)S(1)}, u32[]{:S(2)}, u32[]{:S(2)}) %collective-permute-start.11) | collective-permute-done | bytes 131104 | tf_op jit(solution)/shard_map/ppermute | solution.py:388
  69.4 3.5 %collective-permute-done.8.refs_2_ = f32[128,256]{1,0:T(8,128)S(1)} collective-permute-done((f32[128,256]{1,0:T(8,128)S(1)}, f32[128,256]{1,0:T(8,128)S(1)}, u32[]{:S(2)}, u32[]{:S(2)}) %collective-permute-start.8) | collective-permute-done | bytes 131104 | tf_op jit(solution)/shard_map/ppermute | solution.py:388
  72.8 2.4 %collective-permute-done.9.refs_3_ = f32[128,256]{1,0:T(8,128)S(1)} collective-permute-done((f32[128,256]{1,0:T(8,128)S(1)}, f32[128,256]{1,0:T(8,128)S(1)}, u32[]{:S(2)}, u32[]{:S(2)}) %collective-permute-start.9) | collective-permute-done | bytes 131104 | tf_op jit(solution)/shard_map/ppermute | solution.py:388
  75.9 1.8 %collective-permute-start.19 = (f32[2,128,256]{2,1,0:T(8,128)S(1)}, f32[2,128,256]{2,1,0:T(8,128)S(1)}, u32[]{:S(2)}, u32[]{:S(2)}) collective-permute-start(f32[2,128,256]{2,1,0:T(8,128)S(1)} %get-tuple-element.50), channel_id=1, source_target_pairs={{0,16},{8,24},{16,0},{24,8},{1,17},{9,25},{17,1},{25,9},{2,18},{10... | collective-permute-start | bytes 786440 | tf_op jit(solution)/shard_map/ppermute | solution.py:388
  78.6 1.5 %own.1 = (f32[2,64,128]{2,1,0:T(8,128)S(1)}, f32[2,64,128]{2,1,0:T(8,128)S(1)}) custom-call(s32[3]{0:T(128)S(1)} %pad_add_fusion.pos_ref, f32[8,128,256]{2,1,0:T(8,128)S(1)} %get-tuple-element.45.z_ref, f32[8,128,256]{2,1,0:T(8,128)S(1)} %collective-permute-done.15.zc_ref), custom_call_target="tpu_custom_call" | custom-call | tf_op jit(solution)/shard_map/own/pallas_call | solution.py:367
  80.1 2.0 %collective-permute-start.16 = (f32[2,64,128]{2,1,0:T(8,128)S(1)}, f32[2,64,128]{2,1,0:T(8,128)S(1)}, u32[]{:S(2)}, u32[]{:S(2)}) collective-permute-start(f32[2,64,128]{2,1,0:T(8,128)S(1)} %get-tuple-element.48), channel_id=1, source_target_pairs={{0,1},{1,0},{2,3},{3,2},{4,5},{5,4},{6,7},{7,6},{8,9},{9,8},{10,11... | collective-permute-start | bytes 196616 | tf_op jit(solution)/shard_map/ppermute | solution.py:388
  82.2 2.9 %collective-permute-done.19.first = f32[2,128,256]{2,1,0:T(8,128)S(1)} collective-permute-done((f32[2,128,256]{2,1,0:T(8,128)S(1)}, f32[2,128,256]{2,1,0:T(8,128)S(1)}, u32[]{:S(2)}, u32[]{:S(2)}) %collective-permute-start.19) | collective-permute-done | bytes 262176 | tf_op jit(solution)/shard_map/ppermute | solution.py:388
  85.1 5.1 %collective-permute-done.14.second = f32[2,128,256]{2,1,0:T(8,128)S(1)} collective-permute-done((f32[2,128,256]{2,1,0:T(8,128)S(1)}, f32[2,128,256]{2,1,0:T(8,128)S(1)}, u32[]{:S(2)}, u32[]{:S(2)}) %collective-permute-start.14) | collective-permute-done | bytes 262176 | tf_op jit(solution)/shard_map/ppermute | solution.py:388
  90.3 1.9 %collective-permute-start.17 = (f32[2,64,128]{2,1,0:T(8,128)S(1)}, f32[2,64,128]{2,1,0:T(8,128)S(1)}, u32[]{:S(2)}, u32[]{:S(2)}) collective-permute-start(f32[2,64,128]{2,1,0:T(8,128)S(1)} %add.13), channel_id=1, source_target_pairs={{0,2},{1,3},{2,0},{3,1},{4,6},{5,7},{6,4},{7,5},{8,10},{9,11},{10,... | collective-permute-start | bytes 196616 | tf_op jit(solution)/shard_map/ppermute | solution.py:388
  92.2 2.8 %collective-permute-done.17 = f32[2,64,128]{2,1,0:T(8,128)S(1)} collective-permute-done((f32[2,64,128]{2,1,0:T(8,128)S(1)}, f32[2,64,128]{2,1,0:T(8,128)S(1)}, u32[]{:S(2)}, u32[]{:S(2)}) %collective-permute-start.17) | collective-permute-done | bytes 65568 | tf_op jit(solution)/shard_map/ppermute | solution.py:388
  95.0 1.7 %collective-permute-start.18 = (f32[2,64,128]{2,1,0:T(8,128)S(1)}, f32[2,64,128]{2,1,0:T(8,128)S(1)}, u32[]{:S(2)}, u32[]{:S(2)}) collective-permute-start(f32[2,64,128]{2,1,0:T(8,128)S(1)} %add.14.tie), channel_id=1, source_target_pairs={{0,4},{1,5},{2,6},{3,7},{4,0},{5,1},{6,2},{7,3},{8,12},{9,13},{10,... | collective-permute-start | bytes 196616 | tf_op jit(solution)/shard_map/ppermute | solution.py:388
  96.6 1.5 %cross.1 = (f32[2,64,128]{2,1,0:T(8,128)S(1)}, f32[2,64,128]{2,1,0:T(8,128)S(1)}, f32[2,64,128]{2,1,0:T(8,128)S(1)}, f32[2,64,128]{2,1,0:T(8,128)S(1)}) custom-call(s32[3]{0:T(128)S(1)} %pad_add_fusion.pos_ref, f32[8,128,256]{2,1,0:T(8,128)S(1)} %get-tuple-element.45.z_ref, f32[8,128,256]{2,1,0:T(8,128)S(1)} %collective-permute-done.15.zc_ref, ...), custom_call_target="tpu_custom_call" | custom-call | tf_op jit(solution)/shard_map/cross/pallas_call | solution.py:367
  99.5 1.6 %collective-permute-start.23 = (f32[2,64,128]{2,1,0:T(8,128)S(1)}, f32[2,64,128]{2,1,0:T(8,128)S(1)}, u32[]{:S(2)}, u32[]{:S(2)}) collective-permute-start(f32[2,64,128]{2,1,0:T(8,128)S(1)} %get-tuple-element.54), channel_id=1, source_target_pairs={{0,16},{8,24},{16,0},{24,8},{1,17},{9,25},{17,1},{25,9},{2,18},{10... | collective-permute-start | bytes 196616 | tf_op jit(solution)/shard_map/ppermute | solution.py:388
  102.6 1.6 %collective-permute-done.23.c_ref = f32[2,64,128]{2,1,0:T(8,128)S(1)} collective-permute-done((f32[2,64,128]{2,1,0:T(8,128)S(1)}, f32[2,64,128]{2,1,0:T(8,128)S(1)}, u32[]{:S(2)}, u32[]{:S(2)}) %collective-permute-start.23) | collective-permute-done | bytes 65568 | tf_op jit(solution)/shard_map/ppermute | solution.py:388
  104.2 2.0 %collective-permute-done.24.d_ref = f32[2,64,128]{2,1,0:T(8,128)S(1)} collective-permute-done((f32[2,64,128]{2,1,0:T(8,128)S(1)}, f32[2,64,128]{2,1,0:T(8,128)S(1)}, u32[]{:S(2)}, u32[]{:S(2)}) %collective-permute-start.24) | collective-permute-done | bytes 65568 | tf_op jit(solution)/shard_map/ppermute | solution.py:394
  106.2 1.7 %collective-permute-start.25 = (f32[2,64,128]{2,1,0:T(8,128)S(1)}, f32[2,64,128]{2,1,0:T(8,128)S(1)}, u32[]{:S(2)}, u32[]{:S(2)}) collective-permute-start(f32[2,64,128]{2,1,0:T(8,128)S(1)} %sum.1), channel_id=1, source_target_pairs={{0,2},{1,3},{2,0},{3,1},{4,6},{5,7},{6,4},{7,5},{8,10},{9,11},{10,... | collective-permute-start | bytes 196616 | tf_op jit(solution)/shard_map/ppermute | solution.py:388
  107.9 2.6 %collective-permute-done.25 = f32[2,64,128]{2,1,0:T(8,128)S(1)} collective-permute-done((f32[2,64,128]{2,1,0:T(8,128)S(1)}, f32[2,64,128]{2,1,0:T(8,128)S(1)}, u32[]{:S(2)}, u32[]{:S(2)}) %collective-permute-start.25) | collective-permute-done | bytes 65568 | tf_op jit(solution)/shard_map/ppermute | solution.py:388
  110.6 1.9 %collective-permute-start.26 = (f32[2,64,128]{2,1,0:T(8,128)S(1)}, f32[2,64,128]{2,1,0:T(8,128)S(1)}, u32[]{:S(2)}, u32[]{:S(2)}) collective-permute-start(f32[2,64,128]{2,1,0:T(8,128)S(1)} %add.16.cross), channel_id=1, source_target_pairs={{0,4},{1,5},{2,6},{3,7},{4,0},{5,1},{6,2},{7,3},{8,12},{9,13},{10,... | collective-permute-start | bytes 196616 | tf_op jit(solution)/shard_map/ppermute | solution.py:388
  112.5 3.3 %collective-permute-done.26.cross_other = f32[2,64,128]{2,1,0:T(8,128)S(1)} collective-permute-done((f32[2,64,128]{2,1,0:T(8,128)S(1)}, f32[2,64,128]{2,1,0:T(8,128)S(1)}, u32[]{:S(2)}, u32[]{:S(2)}) %collective-permute-start.26) | collective-permute-done | bytes 65568 | tf_op jit(solution)/shard_map/ppermute | solution.py:388
  116.4 1.8 %collective-permute-start.27 = (f32[4,64,128]{2,1,0:T(8,128)S(1)}, f32[4,64,128]{2,1,0:T(8,128)S(1)}, u32[]{:S(2)}, u32[]{:S(2)}) collective-permute-start(f32[4,64,128]{2,1,0:T(8,128)S(1)} %pair.1.mine), channel_id=1, source_target_pairs={{0,1},{1,0},{2,3},{3,2},{4,5},{5,4},{6,7},{7,6},{8,9},{9,8},{10,11... | collective-permute-start | bytes 393224 | tf_op jit(solution)/shard_map/ppermute | solution.py:388
  118.1 1.3 %output.1 = f32[8,256,128]{2,1,0:T(8,128)} custom-call(f32[8,128,256]{2,1,0:T(8,128)S(1)} %get-tuple-element.45.z_ref), custom_call_target="tpu_custom_call" | custom-call | tf_op jit(solution)/shard_map/output/pallas_call | solution.py:367
  119.4 2.0 %collective-permute-done.27.other = f32[4,64,128]{2,1,0:T(8,128)S(1)} collective-permute-done((f32[4,64,128]{2,1,0:T(8,128)S(1)}, f32[4,64,128]{2,1,0:T(8,128)S(1)}, u32[]{:S(2)}, u32[]{:S(2)}) %collective-permute-start.27) | collective-permute-done | bytes 131104 | tf_op jit(solution)/shard_map/ppermute | solution.py:388
  (58 shorter events, 13.9 us)
Async XLA Ops:
  1.4 1.2 copy-start
  3.5 32.2 %copy-start.1 = (bf16[256,384]{1,0:T(8,128)(2,1)S(1)}, bf16[256,384]{1,0:T(8,128)(2,1)}, u32[]{:S(2)}) copy-start(bf16[256,384]{1,0:T(8,128)(2,1)} %constant.37.fold_ref) | copy-start | bytes 589828
  3.5 32.2 %copy-start.2 = (bf16[256,256]{1,0:T(8,128)(2,1)S(1)}, bf16[256,256]{1,0:T(8,128)(2,1)}, u32[]{:S(2)}) copy-start(bf16[256,256]{1,0:T(8,128)(2,1)} %constant.33.lh_ref) | copy-start | bytes 393220
  3.5 32.2 %copy-start.3 = (bf16[256,256]{1,0:T(8,128)(2,1)S(1)}, bf16[256,256]{1,0:T(8,128)(2,1)}, u32[]{:S(2)}) copy-start(bf16[256,256]{1,0:T(8,128)(2,1)} %constant.36.ll_ref) | copy-start | bytes 393220
  4.5 8.9 %collective-permute-start = (f32[160,256]{1,0:T(8,128)S(1)}, f32[160,256]{1,0:T(8,128)S(1)}, u32[]{:S(2)}, u32[]{:S(2)}) collective-permute-start(f32[160,256]{1,0:T(8,128)S(1)} %get-tuple-element.30), channel_id=1, source_target_pairs={{0,1},{1,0},{2,3},{3,2},{4,5},{5,4},{6,7},{7,6},{8,9},{9,8},{10,11... | collective-permute-start | bytes 491528 | tf_op jit(solution)/shard_map/ppermute | solution.py:388
  7.5 13.1 %collective-permute-start.1 = (f32[160,256]{1,0:T(8,128)S(1)}, f32[160,256]{1,0:T(8,128)S(1)}, u32[]{:S(2)}, u32[]{:S(2)}) collective-permute-start(f32[160,256]{1,0:T(8,128)S(1)} %get-tuple-element.31), channel_id=1, source_target_pairs={{0,2},{1,3},{2,0},{3,1},{4,6},{5,7},{6,4},{7,5},{8,10},{9,11},{10,... | collective-permute-start | bytes 491528 | tf_op jit(solution)/shard_map/ppermute | solution.py:388
  9.1 13.0 %collective-permute-start.2 = (f32[160,256]{1,0:T(8,128)S(1)}, f32[160,256]{1,0:T(8,128)S(1)}, u32[]{:S(2)}, u32[]{:S(2)}) collective-permute-start(f32[160,256]{1,0:T(8,128)S(1)} %get-tuple-element.32), channel_id=1, source_target_pairs={{0,3},{1,2},{2,1},{3,0},{4,7},{5,6},{6,5},{7,4},{8,11},{9,10},{10,... | collective-permute-start | bytes 491528 | tf_op jit(solution)/shard_map/ppermute | solution.py:388
  9.1 13.0 %collective-permute-start.3 = (f32[160,256]{1,0:T(8,128)S(1)}, f32[160,256]{1,0:T(8,128)S(1)}, u32[]{:S(2)}, u32[]{:S(2)}) collective-permute-start(f32[160,256]{1,0:T(8,128)S(1)} %get-tuple-element.33), channel_id=1, source_target_pairs={{0,4},{1,5},{2,6},{3,7},{4,0},{5,1},{6,2},{7,3},{8,12},{9,13},{10,... | collective-permute-start | bytes 491528 | tf_op jit(solution)/shard_map/ppermute | solution.py:388
  12.1 23.6 %collective-permute-start.4 = (f32[160,256]{1,0:T(8,128)S(1)}, f32[160,256]{1,0:T(8,128)S(1)}, u32[]{:S(2)}, u32[]{:S(2)}) collective-permute-start(f32[160,256]{1,0:T(8,128)S(1)} %get-tuple-element.34), channel_id=1, source_target_pairs={{0,5},{1,4},{2,7},{3,6},{4,1},{5,0},{6,3},{7,2},{8,13},{9,12},{10,... | collective-permute-start | bytes 491528 | tf_op jit(solution)/shard_map/ppermute | solution.py:388
  13.4 22.3 %collective-permute-start.5 = (f32[160,256]{1,0:T(8,128)S(1)}, f32[160,256]{1,0:T(8,128)S(1)}, u32[]{:S(2)}, u32[]{:S(2)}) collective-permute-start(f32[160,256]{1,0:T(8,128)S(1)} %get-tuple-element.35), channel_id=1, source_target_pairs={{0,6},{1,7},{2,4},{3,5},{4,2},{5,3},{6,0},{7,1},{8,14},{9,15},{10,... | collective-permute-start | bytes 491528 | tf_op jit(solution)/shard_map/ppermute | solution.py:388
  20.6 15.1 %collective-permute-start.6 = (f32[160,256]{1,0:T(8,128)S(1)}, f32[160,256]{1,0:T(8,128)S(1)}, u32[]{:S(2)}, u32[]{:S(2)}) collective-permute-start(f32[160,256]{1,0:T(8,128)S(1)} %get-tuple-element.36), channel_id=1, source_target_pairs={{0,7},{1,6},{2,5},{3,4},{4,3},{5,2},{6,1},{7,0},{8,15},{9,14},{10,... | collective-permute-start | bytes 491528 | tf_op jit(solution)/shard_map/ppermute | solution.py:388
  45.1 22.0 %collective-permute-start.10 = (f32[128,256]{1,0:T(8,128)S(1)}, f32[128,256]{1,0:T(8,128)S(1)}, u32[]{:S(2)}, u32[]{:S(2)}) collective-permute-start(f32[128,256]{1,0:T(8,128)S(1)} %get-tuple-element.41), channel_id=1, source_target_pairs={{0,4},{1,5},{2,6},{3,7},{4,0},{5,1},{6,2},{7,3},{8,12},{9,13},{10,... | collective-permute-start | bytes 393224 | tf_op jit(solution)/shard_map/ppermute | solution.py:388
  53.2 16.1 %collective-permute-start.11 = (f32[128,256]{1,0:T(8,128)S(1)}, f32[128,256]{1,0:T(8,128)S(1)}, u32[]{:S(2)}, u32[]{:S(2)}) collective-permute-start(f32[128,256]{1,0:T(8,128)S(1)} %get-tuple-element.42), channel_id=1, source_target_pairs={{0,5},{1,4},{2,7},{3,6},{4,1},{5,0},{6,3},{7,2},{8,13},{9,12},{10,... | collective-permute-start | bytes 393224 | tf_op jit(solution)/shard_map/ppermute | solution.py:388
  53.3 16.1 %collective-permute-start.12 = (f32[128,256]{1,0:T(8,128)S(1)}, f32[128,256]{1,0:T(8,128)S(1)}, u32[]{:S(2)}, u32[]{:S(2)}) collective-permute-start(f32[128,256]{1,0:T(8,128)S(1)} %get-tuple-element.43), channel_id=1, source_target_pairs={{0,6},{1,7},{2,4},{3,5},{4,2},{5,3},{6,0},{7,1},{8,14},{9,15},{10,... | collective-permute-start | bytes 393224 | tf_op jit(solution)/shard_map/ppermute | solution.py:388
  53.7 15.6 %collective-permute-start.13 = (f32[128,256]{1,0:T(8,128)S(1)}, f32[128,256]{1,0:T(8,128)S(1)}, u32[]{:S(2)}, u32[]{:S(2)}) collective-permute-start(f32[128,256]{1,0:T(8,128)S(1)} %get-tuple-element.44), channel_id=1, source_target_pairs={{0,7},{1,6},{2,5},{3,4},{4,3},{5,2},{6,1},{7,0},{8,15},{9,14},{10,... | collective-permute-start | bytes 393224 | tf_op jit(solution)/shard_map/ppermute | solution.py:388
  58.0 11.3 %collective-permute-start.7 = (f32[128,256]{1,0:T(8,128)S(1)}, f32[128,256]{1,0:T(8,128)S(1)}, u32[]{:S(2)}, u32[]{:S(2)}) collective-permute-start(f32[128,256]{1,0:T(8,128)S(1)} %get-tuple-element.38), channel_id=1, source_target_pairs={{0,1},{1,0},{2,3},{3,2},{4,5},{5,4},{6,7},{7,6},{8,9},{9,8},{10,11... | collective-permute-start | bytes 393224 | tf_op jit(solution)/shard_map/ppermute | solution.py:388
  67.0 5.8 %collective-permute-start.8 = (f32[128,256]{1,0:T(8,128)S(1)}, f32[128,256]{1,0:T(8,128)S(1)}, u32[]{:S(2)}, u32[]{:S(2)}) collective-permute-start(f32[128,256]{1,0:T(8,128)S(1)} %get-tuple-element.39), channel_id=1, source_target_pairs={{0,2},{1,3},{2,0},{3,1},{4,6},{5,7},{6,4},{7,5},{8,10},{9,11},{10,... | collective-permute-start | bytes 393224 | tf_op jit(solution)/shard_map/ppermute | solution.py:388
  69.3 5.9 %collective-permute-start.9 = (f32[128,256]{1,0:T(8,128)S(1)}, f32[128,256]{1,0:T(8,128)S(1)}, u32[]{:S(2)}, u32[]{:S(2)}) collective-permute-start(f32[128,256]{1,0:T(8,128)S(1)} %get-tuple-element.40), channel_id=1, source_target_pairs={{0,3},{1,2},{2,1},{3,0},{4,7},{5,6},{6,5},{7,4},{8,11},{9,10},{10,... | collective-permute-start | bytes 393224 | tf_op jit(solution)/shard_map/ppermute | solution.py:388
  75.9 2.7 %collective-permute-start.15 = (f32[8,128,256]{2,1,0:T(8,128)S(1)}, f32[8,128,256]{2,1,0:T(8,128)S(1)}, u32[]{:S(2)}, u32[]{:S(2)}) collective-permute-start(f32[8,128,256]{2,1,0:T(8,128)S(1)} %get-tuple-element.45.z_ref), channel_id=1, source_target_pairs={{0,8},{8,0},{16,24},{24,16},{1,9},{9,1},{17,25},{25,17},{2,10},{10... | collective-permute-start | bytes 3145736 | tf_op jit(solution)/shard_map/ppermute | solution.py:388
  75.9 9.2 %collective-permute-start.19 = (f32[2,128,256]{2,1,0:T(8,128)S(1)}, f32[2,128,256]{2,1,0:T(8,128)S(1)}, u32[]{:S(2)}, u32[]{:S(2)}) collective-permute-start(f32[2,128,256]{2,1,0:T(8,128)S(1)} %get-tuple-element.50), channel_id=1, source_target_pairs={{0,16},{8,24},{16,0},{24,8},{1,17},{9,25},{17,1},{25,9},{2,18},{10... | collective-permute-start | bytes 786440 | tf_op jit(solution)/shard_map/ppermute | solution.py:388
  77.8 12.5 %collective-permute-start.14 = (f32[2,128,256]{2,1,0:T(8,128)S(1)}, f32[2,128,256]{2,1,0:T(8,128)S(1)}, u32[]{:S(2)}, u32[]{:S(2)}) collective-permute-start(f32[2,128,256]{2,1,0:T(8,128)S(1)} %get-tuple-element.46), channel_id=1, source_target_pairs={{0,16},{8,24},{16,0},{24,8},{1,17},{9,25},{17,1},{25,9},{2,18},{10... | collective-permute-start | bytes 786440 | tf_op jit(solution)/shard_map/ppermute | solution.py:388
  80.1 5.0 %collective-permute-start.16 = (f32[2,64,128]{2,1,0:T(8,128)S(1)}, f32[2,64,128]{2,1,0:T(8,128)S(1)}, u32[]{:S(2)}, u32[]{:S(2)}) collective-permute-start(f32[2,64,128]{2,1,0:T(8,128)S(1)} %get-tuple-element.48), channel_id=1, source_target_pairs={{0,1},{1,0},{2,3},{3,2},{4,5},{5,4},{6,7},{7,6},{8,9},{9,8},{10,11... | collective-permute-start | bytes 196616 | tf_op jit(solution)/shard_map/ppermute | solution.py:388
  85.1 11.5 %collective-permute-start.20 = (f32[2,128,256]{2,1,0:T(8,128)S(1)}, f32[2,128,256]{2,1,0:T(8,128)S(1)}, u32[]{:S(2)}, u32[]{:S(2)}) collective-permute-start(f32[2,128,256]{2,1,0:T(8,128)S(1)} %collective-permute-done.19.first), channel_id=1, source_target_pairs={{0,8},{8,0},{16,24},{24,16},{1,9},{9,1},{17,25},{25,17},{2,10},{10... | collective-permute-start | bytes 786440 | tf_op jit(solution)/shard_map/ppermute | solution.py:388
  90.3 6.4 %collective-permute-start.21 = (f32[2,128,256]{2,1,0:T(8,128)S(1)}, f32[2,128,256]{2,1,0:T(8,128)S(1)}, u32[]{:S(2)}, u32[]{:S(2)}) collective-permute-start(f32[2,128,256]{2,1,0:T(8,128)S(1)} %collective-permute-done.14.second), channel_id=1, source_target_pairs={{0,8},{8,0},{16,24},{24,16},{1,9},{9,1},{17,25},{25,17},{2,10},{10... | collective-permute-start | bytes 786440 | tf_op jit(solution)/shard_map/ppermute | solution.py:388
  90.3 4.7 %collective-permute-start.17 = (f32[2,64,128]{2,1,0:T(8,128)S(1)}, f32[2,64,128]{2,1,0:T(8,128)S(1)}, u32[]{:S(2)}, u32[]{:S(2)}) collective-permute-start(f32[2,64,128]{2,1,0:T(8,128)S(1)} %add.13), channel_id=1, source_target_pairs={{0,2},{1,3},{2,0},{3,1},{4,6},{5,7},{6,4},{7,5},{8,10},{9,11},{10,... | collective-permute-start | bytes 196616 | tf_op jit(solution)/shard_map/ppermute | solution.py:388
  95.0 6.8 %collective-permute-start.18 = (f32[2,64,128]{2,1,0:T(8,128)S(1)}, f32[2,64,128]{2,1,0:T(8,128)S(1)}, u32[]{:S(2)}, u32[]{:S(2)}) collective-permute-start(f32[2,64,128]{2,1,0:T(8,128)S(1)} %add.14.tie), channel_id=1, source_target_pairs={{0,4},{1,5},{2,6},{3,7},{4,0},{5,1},{6,2},{7,3},{8,12},{9,13},{10,... | collective-permute-start | bytes 196616 | tf_op jit(solution)/shard_map/ppermute | solution.py:388
  98.2 4.4 %collective-permute-start.22 = (f32[2,64,128]{2,1,0:T(8,128)S(1)}, f32[2,64,128]{2,1,0:T(8,128)S(1)}, u32[]{:S(2)}, u32[]{:S(2)}) collective-permute-start(f32[2,64,128]{2,1,0:T(8,128)S(1)} %get-tuple-element.53), channel_id=1, source_target_pairs={{0,1},{1,0},{2,3},{3,2},{4,5},{5,4},{6,7},{7,6},{8,9},{9,8},{10,11... | collective-permute-start | bytes 196616 | tf_op jit(solution)/shard_map/ppermute | solution.py:388
  99.5 4.8 %collective-permute-start.23 = (f32[2,64,128]{2,1,0:T(8,128)S(1)}, f32[2,64,128]{2,1,0:T(8,128)S(1)}, u32[]{:S(2)}, u32[]{:S(2)}) collective-permute-start(f32[2,64,128]{2,1,0:T(8,128)S(1)} %get-tuple-element.54), channel_id=1, source_target_pairs={{0,16},{8,24},{16,0},{24,8},{1,17},{9,25},{17,1},{25,9},{2,18},{10... | collective-permute-start | bytes 196616 | tf_op jit(solution)/shard_map/ppermute | solution.py:388
  101.0 5.2 %collective-permute-start.24 = (f32[2,64,128]{2,1,0:T(8,128)S(1)}, f32[2,64,128]{2,1,0:T(8,128)S(1)}, u32[]{:S(2)}, u32[]{:S(2)}) collective-permute-start(f32[2,64,128]{2,1,0:T(8,128)S(1)} %get-tuple-element.55), channel_id=1, source_target_pairs={{0,17},{1,16},{2,19},{3,18},{4,21},{5,20},{6,23},{7,22},{8,25},{9,... | collective-permute-start | bytes 196616 | tf_op jit(solution)/shard_map/ppermute | solution.py:394
  106.2 4.3 %collective-permute-start.25 = (f32[2,64,128]{2,1,0:T(8,128)S(1)}, f32[2,64,128]{2,1,0:T(8,128)S(1)}, u32[]{:S(2)}, u32[]{:S(2)}) collective-permute-start(f32[2,64,128]{2,1,0:T(8,128)S(1)} %sum.1), channel_id=1, source_target_pairs={{0,2},{1,3},{2,0},{3,1},{4,6},{5,7},{6,4},{7,5},{8,10},{9,11},{10,... | collective-permute-start | bytes 196616 | tf_op jit(solution)/shard_map/ppermute | solution.py:388
  110.6 5.2 %collective-permute-start.26 = (f32[2,64,128]{2,1,0:T(8,128)S(1)}, f32[2,64,128]{2,1,0:T(8,128)S(1)}, u32[]{:S(2)}, u32[]{:S(2)}) collective-permute-start(f32[2,64,128]{2,1,0:T(8,128)S(1)} %add.16.cross), channel_id=1, source_target_pairs={{0,4},{1,5},{2,6},{3,7},{4,0},{5,1},{6,2},{7,3},{8,12},{9,13},{10,... | collective-permute-start | bytes 196616 | tf_op jit(solution)/shard_map/ppermute | solution.py:388
  116.4 5.0 %collective-permute-start.27 = (f32[4,64,128]{2,1,0:T(8,128)S(1)}, f32[4,64,128]{2,1,0:T(8,128)S(1)}, u32[]{:S(2)}, u32[]{:S(2)}) collective-permute-start(f32[4,64,128]{2,1,0:T(8,128)S(1)} %pair.1.mine), channel_id=1, source_target_pairs={{0,1},{1,0},{2,3},{3,2},{4,5},{5,4},{6,7},{7,6},{8,9},{9,8},{10,11... | collective-permute-start | bytes 393224 | tf_op jit(solution)/shard_map/ppermute | solution.py:388
  (5 other events, 4.1 us)

commit v5 on v4

--- a/solution.py
+++ b/solution.py
@@ -149,6 +149,10 @@
         lax.fori_loop(0, nd, body, 0)
 
 
+def arrival_order(nd):
+    return [*range(nd // 2, nd), *range(1, nd // 2), 0]
+
+
 def filter_kernel(nd, nb, total, pos_ref, kb_ref, lh_ref, ll_ref, fold_ref, *refs):
     pieces, outs = refs[:nd], refs[nd : 2 * nd]
     f0_ref, f1_ref, fold_out, spread_out, wh_ref, wl_ref, v_ref, packed = refs[2 * nd :]
@@ -172,9 +176,9 @@
         else:
             lax.fori_loop(0, nd, lambda s, c: (body(s), c)[1], 0)
 
-    for j in range(nd):
-        f0_ref[slab_rows(i ^ j)] = pieces[j][:R]
-        packed[i ^ j] = pieces[j][R:]
+    for piece, j in zip(pieces, arrival_order(nd)):
+        f0_ref[slab_rows(i ^ j)] = piece[:R]
+        packed[i ^ j] = piece[R:]
     wrap(f0_ref)
     build_projectors(nd, packed, wh_ref, wl_ref, v_ref)
 
@@ -465,7 +469,7 @@
     ready = call(
         functools.partial(filter_kernel, nd, nb, float(total)),
         [shape(R, LAT)] * nd,
-        [pos, kb_row, lh, ll, fold] + pieces,
+        [pos, kb_row, lh, ll, fold] + [pieces[j] for j in arrival_order(nd)],
         [
             pltpu.VMEM(((nd * SLAB + 2 * HALO) * nb, LAT), F32),
             pltpu.VMEM(((nd * SLAB + 2 * HALO) * nb, LAT), F32),

time: 123 us -> 125 us (1.016)
  waiting for transfers between devices: 57.8 us -> 68.7 us
  starting transfers between devices: 43.9 us -> 34.5 us
    ppermute x27, waiting for transfers between devices: 55.9 us -> 67 us  [xor_permute(): return lax.ppermute(value, axis, [(k, k ^ step) for k in range(count)])]
    ppermute x27, starting transfers between devices: 43.2 us -> 34 us  [xor_permute(): return lax.ppermute(value, axis, [(k, k ^ step) for k in range(count)])]
  transfers between devices with their start and end apart: 28 -> 28, of which waited for: 17 -> 19; matrix products, arithmetic and copies ran while one was open for 0% -> 0% of each run, Pallas kernels for 4% -> 4%
where the time goes in v5:
time: 125 us
  waiting for transfers between devices  68.7 us (55%)
  starting transfers between devices  34.5 us (28%)
  Pallas kernels  17.2 us (14%)
  local copies, waits for them, and re-layouts  3.41 us (3%)
    ppermute x27, waiting for transfers between devices, xor_permute(): return lax.ppermute(value, axis, [(k, k ^ step) for k in range(count)])  67 us
    ppermute x27, starting transfers between devices, xor_permute(): return lax.ppermute(value, axis, [(k, k ^ step) for k in range(count)])  34 us
    pallas_call x9, Pallas kernels, call(): pl.pallas_call(kernel, out_shape=out_shape, in_specs=specs, out_specs=pl....  17.2 us
    unnamed x18, local copies, waits for them, and re-layouts  3.41 us
  transfers between devices with their start and end apart: 28, of which 19 were waited for; matrix products, arithmetic and copies ran while one was open for 0% of the time, Pallas kernels for 4%

profile of v5, /device:TPU:0, one launch (start us, length us, event | category | flops | bytes accessed | tf_op | source)
XLA Modules:
  0.0 124.8 jit_solution(7748798212414324208)
XLA Ops:
  4.5 4.1 %collective-permute-start = (f32[160,256]{1,0:T(8,128)S(1)}, f32[160,256]{1,0:T(8,128)S(1)}, u32[]{:S(2)}, u32[]{:S(2)}) collective-permute-start(f32[160,256]{1,0:T(8,128)S(1)} %get-tuple-element.29), channel_id=1, source_target_pairs={{0,4},{1,5},{2,6},{3,7},{4,0},{5,1},{6,2},{7,3},{8,12},{9,13},{10,... | collective-permute-start | bytes 491528 | tf_op jit(solution)/shard_map/ppermute | solution.py:392
  9.9 3.6 %collective-permute-start.2 = (f32[160,256]{1,0:T(8,128)S(1)}, f32[160,256]{1,0:T(8,128)S(1)}, u32[]{:S(2)}, u32[]{:S(2)}) collective-permute-start(f32[160,256]{1,0:T(8,128)S(1)} %get-tuple-element.31), channel_id=1, source_target_pairs={{0,6},{1,7},{2,4},{3,5},{4,2},{5,3},{6,0},{7,1},{8,14},{9,15},{10,... | collective-permute-start | bytes 491528 | tf_op jit(solution)/shard_map/ppermute | solution.py:392
  13.5 1.7 %collective-permute-start.4 = (f32[160,256]{1,0:T(8,128)S(1)}, f32[160,256]{1,0:T(8,128)S(1)}, u32[]{:S(2)}, u32[]{:S(2)}) collective-permute-start(f32[160,256]{1,0:T(8,128)S(1)} %get-tuple-element.33), channel_id=1, source_target_pairs={{0,1},{1,0},{2,3},{3,2},{4,5},{5,4},{6,7},{7,6},{8,9},{9,8},{10,11... | collective-permute-start | bytes 491528 | tf_op jit(solution)/shard_map/ppermute | solution.py:392
  15.2 12.5 %collective-permute-done.refs_0_ = f32[160,256]{1,0:T(8,128)S(1)} collective-permute-done((f32[160,256]{1,0:T(8,128)S(1)}, f32[160,256]{1,0:T(8,128)S(1)}, u32[]{:S(2)}, u32[]{:S(2)}) %collective-permute-start) | collective-permute-done | bytes 163872 | tf_op jit(solution)/shard_map/ppermute | solution.py:392
  27.7 4.8 %collective-permute-done.1.refs_1_ = f32[160,256]{1,0:T(8,128)S(1)} collective-permute-done((f32[160,256]{1,0:T(8,128)S(1)}, f32[160,256]{1,0:T(8,128)S(1)}, u32[]{:S(2)}, u32[]{:S(2)}) %collective-permute-start.1) | collective-permute-done | bytes 163872 | tf_op jit(solution)/shard_map/ppermute | solution.py:392
  33.2 1.3 %collective-permute-done.5.refs_5_ = f32[160,256]{1,0:T(8,128)S(1)} collective-permute-done((f32[160,256]{1,0:T(8,128)S(1)}, f32[160,256]{1,0:T(8,128)S(1)}, u32[]{:S(2)}, u32[]{:S(2)}) %collective-permute-start.5) | collective-permute-done | bytes 163872 | tf_op jit(solution)/shard_map/ppermute | solution.py:392
  34.5 4.1 %collective-permute-done.6.refs_6_ = f32[160,256]{1,0:T(8,128)S(1)} collective-permute-done((f32[160,256]{1,0:T(8,128)S(1)}, f32[160,256]{1,0:T(8,128)S(1)}, u32[]{:S(2)}, u32[]{:S(2)}) %collective-permute-start.6) | collective-permute-done | bytes 163872 | tf_op jit(solution)/shard_map/ppermute | solution.py:392
  38.7 9.4 %filter.1 = (f32[128,256]{1,0:T(8,128)S(1)}, f32[128,256]{1,0:T(8,128)S(1)}, f32[128,256]{1,0:T(8,128)S(1)}, f32[128,256]{1,0:T(8,128)S(1)}, f32[128,256]{1,0:T(...) custom-call(s32[3]{0:T(128)S(1)} %pad_add_fusion.pos_ref, ...), custom_call_target="tpu_custom_call" | custom-call | tf_op jit(solution)/shard_map/filter/pallas_call | solution.py:371
  48.1 4.7 %collective-permute-start.10 = (f32[128,256]{1,0:T(8,128)S(1)}, f32[128,256]{1,0:T(8,128)S(1)}, u32[]{:S(2)}, u32[]{:S(2)}) collective-permute-start(f32[128,256]{1,0:T(8,128)S(1)} %get-tuple-element.41), channel_id=1, source_target_pairs={{0,4},{1,5},{2,6},{3,7},{4,0},{5,1},{6,2},{7,3},{8,12},{9,13},{10,... | collective-permute-start | bytes 393224 | tf_op jit(solution)/shard_map/ppermute | solution.py:392
  54.2 3.4 %collective-permute-start.13 = (f32[128,256]{1,0:T(8,128)S(1)}, f32[128,256]{1,0:T(8,128)S(1)}, u32[]{:S(2)}, u32[]{:S(2)}) collective-permute-start(f32[128,256]{1,0:T(8,128)S(1)} %get-tuple-element.44), channel_id=1, source_target_pairs={{0,7},{1,6},{2,5},{3,4},{4,3},{5,2},{6,1},{7,0},{8,15},{9,14},{10,... | collective-permute-start | bytes 393224 | tf_op jit(solution)/shard_map/ppermute | solution.py:392
  57.6 1.5 %collective-permute-start.7 = (f32[128,256]{1,0:T(8,128)S(1)}, f32[128,256]{1,0:T(8,128)S(1)}, u32[]{:S(2)}, u32[]{:S(2)}) collective-permute-start(f32[128,256]{1,0:T(8,128)S(1)} %get-tuple-element.38), channel_id=1, source_target_pairs={{0,1},{1,0},{2,3},{3,2},{4,5},{5,4},{6,7},{7,6},{8,9},{9,8},{10,11... | collective-permute-start | bytes 393224 | tf_op jit(solution)/shard_map/ppermute | solution.py:392
  59.0 8.1 %collective-permute-done.10.refs_4_ = f32[128,256]{1,0:T(8,128)S(1)} collective-permute-done((f32[128,256]{1,0:T(8,128)S(1)}, f32[128,256]{1,0:T(8,128)S(1)}, u32[]{:S(2)}, u32[]{:S(2)}) %collective-permute-start.10) | collective-permute-done | bytes 131104 | tf_op jit(solution)/shard_map/ppermute | solution.py:392
  67.1 3.7 %collective-permute-done.11.refs_5_ = f32[128,256]{1,0:T(8,128)S(1)} collective-permute-done((f32[128,256]{1,0:T(8,128)S(1)}, f32[128,256]{1,0:T(8,128)S(1)}, u32[]{:S(2)}, u32[]{:S(2)}) %collective-permute-start.11) | collective-permute-done | bytes 131104 | tf_op jit(solution)/shard_map/ppermute | solution.py:392
  70.8 1.9 %collective-permute-done.8.refs_2_ = f32[128,256]{1,0:T(8,128)S(1)} collective-permute-done((f32[128,256]{1,0:T(8,128)S(1)}, f32[128,256]{1,0:T(8,128)S(1)}, u32[]{:S(2)}, u32[]{:S(2)}) %collective-permute-start.8) | collective-permute-done | bytes 131104 | tf_op jit(solution)/shard_map/ppermute | solution.py:392
  72.6 4.3 %collective-permute-done.9.refs_3_ = f32[128,256]{1,0:T(8,128)S(1)} collective-permute-done((f32[128,256]{1,0:T(8,128)S(1)}, f32[128,256]{1,0:T(8,128)S(1)}, u32[]{:S(2)}, u32[]{:S(2)}) %collective-permute-start.9) | collective-permute-done | bytes 131104 | tf_op jit(solution)/shard_map/ppermute | solution.py:392
  77.7 1.6 %collective-permute-start.19 = (f32[2,128,256]{2,1,0:T(8,128)S(1)}, f32[2,128,256]{2,1,0:T(8,128)S(1)}, u32[]{:S(2)}, u32[]{:S(2)}) collective-permute-start(f32[2,128,256]{2,1,0:T(8,128)S(1)} %get-tuple-element.50), channel_id=1, source_target_pairs={{0,16},{8,24},{16,0},{24,8},{1,17},{9,25},{17,1},{25,9},{2,18},{10... | collective-permute-start | bytes 786440 | tf_op jit(solution)/shard_map/ppermute | solution.py:392
  80.4 1.5 %own.1 = (f32[2,64,128]{2,1,0:T(8,128)S(1)}, f32[2,64,128]{2,1,0:T(8,128)S(1)}) custom-call(s32[3]{0:T(128)S(1)} %pad_add_fusion.pos_ref, f32[8,128,256]{2,1,0:T(8,128)S(1)} %get-tuple-element.45.z_ref, f32[8,128,256]{2,1,0:T(8,128)S(1)} %collective-permute-done.15.zc_ref), custom_call_target="tpu_custom_call" | custom-call | tf_op jit(solution)/shard_map/own/pallas_call | solution.py:371
  82.6 4.3 %collective-permute-done.19.first = f32[2,128,256]{2,1,0:T(8,128)S(1)} collective-permute-done((f32[2,128,256]{2,1,0:T(8,128)S(1)}, f32[2,128,256]{2,1,0:T(8,128)S(1)}, u32[]{:S(2)}, u32[]{:S(2)}) %collective-permute-start.19) | collective-permute-done | bytes 262176 | tf_op jit(solution)/shard_map/ppermute | solution.py:392
  86.9 5.1 %collective-permute-done.14.second = f32[2,128,256]{2,1,0:T(8,128)S(1)} collective-permute-done((f32[2,128,256]{2,1,0:T(8,128)S(1)}, f32[2,128,256]{2,1,0:T(8,128)S(1)}, u32[]{:S(2)}, u32[]{:S(2)}) %collective-permute-start.14) | collective-permute-done | bytes 262176 | tf_op jit(solution)/shard_map/ppermute | solution.py:392
  92.1 2.3 %collective-permute-start.17 = (f32[2,64,128]{2,1,0:T(8,128)S(1)}, f32[2,64,128]{2,1,0:T(8,128)S(1)}, u32[]{:S(2)}, u32[]{:S(2)}) collective-permute-start(f32[2,64,128]{2,1,0:T(8,128)S(1)} %add.13), channel_id=1, source_target_pairs={{0,2},{1,3},{2,0},{3,1},{4,6},{5,7},{6,4},{7,5},{8,10},{9,11},{10,... | collective-permute-start | bytes 196616 | tf_op jit(solution)/shard_map/ppermute | solution.py:392
  94.3 2.8 %collective-permute-done.17 = f32[2,64,128]{2,1,0:T(8,128)S(1)} collective-permute-done((f32[2,64,128]{2,1,0:T(8,128)S(1)}, f32[2,64,128]{2,1,0:T(8,128)S(1)}, u32[]{:S(2)}, u32[]{:S(2)}) %collective-permute-start.17) | collective-permute-done | bytes 65568 | tf_op jit(solution)/shard_map/ppermute | solution.py:392
  97.9 1.5 %cross.1 = (f32[2,64,128]{2,1,0:T(8,128)S(1)}, f32[2,64,128]{2,1,0:T(8,128)S(1)}, f32[2,64,128]{2,1,0:T(8,128)S(1)}, f32[2,64,128]{2,1,0:T(8,128)S(1)}) custom-call(s32[3]{0:T(128)S(1)} %pad_add_fusion.pos_ref, f32[8,128,256]{2,1,0:T(8,128)S(1)} %get-tuple-element.45.z_ref, f32[8,128,256]{2,1,0:T(8,128)S(1)} %collective-permute-done.15.zc_ref, ...), custom_call_target="tpu_custom_call" | custom-call | tf_op jit(solution)/shard_map/cross/pallas_call | solution.py:371
  99.4 1.5 %collective-permute-start.22 = (f32[2,64,128]{2,1,0:T(8,128)S(1)}, f32[2,64,128]{2,1,0:T(8,128)S(1)}, u32[]{:S(2)}, u32[]{:S(2)}) collective-permute-start(f32[2,64,128]{2,1,0:T(8,128)S(1)} %get-tuple-element.53), channel_id=1, source_target_pairs={{0,1},{1,0},{2,3},{3,2},{4,5},{5,4},{6,7},{7,6},{8,9},{9,8},{10,11... | collective-permute-start | bytes 196616 | tf_op jit(solution)/shard_map/ppermute | solution.py:392
  101.0 1.5 %collective-permute-start.23 = (f32[2,64,128]{2,1,0:T(8,128)S(1)}, f32[2,64,128]{2,1,0:T(8,128)S(1)}, u32[]{:S(2)}, u32[]{:S(2)}) collective-permute-start(f32[2,64,128]{2,1,0:T(8,128)S(1)} %get-tuple-element.54), channel_id=1, source_target_pairs={{0,16},{8,24},{16,0},{24,8},{1,17},{9,25},{17,1},{25,9},{2,18},{10... | collective-permute-start | bytes 196616 | tf_op jit(solution)/shard_map/ppermute | solution.py:392
  103.8 2.2 %collective-permute-done.23.c_ref = f32[2,64,128]{2,1,0:T(8,128)S(1)} collective-permute-done((f32[2,64,128]{2,1,0:T(8,128)S(1)}, f32[2,64,128]{2,1,0:T(8,128)S(1)}, u32[]{:S(2)}, u32[]{:S(2)}) %collective-permute-start.23) | collective-permute-done | bytes 65568 | tf_op jit(solution)/shard_map/ppermute | solution.py:392
  105.9 1.7 %collective-permute-done.24.d_ref = f32[2,64,128]{2,1,0:T(8,128)S(1)} collective-permute-done((f32[2,64,128]{2,1,0:T(8,128)S(1)}, f32[2,64,128]{2,1,0:T(8,128)S(1)}, u32[]{:S(2)}, u32[]{:S(2)}) %collective-permute-start.24) | collective-permute-done | bytes 65568 | tf_op jit(solution)/shard_map/ppermute | solution.py:398
  108.3 3.7 %collective-permute-done.25 = f32[2,64,128]{2,1,0:T(8,128)S(1)} collective-permute-done((f32[2,64,128]{2,1,0:T(8,128)S(1)}, f32[2,64,128]{2,1,0:T(8,128)S(1)}, u32[]{:S(2)}, u32[]{:S(2)}) %collective-permute-start.25) | collective-permute-done | bytes 65568 | tf_op jit(solution)/shard_map/ppermute | solution.py:392
  112.0 2.2 %collective-permute-start.26 = (f32[2,64,128]{2,1,0:T(8,128)S(1)}, f32[2,64,128]{2,1,0:T(8,128)S(1)}, u32[]{:S(2)}, u32[]{:S(2)}) collective-permute-start(f32[2,64,128]{2,1,0:T(8,128)S(1)} %add.16.cross), channel_id=1, source_target_pairs={{0,4},{1,5},{2,6},{3,7},{4,0},{5,1},{6,2},{7,3},{8,12},{9,13},{10,... | collective-permute-start | bytes 196616 | tf_op jit(solution)/shard_map/ppermute | solution.py:392
  114.2 3.8 %collective-permute-done.26.cross_other = f32[2,64,128]{2,1,0:T(8,128)S(1)} collective-permute-done((f32[2,64,128]{2,1,0:T(8,128)S(1)}, f32[2,64,128]{2,1,0:T(8,128)S(1)}, u32[]{:S(2)}, u32[]{:S(2)}) %collective-permute-start.26) | collective-permute-done | bytes 65568 | tf_op jit(solution)/shard_map/ppermute | solution.py:392
  119.1 1.3 %output.1 = f32[8,256,128]{2,1,0:T(8,128)} custom-call(f32[8,128,256]{2,1,0:T(8,128)S(1)} %get-tuple-element.45.z_ref), custom_call_target="tpu_custom_call" | custom-call | tf_op jit(solution)/shard_map/output/pallas_call | solution.py:371
  120.4 3.1 %collective-permute-done.27.other = f32[4,64,128]{2,1,0:T(8,128)S(1)} collective-permute-done((f32[4,64,128]{2,1,0:T(8,128)S(1)}, f32[4,64,128]{2,1,0:T(8,128)S(1)}, u32[]{:S(2)}, u32[]{:S(2)}) %collective-permute-start.27) | collective-permute-done | bytes 131104 | tf_op jit(solution)/shard_map/ppermute | solution.py:392
  123.5 1.3 %place.1 = f32[128,512]{1,0:T(8,128)} custom-call(s32[3]{0:T(128)S(1)} %pad_add_fusion.pos_ref, f32[4,64,128]{2,1,0:T(8,128)S(1)} %pair.1.mine, f32[4,64,128]{2,1,0:T(8,128)S(1)} %collective-permute-done.27.other), custom_call_target="tpu_custom_call" | custom-call | tf_op jit(solution)/shard_map/place/pallas_call | solution.py:371
  (58 shorter events, 13.7 us)
Async XLA Ops:
  1.4 1.2 copy-start
  3.5 35.2 %copy-start.1 = (bf16[256,384]{1,0:T(8,128)(2,1)S(1)}, bf16[256,384]{1,0:T(8,128)(2,1)}, u32[]{:S(2)}) copy-start(bf16[256,384]{1,0:T(8,128)(2,1)} %constant.37.fold_ref) | copy-start | bytes 589828
  3.5 35.2 %copy-start.2 = (bf16[256,256]{1,0:T(8,128)(2,1)S(1)}, bf16[256,256]{1,0:T(8,128)(2,1)}, u32[]{:S(2)}) copy-start(bf16[256,256]{1,0:T(8,128)(2,1)} %constant.33.lh_ref) | copy-start | bytes 393220
  3.5 35.2 %copy-start.3 = (bf16[256,256]{1,0:T(8,128)(2,1)S(1)}, bf16[256,256]{1,0:T(8,128)(2,1)}, u32[]{:S(2)}) copy-start(bf16[256,256]{1,0:T(8,128)(2,1)} %constant.36.ll_ref) | copy-start | bytes 393220
  4.5 23.2 %collective-permute-start = (f32[160,256]{1,0:T(8,128)S(1)}, f32[160,256]{1,0:T(8,128)S(1)}, u32[]{:S(2)}, u32[]{:S(2)}) collective-permute-start(f32[160,256]{1,0:T(8,128)S(1)} %get-tuple-element.29), channel_id=1, source_target_pairs={{0,4},{1,5},{2,6},{3,7},{4,0},{5,1},{6,2},{7,3},{8,12},{9,13},{10,... | collective-permute-start | bytes 491528 | tf_op jit(solution)/shard_map/ppermute | solution.py:392
  8.6 23.9 %collective-permute-start.1 = (f32[160,256]{1,0:T(8,128)S(1)}, f32[160,256]{1,0:T(8,128)S(1)}, u32[]{:S(2)}, u32[]{:S(2)}) collective-permute-start(f32[160,256]{1,0:T(8,128)S(1)} %get-tuple-element.30), channel_id=1, source_target_pairs={{0,5},{1,4},{2,7},{3,6},{4,1},{5,0},{6,3},{7,2},{8,13},{9,12},{10,... | collective-permute-start | bytes 491528 | tf_op jit(solution)/shard_map/ppermute | solution.py:392
  9.9 23.3 %collective-permute-start.2 = (f32[160,256]{1,0:T(8,128)S(1)}, f32[160,256]{1,0:T(8,128)S(1)}, u32[]{:S(2)}, u32[]{:S(2)}) collective-permute-start(f32[160,256]{1,0:T(8,128)S(1)} %get-tuple-element.31), channel_id=1, source_target_pairs={{0,6},{1,7},{2,4},{3,5},{4,2},{5,3},{6,0},{7,1},{8,14},{9,15},{10,... | collective-permute-start | bytes 491528 | tf_op jit(solution)/shard_map/ppermute | solution.py:392
  13.5 19.7 %collective-permute-start.3 = (f32[160,256]{1,0:T(8,128)S(1)}, f32[160,256]{1,0:T(8,128)S(1)}, u32[]{:S(2)}, u32[]{:S(2)}) collective-permute-start(f32[160,256]{1,0:T(8,128)S(1)} %get-tuple-element.32), channel_id=1, source_target_pairs={{0,7},{1,6},{2,5},{3,4},{4,3},{5,2},{6,1},{7,0},{8,15},{9,14},{10,... | collective-permute-start | bytes 491528 | tf_op jit(solution)/shard_map/ppermute | solution.py:392
  13.5 19.7 %collective-permute-start.4 = (f32[160,256]{1,0:T(8,128)S(1)}, f32[160,256]{1,0:T(8,128)S(1)}, u32[]{:S(2)}, u32[]{:S(2)}) collective-permute-start(f32[160,256]{1,0:T(8,128)S(1)} %get-tuple-element.33), channel_id=1, source_target_pairs={{0,1},{1,0},{2,3},{3,2},{4,5},{5,4},{6,7},{7,6},{8,9},{9,8},{10,11... | collective-permute-start | bytes 491528 | tf_op jit(solution)/shard_map/ppermute | solution.py:392
  27.7 6.9 %collective-permute-start.5 = (f32[160,256]{1,0:T(8,128)S(1)}, f32[160,256]{1,0:T(8,128)S(1)}, u32[]{:S(2)}, u32[]{:S(2)}) collective-permute-start(f32[160,256]{1,0:T(8,128)S(1)} %get-tuple-element.34), channel_id=1, source_target_pairs={{0,2},{1,3},{2,0},{3,1},{4,6},{5,7},{6,4},{7,5},{8,10},{9,11},{10,... | collective-permute-start | bytes 491528 | tf_op jit(solution)/shard_map/ppermute | solution.py:392
  32.5 6.2 %collective-permute-start.6 = (f32[160,256]{1,0:T(8,128)S(1)}, f32[160,256]{1,0:T(8,128)S(1)}, u32[]{:S(2)}, u32[]{:S(2)}) collective-permute-start(f32[160,256]{1,0:T(8,128)S(1)} %get-tuple-element.35), channel_id=1, source_target_pairs={{0,3},{1,2},{2,1},{3,0},{4,7},{5,6},{6,5},{7,4},{8,11},{9,10},{10,... | collective-permute-start | bytes 491528 | tf_op jit(solution)/shard_map/ppermute | solution.py:392
  48.1 19.0 %collective-permute-start.10 = (f32[128,256]{1,0:T(8,128)S(1)}, f32[128,256]{1,0:T(8,128)S(1)}, u32[]{:S(2)}, u32[]{:S(2)}) collective-permute-start(f32[128,256]{1,0:T(8,128)S(1)} %get-tuple-element.41), channel_id=1, source_target_pairs={{0,4},{1,5},{2,6},{3,7},{4,0},{5,1},{6,2},{7,3},{8,12},{9,13},{10,... | collective-permute-start | bytes 393224 | tf_op jit(solution)/shard_map/ppermute | solution.py:392
  52.8 18.0 %collective-permute-start.11 = (f32[128,256]{1,0:T(8,128)S(1)}, f32[128,256]{1,0:T(8,128)S(1)}, u32[]{:S(2)}, u32[]{:S(2)}) collective-permute-start(f32[128,256]{1,0:T(8,128)S(1)} %get-tuple-element.42), channel_id=1, source_target_pairs={{0,5},{1,4},{2,7},{3,6},{4,1},{5,0},{6,3},{7,2},{8,13},{9,12},{10,... | collective-permute-start | bytes 393224 | tf_op jit(solution)/shard_map/ppermute | solution.py:392
  53.7 17.0 %collective-permute-start.12 = (f32[128,256]{1,0:T(8,128)S(1)}, f32[128,256]{1,0:T(8,128)S(1)}, u32[]{:S(2)}, u32[]{:S(2)}) collective-permute-start(f32[128,256]{1,0:T(8,128)S(1)} %get-tuple-element.43), channel_id=1, source_target_pairs={{0,6},{1,7},{2,4},{3,5},{4,2},{5,3},{6,0},{7,1},{8,14},{9,15},{10,... | collective-permute-start | bytes 393224 | tf_op jit(solution)/shard_map/ppermute | solution.py:392
  54.2 16.6 %collective-permute-start.13 = (f32[128,256]{1,0:T(8,128)S(1)}, f32[128,256]{1,0:T(8,128)S(1)}, u32[]{:S(2)}, u32[]{:S(2)}) collective-permute-start(f32[128,256]{1,0:T(8,128)S(1)} %get-tuple-element.44), channel_id=1, source_target_pairs={{0,7},{1,6},{2,5},{3,4},{4,3},{5,2},{6,1},{7,0},{8,15},{9,14},{10,... | collective-permute-start | bytes 393224 | tf_op jit(solution)/shard_map/ppermute | solution.py:392
  57.6 13.2 %collective-permute-start.7 = (f32[128,256]{1,0:T(8,128)S(1)}, f32[128,256]{1,0:T(8,128)S(1)}, u32[]{:S(2)}, u32[]{:S(2)}) collective-permute-start(f32[128,256]{1,0:T(8,128)S(1)} %get-tuple-element.38), channel_id=1, source_target_pairs={{0,1},{1,0},{2,3},{3,2},{4,5},{5,4},{6,7},{7,6},{8,9},{9,8},{10,11... | collective-permute-start | bytes 393224 | tf_op jit(solution)/shard_map/ppermute | solution.py:392
  67.1 5.6 %collective-permute-start.8 = (f32[128,256]{1,0:T(8,128)S(1)}, f32[128,256]{1,0:T(8,128)S(1)}, u32[]{:S(2)}, u32[]{:S(2)}) collective-permute-start(f32[128,256]{1,0:T(8,128)S(1)} %get-tuple-element.39), channel_id=1, source_target_pairs={{0,2},{1,3},{2,0},{3,1},{4,6},{5,7},{6,4},{7,5},{8,10},{9,11},{10,... | collective-permute-start | bytes 393224 | tf_op jit(solution)/shard_map/ppermute | solution.py:392
  70.7 6.2 %collective-permute-start.9 = (f32[128,256]{1,0:T(8,128)S(1)}, f32[128,256]{1,0:T(8,128)S(1)}, u32[]{:S(2)}, u32[]{:S(2)}) collective-permute-start(f32[128,256]{1,0:T(8,128)S(1)} %get-tuple-element.40), channel_id=1, source_target_pairs={{0,3},{1,2},{2,1},{3,0},{4,7},{5,6},{6,5},{7,4},{8,11},{9,10},{10,... | collective-permute-start | bytes 393224 | tf_op jit(solution)/shard_map/ppermute | solution.py:392
  77.6 2.7 %collective-permute-start.15 = (f32[8,128,256]{2,1,0:T(8,128)S(1)}, f32[8,128,256]{2,1,0:T(8,128)S(1)}, u32[]{:S(2)}, u32[]{:S(2)}) collective-permute-start(f32[8,128,256]{2,1,0:T(8,128)S(1)} %get-tuple-element.45.z_ref), channel_id=1, source_target_pairs={{0,8},{8,0},{16,24},{24,16},{1,9},{9,1},{17,25},{25,17},{2,10},{10... | collective-permute-start | bytes 3145736 | tf_op jit(solution)/shard_map/ppermute | solution.py:392
  77.7 9.2 %collective-permute-start.19 = (f32[2,128,256]{2,1,0:T(8,128)S(1)}, f32[2,128,256]{2,1,0:T(8,128)S(1)}, u32[]{:S(2)}, u32[]{:S(2)}) collective-permute-start(f32[2,128,256]{2,1,0:T(8,128)S(1)} %get-tuple-element.50), channel_id=1, source_target_pairs={{0,16},{8,24},{16,0},{24,8},{1,17},{9,25},{17,1},{25,9},{2,18},{10... | collective-permute-start | bytes 786440 | tf_op jit(solution)/shard_map/ppermute | solution.py:392
  79.3 12.8 %collective-permute-start.14 = (f32[2,128,256]{2,1,0:T(8,128)S(1)}, f32[2,128,256]{2,1,0:T(8,128)S(1)}, u32[]{:S(2)}, u32[]{:S(2)}) collective-permute-start(f32[2,128,256]{2,1,0:T(8,128)S(1)} %get-tuple-element.46), channel_id=1, source_target_pairs={{0,16},{8,24},{16,0},{24,8},{1,17},{9,25},{17,1},{25,9},{2,18},{10... | collective-permute-start | bytes 786440 | tf_op jit(solution)/shard_map/ppermute | solution.py:392
  81.9 5.0 %collective-permute-start.16 = (f32[2,64,128]{2,1,0:T(8,128)S(1)}, f32[2,64,128]{2,1,0:T(8,128)S(1)}, u32[]{:S(2)}, u32[]{:S(2)}) collective-permute-start(f32[2,64,128]{2,1,0:T(8,128)S(1)} %get-tuple-element.48), channel_id=1, source_target_pairs={{0,1},{1,0},{2,3},{3,2},{4,5},{5,4},{6,7},{7,6},{8,9},{9,8},{10,11... | collective-permute-start | bytes 196616 | tf_op jit(solution)/shard_map/ppermute | solution.py:392
  86.9 11.0 %collective-permute-start.20 = (f32[2,128,256]{2,1,0:T(8,128)S(1)}, f32[2,128,256]{2,1,0:T(8,128)S(1)}, u32[]{:S(2)}, u32[]{:S(2)}) collective-permute-start(f32[2,128,256]{2,1,0:T(8,128)S(1)} %collective-permute-done.19.first), channel_id=1, source_target_pairs={{0,8},{8,0},{16,24},{24,16},{1,9},{9,1},{17,25},{25,17},{2,10},{10... | collective-permute-start | bytes 786440 | tf_op jit(solution)/shard_map/ppermute | solution.py:392
  92.1 5.8 %collective-permute-start.21 = (f32[2,128,256]{2,1,0:T(8,128)S(1)}, f32[2,128,256]{2,1,0:T(8,128)S(1)}, u32[]{:S(2)}, u32[]{:S(2)}) collective-permute-start(f32[2,128,256]{2,1,0:T(8,128)S(1)} %collective-permute-done.14.second), channel_id=1, source_target_pairs={{0,8},{8,0},{16,24},{24,16},{1,9},{9,1},{17,25},{25,17},{2,10},{10... | collective-permute-start | bytes 786440 | tf_op jit(solution)/shard_map/ppermute | solution.py:392
  92.1 5.0 %collective-permute-start.17 = (f32[2,64,128]{2,1,0:T(8,128)S(1)}, f32[2,64,128]{2,1,0:T(8,128)S(1)}, u32[]{:S(2)}, u32[]{:S(2)}) collective-permute-start(f32[2,64,128]{2,1,0:T(8,128)S(1)} %add.13), channel_id=1, source_target_pairs={{0,2},{1,3},{2,0},{3,1},{4,6},{5,7},{6,4},{7,5},{8,10},{9,11},{10,... | collective-permute-start | bytes 196616 | tf_op jit(solution)/shard_map/ppermute | solution.py:392
  97.1 6.6 %collective-permute-start.18 = (f32[2,64,128]{2,1,0:T(8,128)S(1)}, f32[2,64,128]{2,1,0:T(8,128)S(1)}, u32[]{:S(2)}, u32[]{:S(2)}) collective-permute-start(f32[2,64,128]{2,1,0:T(8,128)S(1)} %add.14.tie), channel_id=1, source_target_pairs={{0,4},{1,5},{2,6},{3,7},{4,0},{5,1},{6,2},{7,3},{8,12},{9,13},{10,... | collective-permute-start | bytes 196616 | tf_op jit(solution)/shard_map/ppermute | solution.py:392
  99.4 4.3 %collective-permute-start.22 = (f32[2,64,128]{2,1,0:T(8,128)S(1)}, f32[2,64,128]{2,1,0:T(8,128)S(1)}, u32[]{:S(2)}, u32[]{:S(2)}) collective-permute-start(f32[2,64,128]{2,1,0:T(8,128)S(1)} %get-tuple-element.53), channel_id=1, source_target_pairs={{0,1},{1,0},{2,3},{3,2},{4,5},{5,4},{6,7},{7,6},{8,9},{9,8},{10,11... | collective-permute-start | bytes 196616 | tf_op jit(solution)/shard_map/ppermute | solution.py:392
  101.0 5.0 %collective-permute-start.23 = (f32[2,64,128]{2,1,0:T(8,128)S(1)}, f32[2,64,128]{2,1,0:T(8,128)S(1)}, u32[]{:S(2)}, u32[]{:S(2)}) collective-permute-start(f32[2,64,128]{2,1,0:T(8,128)S(1)} %get-tuple-element.54), channel_id=1, source_target_pairs={{0,16},{8,24},{16,0},{24,8},{1,17},{9,25},{17,1},{25,9},{2,18},{10... | collective-permute-start | bytes 196616 | tf_op jit(solution)/shard_map/ppermute | solution.py:392
  102.5 5.2 %collective-permute-start.24 = (f32[2,64,128]{2,1,0:T(8,128)S(1)}, f32[2,64,128]{2,1,0:T(8,128)S(1)}, u32[]{:S(2)}, u32[]{:S(2)}) collective-permute-start(f32[2,64,128]{2,1,0:T(8,128)S(1)} %get-tuple-element.55), channel_id=1, source_target_pairs={{0,17},{1,16},{2,19},{3,18},{4,21},{5,20},{6,23},{7,22},{8,25},{9,... | collective-permute-start | bytes 196616 | tf_op jit(solution)/shard_map/ppermute | solution.py:398
  107.7 4.3 %collective-permute-start.25 = (f32[2,64,128]{2,1,0:T(8,128)S(1)}, f32[2,64,128]{2,1,0:T(8,128)S(1)}, u32[]{:S(2)}, u32[]{:S(2)}) collective-permute-start(f32[2,64,128]{2,1,0:T(8,128)S(1)} %sum.1), channel_id=1, source_target_pairs={{0,2},{1,3},{2,0},{3,1},{4,6},{5,7},{6,4},{7,5},{8,10},{9,11},{10,... | collective-permute-start | bytes 196616 | tf_op jit(solution)/shard_map/ppermute | solution.py:392
  112.0 5.9 %collective-permute-start.26 = (f32[2,64,128]{2,1,0:T(8,128)S(1)}, f32[2,64,128]{2,1,0:T(8,128)S(1)}, u32[]{:S(2)}, u32[]{:S(2)}) collective-permute-start(f32[2,64,128]{2,1,0:T(8,128)S(1)} %add.16.cross), channel_id=1, source_target_pairs={{0,4},{1,5},{2,6},{3,7},{4,0},{5,1},{6,2},{7,3},{8,12},{9,13},{10,... | collective-permute-start | bytes 196616 | tf_op jit(solution)/shard_map/ppermute | solution.py:392
  118.5 5.0 %collective-permute-start.27 = (f32[4,64,128]{2,1,0:T(8,128)S(1)}, f32[4,64,128]{2,1,0:T(8,128)S(1)}, u32[]{:S(2)}, u32[]{:S(2)}) collective-permute-start(f32[4,64,128]{2,1,0:T(8,128)S(1)} %pair.1.mine), channel_id=1, source_target_pairs={{0,1},{1,0},{2,3},{3,2},{4,5},{5,4},{6,7},{7,6},{8,9},{9,8},{10,11... | collective-permute-start | bytes 393224 | tf_op jit(solution)/shard_map/ppermute | solution.py:392
  (5 other events, 3.6 us)

commit v6 on v5

--- a/solution.py
+++ b/solution.py
@@ -11,6 +11,7 @@
 HALO = 6
 REACH = 4
 SLAB = 8
+CHUNKS = 2
 SIDE = 16
 LAT = SIDE * SIDE
 
@@ -83,7 +84,7 @@
     return hi, lo
 
 
-def split_kernel(nd, nb, pos_ref, cell_ref, x_ref, v_ref, w_ref, code_ref, *refs):
+def split_kernel(nd, nb, chunks, pos_ref, cell_ref, x_ref, v_ref, w_ref, code_ref, *refs):
     outs, (scratch, packed) = refs[:-2], refs[-2:]
     i = pos_ref[0]
     cube = 2 * REACH + 1
@@ -107,14 +108,21 @@
     packed[24:32] = jnp.concatenate([v_ref[:, y, :] for y in range(SIDE)], axis=1)
     for q in range(SLAB):
         scratch[q] = x_ref[q].T
-    for j in range(nd):
-        start = (i ^ j) * nb
-        for q in range(SLAB):
-            outs[j][q * nb : (q + 1) * nb] = scratch[q, pl.ds(pl.multiple_of(start, nb), nb)]
-        outs[j][SLAB * nb :] = packed[...]
-
-
-def build_projectors(nd, scratch, wh_ref, wl_ref, v_ref):
+    for c in range(chunks):
+        for j in range(nd):
+            start = c * (nd * nb) + (i ^ j) * nb
+            out = outs[c * nd + j]
+            for q in range(SLAB):
+                out[q * nb : (q + 1) * nb] = scratch[q, pl.ds(pl.multiple_of(start, nb), nb)]
+            if c == 0:
+                out[SLAB * nb :] = packed[...]
+
+
+def weights_kernel(nd, R, pos_ref, *refs):
+    pieces, (wh_ref, wl_ref, v_ref, scratch) = refs[:nd], refs[nd:]
+    i = pos_ref[0]
+    for piece, j in zip(pieces, arrival_order(nd)):
+        scratch[i ^ j] = piece[R:]
     lat = lax.broadcasted_iota(jnp.int32, (LAT, 256), 0).astype(F32)
     plane = lax.broadcasted_iota(jnp.int32, (16, 1, 1), 0).astype(F32)
     diagonal = -1.5 * COEFFS[0] - CENTRE
@@ -153,9 +161,9 @@
     return [*range(nd // 2, nd), *range(1, nd // 2), 0]
 
 
-def filter_kernel(nd, nb, total, pos_ref, kb_ref, lh_ref, ll_ref, fold_ref, *refs):
+def filter_kernel(nd, nb, total, pos_ref, kb_ref, lh_ref, ll_ref, fold_ref, wh_ref, wl_ref, v_ref, *refs):
     pieces, outs = refs[:nd], refs[nd : 2 * nd]
-    f0_ref, f1_ref, fold_out, spread_out, wh_ref, wl_ref, v_ref, packed = refs[2 * nd :]
+    f0_ref, f1_ref, fold_out, spread_out = refs[2 * nd :]
     i = pos_ref[0]
     R = SLAB * nb
     rows_q = lax.broadcasted_iota(jnp.int32, (SLAB, nb, 256), 0)
@@ -178,9 +186,7 @@
 
     for piece, j in zip(pieces, arrival_order(nd)):
         f0_ref[slab_rows(i ^ j)] = piece[:R]
-        packed[i ^ j] = piece[R:]
     wrap(f0_ref)
-    build_projectors(nd, packed, wh_ref, wl_ref, v_ref)
 
     def apply(ref, finish):
         def project(s):
@@ -253,24 +259,28 @@
 
 
 def join_kernel(nd, nb, pos_ref, *refs):
-    pieces, (z_ref, first_ref, second_ref) = refs[:nd], refs[nd:]
+    pieces, (z_ref, send_ref) = refs[:nd], refs[-2:]
     i, y = pos_ref[0], pos_ref[2]
     for j in range(nd):
         rows = pl.ds(pl.multiple_of((i ^ j) * nb, nb), nb)
         for q in range(SLAB):
             z_ref[q, rows] = pieces[j][q * nb : (q + 1) * nb]
     half = SLAB // 2
-    for q in range(half // 2):
-        first_ref[q] = z_ref[(1 - y) * half + q]
-        second_ref[q] = z_ref[(1 - y) * half + half // 2 + q]
-
-
-def own_kernel(pos_ref, z_ref, zc_ref, keep_ref, send_ref, g_ref):
+    for q in range(half):
+        send_ref[q] = z_ref[(1 - y) * half + q]
+
+
+def bands_of(group, q):
+    return halves(jnp.concatenate([r[q] for r in group], axis=0))
+
+
+def own_kernel(chunks, pos_ref, *refs):
+    zs, cs, (keep_ref, send_ref, g_ref) = refs[:chunks], refs[chunks : 2 * chunks], refs[2 * chunks :]
     i, b = pos_ref[0], pos_ref[1]
     own = core = None
     for q in range(SLAB):
-        zh, zl = halves(z_ref[q])
-        ch, cl = halves(zc_ref[q])
+        zh, zl = bands_of(zs, q)
+        ch, cl = bands_of(cs, q)
         mine, other = dot3(zh, zl, zh, zl, NT), dot3(zh, zl, ch, cl, NT)
         own, core = (mine, other) if own is None else (own + mine, core + other)
     g_ref[b & 1] = own
@@ -285,17 +295,17 @@
         send_ref[c] = g_ref[c, pl.ds(pl.multiple_of((1 - x) * 64, 64), 64)]
 
 
-def cross_kernel(
-    pos_ref, z_ref, zc_ref, first, second, core_first, core_second, tie, keep, send, back, back_send, g_ref, back_ref
-):
+def cross_kernel(chunks, pos_ref, *refs):
+    zs, cs, fs, gs = (refs[k * chunks : (k + 1) * chunks] for k in range(4))
+    tie, keep, send, back, back_send, g_ref, back_ref = refs[4 * chunks :]
     i, b, y = pos_ref[0], pos_ref[1], pos_ref[2]
     half = SLAB // 2
     totals = None
     for q in range(half):
-        zh, zl = halves(z_ref[y * half + q])
-        ch, cl = halves(zc_ref[y * half + q])
-        fh, fl = halves((first, second)[q // (half // 2)][q % (half // 2)])
-        gh, gl = halves((core_first, core_second)[q // (half // 2)][q % (half // 2)])
+        zh, zl = bands_of(zs, y * half + q)
+        ch, cl = bands_of(cs, y * half + q)
+        fh, fl = bands_of(fs, q)
+        gh, gl = bands_of(gs, q)
         now = (
             dot3(zh, zl, fh, fl, NT),
             dot3(zh, zl, gh, gl, NT),
@@ -320,9 +330,9 @@
         out_ref[(1 - y) * 2 + c] = (cross[c] + cross_other[c]) * (1.0 / total)
 
 
-def output_kernel(z_ref, out_ref):
+def output_kernel(*refs):
     for q in range(SLAB):
-        out_ref[q] = z_ref[q].T
+        refs[-1][q] = jnp.concatenate([z[q] for z in refs[:-1]], axis=0).T
 
 
 def place_kernel(pos_ref, mine, other, out_ref):
@@ -433,7 +443,8 @@
     nd = lax.axis_size("dom")
     bands = trial_waves.shape[-1]
     direct = nd == 8
-    real = bands // nd
+    chunks = CHUNKS if direct else 1
+    real = bands // (nd * chunks)
     nb = max(real, 8)
     total = nd * SLAB * LAT
     dom = lax.axis_index("dom") if direct else jnp.int32(0)
@@ -445,8 +456,8 @@
     waves = trial_waves.reshape(SLAB, LAT, bands)
     if direct:
         cut = call(
-            functools.partial(split_kernel, nd, nb),
-            [shape(R + 32, LAT)] * nd,
+            functools.partial(split_kernel, nd, nb, chunks),
+            [shape(R + (0 if c else 32), LAT) for c in range(chunks) for j in range(nd)],
             [pos, atom_cell, waves, potential, proj_weights, point_codes],
             [pltpu.VMEM((SLAB, bands, LAT), F32), pltpu.VMEM((32, 256), F32)],
             "split",
@@ -460,61 +471,73 @@
     lh, ll = split_const(lateral_matrix())
     fold = jnp.asarray(fold_matrix()).astype(BF16)
     kb_row = jnp.concatenate([kb_energy, kb_energy, jnp.zeros((112,), F32)])[None]
-    pieces = swap_all(cut, direct)
+    arrived = [swap_all(cut[c * nd : (c + 1) * nd], direct) for c in range(chunks)]
     if not direct:
-        pieces = [
+        arrived[0] = [
             jnp.concatenate([jnp.pad(p, ((0, 0), (0, nb - real), (0, 0))).reshape(R, LAT), gathered[j]])
-            for j, p in enumerate(pieces)
+            for j, p in enumerate(arrived[0])
         ]
-    ready = call(
-        functools.partial(filter_kernel, nd, nb, float(total)),
-        [shape(R, LAT)] * nd,
-        [pos, kb_row, lh, ll, fold] + [pieces[j] for j in arrival_order(nd)],
-        [
-            pltpu.VMEM(((nd * SLAB + 2 * HALO) * nb, LAT), F32),
-            pltpu.VMEM(((nd * SLAB + 2 * HALO) * nb, LAT), F32),
-            pltpu.VMEM((nd * nb, 256), F32),
-            pltpu.VMEM((nd * nb, 256), F32),
-            pltpu.VMEM((nd * 256, 256), BF16),
-            pltpu.VMEM((nd * 256, 256), BF16),
-            pltpu.VMEM((nd * SLAB, LAT), F32),
-            pltpu.VMEM((nd, 32, 256), F32),
-        ],
-        "filter",
-    )
-    if not direct:
-        ready = [p.reshape(SLAB, nb, LAT)[:, :real] for p in ready]
-    back = swap_all(ready, direct)
+    order = arrival_order(nd)
+    projectors = call(
+        functools.partial(weights_kernel, nd, R),
+        [shape(nd * 256, 256, dtype=BF16), shape(nd * 256, 256, dtype=BF16), shape(nd * SLAB, LAT)],
+        [pos] + [arrived[0][j] for j in order],
+        [pltpu.VMEM((nd, 32, 256), F32)],
+        "weights",
+    )
+    back = []
+    for pieces in arrived:
+        ready = call(
+            functools.partial(filter_kernel, nd, nb, float(total)),
+            [shape(R, LAT)] * nd,
+            [pos, kb_row, lh, ll, fold, *projectors] + [pieces[j] for j in order],
+            [
+                pltpu.VMEM(((nd * SLAB + 2 * HALO) * nb, LAT), F32),
+                pltpu.VMEM(((nd * SLAB + 2 * HALO) * nb, LAT), F32),
+                pltpu.VMEM((nd * nb, 256), F32),
+                pltpu.VMEM((nd * nb, 256), F32),
+            ],
+            "filter",
+        )
+        if not direct:
+            ready = [p.reshape(SLAB, nb, LAT)[:, :real] for p in ready]
+        back.append(swap_all(ready, direct))
     if direct:
         filtered, correlation = finish_direct(back, pos, nb, bands, float(total))
     else:
-        filtered, correlation = finish_plain(jnp.concatenate(back, axis=1), pos_band, band, bands, float(total))
+        filtered, correlation = finish_plain(jnp.concatenate(back[0], axis=1), pos_band, band, bands, float(total))
     return filtered.reshape(trial_waves.shape), correlation
 
 
 def finish_direct(back, pos, nb, bands, total):
-    nd, half = len(back), SLAB // 2
-    z, first, second = call(
-        functools.partial(join_kernel, nd, nb),
-        [shape(SLAB, bands, LAT), shape(half // 2, bands, LAT), shape(half // 2, bands, LAT)],
-        [pos] + back,
-        (),
-        "join",
-    )
-    far_first = xor_permute(first, "band", 2)
-    z_core = xor_permute(z, "band", 1)
-    far_second = xor_permute(second, "band", 2)
+    chunks, nd, half = len(back), len(back[0]), SLAB // 2
+    z, core, far, far_core = [], [], [], []
+    for pieces in back:
+        joined, send = call(
+            functools.partial(join_kernel, nd, nb),
+            [shape(SLAB, nd * nb, LAT), shape(half, nd * nb, LAT)],
+            [pos] + pieces,
+            (),
+            "join",
+            far,
+        )
+        z.append(joined)
+        far.append(xor_permute(send, "band", 2))
+        core.append(xor_permute(joined, "band", 1))
     part = shape(2, bands // 2, bands)
     block = pltpu.VMEM((2, bands, bands), F32)
-    own_keep, own_send = call(own_kernel, [part, part], [pos, z, z_core], [block], "own")
+    own_keep, own_send = call(
+        functools.partial(own_kernel, chunks), [part, part], [pos] + z + core, [block], "own"
+    )
     own_1 = own_keep + xor_permute(own_send, "dom", 1)
-    far_second, own_1 = lax.optimization_barrier((far_second, own_1))
+    far[-1], own_1 = lax.optimization_barrier((far[-1], own_1))
+    far_core = [xor_permute(f, "band", 1) for f in far]
     own_2 = own_1 + xor_permute(own_1, "dom", 2)
     own = own_2 + xor_permute(own_2, "dom", 4)
     keep, send, back_keep, back_send = call(
-        cross_kernel,
+        functools.partial(cross_kernel, chunks),
         [part] * 4,
-        [pos, z, z_core, far_first, far_second, xor_permute(far_first, "band", 1), xor_permute(far_second, "band", 1)],
+        [pos] + z + core + far + far_core,
         [block, block],
         "cross",
         [own_2],
@@ -540,7 +563,7 @@
         (),
         "pair",
     )
-    filtered = call(output_kernel, shape(SLAB, LAT, bands), [z], (), "output")
+    filtered = call(output_kernel, shape(SLAB, LAT, bands), z, (), "output")
     correlation = call(place_kernel, shape(bands, 4 * bands), [pos, rows, xor_permute(rows, "dom", 1)], (), "place")
     return filtered, correlation
 

time: 125 us -> 134 us (1.072)
  starting transfers between devices: 34.5 us -> 57.4 us
  waiting for transfers between devices: 68.7 us -> 48 us
  Pallas kernels: 17.2 us -> 23.8 us
    ppermute x27 -> x42, starting transfers between devices: 34 us -> 54.7 us  [xor_permute(): return lax.ppermute(value, axis, [(k, k ^ step) for k in range(count)])]
    ppermute x27 -> x42, waiting for transfers between devices: 67 us -> 47.3 us  [xor_permute(): return lax.ppermute(value, axis, [(k, k ^ step) for k in range(count)])]
    pallas_call x9 -> x12, Pallas kernels: 17.2 us -> 23.8 us  [call(): pl.pallas_call(kernel, out_shape=out_shape, in_specs=specs, out_specs=pl....]
    ppermute x1, starting transfers between devices: 0.5 us -> 2.62 us  [both_permute(): return lax.ppermute(value, ('band', 'dom'), pairs)]
  transfers between devices with their start and end apart: 28 -> 43, of which waited for: 19 -> 23; matrix products, arithmetic and copies ran while one was open for 0% -> 0% of each run, Pallas kernels for 4% -> 9%
where the time goes in v6:
time: 134 us
  starting transfers between devices  57.4 us (43%)
  waiting for transfers between devices  48 us (36%)
  Pallas kernels  23.8 us (18%)
  local copies, waits for them, and re-layouts  3.41 us (3%)
    ppermute x42, starting transfers between devices, xor_permute(): return lax.ppermute(value, axis, [(k, k ^ step) for k in range(count)])  54.7 us
    ppermute x42, waiting for transfers between devices, xor_permute(): return lax.ppermute(value, axis, [(k, k ^ step) for k in range(count)])  47.3 us
    pallas_call x12, Pallas kernels, call(): pl.pallas_call(kernel, out_shape=out_shape, in_specs=specs, out_specs=pl....  23.8 us
    unnamed x18, local copies, waits for them, and re-layouts  3.41 us
  transfers between devices with their start and end apart: 43, of which 23 were waited for; matrix products, arithmetic and copies ran while one was open for 0% of the time, Pallas kernels for 9%

profile of v6, /device:TPU:0, one launch (start us, length us, event | category | flops | bytes accessed | tf_op | source)
XLA Modules:
  0.0 133.6 jit_solution(2177731672671530768)
XLA Ops:
  4.5 4.1 %collective-permute-start = (f32[96,256]{1,0:T(8,128)S(1)}, f32[96,256]{1,0:T(8,128)S(1)}, u32[]{:S(2)}, u32[]{:S(2)}) collective-permute-start(f32[96,256]{1,0:T(8,128)S(1)} %get-tuple-element.49), channel_id=1, source_target_pairs={{0,4},{1,5},{2,6},{3,7},{4,0},{5,1},{6,2},{7,3},{8,12},{9,13},{10,... | collective-permute-start | bytes 294920 | tf_op jit(solution)/shard_map/ppermute | solution.py:402
  9.9 3.6 %collective-permute-start.2 = (f32[96,256]{1,0:T(8,128)S(1)}, f32[96,256]{1,0:T(8,128)S(1)}, u32[]{:S(2)}, u32[]{:S(2)}) collective-permute-start(f32[96,256]{1,0:T(8,128)S(1)} %get-tuple-element.51), channel_id=1, source_target_pairs={{0,6},{1,7},{2,4},{3,5},{4,2},{5,3},{6,0},{7,1},{8,14},{9,15},{10,... | collective-permute-start | bytes 294920 | tf_op jit(solution)/shard_map/ppermute | solution.py:402
  15.2 5.5 %collective-permute-done.refs_0_ = f32[96,256]{1,0:T(8,128)S(1)} collective-permute-done((f32[96,256]{1,0:T(8,128)S(1)}, f32[96,256]{1,0:T(8,128)S(1)}, u32[]{:S(2)}, u32[]{:S(2)}) %collective-permute-start) | collective-permute-done | bytes 98336 | tf_op jit(solution)/shard_map/ppermute | solution.py:402
  20.7 3.2 %collective-permute-done.1.refs_1_ = f32[96,256]{1,0:T(8,128)S(1)} collective-permute-done((f32[96,256]{1,0:T(8,128)S(1)}, f32[96,256]{1,0:T(8,128)S(1)}, u32[]{:S(2)}, u32[]{:S(2)}) %collective-permute-start.1) | collective-permute-done | bytes 98336 | tf_op jit(solution)/shard_map/ppermute | solution.py:402
  26.0 3.4 %collective-permute-done.6.refs_6_ = f32[96,256]{1,0:T(8,128)S(1)} collective-permute-done((f32[96,256]{1,0:T(8,128)S(1)}, f32[96,256]{1,0:T(8,128)S(1)}, u32[]{:S(2)}, u32[]{:S(2)}) %collective-permute-start.6) | collective-permute-done | bytes 98336 | tf_op jit(solution)/shard_map/ppermute | solution.py:402
  29.4 2.1 %weights.1 = (bf16[2048,256]{1,0:T(8,128)(2,1)S(1)}, bf16[2048,256]{1,0:T(8,128)(2,1)S(1)}, f32[64,256]{1,0:T(8,128)S(1)}) custom-call(s32[3]{0:T(128)S(1)} %pad_add_fusion.pos_ref, f32[96,256]{1,0:T(8,128)S(1)} %collective-permute-done.refs_0_, f32[96,256]{1,0:T(8,128)S(1)} %collective-permute-done.1.refs_1_, f32[96,256]{1,0:T(8,128)S(1)} %collective-permute-done.2.refs_2_, ...), custom_call_target="tpu_custom_call" | custom-call | tf_op jit(solution)/shard_map/weights/pallas_call | solution.py:381
  31.6 6.7 %filter.2 = (f32[64,256]{1,0:T(8,128)S(1)}, f32[64,256]{1,0:T(8,128)S(1)}, f32[64,256]{1,0:T(8,128)S(1)}, f32[64,256]{1,0:T(8,128)S(1)}, f32[64,256]{1,0:T(8,128...) custom-call(s32[3]{0:T(128)S(1)} %pad_add_fusion.pos_ref, ...), custom_call_target="tpu_custom_call" | custom-call | tf_op jit(solution)/shard_map/filter/pallas_call | solution.py:381
  39.2 2.6 %collective-permute-start.9 = (f32[64,256]{1,0:T(8,128)S(1)}, f32[64,256]{1,0:T(8,128)S(1)}, u32[]{:S(2)}, u32[]{:S(2)}) collective-permute-start(f32[64,256]{1,0:T(8,128)S(1)} %get-tuple-element.63), channel_id=1, source_target_pairs={{0,3},{1,2},{2,1},{3,0},{4,7},{5,6},{6,5},{7,4},{8,11},{9,10},{10,... | collective-permute-start | bytes 196616 | tf_op jit(solution)/shard_map/ppermute | solution.py:402
  41.8 2.4 %collective-permute-start.10 = (f32[64,256]{1,0:T(8,128)S(1)}, f32[64,256]{1,0:T(8,128)S(1)}, u32[]{:S(2)}, u32[]{:S(2)}) collective-permute-start(f32[64,256]{1,0:T(8,128)S(1)} %get-tuple-element.64), channel_id=1, source_target_pairs={{0,4},{1,5},{2,6},{3,7},{4,0},{5,1},{6,2},{7,3},{8,12},{9,13},{10,... | collective-permute-start | bytes 196616 | tf_op jit(solution)/shard_map/ppermute | solution.py:402
  44.5 2.8 %collective-permute-start.12 = (f32[64,256]{1,0:T(8,128)S(1)}, f32[64,256]{1,0:T(8,128)S(1)}, u32[]{:S(2)}, u32[]{:S(2)}) collective-permute-start(f32[64,256]{1,0:T(8,128)S(1)} %get-tuple-element.66), channel_id=1, source_target_pairs={{0,6},{1,7},{2,4},{3,5},{4,2},{5,3},{6,0},{7,1},{8,14},{9,15},{10,... | collective-permute-start | bytes 196616 | tf_op jit(solution)/shard_map/ppermute | solution.py:402
  47.3 2.2 %collective-permute-start.13 = (f32[64,256]{1,0:T(8,128)S(1)}, f32[64,256]{1,0:T(8,128)S(1)}, u32[]{:S(2)}, u32[]{:S(2)}) collective-permute-start(f32[64,256]{1,0:T(8,128)S(1)} %get-tuple-element.67), channel_id=1, source_target_pairs={{0,7},{1,6},{2,5},{3,4},{4,3},{5,2},{6,1},{7,0},{8,15},{9,14},{10,... | collective-permute-start | bytes 196616 | tf_op jit(solution)/shard_map/ppermute | solution.py:402
  50.1 2.2 %collective-permute-done.10.refs_4_ = f32[64,256]{1,0:T(8,128)S(1)} collective-permute-done((f32[64,256]{1,0:T(8,128)S(1)}, f32[64,256]{1,0:T(8,128)S(1)}, u32[]{:S(2)}, u32[]{:S(2)}) %collective-permute-start.10) | collective-permute-done | bytes 65568 | tf_op jit(solution)/shard_map/ppermute | solution.py:402
  52.2 4.4 %collective-permute-done.11.refs_5_ = f32[64,256]{1,0:T(8,128)S(1)} collective-permute-done((f32[64,256]{1,0:T(8,128)S(1)}, f32[64,256]{1,0:T(8,128)S(1)}, u32[]{:S(2)}, u32[]{:S(2)}) %collective-permute-start.11) | collective-permute-done | bytes 65568 | tf_op jit(solution)/shard_map/ppermute | solution.py:402
  56.6 1.9 %collective-permute-start.16 = (f32[64,256]{1,0:T(8,128)S(1)}, f32[64,256]{1,0:T(8,128)S(1)}, u32[]{:S(2)}, u32[]{:S(2)}) collective-permute-start(f32[64,256]{1,0:T(8,128)S(1)} %get-tuple-element.71), channel_id=1, source_target_pairs={{0,6},{1,7},{2,4},{3,5},{4,2},{5,3},{6,0},{7,1},{8,14},{9,15},{10,... | collective-permute-start | bytes 196616 | tf_op jit(solution)/shard_map/ppermute | solution.py:402
  60.7 3.0 %collective-permute-start.17 = (f32[64,256]{1,0:T(8,128)S(1)}, f32[64,256]{1,0:T(8,128)S(1)}, u32[]{:S(2)}, u32[]{:S(2)}) collective-permute-start(f32[64,256]{1,0:T(8,128)S(1)} %get-tuple-element.72), channel_id=1, source_target_pairs={{0,7},{1,6},{2,5},{3,4},{4,3},{5,2},{6,1},{7,0},{8,15},{9,14},{10,... | collective-permute-start | bytes 196616 | tf_op jit(solution)/shard_map/ppermute | solution.py:402
  64.4 1.9 %collective-permute-start.19 = (f32[64,256]{1,0:T(8,128)S(1)}, f32[64,256]{1,0:T(8,128)S(1)}, u32[]{:S(2)}, u32[]{:S(2)}) collective-permute-start(f32[64,256]{1,0:T(8,128)S(1)} %get-tuple-element.74), channel_id=1, source_target_pairs={{0,2},{1,3},{2,0},{3,1},{4,6},{5,7},{6,4},{7,5},{8,10},{9,11},{10,... | collective-permute-start | bytes 196616 | tf_op jit(solution)/shard_map/ppermute | solution.py:402
  68.6 2.8 %collective-permute-done.20.refs_6_ = f32[64,256]{1,0:T(8,128)S(1)} collective-permute-done((f32[64,256]{1,0:T(8,128)S(1)}, f32[64,256]{1,0:T(8,128)S(1)}, u32[]{:S(2)}, u32[]{:S(2)}) %collective-permute-start.20) | collective-permute-done | bytes 65568 | tf_op jit(solution)/shard_map/ppermute | solution.py:402
  71.4 6.6 %filter.3 = (f32[64,256]{1,0:T(8,128)S(1)}, f32[64,256]{1,0:T(8,128)S(1)}, f32[64,256]{1,0:T(8,128)S(1)}, f32[64,256]{1,0:T(8,128)S(1)}, f32[64,256]{1,0:T(8,128...) custom-call(s32[3]{0:T(128)S(1)} %pad_add_fusion.pos_ref, ...), custom_call_target="tpu_custom_call" | custom-call | tf_op jit(solution)/shard_map/filter/pallas_call | solution.py:381
  78.0 2.0 %collective-permute-start.21 = (f32[64,256]{1,0:T(8,128)S(1)}, f32[64,256]{1,0:T(8,128)S(1)}, u32[]{:S(2)}, u32[]{:S(2)}) collective-permute-start(f32[64,256]{1,0:T(8,128)S(1)} %get-tuple-element.78), channel_id=1, source_target_pairs={{0,1},{1,0},{2,3},{3,2},{4,5},{5,4},{6,7},{7,6},{8,9},{9,8},{10,11... | collective-permute-start | bytes 196616 | tf_op jit(solution)/shard_map/ppermute | solution.py:402
  81.6 1.9 %collective-permute-start.24 = (f32[64,256]{1,0:T(8,128)S(1)}, f32[64,256]{1,0:T(8,128)S(1)}, u32[]{:S(2)}, u32[]{:S(2)}) collective-permute-start(f32[64,256]{1,0:T(8,128)S(1)} %get-tuple-element.81), channel_id=1, source_target_pairs={{0,4},{1,5},{2,6},{3,7},{4,0},{5,1},{6,2},{7,3},{8,12},{9,13},{10,... | collective-permute-start | bytes 196616 | tf_op jit(solution)/shard_map/ppermute | solution.py:402
  83.5 2.4 %collective-permute-start.25 = (f32[64,256]{1,0:T(8,128)S(1)}, f32[64,256]{1,0:T(8,128)S(1)}, u32[]{:S(2)}, u32[]{:S(2)}) collective-permute-start(f32[64,256]{1,0:T(8,128)S(1)} %get-tuple-element.82), channel_id=1, source_target_pairs={{0,5},{1,4},{2,7},{3,6},{4,1},{5,0},{6,3},{7,2},{8,13},{9,12},{10,... | collective-permute-start | bytes 196616 | tf_op jit(solution)/shard_map/ppermute | solution.py:402
  87.4 2.3 %collective-permute-start.27 = (f32[64,256]{1,0:T(8,128)S(1)}, f32[64,256]{1,0:T(8,128)S(1)}, u32[]{:S(2)}, u32[]{:S(2)}) collective-permute-start(f32[64,256]{1,0:T(8,128)S(1)} %get-tuple-element.84), channel_id=1, source_target_pairs={{0,7},{1,6},{2,5},{3,4},{4,3},{5,2},{6,1},{7,0},{8,15},{9,14},{10,... | collective-permute-start | bytes 196616 | tf_op jit(solution)/shard_map/ppermute | solution.py:402
  89.7 2.4 %collective-permute-done.26.refs_6_ = f32[64,256]{1,0:T(8,128)S(1)} collective-permute-done((f32[64,256]{1,0:T(8,128)S(1)}, f32[64,256]{1,0:T(8,128)S(1)}, u32[]{:S(2)}, u32[]{:S(2)}) %collective-permute-start.26) | collective-permute-done | bytes 65568 | tf_op jit(solution)/shard_map/ppermute | solution.py:402
  92.1 2.2 %collective-permute-done.27.refs_7_ = f32[64,256]{1,0:T(8,128)S(1)} collective-permute-done((f32[64,256]{1,0:T(8,128)S(1)}, f32[64,256]{1,0:T(8,128)S(1)}, u32[]{:S(2)}, u32[]{:S(2)}) %collective-permute-start.27) | collective-permute-done | bytes 65568 | tf_op jit(solution)/shard_map/ppermute | solution.py:402
  99.7 3.1 %collective-permute-done.32 = f32[2,64,128]{2,1,0:T(8,128)S(1)} collective-permute-done((f32[2,64,128]{2,1,0:T(8,128)S(1)}, f32[2,64,128]{2,1,0:T(8,128)S(1)}, u32[]{:S(2)}, u32[]{:S(2)}) %collective-permute-start.32) | collective-permute-done | bytes 65568 | tf_op jit(solution)/shard_map/ppermute | solution.py:402
  103.7 4.5 %collective-permute-done.33 = f32[2,64,128]{2,1,0:T(8,128)S(1)} collective-permute-done((f32[2,64,128]{2,1,0:T(8,128)S(1)}, f32[2,64,128]{2,1,0:T(8,128)S(1)}, u32[]{:S(2)}, u32[]{:S(2)}) %collective-permute-start.33) | collective-permute-done | bytes 65568 | tf_op jit(solution)/shard_map/ppermute | solution.py:402
  112.0 2.6 %collective-permute-start.39 = (f32[2,64,128]{2,1,0:T(8,128)S(1)}, f32[2,64,128]{2,1,0:T(8,128)S(1)}, u32[]{:S(2)}, u32[]{:S(2)}) collective-permute-start(f32[2,64,128]{2,1,0:T(8,128)S(1)} %get-tuple-element.95), channel_id=1, source_target_pairs={{0,17},{1,16},{2,19},{3,18},{4,21},{5,20},{6,23},{7,22},{8,25},{9,... | collective-permute-start | bytes 196616 | tf_op jit(solution)/shard_map/ppermute | solution.py:408
  117.2 1.8 %collective-permute-start.40 = (f32[2,64,128]{2,1,0:T(8,128)S(1)}, f32[2,64,128]{2,1,0:T(8,128)S(1)}, u32[]{:S(2)}, u32[]{:S(2)}) collective-permute-start(f32[2,64,128]{2,1,0:T(8,128)S(1)} %sum.1), channel_id=1, source_target_pairs={{0,2},{1,3},{2,0},{3,1},{4,6},{5,7},{6,4},{7,5},{8,10},{9,11},{10,... | collective-permute-start | bytes 196616 | tf_op jit(solution)/shard_map/ppermute | solution.py:402
  119.0 2.5 %collective-permute-done.40 = f32[2,64,128]{2,1,0:T(8,128)S(1)} collective-permute-done((f32[2,64,128]{2,1,0:T(8,128)S(1)}, f32[2,64,128]{2,1,0:T(8,128)S(1)}, u32[]{:S(2)}, u32[]{:S(2)}) %collective-permute-start.40) | collective-permute-done | bytes 65568 | tf_op jit(solution)/shard_map/ppermute | solution.py:402
  121.6 2.4 %collective-permute-start.41 = (f32[2,64,128]{2,1,0:T(8,128)S(1)}, f32[2,64,128]{2,1,0:T(8,128)S(1)}, u32[]{:S(2)}, u32[]{:S(2)}) collective-permute-start(f32[2,64,128]{2,1,0:T(8,128)S(1)} %add.16.cross), channel_id=1, source_target_pairs={{0,4},{1,5},{2,6},{3,7},{4,0},{5,1},{6,2},{7,3},{8,12},{9,13},{10,... | collective-permute-start | bytes 196616 | tf_op jit(solution)/shard_map/ppermute | solution.py:402
  124.0 2.8 %collective-permute-done.41.cross_other = f32[2,64,128]{2,1,0:T(8,128)S(1)} collective-permute-done((f32[2,64,128]{2,1,0:T(8,128)S(1)}, f32[2,64,128]{2,1,0:T(8,128)S(1)}, u32[]{:S(2)}, u32[]{:S(2)}) %collective-permute-start.41) | collective-permute-done | bytes 65568 | tf_op jit(solution)/shard_map/ppermute | solution.py:402
  127.3 2.0 %collective-permute-start.42 = (f32[4,64,128]{2,1,0:T(8,128)S(1)}, f32[4,64,128]{2,1,0:T(8,128)S(1)}, u32[]{:S(2)}, u32[]{:S(2)}) collective-permute-start(f32[4,64,128]{2,1,0:T(8,128)S(1)} %pair.1.mine), channel_id=1, source_target_pairs={{0,1},{1,0},{2,3},{3,2},{4,5},{5,4},{6,7},{7,6},{8,9},{9,8},{10,11... | collective-permute-start | bytes 393224 | tf_op jit(solution)/shard_map/ppermute | solution.py:402
  (91 shorter events, 36.4 us)
Async XLA Ops:
  4.5 16.2 %collective-permute-start = (f32[96,256]{1,0:T(8,128)S(1)}, f32[96,256]{1,0:T(8,128)S(1)}, u32[]{:S(2)}, u32[]{:S(2)}) collective-permute-start(f32[96,256]{1,0:T(8,128)S(1)} %get-tuple-element.49), channel_id=1, source_target_pairs={{0,4},{1,5},{2,6},{3,7},{4,0},{5,1},{6,2},{7,3},{8,12},{9,13},{10,... | collective-permute-start | bytes 294920 | tf_op jit(solution)/shard_map/ppermute | solution.py:402
  8.6 15.3 %collective-permute-start.1 = (f32[96,256]{1,0:T(8,128)S(1)}, f32[96,256]{1,0:T(8,128)S(1)}, u32[]{:S(2)}, u32[]{:S(2)}) collective-permute-start(f32[96,256]{1,0:T(8,128)S(1)} %get-tuple-element.50), channel_id=1, source_target_pairs={{0,5},{1,4},{2,7},{3,6},{4,1},{5,0},{6,3},{7,2},{8,13},{9,12},{10,... | collective-permute-start | bytes 294920 | tf_op jit(solution)/shard_map/ppermute | solution.py:402
  9.9 14.8 %collective-permute-start.2 = (f32[96,256]{1,0:T(8,128)S(1)}, f32[96,256]{1,0:T(8,128)S(1)}, u32[]{:S(2)}, u32[]{:S(2)}) collective-permute-start(f32[96,256]{1,0:T(8,128)S(1)} %get-tuple-element.51), channel_id=1, source_target_pairs={{0,6},{1,7},{2,4},{3,5},{4,2},{5,3},{6,0},{7,1},{8,14},{9,15},{10,... | collective-permute-start | bytes 294920 | tf_op jit(solution)/shard_map/ppermute | solution.py:402
  13.5 11.2 %collective-permute-start.3 = (f32[96,256]{1,0:T(8,128)S(1)}, f32[96,256]{1,0:T(8,128)S(1)}, u32[]{:S(2)}, u32[]{:S(2)}) collective-permute-start(f32[96,256]{1,0:T(8,128)S(1)} %get-tuple-element.52), channel_id=1, source_target_pairs={{0,7},{1,6},{2,5},{3,4},{4,3},{5,2},{6,1},{7,0},{8,15},{9,14},{10,... | collective-permute-start | bytes 294920 | tf_op jit(solution)/shard_map/ppermute | solution.py:402
  13.5 11.2 %collective-permute-start.4 = (f32[96,256]{1,0:T(8,128)S(1)}, f32[96,256]{1,0:T(8,128)S(1)}, u32[]{:S(2)}, u32[]{:S(2)}) collective-permute-start(f32[96,256]{1,0:T(8,128)S(1)} %get-tuple-element.53), channel_id=1, source_target_pairs={{0,1},{1,0},{2,3},{3,2},{4,5},{5,4},{6,7},{7,6},{8,9},{9,8},{10,11... | collective-permute-start | bytes 294920 | tf_op jit(solution)/shard_map/ppermute | solution.py:402
  20.7 5.3 %collective-permute-start.5 = (f32[96,256]{1,0:T(8,128)S(1)}, f32[96,256]{1,0:T(8,128)S(1)}, u32[]{:S(2)}, u32[]{:S(2)}) collective-permute-start(f32[96,256]{1,0:T(8,128)S(1)} %get-tuple-element.54), channel_id=1, source_target_pairs={{0,2},{1,3},{2,0},{3,1},{4,6},{5,7},{6,4},{7,5},{8,10},{9,11},{10,... | collective-permute-start | bytes 294920 | tf_op jit(solution)/shard_map/ppermute | solution.py:402
  23.9 5.5 %collective-permute-start.6 = (f32[96,256]{1,0:T(8,128)S(1)}, f32[96,256]{1,0:T(8,128)S(1)}, u32[]{:S(2)}, u32[]{:S(2)}) collective-permute-start(f32[96,256]{1,0:T(8,128)S(1)} %get-tuple-element.55), channel_id=1, source_target_pairs={{0,3},{1,2},{2,1},{3,0},{4,7},{5,6},{6,5},{7,4},{8,11},{9,10},{10,... | collective-permute-start | bytes 294920 | tf_op jit(solution)/shard_map/ppermute | solution.py:402
  38.2 6.2 %collective-permute-start.7 = (f32[64,256]{1,0:T(8,128)S(1)}, f32[64,256]{1,0:T(8,128)S(1)}, u32[]{:S(2)}, u32[]{:S(2)}) collective-permute-start(f32[64,256]{1,0:T(8,128)S(1)} %get-tuple-element.61), channel_id=1, source_target_pairs={{0,1},{1,0},{2,3},{3,2},{4,5},{5,4},{6,7},{7,6},{8,9},{9,8},{10,11... | collective-permute-start | bytes 196616 | tf_op jit(solution)/shard_map/ppermute | solution.py:402
  38.6 8.7 %collective-permute-start.8 = (f32[64,256]{1,0:T(8,128)S(1)}, f32[64,256]{1,0:T(8,128)S(1)}, u32[]{:S(2)}, u32[]{:S(2)}) collective-permute-start(f32[64,256]{1,0:T(8,128)S(1)} %get-tuple-element.62), channel_id=1, source_target_pairs={{0,2},{1,3},{2,0},{3,1},{4,6},{5,7},{6,4},{7,5},{8,10},{9,11},{10,... | collective-permute-start | bytes 196616 | tf_op jit(solution)/shard_map/ppermute | solution.py:402
  39.2 10.3 %collective-permute-start.9 = (f32[64,256]{1,0:T(8,128)S(1)}, f32[64,256]{1,0:T(8,128)S(1)}, u32[]{:S(2)}, u32[]{:S(2)}) collective-permute-start(f32[64,256]{1,0:T(8,128)S(1)} %get-tuple-element.63), channel_id=1, source_target_pairs={{0,3},{1,2},{2,1},{3,0},{4,7},{5,6},{6,5},{7,4},{8,11},{9,10},{10,... | collective-permute-start | bytes 196616 | tf_op jit(solution)/shard_map/ppermute | solution.py:402
  41.8 10.4 %collective-permute-start.10 = (f32[64,256]{1,0:T(8,128)S(1)}, f32[64,256]{1,0:T(8,128)S(1)}, u32[]{:S(2)}, u32[]{:S(2)}) collective-permute-start(f32[64,256]{1,0:T(8,128)S(1)} %get-tuple-element.64), channel_id=1, source_target_pairs={{0,4},{1,5},{2,6},{3,7},{4,0},{5,1},{6,2},{7,3},{8,12},{9,13},{10,... | collective-permute-start | bytes 196616 | tf_op jit(solution)/shard_map/ppermute | solution.py:402
  44.2 12.4 %collective-permute-start.11 = (f32[64,256]{1,0:T(8,128)S(1)}, f32[64,256]{1,0:T(8,128)S(1)}, u32[]{:S(2)}, u32[]{:S(2)}) collective-permute-start(f32[64,256]{1,0:T(8,128)S(1)} %get-tuple-element.65), channel_id=1, source_target_pairs={{0,5},{1,4},{2,7},{3,6},{4,1},{5,0},{6,3},{7,2},{8,13},{9,12},{10,... | collective-permute-start | bytes 196616 | tf_op jit(solution)/shard_map/ppermute | solution.py:402
  44.5 14.0 %collective-permute-start.12 = (f32[64,256]{1,0:T(8,128)S(1)}, f32[64,256]{1,0:T(8,128)S(1)}, u32[]{:S(2)}, u32[]{:S(2)}) collective-permute-start(f32[64,256]{1,0:T(8,128)S(1)} %get-tuple-element.66), channel_id=1, source_target_pairs={{0,6},{1,7},{2,4},{3,5},{4,2},{5,3},{6,0},{7,1},{8,14},{9,15},{10,... | collective-permute-start | bytes 196616 | tf_op jit(solution)/shard_map/ppermute | solution.py:402
  47.3 11.2 %collective-permute-start.13 = (f32[64,256]{1,0:T(8,128)S(1)}, f32[64,256]{1,0:T(8,128)S(1)}, u32[]{:S(2)}, u32[]{:S(2)}) collective-permute-start(f32[64,256]{1,0:T(8,128)S(1)} %get-tuple-element.67), channel_id=1, source_target_pairs={{0,7},{1,6},{2,5},{3,4},{4,3},{5,2},{6,1},{7,0},{8,15},{9,14},{10,... | collective-permute-start | bytes 196616 | tf_op jit(solution)/shard_map/ppermute | solution.py:402
  49.5 14.2 %collective-permute-start.14 = (f32[64,256]{1,0:T(8,128)S(1)}, f32[64,256]{1,0:T(8,128)S(1)}, u32[]{:S(2)}, u32[]{:S(2)}) collective-permute-start(f32[64,256]{1,0:T(8,128)S(1)} %get-tuple-element.69), channel_id=1, source_target_pairs={{0,4},{1,5},{2,6},{3,7},{4,0},{5,1},{6,2},{7,3},{8,12},{9,13},{10,... | collective-permute-start | bytes 196616 | tf_op jit(solution)/shard_map/ppermute | solution.py:402
  52.2 12.1 %collective-permute-start.15 = (f32[64,256]{1,0:T(8,128)S(1)}, f32[64,256]{1,0:T(8,128)S(1)}, u32[]{:S(2)}, u32[]{:S(2)}) collective-permute-start(f32[64,256]{1,0:T(8,128)S(1)} %get-tuple-element.70), channel_id=1, source_target_pairs={{0,5},{1,4},{2,7},{3,6},{4,1},{5,0},{6,3},{7,2},{8,13},{9,12},{10,... | collective-permute-start | bytes 196616 | tf_op jit(solution)/shard_map/ppermute | solution.py:402
  56.6 9.6 %collective-permute-start.16 = (f32[64,256]{1,0:T(8,128)S(1)}, f32[64,256]{1,0:T(8,128)S(1)}, u32[]{:S(2)}, u32[]{:S(2)}) collective-permute-start(f32[64,256]{1,0:T(8,128)S(1)} %get-tuple-element.71), channel_id=1, source_target_pairs={{0,6},{1,7},{2,4},{3,5},{4,2},{5,3},{6,0},{7,1},{8,14},{9,15},{10,... | collective-permute-start | bytes 196616 | tf_op jit(solution)/shard_map/ppermute | solution.py:402
  59.1 35.2 %collective-permute-start.28 = (f32[4,64,256]{2,1,0:T(8,128)S(1)}, f32[4,64,256]{2,1,0:T(8,128)S(1)}, u32[]{:S(2)}, u32[]{:S(2)}) collective-permute-start(f32[4,64,256]{2,1,0:T(8,128)S(1)} %get-tuple-element.85), channel_id=1, source_target_pairs={{0,16},{8,24},{16,0},{24,8},{1,17},{9,25},{17,1},{25,9},{2,18},{10... | collective-permute-start | bytes 786440 | tf_op jit(solution)/shard_map/ppermute | solution.py:402
  60.7 7.6 %collective-permute-start.17 = (f32[64,256]{1,0:T(8,128)S(1)}, f32[64,256]{1,0:T(8,128)S(1)}, u32[]{:S(2)}, u32[]{:S(2)}) collective-permute-start(f32[64,256]{1,0:T(8,128)S(1)} %get-tuple-element.72), channel_id=1, source_target_pairs={{0,7},{1,6},{2,5},{3,4},{4,3},{5,2},{6,1},{7,0},{8,15},{9,14},{10,... | collective-permute-start | bytes 196616 | tf_op jit(solution)/shard_map/ppermute | solution.py:402
  78.0 5.5 %collective-permute-start.21 = (f32[64,256]{1,0:T(8,128)S(1)}, f32[64,256]{1,0:T(8,128)S(1)}, u32[]{:S(2)}, u32[]{:S(2)}) collective-permute-start(f32[64,256]{1,0:T(8,128)S(1)} %get-tuple-element.78), channel_id=1, source_target_pairs={{0,1},{1,0},{2,3},{3,2},{4,5},{5,4},{6,7},{7,6},{8,9},{9,8},{10,11... | collective-permute-start | bytes 196616 | tf_op jit(solution)/shard_map/ppermute | solution.py:402
  80.1 5.9 %collective-permute-start.22 = (f32[64,256]{1,0:T(8,128)S(1)}, f32[64,256]{1,0:T(8,128)S(1)}, u32[]{:S(2)}, u32[]{:S(2)}) collective-permute-start(f32[64,256]{1,0:T(8,128)S(1)} %get-tuple-element.79), channel_id=1, source_target_pairs={{0,2},{1,3},{2,0},{3,1},{4,6},{5,7},{6,4},{7,5},{8,10},{9,11},{10,... | collective-permute-start | bytes 196616 | tf_op jit(solution)/shard_map/ppermute | solution.py:402
  80.1 7.2 %collective-permute-start.23 = (f32[64,256]{1,0:T(8,128)S(1)}, f32[64,256]{1,0:T(8,128)S(1)}, u32[]{:S(2)}, u32[]{:S(2)}) collective-permute-start(f32[64,256]{1,0:T(8,128)S(1)} %get-tuple-element.80), channel_id=1, source_target_pairs={{0,3},{1,2},{2,1},{3,0},{4,7},{5,6},{6,5},{7,4},{8,11},{9,10},{10,... | collective-permute-start | bytes 196616 | tf_op jit(solution)/shard_map/ppermute | solution.py:402
  81.6 8.1 %collective-permute-start.24 = (f32[64,256]{1,0:T(8,128)S(1)}, f32[64,256]{1,0:T(8,128)S(1)}, u32[]{:S(2)}, u32[]{:S(2)}) collective-permute-start(f32[64,256]{1,0:T(8,128)S(1)} %get-tuple-element.81), channel_id=1, source_target_pairs={{0,4},{1,5},{2,6},{3,7},{4,0},{5,1},{6,2},{7,3},{8,12},{9,13},{10,... | collective-permute-start | bytes 196616 | tf_op jit(solution)/shard_map/ppermute | solution.py:402
  83.5 6.2 %collective-permute-start.25 = (f32[64,256]{1,0:T(8,128)S(1)}, f32[64,256]{1,0:T(8,128)S(1)}, u32[]{:S(2)}, u32[]{:S(2)}) collective-permute-start(f32[64,256]{1,0:T(8,128)S(1)} %get-tuple-element.82), channel_id=1, source_target_pairs={{0,5},{1,4},{2,7},{3,6},{4,1},{5,0},{6,3},{7,2},{8,13},{9,12},{10,... | collective-permute-start | bytes 196616 | tf_op jit(solution)/shard_map/ppermute | solution.py:402
  85.9 6.2 %collective-permute-start.26 = (f32[64,256]{1,0:T(8,128)S(1)}, f32[64,256]{1,0:T(8,128)S(1)}, u32[]{:S(2)}, u32[]{:S(2)}) collective-permute-start(f32[64,256]{1,0:T(8,128)S(1)} %get-tuple-element.83), channel_id=1, source_target_pairs={{0,6},{1,7},{2,4},{3,5},{4,2},{5,3},{6,0},{7,1},{8,14},{9,15},{10,... | collective-permute-start | bytes 196616 | tf_op jit(solution)/shard_map/ppermute | solution.py:402
  87.4 7.0 %collective-permute-start.27 = (f32[64,256]{1,0:T(8,128)S(1)}, f32[64,256]{1,0:T(8,128)S(1)}, u32[]{:S(2)}, u32[]{:S(2)}) collective-permute-start(f32[64,256]{1,0:T(8,128)S(1)} %get-tuple-element.84), channel_id=1, source_target_pairs={{0,7},{1,6},{2,5},{3,4},{4,3},{5,2},{6,1},{7,0},{8,15},{9,14},{10,... | collective-permute-start | bytes 196616 | tf_op jit(solution)/shard_map/ppermute | solution.py:402
  89.7 5.9 %collective-permute-start.30 = (f32[8,64,256]{2,1,0:T(8,128)S(1)}, f32[8,64,256]{2,1,0:T(8,128)S(1)}, u32[]{:S(2)}, u32[]{:S(2)}) collective-permute-start(f32[8,64,256]{2,1,0:T(8,128)S(1)} %get-tuple-element.68.refs_0_), channel_id=1, source_target_pairs={{0,8},{8,0},{16,24},{24,16},{1,9},{9,1},{17,25},{25,17},{2,10},{10... | collective-permute-start | bytes 1572872 | tf_op jit(solution)/shard_map/ppermute | solution.py:402
  95.0 8.7 %collective-permute-start.29 = (f32[4,64,256]{2,1,0:T(8,128)S(1)}, f32[4,64,256]{2,1,0:T(8,128)S(1)}, u32[]{:S(2)}, u32[]{:S(2)}) collective-permute-start(f32[4,64,256]{2,1,0:T(8,128)S(1)} %get-tuple-element.87), channel_id=1, source_target_pairs={{0,16},{8,24},{16,0},{24,8},{1,17},{9,25},{17,1},{25,9},{2,18},{10... | collective-permute-start | bytes 786440 | tf_op jit(solution)/shard_map/ppermute | solution.py:402
  99.7 9.8 %collective-permute-start.35 = (f32[4,64,256]{2,1,0:T(8,128)S(1)}, f32[4,64,256]{2,1,0:T(8,128)S(1)}, u32[]{:S(2)}, u32[]{:S(2)}) collective-permute-start(f32[4,64,256]{2,1,0:T(8,128)S(1)} %collective-permute-done.28.refs_8_.refs_4_), channel_id=1, source_target_pairs={{0,8},{8,0},{16,24},{24,16},{1,9},{9,1},{17,25},{25,17},{2,10},{10... | collective-permute-start | bytes 786440 | tf_op jit(solution)/shard_map/ppermute | solution.py:402
  103.7 5.8 %collective-permute-start.36 = (f32[4,64,256]{2,1,0:T(8,128)S(1)}, f32[4,64,256]{2,1,0:T(8,128)S(1)}, u32[]{:S(2)}, u32[]{:S(2)}) collective-permute-start(f32[4,64,256]{2,1,0:T(8,128)S(1)} %collective-permute-done.29.refs_5_), channel_id=1, source_target_pairs={{0,8},{8,0},{16,24},{24,16},{1,9},{9,1},{17,25},{25,17},{2,10},{10... | collective-permute-start | bytes 786440 | tf_op jit(solution)/shard_map/ppermute | solution.py:402
  108.3 6.4 %collective-permute-start.34 = (f32[2,64,128]{2,1,0:T(8,128)S(1)}, f32[2,64,128]{2,1,0:T(8,128)S(1)}, u32[]{:S(2)}, u32[]{:S(2)}) collective-permute-start(f32[2,64,128]{2,1,0:T(8,128)S(1)} %add.14.refs_8_), channel_id=1, source_target_pairs={{0,4},{1,5},{2,6},{3,7},{4,0},{5,1},{6,2},{7,3},{8,12},{9,13},{10,... | collective-permute-start | bytes 196616 | tf_op jit(solution)/shard_map/ppermute | solution.py:402
  121.6 5.2 %collective-permute-start.41 = (f32[2,64,128]{2,1,0:T(8,128)S(1)}, f32[2,64,128]{2,1,0:T(8,128)S(1)}, u32[]{:S(2)}, u32[]{:S(2)}) collective-permute-start(f32[2,64,128]{2,1,0:T(8,128)S(1)} %add.16.cross), channel_id=1, source_target_pairs={{0,4},{1,5},{2,6},{3,7},{4,0},{5,1},{6,2},{7,3},{8,12},{9,13},{10,... | collective-permute-start | bytes 196616 | tf_op jit(solution)/shard_map/ppermute | solution.py:402
  (20 other events, 60.5 us)

commit v7 on v5

--- a/solution.py
+++ b/solution.py
@@ -83,9 +83,20 @@
     return hi, lo
 
 
-def split_kernel(nd, nb, pos_ref, cell_ref, x_ref, v_ref, w_ref, code_ref, *refs):
-    outs, (scratch, packed) = refs[:-2], refs[-2:]
-    i = pos_ref[0]
+def split_kernel(nd, nb, cell_hbm, x_hbm, v_hbm, w_hbm, code_hbm, *refs):
+    outs, (cell_ref, x_ref, v_ref, w_ref, code_ref, scratch, packed, sems) = refs[:nd], refs[nd:]
+    copies = [
+        pltpu.make_async_copy(source, target, sems.at[k])
+        for k, (source, target) in enumerate(
+            ((x_hbm, x_ref), (cell_hbm, cell_ref), (v_hbm, v_ref), (w_hbm, w_ref), (code_hbm, code_ref))
+        )
+    ]
+    for copy in copies:
+        copy.start()
+    i = lax.axis_index("dom")
+    for copy in copies[1:]:
+        copy.wait()
+    cell = cell_ref[...].astype(F32)
     cube = 2 * REACH + 1
     code = code_ref[...].astype(F32)
     off_x = jnp.floor((code + 0.5) * (1.0 / (cube * cube)))
@@ -95,7 +106,8 @@
     for a in range(2):
         packed[a * 8 : a * 8 + 8] = w_ref[a]
         cell_x, cell_y, cell_z = (
-            lax.rem(cell_ref[a, k], n).astype(F32) for k, n in enumerate((SLAB, SIDE, SIDE))
+            cell[a : a + 1, k : k + 1] - n * jnp.floor(cell[a : a + 1, k : k + 1] * (1.0 / n))
+            for k, n in enumerate((SLAB, SIDE, SIDE))
         )
         y = off_y[a : a + 1] + (cell_y + float(SIDE - REACH))
         z = off_z[a : a + 1] + (cell_z + float(SIDE - REACH))
@@ -105,6 +117,7 @@
         packed[18 + a : 19 + a] = y * SIDE + z
     packed[20:24] = jnp.zeros((4, LAT), F32)
     packed[24:32] = jnp.concatenate([v_ref[:, y, :] for y in range(SIDE)], axis=1)
+    copies[0].wait()
     for q in range(SLAB):
         scratch[q] = x_ref[q].T
     for j in range(nd):
@@ -155,7 +168,7 @@
 
 def filter_kernel(nd, nb, total, pos_ref, kb_ref, lh_ref, ll_ref, fold_ref, *refs):
     pieces, outs = refs[:nd], refs[nd : 2 * nd]
-    f0_ref, f1_ref, fold_out, spread_out, wh_ref, wl_ref, v_ref, packed = refs[2 * nd :]
+    f0_ref, f1_ref, fold_out, spread_out, wh_ref, wl_ref, v_ref, packed, fh_ref, fl_ref, acc_ref = refs[2 * nd :]
     i = pos_ref[0]
     R = SLAB * nb
     rows_q = lax.broadcasted_iota(jnp.int32, (SLAB, nb, 256), 0)
@@ -184,12 +197,24 @@
 
     def apply(ref, finish):
         def project(s):
+            rows = pl.ds(pl.multiple_of(s * R, R), R)
             fh, fl = halves(ref[slab_rows(s)])
+            fh_ref[rows] = fh
+            fl_ref[rows] = fl
             w = pl.ds(pl.multiple_of(s * 256, 256), 256)
             g = dot3(fh, fl, wh_ref[w], wl_ref[w], NT).reshape(SLAB, nb, 256)
             fold_out[pl.ds(pl.multiple_of(s * nb, nb), nb)] = jnp.sum(jnp.where(same, g, 0.0), axis=0)
 
+        def lateral(s):
+            rows = pl.ds(pl.multiple_of(s * 4 * R, 4 * R), 4 * R)
+            acc_ref[rows] = dot3(fh_ref[rows], fl_ref[rows], lh_ref[...], ll_ref[...])
+
         each(project)
+        if nd <= 8:
+            for s in range(nd // 4):
+                lateral(s)
+        else:
+            lax.fori_loop(0, nd // 4, lambda s, c: (lateral(s), c)[1], 0)
         gh, gl = halves(fold_out[...])
         h = dot(gh, fold_ref[...]) + dot(gl, fold_ref[...])
         below, at, above = h[:, :128], h[:, 128:256], h[:, 256:]
@@ -207,11 +232,10 @@
 
         def step(s):
             f = ref[slab_rows(s)]
-            fh, fl = halves(f)
             x = jnp.where(same, spread_out[pl.ds(pl.multiple_of(s * nb, nb), nb)][None], 0.0).reshape(R, 256)
             xh, xl = halves(x)
             w = pl.ds(pl.multiple_of(s * 256, 256), 256)
-            acc = dot3(xh, xl, wh_ref[w], wl_ref[w]) + dot3(fh, fl, lh_ref[...], ll_ref[...])
+            acc = dot3(xh, xl, wh_ref[w], wl_ref[w]) + acc_ref[pl.ds(pl.multiple_of(s * R, R), R)]
             v = v_ref[pl.ds(pl.multiple_of(s * SLAB, SLAB), SLAB)]
             acc = acc + (f.reshape(SLAB, nb, LAT) * v[:, None, :]).reshape(R, LAT)
             for k in range(1, HALO + 1):
@@ -313,11 +337,11 @@
     out_ref[...] = (a_ref[...] + b_ref[...]) + (c_ref[...] + d_ref[...])
 
 
-def pair_kernel(total, pos_ref, own, cross, cross_other, out_ref):
+def pair_kernel(total, pos_ref, own, cross, near, far, far_near, out_ref):
     y = pos_ref[2]
     for c in range(2):
         out_ref[y * 2 + c] = own[c] * (1.0 / total)
-        out_ref[(1 - y) * 2 + c] = (cross[c] + cross_other[c]) * (1.0 / total)
+        out_ref[(1 - y) * 2 + c] = ((cross[c] + near[c]) + (far[c] + far_near[c])) * (1.0 / total)
 
 
 def output_kernel(z_ref, out_ref):
@@ -447,9 +471,19 @@
         cut = call(
             functools.partial(split_kernel, nd, nb),
             [shape(R + 32, LAT)] * nd,
-            [pos, atom_cell, waves, potential, proj_weights, point_codes],
-            [pltpu.VMEM((SLAB, bands, LAT), F32), pltpu.VMEM((32, 256), F32)],
+            [],
+            [
+                pltpu.VMEM(atom_cell.shape, jnp.int32),
+                pltpu.VMEM(waves.shape, F32),
+                pltpu.VMEM(potential.shape, F32),
+                pltpu.VMEM(proj_weights.shape, F32),
+                pltpu.VMEM(point_codes.shape, jnp.int32),
+                pltpu.VMEM((SLAB, bands, LAT), F32),
+                pltpu.VMEM((32, 256), F32),
+                pltpu.SemaphoreType.DMA((5,)),
+            ],
             "split",
+            [atom_cell, waves, potential, proj_weights, point_codes],
         )
     else:
         packed = packed_atoms(potential, proj_weights, atom_cell, point_codes)
@@ -479,6 +513,9 @@
             pltpu.VMEM((nd * 256, 256), BF16),
             pltpu.VMEM((nd * SLAB, LAT), F32),
             pltpu.VMEM((nd, 32, 256), F32),
+            pltpu.VMEM((nd * R, LAT), BF16),
+            pltpu.VMEM((nd * R, LAT), BF16),
+            pltpu.VMEM((nd * R, LAT), F32),
         ],
         "filter",
     )
@@ -508,8 +545,8 @@
     block = pltpu.VMEM((2, bands, bands), F32)
     own_keep, own_send = call(own_kernel, [part, part], [pos, z, z_core], [block], "own")
     own_1 = own_keep + xor_permute(own_send, "dom", 1)
-    far_second, own_1 = lax.optimization_barrier((far_second, own_1))
     own_2 = own_1 + xor_permute(own_1, "dom", 2)
+    far_second, own_2 = lax.optimization_barrier((far_second, own_2))
     own = own_2 + xor_permute(own_2, "dom", 4)
     keep, send, back_keep, back_send = call(
         cross_kernel,
@@ -532,11 +569,10 @@
         "sum",
         [own],
     )
-    cross = cross + xor_permute(cross, "dom", 2)
     rows = call(
         functools.partial(pair_kernel, total),
         shape(4, bands // 2, bands),
-        [pos, own, cross, xor_permute(cross, "dom", 4)],
+        [pos, own, cross] + [xor_permute(cross, "dom", step) for step in (2, 4, 6)],
         (),
         "pair",
     )

time: 125 us -> 120 us (0.960)
  waiting for transfers between devices: 68.7 us -> 60.6 us
  starting transfers between devices: 34.5 us -> 37.2 us
  local copies, waits for them, and re-layouts: 3.41 us -> 4.8 us
    ppermute x27 -> x28, waiting for transfers between devices: 67 us -> 58.2 us  [xor_permute(): return lax.ppermute(value, axis, [(k, k ^ step) for k in range(count)])]
    ppermute x27 -> x28, starting transfers between devices: 34 us -> 36.5 us  [xor_permute(): return lax.ppermute(value, axis, [(k, k ^ step) for k in range(count)])]
    unnamed x18, local copies, waits for them, and re-layouts: 3.41 us -> 4.79 us
  transfers between devices with their start and end apart: 28 -> 29, of which waited for: 19 -> 20; matrix products, arithmetic and copies ran while one was open for 0% -> 0% of each run, Pallas kernels for 4% -> 4%
where the time goes in v7:
time: 120 us
  waiting for transfers between devices  60.6 us (50%)
  starting transfers between devices  37.2 us (31%)
  Pallas kernels  16.5 us (14%)
  local copies, waits for them, and re-layouts  4.8 us (4%)
    ppermute x28, waiting for transfers between devices, xor_permute(): return lax.ppermute(value, axis, [(k, k ^ step) for k in range(count)])  58.2 us
    ppermute x28, starting transfers between devices, xor_permute(): return lax.ppermute(value, axis, [(k, k ^ step) for k in range(count)])  36.5 us
    pallas_call x9, Pallas kernels, call(): pl.pallas_call(kernel, out_shape=out_shape, in_specs=specs, out_specs=pl....  16.5 us
    unnamed x18, local copies, waits for them, and re-layouts  4.79 us
    ppermute x1, waiting for transfers between devices, both_permute(): return lax.ppermute(value, ('band', 'dom'), pairs)  2.42 us
  transfers between devices with their start and end apart: 29, of which 20 were waited for; matrix products, arithmetic and copies ran while one was open for 0% of the time, Pallas kernels for 4%

profile of v7, /device:TPU:0, one launch (start us, length us, event | category | flops | bytes accessed | tf_op | source)
XLA Modules:
  0.0 120.1 jit_solution(4908406985583316300)
XLA Ops:
  5.5 4.1 %collective-permute-start = (f32[160,256]{1,0:T(8,128)S(1)}, f32[160,256]{1,0:T(8,128)S(1)}, u32[]{:S(2)}, u32[]{:S(2)}) collective-permute-start(f32[160,256]{1,0:T(8,128)S(1)} %get-tuple-element.29), channel_id=1, source_target_pairs={{0,4},{1,5},{2,6},{3,7},{4,0},{5,1},{6,2},{7,3},{8,12},{9,13},{10,... | collective-permute-start | bytes 491528 | tf_op jit(solution)/shard_map/ppermute | solution.py:416
  9.6 1.3 %collective-permute-start.1 = (f32[160,256]{1,0:T(8,128)S(1)}, f32[160,256]{1,0:T(8,128)S(1)}, u32[]{:S(2)}, u32[]{:S(2)}) collective-permute-start(f32[160,256]{1,0:T(8,128)S(1)} %get-tuple-element.30), channel_id=1, source_target_pairs={{0,5},{1,4},{2,7},{3,6},{4,1},{5,0},{6,3},{7,2},{8,13},{9,12},{10,... | collective-permute-start | bytes 491528 | tf_op jit(solution)/shard_map/ppermute | solution.py:416
  10.9 3.6 %collective-permute-start.2 = (f32[160,256]{1,0:T(8,128)S(1)}, f32[160,256]{1,0:T(8,128)S(1)}, u32[]{:S(2)}, u32[]{:S(2)}) collective-permute-start(f32[160,256]{1,0:T(8,128)S(1)} %get-tuple-element.31), channel_id=1, source_target_pairs={{0,6},{1,7},{2,4},{3,5},{4,2},{5,3},{6,0},{7,1},{8,14},{9,15},{10,... | collective-permute-start | bytes 491528 | tf_op jit(solution)/shard_map/ppermute | solution.py:416
  14.5 1.7 %collective-permute-start.4 = (f32[160,256]{1,0:T(8,128)S(1)}, f32[160,256]{1,0:T(8,128)S(1)}, u32[]{:S(2)}, u32[]{:S(2)}) collective-permute-start(f32[160,256]{1,0:T(8,128)S(1)} %get-tuple-element.33), channel_id=1, source_target_pairs={{0,1},{1,0},{2,3},{3,2},{4,5},{5,4},{6,7},{7,6},{8,9},{9,8},{10,11... | collective-permute-start | bytes 491528 | tf_op jit(solution)/shard_map/ppermute | solution.py:416
  16.2 12.5 %collective-permute-done.refs_0_ = f32[160,256]{1,0:T(8,128)S(1)} collective-permute-done((f32[160,256]{1,0:T(8,128)S(1)}, f32[160,256]{1,0:T(8,128)S(1)}, u32[]{:S(2)}, u32[]{:S(2)}) %collective-permute-start) | collective-permute-done | bytes 163872 | tf_op jit(solution)/shard_map/ppermute | solution.py:416
  28.7 4.8 %collective-permute-done.1.refs_1_ = f32[160,256]{1,0:T(8,128)S(1)} collective-permute-done((f32[160,256]{1,0:T(8,128)S(1)}, f32[160,256]{1,0:T(8,128)S(1)}, u32[]{:S(2)}, u32[]{:S(2)}) %collective-permute-start.1) | collective-permute-done | bytes 163872 | tf_op jit(solution)/shard_map/ppermute | solution.py:416
  34.3 1.2 %collective-permute-done.5.refs_5_ = f32[160,256]{1,0:T(8,128)S(1)} collective-permute-done((f32[160,256]{1,0:T(8,128)S(1)}, f32[160,256]{1,0:T(8,128)S(1)}, u32[]{:S(2)}, u32[]{:S(2)}) %collective-permute-start.5) | collective-permute-done | bytes 163872 | tf_op jit(solution)/shard_map/ppermute | solution.py:416
  35.6 4.1 %collective-permute-done.6.refs_6_ = f32[160,256]{1,0:T(8,128)S(1)} collective-permute-done((f32[160,256]{1,0:T(8,128)S(1)}, f32[160,256]{1,0:T(8,128)S(1)}, u32[]{:S(2)}, u32[]{:S(2)}) %collective-permute-start.6) | collective-permute-done | bytes 163872 | tf_op jit(solution)/shard_map/ppermute | solution.py:416
  39.7 8.9 %filter.1 = (f32[128,256]{1,0:T(8,128)S(1)}, f32[128,256]{1,0:T(8,128)S(1)}, f32[128,256]{1,0:T(8,128)S(1)}, f32[128,256]{1,0:T(8,128)S(1)}, f32[128,256]{1,0:T(...) custom-call(s32[3]{0:T(128)S(1)} %pad_add_fusion.pos_ref, ...), custom_call_target="tpu_custom_call" | custom-call | tf_op jit(solution)/shard_map/filter/pallas_call | solution.py:395
  48.6 4.7 %collective-permute-start.10 = (f32[128,256]{1,0:T(8,128)S(1)}, f32[128,256]{1,0:T(8,128)S(1)}, u32[]{:S(2)}, u32[]{:S(2)}) collective-permute-start(f32[128,256]{1,0:T(8,128)S(1)} %get-tuple-element.41), channel_id=1, source_target_pairs={{0,4},{1,5},{2,6},{3,7},{4,0},{5,1},{6,2},{7,3},{8,12},{9,13},{10,... | collective-permute-start | bytes 393224 | tf_op jit(solution)/shard_map/ppermute | solution.py:416
  54.7 3.4 %collective-permute-start.13 = (f32[128,256]{1,0:T(8,128)S(1)}, f32[128,256]{1,0:T(8,128)S(1)}, u32[]{:S(2)}, u32[]{:S(2)}) collective-permute-start(f32[128,256]{1,0:T(8,128)S(1)} %get-tuple-element.44), channel_id=1, source_target_pairs={{0,7},{1,6},{2,5},{3,4},{4,3},{5,2},{6,1},{7,0},{8,15},{9,14},{10,... | collective-permute-start | bytes 393224 | tf_op jit(solution)/shard_map/ppermute | solution.py:416
  58.1 1.5 %collective-permute-start.7 = (f32[128,256]{1,0:T(8,128)S(1)}, f32[128,256]{1,0:T(8,128)S(1)}, u32[]{:S(2)}, u32[]{:S(2)}) collective-permute-start(f32[128,256]{1,0:T(8,128)S(1)} %get-tuple-element.38), channel_id=1, source_target_pairs={{0,1},{1,0},{2,3},{3,2},{4,5},{5,4},{6,7},{7,6},{8,9},{9,8},{10,11... | collective-permute-start | bytes 393224 | tf_op jit(solution)/shard_map/ppermute | solution.py:416
  59.6 8.1 %collective-permute-done.10.refs_4_ = f32[128,256]{1,0:T(8,128)S(1)} collective-permute-done((f32[128,256]{1,0:T(8,128)S(1)}, f32[128,256]{1,0:T(8,128)S(1)}, u32[]{:S(2)}, u32[]{:S(2)}) %collective-permute-start.10) | collective-permute-done | bytes 131104 | tf_op jit(solution)/shard_map/ppermute | solution.py:416
  67.6 3.7 %collective-permute-done.11.refs_5_ = f32[128,256]{1,0:T(8,128)S(1)} collective-permute-done((f32[128,256]{1,0:T(8,128)S(1)}, f32[128,256]{1,0:T(8,128)S(1)}, u32[]{:S(2)}, u32[]{:S(2)}) %collective-permute-start.11) | collective-permute-done | bytes 131104 | tf_op jit(solution)/shard_map/ppermute | solution.py:416
  71.3 1.9 %collective-permute-done.8.refs_2_ = f32[128,256]{1,0:T(8,128)S(1)} collective-permute-done((f32[128,256]{1,0:T(8,128)S(1)}, f32[128,256]{1,0:T(8,128)S(1)}, u32[]{:S(2)}, u32[]{:S(2)}) %collective-permute-start.8) | collective-permute-done | bytes 131104 | tf_op jit(solution)/shard_map/ppermute | solution.py:416
  73.2 4.3 %collective-permute-done.9.refs_3_ = f32[128,256]{1,0:T(8,128)S(1)} collective-permute-done((f32[128,256]{1,0:T(8,128)S(1)}, f32[128,256]{1,0:T(8,128)S(1)}, u32[]{:S(2)}, u32[]{:S(2)}) %collective-permute-start.9) | collective-permute-done | bytes 131104 | tf_op jit(solution)/shard_map/ppermute | solution.py:416
  78.2 1.6 %collective-permute-start.19 = (f32[2,128,256]{2,1,0:T(8,128)S(1)}, f32[2,128,256]{2,1,0:T(8,128)S(1)}, u32[]{:S(2)}, u32[]{:S(2)}) collective-permute-start(f32[2,128,256]{2,1,0:T(8,128)S(1)} %get-tuple-element.50), channel_id=1, source_target_pairs={{0,16},{8,24},{16,0},{24,8},{1,17},{9,25},{17,1},{25,9},{2,18},{10... | collective-permute-start | bytes 786440 | tf_op jit(solution)/shard_map/ppermute | solution.py:416
  80.9 1.5 %own.1 = (f32[2,64,128]{2,1,0:T(8,128)S(1)}, f32[2,64,128]{2,1,0:T(8,128)S(1)}) custom-call(s32[3]{0:T(128)S(1)} %pad_add_fusion.pos_ref, f32[8,128,256]{2,1,0:T(8,128)S(1)} %get-tuple-element.45.z_ref, f32[8,128,256]{2,1,0:T(8,128)S(1)} %collective-permute-done.15.zc_ref), custom_call_target="tpu_custom_call" | custom-call | tf_op jit(solution)/shard_map/own/pallas_call | solution.py:395
  83.1 3.7 %collective-permute-done.16 = f32[2,64,128]{2,1,0:T(8,128)S(1)} collective-permute-done((f32[2,64,128]{2,1,0:T(8,128)S(1)}, f32[2,64,128]{2,1,0:T(8,128)S(1)}, u32[]{:S(2)}, u32[]{:S(2)}) %collective-permute-start.16) | collective-permute-done | bytes 65568 | tf_op jit(solution)/shard_map/ppermute | solution.py:416
  86.8 2.3 %collective-permute-start.17 = (f32[2,64,128]{2,1,0:T(8,128)S(1)}, f32[2,64,128]{2,1,0:T(8,128)S(1)}, u32[]{:S(2)}, u32[]{:S(2)}) collective-permute-start(f32[2,64,128]{2,1,0:T(8,128)S(1)} %add.10), channel_id=1, source_target_pairs={{0,2},{1,3},{2,0},{3,1},{4,6},{5,7},{6,4},{7,5},{8,10},{9,11},{10,... | collective-permute-start | bytes 196616 | tf_op jit(solution)/shard_map/ppermute | solution.py:416
  89.1 2.2 %collective-permute-done.17 = f32[2,64,128]{2,1,0:T(8,128)S(1)} collective-permute-done((f32[2,64,128]{2,1,0:T(8,128)S(1)}, f32[2,64,128]{2,1,0:T(8,128)S(1)}, u32[]{:S(2)}, u32[]{:S(2)}) %collective-permute-start.17) | collective-permute-done | bytes 65568 | tf_op jit(solution)/shard_map/ppermute | solution.py:416
  94.1 1.5 %cross.1 = (f32[2,64,128]{2,1,0:T(8,128)S(1)}, f32[2,64,128]{2,1,0:T(8,128)S(1)}, f32[2,64,128]{2,1,0:T(8,128)S(1)}, f32[2,64,128]{2,1,0:T(8,128)S(1)}) custom-call(s32[3]{0:T(128)S(1)} %pad_add_fusion.pos_ref, f32[8,128,256]{2,1,0:T(8,128)S(1)} %get-tuple-element.45.z_ref, f32[8,128,256]{2,1,0:T(8,128)S(1)} %collective-permute-done.15.zc_ref, ...), custom_call_target="tpu_custom_call" | custom-call | tf_op jit(solution)/shard_map/cross/pallas_call | solution.py:395
  95.6 1.3 %collective-permute-start.22 = (f32[2,64,128]{2,1,0:T(8,128)S(1)}, f32[2,64,128]{2,1,0:T(8,128)S(1)}, u32[]{:S(2)}, u32[]{:S(2)}) collective-permute-start(f32[2,64,128]{2,1,0:T(8,128)S(1)} %get-tuple-element.53), channel_id=1, source_target_pairs={{0,1},{1,0},{2,3},{3,2},{4,5},{5,4},{6,7},{7,6},{8,9},{9,8},{10,11... | collective-permute-start | bytes 196616 | tf_op jit(solution)/shard_map/ppermute | solution.py:416
  96.9 1.5 %collective-permute-start.23 = (f32[2,64,128]{2,1,0:T(8,128)S(1)}, f32[2,64,128]{2,1,0:T(8,128)S(1)}, u32[]{:S(2)}, u32[]{:S(2)}) collective-permute-start(f32[2,64,128]{2,1,0:T(8,128)S(1)} %get-tuple-element.54), channel_id=1, source_target_pairs={{0,16},{8,24},{16,0},{24,8},{1,17},{9,25},{17,1},{25,9},{2,18},{10... | collective-permute-start | bytes 196616 | tf_op jit(solution)/shard_map/ppermute | solution.py:416
  101.2 2.4 %collective-permute-done.24.d_ref = f32[2,64,128]{2,1,0:T(8,128)S(1)} collective-permute-done((f32[2,64,128]{2,1,0:T(8,128)S(1)}, f32[2,64,128]{2,1,0:T(8,128)S(1)}, u32[]{:S(2)}, u32[]{:S(2)}) %collective-permute-start.24) | collective-permute-done | bytes 65568 | tf_op jit(solution)/shard_map/ppermute | solution.py:422
  103.6 2.1 %collective-permute-start.25 = (f32[2,64,128]{2,1,0:T(8,128)S(1)}, f32[2,64,128]{2,1,0:T(8,128)S(1)}, u32[]{:S(2)}, u32[]{:S(2)}) collective-permute-start(f32[2,64,128]{2,1,0:T(8,128)S(1)} %sum.1.cross), channel_id=1, source_target_pairs={{0,2},{1,3},{2,0},{3,1},{4,6},{5,7},{6,4},{7,5},{8,10},{9,11},{10,... | collective-permute-start | bytes 196616 | tf_op jit(solution)/shard_map/ppermute | solution.py:416
  105.7 1.4 %collective-permute-start.26 = (f32[2,64,128]{2,1,0:T(8,128)S(1)}, f32[2,64,128]{2,1,0:T(8,128)S(1)}, u32[]{:S(2)}, u32[]{:S(2)}) collective-permute-start(f32[2,64,128]{2,1,0:T(8,128)S(1)} %sum.1.cross), channel_id=1, source_target_pairs={{0,4},{1,5},{2,6},{3,7},{4,0},{5,1},{6,2},{7,3},{8,12},{9,13},{10,... | collective-permute-start | bytes 196616 | tf_op jit(solution)/shard_map/ppermute | solution.py:416
  108.7 2.9 %collective-permute-done.26.far = f32[2,64,128]{2,1,0:T(8,128)S(1)} collective-permute-done((f32[2,64,128]{2,1,0:T(8,128)S(1)}, f32[2,64,128]{2,1,0:T(8,128)S(1)}, u32[]{:S(2)}, u32[]{:S(2)}) %collective-permute-start.26) | collective-permute-done | bytes 65568 | tf_op jit(solution)/shard_map/ppermute | solution.py:416
  111.6 1.6 %collective-permute-done.27.far_near = f32[2,64,128]{2,1,0:T(8,128)S(1)} collective-permute-done((f32[2,64,128]{2,1,0:T(8,128)S(1)}, f32[2,64,128]{2,1,0:T(8,128)S(1)}, u32[]{:S(2)}, u32[]{:S(2)}) %collective-permute-start.27) | collective-permute-done | bytes 65568 | tf_op jit(solution)/shard_map/ppermute | solution.py:416
  114.9 1.3 %output.1 = f32[8,256,128]{2,1,0:T(8,128)} custom-call(f32[8,128,256]{2,1,0:T(8,128)S(1)} %get-tuple-element.45.z_ref), custom_call_target="tpu_custom_call" | custom-call | tf_op jit(solution)/shard_map/output/pallas_call | solution.py:395
  116.2 2.6 %collective-permute-done.28.other = f32[4,64,128]{2,1,0:T(8,128)S(1)} collective-permute-done((f32[4,64,128]{2,1,0:T(8,128)S(1)}, f32[4,64,128]{2,1,0:T(8,128)S(1)}, u32[]{:S(2)}, u32[]{:S(2)}) %collective-permute-start.28) | collective-permute-done | bytes 131104 | tf_op jit(solution)/shard_map/ppermute | solution.py:416
  118.8 1.3 %place.1 = f32[128,512]{1,0:T(8,128)} custom-call(s32[3]{0:T(128)S(1)} %pad_add_fusion.pos_ref, f32[4,64,128]{2,1,0:T(8,128)S(1)} %pair.1.mine, f32[4,64,128]{2,1,0:T(8,128)S(1)} %collective-permute-done.28.other), custom_call_target="tpu_custom_call" | custom-call | tf_op jit(solution)/shard_map/place/pallas_call | solution.py:395
  (59 shorter events, 18.4 us)
Async XLA Ops:
  4.8 34.9 %copy-start.1 = (bf16[256,384]{1,0:T(8,128)(2,1)S(1)}, bf16[256,384]{1,0:T(8,128)(2,1)}, u32[]{:S(2)}) copy-start(bf16[256,384]{1,0:T(8,128)(2,1)} %constant.37.fold_ref) | copy-start | bytes 589828
  4.8 34.9 %copy-start.2 = (bf16[256,256]{1,0:T(8,128)(2,1)S(1)}, bf16[256,256]{1,0:T(8,128)(2,1)}, u32[]{:S(2)}) copy-start(bf16[256,256]{1,0:T(8,128)(2,1)} %constant.33.lh_ref) | copy-start | bytes 393220
  4.8 34.9 %copy-start.3 = (bf16[256,256]{1,0:T(8,128)(2,1)S(1)}, bf16[256,256]{1,0:T(8,128)(2,1)}, u32[]{:S(2)}) copy-start(bf16[256,256]{1,0:T(8,128)(2,1)} %constant.36.ll_ref) | copy-start | bytes 393220
  5.5 23.2 %collective-permute-start = (f32[160,256]{1,0:T(8,128)S(1)}, f32[160,256]{1,0:T(8,128)S(1)}, u32[]{:S(2)}, u32[]{:S(2)}) collective-permute-start(f32[160,256]{1,0:T(8,128)S(1)} %get-tuple-element.29), channel_id=1, source_target_pairs={{0,4},{1,5},{2,6},{3,7},{4,0},{5,1},{6,2},{7,3},{8,12},{9,13},{10,... | collective-permute-start | bytes 491528 | tf_op jit(solution)/shard_map/ppermute | solution.py:416
  9.6 23.9 %collective-permute-start.1 = (f32[160,256]{1,0:T(8,128)S(1)}, f32[160,256]{1,0:T(8,128)S(1)}, u32[]{:S(2)}, u32[]{:S(2)}) collective-permute-start(f32[160,256]{1,0:T(8,128)S(1)} %get-tuple-element.30), channel_id=1, source_target_pairs={{0,5},{1,4},{2,7},{3,6},{4,1},{5,0},{6,3},{7,2},{8,13},{9,12},{10,... | collective-permute-start | bytes 491528 | tf_op jit(solution)/shard_map/ppermute | solution.py:416
  10.9 23.4 %collective-permute-start.2 = (f32[160,256]{1,0:T(8,128)S(1)}, f32[160,256]{1,0:T(8,128)S(1)}, u32[]{:S(2)}, u32[]{:S(2)}) collective-permute-start(f32[160,256]{1,0:T(8,128)S(1)} %get-tuple-element.31), channel_id=1, source_target_pairs={{0,6},{1,7},{2,4},{3,5},{4,2},{5,3},{6,0},{7,1},{8,14},{9,15},{10,... | collective-permute-start | bytes 491528 | tf_op jit(solution)/shard_map/ppermute | solution.py:416
  14.5 19.8 %collective-permute-start.3 = (f32[160,256]{1,0:T(8,128)S(1)}, f32[160,256]{1,0:T(8,128)S(1)}, u32[]{:S(2)}, u32[]{:S(2)}) collective-permute-start(f32[160,256]{1,0:T(8,128)S(1)} %get-tuple-element.32), channel_id=1, source_target_pairs={{0,7},{1,6},{2,5},{3,4},{4,3},{5,2},{6,1},{7,0},{8,15},{9,14},{10,... | collective-permute-start | bytes 491528 | tf_op jit(solution)/shard_map/ppermute | solution.py:416
  14.5 19.8 %collective-permute-start.4 = (f32[160,256]{1,0:T(8,128)S(1)}, f32[160,256]{1,0:T(8,128)S(1)}, u32[]{:S(2)}, u32[]{:S(2)}) collective-permute-start(f32[160,256]{1,0:T(8,128)S(1)} %get-tuple-element.33), channel_id=1, source_target_pairs={{0,1},{1,0},{2,3},{3,2},{4,5},{5,4},{6,7},{7,6},{8,9},{9,8},{10,11... | collective-permute-start | bytes 491528 | tf_op jit(solution)/shard_map/ppermute | solution.py:416
  28.7 6.9 %collective-permute-start.5 = (f32[160,256]{1,0:T(8,128)S(1)}, f32[160,256]{1,0:T(8,128)S(1)}, u32[]{:S(2)}, u32[]{:S(2)}) collective-permute-start(f32[160,256]{1,0:T(8,128)S(1)} %get-tuple-element.34), channel_id=1, source_target_pairs={{0,2},{1,3},{2,0},{3,1},{4,6},{5,7},{6,4},{7,5},{8,10},{9,11},{10,... | collective-permute-start | bytes 491528 | tf_op jit(solution)/shard_map/ppermute | solution.py:416
  33.5 6.2 %collective-permute-start.6 = (f32[160,256]{1,0:T(8,128)S(1)}, f32[160,256]{1,0:T(8,128)S(1)}, u32[]{:S(2)}, u32[]{:S(2)}) collective-permute-start(f32[160,256]{1,0:T(8,128)S(1)} %get-tuple-element.35), channel_id=1, source_target_pairs={{0,3},{1,2},{2,1},{3,0},{4,7},{5,6},{6,5},{7,4},{8,11},{9,10},{10,... | collective-permute-start | bytes 491528 | tf_op jit(solution)/shard_map/ppermute | solution.py:416
  48.6 19.0 %collective-permute-start.10 = (f32[128,256]{1,0:T(8,128)S(1)}, f32[128,256]{1,0:T(8,128)S(1)}, u32[]{:S(2)}, u32[]{:S(2)}) collective-permute-start(f32[128,256]{1,0:T(8,128)S(1)} %get-tuple-element.41), channel_id=1, source_target_pairs={{0,4},{1,5},{2,6},{3,7},{4,0},{5,1},{6,2},{7,3},{8,12},{9,13},{10,... | collective-permute-start | bytes 393224 | tf_op jit(solution)/shard_map/ppermute | solution.py:416
  53.3 18.0 %collective-permute-start.11 = (f32[128,256]{1,0:T(8,128)S(1)}, f32[128,256]{1,0:T(8,128)S(1)}, u32[]{:S(2)}, u32[]{:S(2)}) collective-permute-start(f32[128,256]{1,0:T(8,128)S(1)} %get-tuple-element.42), channel_id=1, source_target_pairs={{0,5},{1,4},{2,7},{3,6},{4,1},{5,0},{6,3},{7,2},{8,13},{9,12},{10,... | collective-permute-start | bytes 393224 | tf_op jit(solution)/shard_map/ppermute | solution.py:416
  54.3 17.0 %collective-permute-start.12 = (f32[128,256]{1,0:T(8,128)S(1)}, f32[128,256]{1,0:T(8,128)S(1)}, u32[]{:S(2)}, u32[]{:S(2)}) collective-permute-start(f32[128,256]{1,0:T(8,128)S(1)} %get-tuple-element.43), channel_id=1, source_target_pairs={{0,6},{1,7},{2,4},{3,5},{4,2},{5,3},{6,0},{7,1},{8,14},{9,15},{10,... | collective-permute-start | bytes 393224 | tf_op jit(solution)/shard_map/ppermute | solution.py:416
  54.7 16.5 %collective-permute-start.13 = (f32[128,256]{1,0:T(8,128)S(1)}, f32[128,256]{1,0:T(8,128)S(1)}, u32[]{:S(2)}, u32[]{:S(2)}) collective-permute-start(f32[128,256]{1,0:T(8,128)S(1)} %get-tuple-element.44), channel_id=1, source_target_pairs={{0,7},{1,6},{2,5},{3,4},{4,3},{5,2},{6,1},{7,0},{8,15},{9,14},{10,... | collective-permute-start | bytes 393224 | tf_op jit(solution)/shard_map/ppermute | solution.py:416
  58.1 13.2 %collective-permute-start.7 = (f32[128,256]{1,0:T(8,128)S(1)}, f32[128,256]{1,0:T(8,128)S(1)}, u32[]{:S(2)}, u32[]{:S(2)}) collective-permute-start(f32[128,256]{1,0:T(8,128)S(1)} %get-tuple-element.38), channel_id=1, source_target_pairs={{0,1},{1,0},{2,3},{3,2},{4,5},{5,4},{6,7},{7,6},{8,9},{9,8},{10,11... | collective-permute-start | bytes 393224 | tf_op jit(solution)/shard_map/ppermute | solution.py:416
  67.6 5.6 %collective-permute-start.8 = (f32[128,256]{1,0:T(8,128)S(1)}, f32[128,256]{1,0:T(8,128)S(1)}, u32[]{:S(2)}, u32[]{:S(2)}) collective-permute-start(f32[128,256]{1,0:T(8,128)S(1)} %get-tuple-element.39), channel_id=1, source_target_pairs={{0,2},{1,3},{2,0},{3,1},{4,6},{5,7},{6,4},{7,5},{8,10},{9,11},{10,... | collective-permute-start | bytes 393224 | tf_op jit(solution)/shard_map/ppermute | solution.py:416
  71.3 6.2 %collective-permute-start.9 = (f32[128,256]{1,0:T(8,128)S(1)}, f32[128,256]{1,0:T(8,128)S(1)}, u32[]{:S(2)}, u32[]{:S(2)}) collective-permute-start(f32[128,256]{1,0:T(8,128)S(1)} %get-tuple-element.40), channel_id=1, source_target_pairs={{0,3},{1,2},{2,1},{3,0},{4,7},{5,6},{6,5},{7,4},{8,11},{9,10},{10,... | collective-permute-start | bytes 393224 | tf_op jit(solution)/shard_map/ppermute | solution.py:416
  78.2 2.7 %collective-permute-start.15 = (f32[8,128,256]{2,1,0:T(8,128)S(1)}, f32[8,128,256]{2,1,0:T(8,128)S(1)}, u32[]{:S(2)}, u32[]{:S(2)}) collective-permute-start(f32[8,128,256]{2,1,0:T(8,128)S(1)} %get-tuple-element.45.z_ref), channel_id=1, source_target_pairs={{0,8},{8,0},{16,24},{24,16},{1,9},{9,1},{17,25},{25,17},{2,10},{10... | collective-permute-start | bytes 3145736 | tf_op jit(solution)/shard_map/ppermute | solution.py:416
  78.2 10.9 %collective-permute-start.19 = (f32[2,128,256]{2,1,0:T(8,128)S(1)}, f32[2,128,256]{2,1,0:T(8,128)S(1)}, u32[]{:S(2)}, u32[]{:S(2)}) collective-permute-start(f32[2,128,256]{2,1,0:T(8,128)S(1)} %get-tuple-element.50), channel_id=1, source_target_pairs={{0,16},{8,24},{16,0},{24,8},{1,17},{9,25},{17,1},{25,9},{2,18},{10... | collective-permute-start | bytes 786440 | tf_op jit(solution)/shard_map/ppermute | solution.py:416
  79.8 12.8 %collective-permute-start.14 = (f32[2,128,256]{2,1,0:T(8,128)S(1)}, f32[2,128,256]{2,1,0:T(8,128)S(1)}, u32[]{:S(2)}, u32[]{:S(2)}) collective-permute-start(f32[2,128,256]{2,1,0:T(8,128)S(1)} %get-tuple-element.46), channel_id=1, source_target_pairs={{0,16},{8,24},{16,0},{24,8},{1,17},{9,25},{17,1},{25,9},{2,18},{10... | collective-permute-start | bytes 786440 | tf_op jit(solution)/shard_map/ppermute | solution.py:416
  82.4 4.3 %collective-permute-start.16 = (f32[2,64,128]{2,1,0:T(8,128)S(1)}, f32[2,64,128]{2,1,0:T(8,128)S(1)}, u32[]{:S(2)}, u32[]{:S(2)}) collective-permute-start(f32[2,64,128]{2,1,0:T(8,128)S(1)} %get-tuple-element.48), channel_id=1, source_target_pairs={{0,1},{1,0},{2,3},{3,2},{4,5},{5,4},{6,7},{7,6},{8,9},{9,8},{10,11... | collective-permute-start | bytes 196616 | tf_op jit(solution)/shard_map/ppermute | solution.py:416
  86.8 4.6 %collective-permute-start.17 = (f32[2,64,128]{2,1,0:T(8,128)S(1)}, f32[2,64,128]{2,1,0:T(8,128)S(1)}, u32[]{:S(2)}, u32[]{:S(2)}) collective-permute-start(f32[2,64,128]{2,1,0:T(8,128)S(1)} %add.10), channel_id=1, source_target_pairs={{0,2},{1,3},{2,0},{3,1},{4,6},{5,7},{6,4},{7,5},{8,10},{9,11},{10,... | collective-permute-start | bytes 196616 | tf_op jit(solution)/shard_map/ppermute | solution.py:416
  89.1 4.7 %collective-permute-start.20 = (f32[2,128,256]{2,1,0:T(8,128)S(1)}, f32[2,128,256]{2,1,0:T(8,128)S(1)}, u32[]{:S(2)}, u32[]{:S(2)}) collective-permute-start(f32[2,128,256]{2,1,0:T(8,128)S(1)} %collective-permute-done.19.first), channel_id=1, source_target_pairs={{0,8},{8,0},{16,24},{24,16},{1,9},{9,1},{17,25},{25,17},{2,10},{10... | collective-permute-start | bytes 786440 | tf_op jit(solution)/shard_map/ppermute | solution.py:416
  92.6 1.5 %collective-permute-start.21 = (f32[2,128,256]{2,1,0:T(8,128)S(1)}, f32[2,128,256]{2,1,0:T(8,128)S(1)}, u32[]{:S(2)}, u32[]{:S(2)}) collective-permute-start(f32[2,128,256]{2,1,0:T(8,128)S(1)} %collective-permute-done.14.second), channel_id=1, source_target_pairs={{0,8},{8,0},{16,24},{24,16},{1,9},{9,1},{17,25},{25,17},{2,10},{10... | collective-permute-start | bytes 786440 | tf_op jit(solution)/shard_map/ppermute | solution.py:416
  92.6 6.6 %collective-permute-start.18 = (f32[2,64,128]{2,1,0:T(8,128)S(1)}, f32[2,64,128]{2,1,0:T(8,128)S(1)}, u32[]{:S(2)}, u32[]{:S(2)}) collective-permute-start(f32[2,64,128]{2,1,0:T(8,128)S(1)} %add.11.tie), channel_id=1, source_target_pairs={{0,4},{1,5},{2,6},{3,7},{4,0},{5,1},{6,2},{7,3},{8,12},{9,13},{10,... | collective-permute-start | bytes 196616 | tf_op jit(solution)/shard_map/ppermute | solution.py:416
  95.6 4.3 %collective-permute-start.22 = (f32[2,64,128]{2,1,0:T(8,128)S(1)}, f32[2,64,128]{2,1,0:T(8,128)S(1)}, u32[]{:S(2)}, u32[]{:S(2)}) collective-permute-start(f32[2,64,128]{2,1,0:T(8,128)S(1)} %get-tuple-element.53), channel_id=1, source_target_pairs={{0,1},{1,0},{2,3},{3,2},{4,5},{5,4},{6,7},{7,6},{8,9},{9,8},{10,11... | collective-permute-start | bytes 196616 | tf_op jit(solution)/shard_map/ppermute | solution.py:416
  96.9 4.3 %collective-permute-start.23 = (f32[2,64,128]{2,1,0:T(8,128)S(1)}, f32[2,64,128]{2,1,0:T(8,128)S(1)}, u32[]{:S(2)}, u32[]{:S(2)}) collective-permute-start(f32[2,64,128]{2,1,0:T(8,128)S(1)} %get-tuple-element.54), channel_id=1, source_target_pairs={{0,16},{8,24},{16,0},{24,8},{1,17},{9,25},{17,1},{25,9},{2,18},{10... | collective-permute-start | bytes 196616 | tf_op jit(solution)/shard_map/ppermute | solution.py:416
  98.4 5.2 %collective-permute-start.24 = (f32[2,64,128]{2,1,0:T(8,128)S(1)}, f32[2,64,128]{2,1,0:T(8,128)S(1)}, u32[]{:S(2)}, u32[]{:S(2)}) collective-permute-start(f32[2,64,128]{2,1,0:T(8,128)S(1)} %get-tuple-element.55), channel_id=1, source_target_pairs={{0,17},{1,16},{2,19},{3,18},{4,21},{5,20},{6,23},{7,22},{8,25},{9,... | collective-permute-start | bytes 196616 | tf_op jit(solution)/shard_map/ppermute | solution.py:422
  103.6 5.1 %collective-permute-start.25 = (f32[2,64,128]{2,1,0:T(8,128)S(1)}, f32[2,64,128]{2,1,0:T(8,128)S(1)}, u32[]{:S(2)}, u32[]{:S(2)}) collective-permute-start(f32[2,64,128]{2,1,0:T(8,128)S(1)} %sum.1.cross), channel_id=1, source_target_pairs={{0,2},{1,3},{2,0},{3,1},{4,6},{5,7},{6,4},{7,5},{8,10},{9,11},{10,... | collective-permute-start | bytes 196616 | tf_op jit(solution)/shard_map/ppermute | solution.py:416
  105.7 5.9 %collective-permute-start.26 = (f32[2,64,128]{2,1,0:T(8,128)S(1)}, f32[2,64,128]{2,1,0:T(8,128)S(1)}, u32[]{:S(2)}, u32[]{:S(2)}) collective-permute-start(f32[2,64,128]{2,1,0:T(8,128)S(1)} %sum.1.cross), channel_id=1, source_target_pairs={{0,4},{1,5},{2,6},{3,7},{4,0},{5,1},{6,2},{7,3},{8,12},{9,13},{10,... | collective-permute-start | bytes 196616 | tf_op jit(solution)/shard_map/ppermute | solution.py:416
  107.1 6.1 %collective-permute-start.27 = (f32[2,64,128]{2,1,0:T(8,128)S(1)}, f32[2,64,128]{2,1,0:T(8,128)S(1)}, u32[]{:S(2)}, u32[]{:S(2)}) collective-permute-start(f32[2,64,128]{2,1,0:T(8,128)S(1)} %sum.1.cross), channel_id=1, source_target_pairs={{0,6},{1,7},{2,4},{3,5},{4,2},{5,3},{6,0},{7,1},{8,14},{9,15},{10,... | collective-permute-start | bytes 196616 | tf_op jit(solution)/shard_map/ppermute | solution.py:416
  113.8 5.0 %collective-permute-start.28 = (f32[4,64,128]{2,1,0:T(8,128)S(1)}, f32[4,64,128]{2,1,0:T(8,128)S(1)}, u32[]{:S(2)}, u32[]{:S(2)}) collective-permute-start(f32[4,64,128]{2,1,0:T(8,128)S(1)} %pair.1.mine), channel_id=1, source_target_pairs={{0,1},{1,0},{2,3},{3,2},{4,5},{5,4},{6,7},{7,6},{8,9},{9,8},{10,11... | collective-permute-start | bytes 393224 | tf_op jit(solution)/shard_map/ppermute | solution.py:416
  (6 other events, 4.8 us)

commit v8 on v7

--- a/solution.py
+++ b/solution.py
@@ -167,8 +167,8 @@
 
 
 def filter_kernel(nd, nb, total, pos_ref, kb_ref, lh_ref, ll_ref, fold_ref, *refs):
-    pieces, outs = refs[:nd], refs[nd : 2 * nd]
-    f0_ref, f1_ref, fold_out, spread_out, wh_ref, wl_ref, v_ref, packed, fh_ref, fl_ref, acc_ref = refs[2 * nd :]
+    pieces, outs = refs[:nd], refs[nd : 3 * nd]
+    f0_ref, f1_ref, fold_out, spread_out, wh_ref, wl_ref, v_ref, packed, fh_ref, fl_ref, acc_ref = refs[3 * nd :]
     i = pos_ref[0]
     R = SLAB * nb
     rows_q = lax.broadcasted_iota(jnp.int32, (SLAB, nb, 256), 0)
@@ -271,90 +271,81 @@
 
         square = lax.fori_loop(0, nd, add, square)
     scale = 1.0 / jnp.sqrt(jnp.sum(square, axis=1, keepdims=True) / total + EPSILON)
+    chip, half = pos_ref[2], SLAB // 2
     for j in range(nd):
-        y = f0_ref[slab_rows(i ^ j)].reshape(SLAB, nb, LAT)
-        outs[j][...] = (y * scale[None]).reshape(R, LAT)
+        for h, out in ((1 - chip, outs[j]), (chip, outs[nd + j])):
+            start = ((i ^ j) * SLAB + HALO + h * half) * nb
+            y = f0_ref[pl.ds(pl.multiple_of(start, nb), half * nb)].reshape(half, nb, LAT)
+            out[...] = (y * scale[None]).reshape(half * nb, LAT)
 
 
 def join_kernel(nd, nb, pos_ref, *refs):
-    pieces, (z_ref, first_ref, second_ref) = refs[:nd], refs[nd:]
-    i, y = pos_ref[0], pos_ref[2]
+    pieces, z_ref = refs[:nd], refs[-1]
+    i = pos_ref[0]
     for j in range(nd):
         rows = pl.ds(pl.multiple_of((i ^ j) * nb, nb), nb)
-        for q in range(SLAB):
+        for q in range(SLAB // 2):
             z_ref[q, rows] = pieces[j][q * nb : (q + 1) * nb]
-    half = SLAB // 2
-    for q in range(half // 2):
-        first_ref[q] = z_ref[(1 - y) * half + q]
-        second_ref[q] = z_ref[(1 - y) * half + half // 2 + q]
-
-
-def own_kernel(pos_ref, z_ref, zc_ref, keep_ref, send_ref, g_ref):
-    i, b = pos_ref[0], pos_ref[1]
-    own = core = None
-    for q in range(SLAB):
-        zh, zl = halves(z_ref[q])
-        ch, cl = halves(zc_ref[q])
-        mine, other = dot3(zh, zl, zh, zl, NT), dot3(zh, zl, ch, cl, NT)
-        own, core = (mine, other) if own is None else (own + mine, core + other)
-    g_ref[b & 1] = own
-    g_ref[(b & 1) ^ 1] = core
-    cut_rows(i, g_ref, keep_ref, send_ref)
-
-
-def cut_rows(i, g_ref, keep_ref, send_ref):
-    x = i & 1
-    for c in range(2):
-        keep_ref[c] = g_ref[c, pl.ds(pl.multiple_of(x * 64, 64), 64)]
-        send_ref[c] = g_ref[c, pl.ds(pl.multiple_of((1 - x) * 64, 64), 64)]
-
-
-def cross_kernel(
-    pos_ref, z_ref, zc_ref, first, second, core_first, core_second, tie, keep, send, back, back_send, g_ref, back_ref
-):
-    i, b, y = pos_ref[0], pos_ref[1], pos_ref[2]
-    half = SLAB // 2
+
+
+def blocks_kernel(pos_ref, za, zb, ca, cb, far, far_core, keep, send, back, back_send, g_ref, back_ref):
+    i, c = pos_ref[0], pos_ref[1] & 1
     totals = None
-    for q in range(half):
-        zh, zl = halves(z_ref[y * half + q])
-        ch, cl = halves(zc_ref[y * half + q])
-        fh, fl = halves((first, second)[q // (half // 2)][q % (half // 2)])
-        gh, gl = halves((core_first, core_second)[q // (half // 2)][q % (half // 2)])
+    for q in range(SLAB // 2):
+        zh, zl = halves(zb[q])
+        ch, cl = halves(cb[q])
+        fh, fl = halves(far[q])
+        gh, gl = halves(far_core[q])
+        wh, wl = halves(za[q])
+        xh, xl = halves(ca[q])
         now = (
+            dot3(zh, zl, zh, zl, NT) + dot3(wh, wl, wh, wl, NT),
+            dot3(zh, zl, ch, cl, NT) + dot3(wh, wl, xh, xl, NT),
             dot3(zh, zl, fh, fl, NT),
             dot3(zh, zl, gh, gl, NT),
             dot3(fh, fl, zh, zl, NT),
             dot3(fh, fl, ch, cl, NT),
         )
         totals = now if totals is None else tuple(t + n for t, n in zip(totals, now))
-    c = b & 1
-    g_ref[c], g_ref[c ^ 1], back_ref[c], back_ref[c ^ 1] = totals
-    cut_rows(i, g_ref, keep, send)
-    cut_rows(i, back_ref, back, back_send)
-
-
-def sum_kernel(a_ref, b_ref, c_ref, d_ref, tie, out_ref):
-    out_ref[...] = (a_ref[...] + b_ref[...]) + (c_ref[...] + d_ref[...])
-
-
-def pair_kernel(total, pos_ref, own, cross, near, far, far_near, out_ref):
+    g_ref[c], g_ref[c ^ 1], g_ref[2 + c], g_ref[2 + (c ^ 1)], back_ref[c], back_ref[c ^ 1] = totals
+    cut_rows(i & 1, g_ref, keep, send)
+    cut_rows(i & 1, back_ref, back, back_send)
+
+
+def cut_rows(bit, g_ref, keep_ref, send_ref):
+    size = keep_ref.shape[1]
+    keep_ref[...] = g_ref[:, pl.ds(pl.multiple_of(bit * size, size), size)]
+    send_ref[...] = g_ref[:, pl.ds(pl.multiple_of((1 - bit) * size, size), size)]
+
+
+def sum_kernel(pos_ref, keep, other, back, back_other, keep_ref, send_ref, sum_ref):
+    sum_ref[0:2] = keep[0:2] + other[0:2]
+    sum_ref[2:4] = (keep[2:4] + other[2:4]) + (back[...] + back_other[...])
+    cut_rows((pos_ref[0] >> 1) & 1, sum_ref, keep_ref, send_ref)
+
+
+def pair_kernel(total, pos_ref, mine, other, out_ref):
     y = pos_ref[2]
     for c in range(2):
-        out_ref[y * 2 + c] = own[c] * (1.0 / total)
-        out_ref[(1 - y) * 2 + c] = ((cross[c] + near[c]) + (far[c] + far_near[c])) * (1.0 / total)
-
-
-def output_kernel(z_ref, out_ref):
-    for q in range(SLAB):
-        out_ref[q] = z_ref[q].T
-
-
-def place_kernel(pos_ref, mine, other, out_ref):
-    x = pos_ref[0] & 1
-    for k in range(4):
-        lanes = slice(k * 128, (k + 1) * 128)
-        out_ref[pl.ds(pl.multiple_of(x * 64, 64), 64), lanes] = mine[k]
-        out_ref[pl.ds(pl.multiple_of((1 - x) * 64, 64), 64), lanes] = other[k]
+        out_ref[y * 2 + c] = (mine[c] + other[c]) * (1.0 / total)
+        out_ref[(1 - y) * 2 + c] = (mine[2 + c] + other[2 + c]) * (1.0 / total)
+
+
+def output_kernel(pos_ref, za, zb, out_ref):
+    y, half = pos_ref[2], SLAB // 2
+    for q in range(half):
+        out_ref[(1 - y) * half + q] = za[q].T
+        out_ref[y * half + q] = zb[q].T
+
+
+def place_kernel(pos_ref, *refs):
+    pieces, out_ref = refs[:-1], refs[-1]
+    size = pieces[0].shape[1]
+    for j, piece in enumerate(pieces):
+        source = pos_ref[0] ^ j
+        start = (source & 1) * (2 * size) + ((source >> 1) & 1) * size
+        for k in range(4):
+            out_ref[pl.ds(pl.multiple_of(start, size), size), k * 128 : (k + 1) * 128] = piece[k]
 
 
 def gram_kernel(pos_ref, own, core, far, far_core, g_ref, far_ref):
@@ -387,10 +378,11 @@
     far_ref[(b & 1) ^ 1] = totals["back_core"]
 
 
-def call(kernel, out_shape, operands, scratch=(), name=None, ties=()):
+def call(kernel, out_shape, operands, scratch=(), name=None, ties=(), hbm=()):
     specs = [
         pl.BlockSpec(memory_space=pltpu.SMEM if o.dtype == jnp.int32 and o.size < 128 else pltpu.VMEM) for o in operands
-    ] + [pl.BlockSpec(memory_space=pl.ANY) for _ in ties]
+    ]
+    specs = [pl.BlockSpec(memory_space=pltpu.HBM) for _ in hbm] + specs + [pl.BlockSpec(memory_space=pl.ANY) for _ in ties]
     single = not isinstance(out_shape, (list, tuple))
     return pl.pallas_call(
         kernel,
@@ -404,7 +396,7 @@
         scratch_shapes=list(scratch),
         compiler_params=pltpu.CompilerParams(vmem_limit_bytes=VMEM_LIMIT),
         name=name,
-    )(*operands, *ties)
+    )(*hbm, *operands, *ties)
 
 
 def shape(*dims, dtype=F32):
@@ -462,7 +454,7 @@
     total = nd * SLAB * LAT
     dom = lax.axis_index("dom") if direct else jnp.int32(0)
     band = lax.axis_index("band")
-    pos = jnp.stack([dom, band if direct else jnp.int32(0), band // 2]).astype(jnp.int32)
+    pos = jnp.stack([dom, band if direct else jnp.int32(0), band // 2 if direct else jnp.int32(0)]).astype(jnp.int32)
     pos_band = jnp.stack([dom, band, band // 2]).astype(jnp.int32)
     R = SLAB * nb
 
@@ -483,7 +475,7 @@
                 pltpu.SemaphoreType.DMA((5,)),
             ],
             "split",
-            [atom_cell, waves, potential, proj_weights, point_codes],
+            hbm=[atom_cell, waves, potential, proj_weights, point_codes],
         )
     else:
         packed = packed_atoms(potential, proj_weights, atom_cell, point_codes)
@@ -502,7 +494,7 @@
         ]
     ready = call(
         functools.partial(filter_kernel, nd, nb, float(total)),
-        [shape(R, LAT)] * nd,
+        [shape(R // 2, LAT)] * (2 * nd),
         [pos, kb_row, lh, ll, fold] + [pieces[j] for j in arrival_order(nd)],
         [
             pltpu.VMEM(((nd * SLAB + 2 * HALO) * nb, LAT), F32),
@@ -519,65 +511,60 @@
         ],
         "filter",
     )
-    if not direct:
-        ready = [p.reshape(SLAB, nb, LAT)[:, :real] for p in ready]
-    back = swap_all(ready, direct)
     if direct:
-        filtered, correlation = finish_direct(back, pos, nb, bands, float(total))
+        filtered, correlation = finish_direct(swap_all(ready[:nd], True), swap_all(ready[nd:], True), pos, bands, float(total))
     else:
+        ready = [
+            jnp.concatenate([ready[nd + j], ready[j]]).reshape(SLAB, nb, LAT)[:, :real] for j in range(nd)
+        ]
+        back = swap_all(ready, False)
         filtered, correlation = finish_plain(jnp.concatenate(back, axis=1), pos_band, band, bands, float(total))
     return filtered.reshape(trial_waves.shape), correlation
 
 
-def finish_direct(back, pos, nb, bands, total):
-    nd, half = len(back), SLAB // 2
-    z, first, second = call(
-        functools.partial(join_kernel, nd, nb),
-        [shape(SLAB, bands, LAT), shape(half // 2, bands, LAT), shape(half // 2, bands, LAT)],
-        [pos] + back,
+def finish_direct(first, second, pos, bands, total):
+    nd, half = len(first), SLAB // 2
+    nb = bands // nd
+
+    def join(pieces, ties):
+        return call(
+            functools.partial(join_kernel, nd, nb), shape(half, bands, LAT), [pos] + pieces, (), "join", ties
+        )
+
+    za = join(first, [])
+    far = xor_permute(za, "band", 2)
+    core_a = xor_permute(za, "band", 1)
+    zb = join(second, [far])
+    core_b = xor_permute(zb, "band", 1)
+    far_core = xor_permute(far, "band", 1)
+    part, share = shape(4, bands // 2, bands), shape(2, bands // 2, bands)
+    keep, send, back, back_send = call(
+        blocks_kernel,
+        [part, part, share, share],
+        [pos, za, zb, core_a, core_b, far, far_core],
+        [pltpu.VMEM((4, bands, bands), F32), pltpu.VMEM((2, bands, bands), F32)],
+        "blocks",
+    )
+    piece = shape(4, bands // 4, bands)
+    keep, send = call(
+        sum_kernel,
+        [piece, piece],
+        [pos, keep, xor_permute(send, "dom", 1), xor_permute(back, "band", 2), both_permute(back_send)],
+        [pltpu.VMEM((4, bands // 2, bands), F32)],
+        "sum",
+    )
+    mine = keep + xor_permute(send, "dom", 2)
+    rows = call(
+        functools.partial(pair_kernel, total), piece, [pos, mine, xor_permute(mine, "dom", 4)], (), "pair"
+    )
+    filtered = call(output_kernel, shape(SLAB, LAT, bands), [pos, za, zb], (), "output")
+    correlation = call(
+        place_kernel,
+        shape(bands, 4 * bands),
+        [pos, rows] + [xor_permute(rows, "dom", step) for step in (1, 2, 3)],
         (),
-        "join",
-    )
-    far_first = xor_permute(first, "band", 2)
-    z_core = xor_permute(z, "band", 1)
-    far_second = xor_permute(second, "band", 2)
-    part = shape(2, bands // 2, bands)
-    block = pltpu.VMEM((2, bands, bands), F32)
-    own_keep, own_send = call(own_kernel, [part, part], [pos, z, z_core], [block], "own")
-    own_1 = own_keep + xor_permute(own_send, "dom", 1)
-    own_2 = own_1 + xor_permute(own_1, "dom", 2)
-    far_second, own_2 = lax.optimization_barrier((far_second, own_2))
-    own = own_2 + xor_permute(own_2, "dom", 4)
-    keep, send, back_keep, back_send = call(
-        cross_kernel,
-        [part] * 4,
-        [pos, z, z_core, far_first, far_second, xor_permute(far_first, "band", 1), xor_permute(far_second, "band", 1)],
-        [block, block],
-        "cross",
-        [own_2],
-    )
-    cross = call(
-        sum_kernel,
-        part,
-        [
-            keep,
-            xor_permute(send, "dom", 1),
-            xor_permute(back_keep, "band", 2),
-            both_permute(back_send),
-        ],
-        (),
-        "sum",
-        [own],
-    )
-    rows = call(
-        functools.partial(pair_kernel, total),
-        shape(4, bands // 2, bands),
-        [pos, own, cross] + [xor_permute(cross, "dom", step) for step in (2, 4, 6)],
-        (),
-        "pair",
-    )
-    filtered = call(output_kernel, shape(SLAB, LAT, bands), [z], (), "output")
-    correlation = call(place_kernel, shape(bands, 4 * bands), [pos, rows, xor_permute(rows, "dom", 1)], (), "place")
+        "place",
+    )
     return filtered, correlation
 
 
@@ -591,7 +578,7 @@
         (),
         "gram",
     )
-    filtered = call(output_kernel, shape(SLAB, LAT, bands), [z], (), "output")
+    filtered = z.transpose(0, 2, 1)
     start = (1 - band // 2) * 2
     cross = lax.dynamic_slice_in_dim(gram, start, 2, 0) + xor_permute(gram_far, "band", 2)
     gram = lax.dynamic_update_slice_in_dim(gram, cross, start, 0)

time: 120 us -> 118 us (0.983)
  waiting for transfers between devices: 60.6 us -> 46.5 us
  starting transfers between devices: 37.2 us -> 48.5 us
    ppermute x28 -> x32, waiting for transfers between devices: 58.2 us -> 44.1 us  [xor_permute(): return lax.ppermute(value, axis, [(k, k ^ step) for k in range(count)])]
    ppermute x28 -> x32, starting transfers between devices: 36.5 us -> 45.8 us  [xor_permute(): return lax.ppermute(value, axis, [(k, k ^ step) for k in range(count)])]
    ppermute x1, starting transfers between devices: 0.78 us -> 2.74 us  [both_permute(): return lax.ppermute(value, ('band', 'dom'), pairs)]
  transfers between devices with their start and end apart: 29 -> 33, of which waited for: 20 -> 17; matrix products, arithmetic and copies ran while one was open for 0% -> 0% of each run, Pallas kernels for 4% -> 2%
where the time goes in v8:
time: 118 us
  starting transfers between devices  48.5 us (41%)
  waiting for transfers between devices  46.5 us (39%)
  Pallas kernels  17.4 us (15%)
  local copies, waits for them, and re-layouts  4.8 us (4%)
    ppermute x32, starting transfers between devices, xor_permute(): return lax.ppermute(value, axis, [(k, k ^ step) for k in range(count)])  45.8 us
    ppermute x32, waiting for transfers between devices, xor_permute(): return lax.ppermute(value, axis, [(k, k ^ step) for k in range(count)])  44.1 us
    pallas_call x9, Pallas kernels, call(): pl.pallas_call(kernel, out_shape=out_shape, in_specs=specs, out_specs=pl....  17.4 us
    unnamed x18, local copies, waits for them, and re-layouts  4.79 us
    ppermute x1, starting transfers between devices, both_permute(): return lax.ppermute(value, ('band', 'dom'), pairs)  2.74 us
    ppermute x1, waiting for transfers between devices, both_permute(): return lax.ppermute(value, ('band', 'dom'), pairs)  2.38 us
  transfers between devices with their start and end apart: 33, of which 17 were waited for; matrix products, arithmetic and copies ran while one was open for 0% of the time, Pallas kernels for 2%

profile of v8, /device:TPU:0, one launch (start us, length us, event | category | flops | bytes accessed | tf_op | source)
XLA Modules:
  0.0 118.1 jit_solution(16492270375120623097)
XLA Ops:
  5.5 4.1 %collective-permute-start = (f32[160,256]{1,0:T(8,128)S(1)}, f32[160,256]{1,0:T(8,128)S(1)}, u32[]{:S(2)}, u32[]{:S(2)}) collective-permute-start(f32[160,256]{1,0:T(8,128)S(1)} %get-tuple-element.32), channel_id=1, source_target_pairs={{0,4},{1,5},{2,6},{3,7},{4,0},{5,1},{6,2},{7,3},{8,12},{9,13},{10,... | collective-permute-start | bytes 491528 | tf_op jit(solution)/shard_map/ppermute | solution.py:408
  9.6 1.3 %collective-permute-start.1 = (f32[160,256]{1,0:T(8,128)S(1)}, f32[160,256]{1,0:T(8,128)S(1)}, u32[]{:S(2)}, u32[]{:S(2)}) collective-permute-start(f32[160,256]{1,0:T(8,128)S(1)} %get-tuple-element.33), channel_id=1, source_target_pairs={{0,5},{1,4},{2,7},{3,6},{4,1},{5,0},{6,3},{7,2},{8,13},{9,12},{10,... | collective-permute-start | bytes 491528 | tf_op jit(solution)/shard_map/ppermute | solution.py:408
  10.9 3.6 %collective-permute-start.2 = (f32[160,256]{1,0:T(8,128)S(1)}, f32[160,256]{1,0:T(8,128)S(1)}, u32[]{:S(2)}, u32[]{:S(2)}) collective-permute-start(f32[160,256]{1,0:T(8,128)S(1)} %get-tuple-element.34), channel_id=1, source_target_pairs={{0,6},{1,7},{2,4},{3,5},{4,2},{5,3},{6,0},{7,1},{8,14},{9,15},{10,... | collective-permute-start | bytes 491528 | tf_op jit(solution)/shard_map/ppermute | solution.py:408
  14.5 1.7 %collective-permute-start.4 = (f32[160,256]{1,0:T(8,128)S(1)}, f32[160,256]{1,0:T(8,128)S(1)}, u32[]{:S(2)}, u32[]{:S(2)}) collective-permute-start(f32[160,256]{1,0:T(8,128)S(1)} %get-tuple-element.36), channel_id=1, source_target_pairs={{0,1},{1,0},{2,3},{3,2},{4,5},{5,4},{6,7},{7,6},{8,9},{9,8},{10,11... | collective-permute-start | bytes 491528 | tf_op jit(solution)/shard_map/ppermute | solution.py:408
  16.2 12.5 %collective-permute-done.refs_0_ = f32[160,256]{1,0:T(8,128)S(1)} collective-permute-done((f32[160,256]{1,0:T(8,128)S(1)}, f32[160,256]{1,0:T(8,128)S(1)}, u32[]{:S(2)}, u32[]{:S(2)}) %collective-permute-start) | collective-permute-done | bytes 163872 | tf_op jit(solution)/shard_map/ppermute | solution.py:408
  28.7 4.8 %collective-permute-done.1.refs_1_ = f32[160,256]{1,0:T(8,128)S(1)} collective-permute-done((f32[160,256]{1,0:T(8,128)S(1)}, f32[160,256]{1,0:T(8,128)S(1)}, u32[]{:S(2)}, u32[]{:S(2)}) %collective-permute-start.1) | collective-permute-done | bytes 163872 | tf_op jit(solution)/shard_map/ppermute | solution.py:408
  34.3 1.2 %collective-permute-done.5.refs_5_ = f32[160,256]{1,0:T(8,128)S(1)} collective-permute-done((f32[160,256]{1,0:T(8,128)S(1)}, f32[160,256]{1,0:T(8,128)S(1)}, u32[]{:S(2)}, u32[]{:S(2)}) %collective-permute-start.5) | collective-permute-done | bytes 163872 | tf_op jit(solution)/shard_map/ppermute | solution.py:408
  35.6 4.1 %collective-permute-done.6.refs_6_ = f32[160,256]{1,0:T(8,128)S(1)} collective-permute-done((f32[160,256]{1,0:T(8,128)S(1)}, f32[160,256]{1,0:T(8,128)S(1)}, u32[]{:S(2)}, u32[]{:S(2)}) %collective-permute-start.6) | collective-permute-done | bytes 163872 | tf_op jit(solution)/shard_map/ppermute | solution.py:408
  39.7 8.9 %filter.1 = (f32[64,256]{1,0:T(8,128)S(1)}, f32[64,256]{1,0:T(8,128)S(1)}, f32[64,256]{1,0:T(8,128)S(1)}, f32[64,256]{1,0:T(8,128)S(1)}, f32[64,256]{1,0:T(8,128...) custom-call(s32[3]{0:T(128)S(1)} %pad_add_fusion.pos_ref, ...), custom_call_target="tpu_custom_call" | custom-call | tf_op jit(solution)/shard_map/filter/pallas_call | solution.py:387
  48.9 3.7 %collective-permute-start.8 = (f32[64,256]{1,0:T(8,128)S(1)}, f32[64,256]{1,0:T(8,128)S(1)}, u32[]{:S(2)}, u32[]{:S(2)}) collective-permute-start(f32[64,256]{1,0:T(8,128)S(1)} %get-tuple-element.42), channel_id=1, source_target_pairs={{0,2},{1,3},{2,0},{3,1},{4,6},{5,7},{6,4},{7,5},{8,10},{9,11},{10,... | collective-permute-start | bytes 196616 | tf_op jit(solution)/shard_map/ppermute | solution.py:408
  53.0 3.8 %collective-permute-start.10 = (f32[64,256]{1,0:T(8,128)S(1)}, f32[64,256]{1,0:T(8,128)S(1)}, u32[]{:S(2)}, u32[]{:S(2)}) collective-permute-start(f32[64,256]{1,0:T(8,128)S(1)} %get-tuple-element.44), channel_id=1, source_target_pairs={{0,4},{1,5},{2,6},{3,7},{4,0},{5,1},{6,2},{7,3},{8,12},{9,13},{10,... | collective-permute-start | bytes 196616 | tf_op jit(solution)/shard_map/ppermute | solution.py:408
  57.7 2.4 %collective-permute-start.12 = (f32[64,256]{1,0:T(8,128)S(1)}, f32[64,256]{1,0:T(8,128)S(1)}, u32[]{:S(2)}, u32[]{:S(2)}) collective-permute-start(f32[64,256]{1,0:T(8,128)S(1)} %get-tuple-element.46), channel_id=1, source_target_pairs={{0,6},{1,7},{2,4},{3,5},{4,2},{5,3},{6,0},{7,1},{8,14},{9,15},{10,... | collective-permute-start | bytes 196616 | tf_op jit(solution)/shard_map/ppermute | solution.py:408
  60.1 1.5 %collective-permute-start.13 = (f32[64,256]{1,0:T(8,128)S(1)}, f32[64,256]{1,0:T(8,128)S(1)}, u32[]{:S(2)}, u32[]{:S(2)}) collective-permute-start(f32[64,256]{1,0:T(8,128)S(1)} %get-tuple-element.47), channel_id=1, source_target_pairs={{0,7},{1,6},{2,5},{3,4},{4,3},{5,2},{6,1},{7,0},{8,15},{9,14},{10,... | collective-permute-start | bytes 196616 | tf_op jit(solution)/shard_map/ppermute | solution.py:408
  61.5 4.2 %collective-permute-done.11.refs_5_ = f32[64,256]{1,0:T(8,128)S(1)} collective-permute-done((f32[64,256]{1,0:T(8,128)S(1)}, f32[64,256]{1,0:T(8,128)S(1)}, u32[]{:S(2)}, u32[]{:S(2)}) %collective-permute-start.11) | collective-permute-done | bytes 65568 | tf_op jit(solution)/shard_map/ppermute | solution.py:408
  65.7 1.4 %collective-permute-done.13.refs_7_ = f32[64,256]{1,0:T(8,128)S(1)} collective-permute-done((f32[64,256]{1,0:T(8,128)S(1)}, f32[64,256]{1,0:T(8,128)S(1)}, u32[]{:S(2)}, u32[]{:S(2)}) %collective-permute-start.13) | collective-permute-done | bytes 65568 | tf_op jit(solution)/shard_map/ppermute | solution.py:408
  67.7 1.6 %collective-permute-start.21 = (f32[4,128,256]{2,1,0:T(8,128)S(1)}, f32[4,128,256]{2,1,0:T(8,128)S(1)}, u32[]{:S(2)}, u32[]{:S(2)}) collective-permute-start(f32[4,128,256]{2,1,0:T(8,128)S(1)} %join.2.za), channel_id=1, source_target_pairs={{0,16},{8,24},{16,0},{24,8},{1,17},{9,25},{17,1},{25,9},{2,18},{10... | collective-permute-start | bytes 1572872 | tf_op jit(solution)/shard_map/ppermute | solution.py:408
  69.9 3.1 %collective-permute-start.15 = (f32[64,256]{1,0:T(8,128)S(1)}, f32[64,256]{1,0:T(8,128)S(1)}, u32[]{:S(2)}, u32[]{:S(2)}) collective-permute-start(f32[64,256]{1,0:T(8,128)S(1)} %get-tuple-element.50), channel_id=1, source_target_pairs={{0,2},{1,3},{2,0},{3,1},{4,6},{5,7},{6,4},{7,5},{8,10},{9,11},{10,... | collective-permute-start | bytes 196616 | tf_op jit(solution)/shard_map/ppermute | solution.py:408
  73.3 2.5 %collective-permute-start.17 = (f32[64,256]{1,0:T(8,128)S(1)}, f32[64,256]{1,0:T(8,128)S(1)}, u32[]{:S(2)}, u32[]{:S(2)}) collective-permute-start(f32[64,256]{1,0:T(8,128)S(1)} %get-tuple-element.52), channel_id=1, source_target_pairs={{0,4},{1,5},{2,6},{3,7},{4,0},{5,1},{6,2},{7,3},{8,12},{9,13},{10,... | collective-permute-start | bytes 196616 | tf_op jit(solution)/shard_map/ppermute | solution.py:408
  76.8 2.9 %collective-permute-start.19 = (f32[64,256]{1,0:T(8,128)S(1)}, f32[64,256]{1,0:T(8,128)S(1)}, u32[]{:S(2)}, u32[]{:S(2)}) collective-permute-start(f32[64,256]{1,0:T(8,128)S(1)} %get-tuple-element.54), channel_id=1, source_target_pairs={{0,6},{1,7},{2,4},{3,5},{4,2},{5,3},{6,0},{7,1},{8,14},{9,15},{10,... | collective-permute-start | bytes 196616 | tf_op jit(solution)/shard_map/ppermute | solution.py:408
  79.8 1.5 %collective-permute-start.20 = (f32[64,256]{1,0:T(8,128)S(1)}, f32[64,256]{1,0:T(8,128)S(1)}, u32[]{:S(2)}, u32[]{:S(2)}) collective-permute-start(f32[64,256]{1,0:T(8,128)S(1)} %get-tuple-element.55), channel_id=1, source_target_pairs={{0,7},{1,6},{2,5},{3,4},{4,3},{5,2},{6,1},{7,0},{8,15},{9,14},{10,... | collective-permute-start | bytes 196616 | tf_op jit(solution)/shard_map/ppermute | solution.py:408
  81.4 4.2 %collective-permute-done.18.refs_5_ = f32[64,256]{1,0:T(8,128)S(1)} collective-permute-done((f32[64,256]{1,0:T(8,128)S(1)}, f32[64,256]{1,0:T(8,128)S(1)}, u32[]{:S(2)}, u32[]{:S(2)}) %collective-permute-start.18) | collective-permute-done | bytes 65568 | tf_op jit(solution)/shard_map/ppermute | solution.py:408
  88.0 1.4 %collective-permute-done.23.cb = f32[4,128,256]{2,1,0:T(8,128)S(1)} collective-permute-done((f32[4,128,256]{2,1,0:T(8,128)S(1)}, f32[4,128,256]{2,1,0:T(8,128)S(1)}, u32[]{:S(2)}, u32[]{:S(2)}) %collective-permute-start.23) | collective-permute-done | bytes 524320 | tf_op jit(solution)/shard_map/ppermute | solution.py:408
  90.2 2.3 %blocks.1 = (f32[4,64,128]{2,1,0:T(8,128)S(1)}, f32[4,64,128]{2,1,0:T(8,128)S(1)}, f32[2,64,128]{2,1,0:T(8,128)S(1)}, f32[2,64,128]{2,1,0:T(8,128)S(1)}) custom-call(s32[3]{0:T(128)S(1)} %pad_add_fusion.pos_ref, f32[4,128,256]{2,1,0:T(8,128)S(1)} %join.2.za, f32[4,128,256]{2,1,0:T(8,128)S(1)} %join.3.zb, f32[4,128,256]{2,1,0:T(8,128)S(1)} %collective-permute-done.22.ca, ...), custom_call_target="tpu_custom_call" | custom-call | tf_op jit(solution)/shard_map/blocks/pallas_call | solution.py:387
  93.3 2.7 %collective-permute-start.27 = (f32[2,64,128]{2,1,0:T(8,128)S(1)}, f32[2,64,128]{2,1,0:T(8,128)S(1)}, u32[]{:S(2)}, u32[]{:S(2)}) collective-permute-start(f32[2,64,128]{2,1,0:T(8,128)S(1)} %get-tuple-element.59), channel_id=1, source_target_pairs={{0,17},{1,16},{2,19},{3,18},{4,21},{5,20},{6,23},{7,22},{8,25},{9,... | collective-permute-start | bytes 196616 | tf_op jit(solution)/shard_map/ppermute | solution.py:414
  97.1 2.4 %collective-permute-done.27.back_other = f32[2,64,128]{2,1,0:T(8,128)S(1)} collective-permute-done((f32[2,64,128]{2,1,0:T(8,128)S(1)}, f32[2,64,128]{2,1,0:T(8,128)S(1)}, u32[]{:S(2)}, u32[]{:S(2)}) %collective-permute-start.27) | collective-permute-done | bytes 65568 | tf_op jit(solution)/shard_map/ppermute | solution.py:414
  100.1 1.6 %collective-permute-start.28 = (f32[4,32,128]{2,1,0:T(8,128)S(1)}, f32[4,32,128]{2,1,0:T(8,128)S(1)}, u32[]{:S(2)}, u32[]{:S(2)}) collective-permute-start(f32[4,32,128]{2,1,0:T(8,128)S(1)} %get-tuple-element.61), channel_id=1, source_target_pairs={{0,2},{1,3},{2,0},{3,1},{4,6},{5,7},{6,4},{7,5},{8,10},{9,11},{10,... | collective-permute-start | bytes 196616 | tf_op jit(solution)/shard_map/ppermute | solution.py:408
  101.7 2.7 %collective-permute-done.28 = f32[4,32,128]{2,1,0:T(8,128)S(1)} collective-permute-done((f32[4,32,128]{2,1,0:T(8,128)S(1)}, f32[4,32,128]{2,1,0:T(8,128)S(1)}, u32[]{:S(2)}, u32[]{:S(2)}) %collective-permute-start.28) | collective-permute-done | bytes 65568 | tf_op jit(solution)/shard_map/ppermute | solution.py:408
  104.4 2.1 %collective-permute-start.29 = (f32[4,32,128]{2,1,0:T(8,128)S(1)}, f32[4,32,128]{2,1,0:T(8,128)S(1)}, u32[]{:S(2)}, u32[]{:S(2)}) collective-permute-start(f32[4,32,128]{2,1,0:T(8,128)S(1)} %add.4.mine), channel_id=1, source_target_pairs={{0,4},{1,5},{2,6},{3,7},{4,0},{5,1},{6,2},{7,3},{8,12},{9,13},{10,... | collective-permute-start | bytes 196616 | tf_op jit(solution)/shard_map/ppermute | solution.py:408
  106.5 3.2 %collective-permute-done.29.other = f32[4,32,128]{2,1,0:T(8,128)S(1)} collective-permute-done((f32[4,32,128]{2,1,0:T(8,128)S(1)}, f32[4,32,128]{2,1,0:T(8,128)S(1)}, u32[]{:S(2)}, u32[]{:S(2)}) %collective-permute-start.29) | collective-permute-done | bytes 65568 | tf_op jit(solution)/shard_map/ppermute | solution.py:408
  110.2 2.0 %collective-permute-start.32 = (f32[4,32,128]{2,1,0:T(8,128)S(1)}, f32[4,32,128]{2,1,0:T(8,128)S(1)}, u32[]{:S(2)}, u32[]{:S(2)}) collective-permute-start(f32[4,32,128]{2,1,0:T(8,128)S(1)} %pair.1.refs_0_), channel_id=1, source_target_pairs={{0,3},{1,2},{2,1},{3,0},{4,7},{5,6},{6,5},{7,4},{8,11},{9,10},{10,... | collective-permute-start | bytes 196616 | tf_op jit(solution)/shard_map/ppermute | solution.py:408
  113.8 1.8 %output.1 = f32[8,256,128]{2,1,0:T(8,128)} custom-call(s32[3]{0:T(128)S(1)} %pad_add_fusion.pos_ref, f32[4,128,256]{2,1,0:T(8,128)S(1)} %join.2.za, f32[4,128,256]{2,1,0:T(8,128)S(1)} %join.3.zb), custom_call_target="tpu_custom_call" | custom-call | tf_op jit(solution)/shard_map/output/pallas_call | solution.py:387
  116.8 1.3 %place.1 = f32[128,512]{1,0:T(8,128)} custom-call(s32[3]{0:T(128)S(1)} %pad_add_fusion.pos_ref, f32[4,32,128]{2,1,0:T(8,128)S(1)} %pair.1.refs_0_, f32[4,32,128]{2,1,0:T(8,128)S(1)} %collective-permute-done.30.refs_1_, f32[4,32,128]{2,1,0:T(8,128)S(1)} %collective-permute-done.31.refs_2_, f32[4,32,128]{2,1,0:T(8,128)S(1)} %collective-permute-done.32.refs_3_), custom_call_target="tpu_custom_call" | custom-call | tf_op jit(solution)/shard_map/place/pallas_call | solution.py:387
  (65 shorter events, 18.8 us)
Async XLA Ops:
  5.5 23.2 %collective-permute-start = (f32[160,256]{1,0:T(8,128)S(1)}, f32[160,256]{1,0:T(8,128)S(1)}, u32[]{:S(2)}, u32[]{:S(2)}) collective-permute-start(f32[160,256]{1,0:T(8,128)S(1)} %get-tuple-element.32), channel_id=1, source_target_pairs={{0,4},{1,5},{2,6},{3,7},{4,0},{5,1},{6,2},{7,3},{8,12},{9,13},{10,... | collective-permute-start | bytes 491528 | tf_op jit(solution)/shard_map/ppermute | solution.py:408
  9.6 23.9 %collective-permute-start.1 = (f32[160,256]{1,0:T(8,128)S(1)}, f32[160,256]{1,0:T(8,128)S(1)}, u32[]{:S(2)}, u32[]{:S(2)}) collective-permute-start(f32[160,256]{1,0:T(8,128)S(1)} %get-tuple-element.33), channel_id=1, source_target_pairs={{0,5},{1,4},{2,7},{3,6},{4,1},{5,0},{6,3},{7,2},{8,13},{9,12},{10,... | collective-permute-start | bytes 491528 | tf_op jit(solution)/shard_map/ppermute | solution.py:408
  10.9 23.4 %collective-permute-start.2 = (f32[160,256]{1,0:T(8,128)S(1)}, f32[160,256]{1,0:T(8,128)S(1)}, u32[]{:S(2)}, u32[]{:S(2)}) collective-permute-start(f32[160,256]{1,0:T(8,128)S(1)} %get-tuple-element.34), channel_id=1, source_target_pairs={{0,6},{1,7},{2,4},{3,5},{4,2},{5,3},{6,0},{7,1},{8,14},{9,15},{10,... | collective-permute-start | bytes 491528 | tf_op jit(solution)/shard_map/ppermute | solution.py:408
  14.5 19.8 %collective-permute-start.3 = (f32[160,256]{1,0:T(8,128)S(1)}, f32[160,256]{1,0:T(8,128)S(1)}, u32[]{:S(2)}, u32[]{:S(2)}) collective-permute-start(f32[160,256]{1,0:T(8,128)S(1)} %get-tuple-element.35), channel_id=1, source_target_pairs={{0,7},{1,6},{2,5},{3,4},{4,3},{5,2},{6,1},{7,0},{8,15},{9,14},{10,... | collective-permute-start | bytes 491528 | tf_op jit(solution)/shard_map/ppermute | solution.py:408
  14.5 19.8 %collective-permute-start.4 = (f32[160,256]{1,0:T(8,128)S(1)}, f32[160,256]{1,0:T(8,128)S(1)}, u32[]{:S(2)}, u32[]{:S(2)}) collective-permute-start(f32[160,256]{1,0:T(8,128)S(1)} %get-tuple-element.36), channel_id=1, source_target_pairs={{0,1},{1,0},{2,3},{3,2},{4,5},{5,4},{6,7},{7,6},{8,9},{9,8},{10,11... | collective-permute-start | bytes 491528 | tf_op jit(solution)/shard_map/ppermute | solution.py:408
  28.7 6.9 %collective-permute-start.5 = (f32[160,256]{1,0:T(8,128)S(1)}, f32[160,256]{1,0:T(8,128)S(1)}, u32[]{:S(2)}, u32[]{:S(2)}) collective-permute-start(f32[160,256]{1,0:T(8,128)S(1)} %get-tuple-element.37), channel_id=1, source_target_pairs={{0,2},{1,3},{2,0},{3,1},{4,6},{5,7},{6,4},{7,5},{8,10},{9,11},{10,... | collective-permute-start | bytes 491528 | tf_op jit(solution)/shard_map/ppermute | solution.py:408
  33.5 6.2 %collective-permute-start.6 = (f32[160,256]{1,0:T(8,128)S(1)}, f32[160,256]{1,0:T(8,128)S(1)}, u32[]{:S(2)}, u32[]{:S(2)}) collective-permute-start(f32[160,256]{1,0:T(8,128)S(1)} %get-tuple-element.38), channel_id=1, source_target_pairs={{0,3},{1,2},{2,1},{3,0},{4,7},{5,6},{6,5},{7,4},{8,11},{9,10},{10,... | collective-permute-start | bytes 491528 | tf_op jit(solution)/shard_map/ppermute | solution.py:408
  48.6 9.1 %collective-permute-start.7 = (f32[64,256]{1,0:T(8,128)S(1)}, f32[64,256]{1,0:T(8,128)S(1)}, u32[]{:S(2)}, u32[]{:S(2)}) collective-permute-start(f32[64,256]{1,0:T(8,128)S(1)} %get-tuple-element.41), channel_id=1, source_target_pairs={{0,1},{1,0},{2,3},{3,2},{4,5},{5,4},{6,7},{7,6},{8,9},{9,8},{10,11... | collective-permute-start | bytes 196616 | tf_op jit(solution)/shard_map/ppermute | solution.py:408
  48.9 11.2 %collective-permute-start.8 = (f32[64,256]{1,0:T(8,128)S(1)}, f32[64,256]{1,0:T(8,128)S(1)}, u32[]{:S(2)}, u32[]{:S(2)}) collective-permute-start(f32[64,256]{1,0:T(8,128)S(1)} %get-tuple-element.42), channel_id=1, source_target_pairs={{0,2},{1,3},{2,0},{3,1},{4,6},{5,7},{6,4},{7,5},{8,10},{9,11},{10,... | collective-permute-start | bytes 196616 | tf_op jit(solution)/shard_map/ppermute | solution.py:408
  52.6 8.9 %collective-permute-start.9 = (f32[64,256]{1,0:T(8,128)S(1)}, f32[64,256]{1,0:T(8,128)S(1)}, u32[]{:S(2)}, u32[]{:S(2)}) collective-permute-start(f32[64,256]{1,0:T(8,128)S(1)} %get-tuple-element.43), channel_id=1, source_target_pairs={{0,3},{1,2},{2,1},{3,0},{4,7},{5,6},{6,5},{7,4},{8,11},{9,10},{10,... | collective-permute-start | bytes 196616 | tf_op jit(solution)/shard_map/ppermute | solution.py:408
  53.0 8.6 %collective-permute-start.10 = (f32[64,256]{1,0:T(8,128)S(1)}, f32[64,256]{1,0:T(8,128)S(1)}, u32[]{:S(2)}, u32[]{:S(2)}) collective-permute-start(f32[64,256]{1,0:T(8,128)S(1)} %get-tuple-element.44), channel_id=1, source_target_pairs={{0,4},{1,5},{2,6},{3,7},{4,0},{5,1},{6,2},{7,3},{8,12},{9,13},{10,... | collective-permute-start | bytes 196616 | tf_op jit(solution)/shard_map/ppermute | solution.py:408
  56.8 8.9 %collective-permute-start.11 = (f32[64,256]{1,0:T(8,128)S(1)}, f32[64,256]{1,0:T(8,128)S(1)}, u32[]{:S(2)}, u32[]{:S(2)}) collective-permute-start(f32[64,256]{1,0:T(8,128)S(1)} %get-tuple-element.45), channel_id=1, source_target_pairs={{0,5},{1,4},{2,7},{3,6},{4,1},{5,0},{6,3},{7,2},{8,13},{9,12},{10,... | collective-permute-start | bytes 196616 | tf_op jit(solution)/shard_map/ppermute | solution.py:408
  57.7 8.0 %collective-permute-start.12 = (f32[64,256]{1,0:T(8,128)S(1)}, f32[64,256]{1,0:T(8,128)S(1)}, u32[]{:S(2)}, u32[]{:S(2)}) collective-permute-start(f32[64,256]{1,0:T(8,128)S(1)} %get-tuple-element.46), channel_id=1, source_target_pairs={{0,6},{1,7},{2,4},{3,5},{4,2},{5,3},{6,0},{7,1},{8,14},{9,15},{10,... | collective-permute-start | bytes 196616 | tf_op jit(solution)/shard_map/ppermute | solution.py:408
  60.1 7.1 %collective-permute-start.13 = (f32[64,256]{1,0:T(8,128)S(1)}, f32[64,256]{1,0:T(8,128)S(1)}, u32[]{:S(2)}, u32[]{:S(2)}) collective-permute-start(f32[64,256]{1,0:T(8,128)S(1)} %get-tuple-element.47), channel_id=1, source_target_pairs={{0,7},{1,6},{2,5},{3,4},{4,3},{5,2},{6,1},{7,0},{8,15},{9,14},{10,... | collective-permute-start | bytes 196616 | tf_op jit(solution)/shard_map/ppermute | solution.py:408
  67.7 19.1 %collective-permute-start.21 = (f32[4,128,256]{2,1,0:T(8,128)S(1)}, f32[4,128,256]{2,1,0:T(8,128)S(1)}, u32[]{:S(2)}, u32[]{:S(2)}) collective-permute-start(f32[4,128,256]{2,1,0:T(8,128)S(1)} %join.2.za), channel_id=1, source_target_pairs={{0,16},{8,24},{16,0},{24,8},{1,17},{9,25},{17,1},{25,9},{2,18},{10... | collective-permute-start | bytes 1572872 | tf_op jit(solution)/shard_map/ppermute | solution.py:408
  69.3 6.5 %collective-permute-start.14 = (f32[64,256]{1,0:T(8,128)S(1)}, f32[64,256]{1,0:T(8,128)S(1)}, u32[]{:S(2)}, u32[]{:S(2)}) collective-permute-start(f32[64,256]{1,0:T(8,128)S(1)} %get-tuple-element.49), channel_id=1, source_target_pairs={{0,1},{1,0},{2,3},{3,2},{4,5},{5,4},{6,7},{7,6},{8,9},{9,8},{10,11... | collective-permute-start | bytes 196616 | tf_op jit(solution)/shard_map/ppermute | solution.py:408
  69.9 7.0 %collective-permute-start.15 = (f32[64,256]{1,0:T(8,128)S(1)}, f32[64,256]{1,0:T(8,128)S(1)}, u32[]{:S(2)}, u32[]{:S(2)}) collective-permute-start(f32[64,256]{1,0:T(8,128)S(1)} %get-tuple-element.50), channel_id=1, source_target_pairs={{0,2},{1,3},{2,0},{3,1},{4,6},{5,7},{6,4},{7,5},{8,10},{9,11},{10,... | collective-permute-start | bytes 196616 | tf_op jit(solution)/shard_map/ppermute | solution.py:408
  73.0 6.8 %collective-permute-start.16 = (f32[64,256]{1,0:T(8,128)S(1)}, f32[64,256]{1,0:T(8,128)S(1)}, u32[]{:S(2)}, u32[]{:S(2)}) collective-permute-start(f32[64,256]{1,0:T(8,128)S(1)} %get-tuple-element.51), channel_id=1, source_target_pairs={{0,3},{1,2},{2,1},{3,0},{4,7},{5,6},{6,5},{7,4},{8,11},{9,10},{10,... | collective-permute-start | bytes 196616 | tf_op jit(solution)/shard_map/ppermute | solution.py:408
  73.3 8.1 %collective-permute-start.17 = (f32[64,256]{1,0:T(8,128)S(1)}, f32[64,256]{1,0:T(8,128)S(1)}, u32[]{:S(2)}, u32[]{:S(2)}) collective-permute-start(f32[64,256]{1,0:T(8,128)S(1)} %get-tuple-element.52), channel_id=1, source_target_pairs={{0,4},{1,5},{2,6},{3,7},{4,0},{5,1},{6,2},{7,3},{8,12},{9,13},{10,... | collective-permute-start | bytes 196616 | tf_op jit(solution)/shard_map/ppermute | solution.py:408
  75.8 9.8 %collective-permute-start.18 = (f32[64,256]{1,0:T(8,128)S(1)}, f32[64,256]{1,0:T(8,128)S(1)}, u32[]{:S(2)}, u32[]{:S(2)}) collective-permute-start(f32[64,256]{1,0:T(8,128)S(1)} %get-tuple-element.53), channel_id=1, source_target_pairs={{0,5},{1,4},{2,7},{3,6},{4,1},{5,0},{6,3},{7,2},{8,13},{9,12},{10,... | collective-permute-start | bytes 196616 | tf_op jit(solution)/shard_map/ppermute | solution.py:408
  76.8 8.8 %collective-permute-start.19 = (f32[64,256]{1,0:T(8,128)S(1)}, f32[64,256]{1,0:T(8,128)S(1)}, u32[]{:S(2)}, u32[]{:S(2)}) collective-permute-start(f32[64,256]{1,0:T(8,128)S(1)} %get-tuple-element.54), channel_id=1, source_target_pairs={{0,6},{1,7},{2,4},{3,5},{4,2},{5,3},{6,0},{7,1},{8,14},{9,15},{10,... | collective-permute-start | bytes 196616 | tf_op jit(solution)/shard_map/ppermute | solution.py:408
  79.8 7.1 %collective-permute-start.20 = (f32[64,256]{1,0:T(8,128)S(1)}, f32[64,256]{1,0:T(8,128)S(1)}, u32[]{:S(2)}, u32[]{:S(2)}) collective-permute-start(f32[64,256]{1,0:T(8,128)S(1)} %get-tuple-element.55), channel_id=1, source_target_pairs={{0,7},{1,6},{2,5},{3,4},{4,3},{5,2},{6,1},{7,0},{8,15},{9,14},{10,... | collective-permute-start | bytes 196616 | tf_op jit(solution)/shard_map/ppermute | solution.py:408
  81.4 6.6 %collective-permute-start.22 = (f32[4,128,256]{2,1,0:T(8,128)S(1)}, f32[4,128,256]{2,1,0:T(8,128)S(1)}, u32[]{:S(2)}, u32[]{:S(2)}) collective-permute-start(f32[4,128,256]{2,1,0:T(8,128)S(1)} %join.2.za), channel_id=1, source_target_pairs={{0,8},{8,0},{16,24},{24,16},{1,9},{9,1},{17,25},{25,17},{2,10},{10... | collective-permute-start | bytes 1572872 | tf_op jit(solution)/shard_map/ppermute | solution.py:408
  87.5 2.6 %collective-permute-start.24 = (f32[4,128,256]{2,1,0:T(8,128)S(1)}, f32[4,128,256]{2,1,0:T(8,128)S(1)}, u32[]{:S(2)}, u32[]{:S(2)}) collective-permute-start(f32[4,128,256]{2,1,0:T(8,128)S(1)} %collective-permute-done.21.refs_8_.far), channel_id=1, source_target_pairs={{0,8},{8,0},{16,24},{24,16},{1,9},{9,1},{17,25},{25,17},{2,10},{10... | collective-permute-start | bytes 1572872 | tf_op jit(solution)/shard_map/ppermute | solution.py:408
  92.5 7.0 %collective-permute-start.25 = (f32[4,64,128]{2,1,0:T(8,128)S(1)}, f32[4,64,128]{2,1,0:T(8,128)S(1)}, u32[]{:S(2)}, u32[]{:S(2)}) collective-permute-start(f32[4,64,128]{2,1,0:T(8,128)S(1)} %get-tuple-element.57), channel_id=1, source_target_pairs={{0,1},{1,0},{2,3},{3,2},{4,5},{5,4},{6,7},{7,6},{8,9},{9,8},{10,11... | collective-permute-start | bytes 393224 | tf_op jit(solution)/shard_map/ppermute | solution.py:408
  92.8 4.3 %collective-permute-start.26 = (f32[2,64,128]{2,1,0:T(8,128)S(1)}, f32[2,64,128]{2,1,0:T(8,128)S(1)}, u32[]{:S(2)}, u32[]{:S(2)}) collective-permute-start(f32[2,64,128]{2,1,0:T(8,128)S(1)} %get-tuple-element.58), channel_id=1, source_target_pairs={{0,16},{8,24},{16,0},{24,8},{1,17},{9,25},{17,1},{25,9},{2,18},{10... | collective-permute-start | bytes 196616 | tf_op jit(solution)/shard_map/ppermute | solution.py:408
  93.3 6.1 %collective-permute-start.27 = (f32[2,64,128]{2,1,0:T(8,128)S(1)}, f32[2,64,128]{2,1,0:T(8,128)S(1)}, u32[]{:S(2)}, u32[]{:S(2)}) collective-permute-start(f32[2,64,128]{2,1,0:T(8,128)S(1)} %get-tuple-element.59), channel_id=1, source_target_pairs={{0,17},{1,16},{2,19},{3,18},{4,21},{5,20},{6,23},{7,22},{8,25},{9,... | collective-permute-start | bytes 196616 | tf_op jit(solution)/shard_map/ppermute | solution.py:414
  100.1 4.3 %collective-permute-start.28 = (f32[4,32,128]{2,1,0:T(8,128)S(1)}, f32[4,32,128]{2,1,0:T(8,128)S(1)}, u32[]{:S(2)}, u32[]{:S(2)}) collective-permute-start(f32[4,32,128]{2,1,0:T(8,128)S(1)} %get-tuple-element.61), channel_id=1, source_target_pairs={{0,2},{1,3},{2,0},{3,1},{4,6},{5,7},{6,4},{7,5},{8,10},{9,11},{10,... | collective-permute-start | bytes 196616 | tf_op jit(solution)/shard_map/ppermute | solution.py:408
  104.4 5.2 %collective-permute-start.29 = (f32[4,32,128]{2,1,0:T(8,128)S(1)}, f32[4,32,128]{2,1,0:T(8,128)S(1)}, u32[]{:S(2)}, u32[]{:S(2)}) collective-permute-start(f32[4,32,128]{2,1,0:T(8,128)S(1)} %add.4.mine), channel_id=1, source_target_pairs={{0,4},{1,5},{2,6},{3,7},{4,0},{5,1},{6,2},{7,3},{8,12},{9,13},{10,... | collective-permute-start | bytes 196616 | tf_op jit(solution)/shard_map/ppermute | solution.py:408
  110.2 5.4 %collective-permute-start.32 = (f32[4,32,128]{2,1,0:T(8,128)S(1)}, f32[4,32,128]{2,1,0:T(8,128)S(1)}, u32[]{:S(2)}, u32[]{:S(2)}) collective-permute-start(f32[4,32,128]{2,1,0:T(8,128)S(1)} %pair.1.refs_0_), channel_id=1, source_target_pairs={{0,3},{1,2},{2,1},{3,0},{4,7},{5,6},{6,5},{7,4},{8,11},{9,10},{10,... | collective-permute-start | bytes 196616 | tf_op jit(solution)/shard_map/ppermute | solution.py:408
  112.2 4.3 %collective-permute-start.31 = (f32[4,32,128]{2,1,0:T(8,128)S(1)}, f32[4,32,128]{2,1,0:T(8,128)S(1)}, u32[]{:S(2)}, u32[]{:S(2)}) collective-permute-start(f32[4,32,128]{2,1,0:T(8,128)S(1)} %pair.1.refs_0_), channel_id=1, source_target_pairs={{0,2},{1,3},{2,0},{3,1},{4,6},{5,7},{6,4},{7,5},{8,10},{9,11},{10,... | collective-permute-start | bytes 196616 | tf_op jit(solution)/shard_map/ppermute | solution.py:408
  112.5 4.3 %collective-permute-start.30 = (f32[4,32,128]{2,1,0:T(8,128)S(1)}, f32[4,32,128]{2,1,0:T(8,128)S(1)}, u32[]{:S(2)}, u32[]{:S(2)}) collective-permute-start(f32[4,32,128]{2,1,0:T(8,128)S(1)} %pair.1.refs_0_), channel_id=1, source_target_pairs={{0,1},{1,0},{2,3},{3,2},{4,5},{5,4},{6,7},{7,6},{8,9},{9,8},{10,11... | collective-permute-start | bytes 196616 | tf_op jit(solution)/shard_map/ppermute | solution.py:408
  (10 other events, 111.6 us)

commit v9 on v8

--- a/solution.py
+++ b/solution.py
@@ -11,6 +11,7 @@
 HALO = 6
 REACH = 4
 SLAB = 8
+PARTS = 4
 SIDE = 16
 LAT = SIDE * SIDE
 
@@ -83,48 +84,16 @@
     return hi, lo
 
 
-def split_kernel(nd, nb, cell_hbm, x_hbm, v_hbm, w_hbm, code_hbm, *refs):
-    outs, (cell_ref, x_ref, v_ref, w_ref, code_ref, scratch, packed, sems) = refs[:nd], refs[nd:]
-    copies = [
-        pltpu.make_async_copy(source, target, sems.at[k])
-        for k, (source, target) in enumerate(
-            ((x_hbm, x_ref), (cell_hbm, cell_ref), (v_hbm, v_ref), (w_hbm, w_ref), (code_hbm, code_ref))
-        )
-    ]
-    for copy in copies:
-        copy.start()
+def split_kernel(nd, nb, x_ref, packed_ref, *refs):
+    outs, scratch = refs[:-1], refs[-1]
     i = lax.axis_index("dom")
-    for copy in copies[1:]:
-        copy.wait()
-    cell = cell_ref[...].astype(F32)
-    cube = 2 * REACH + 1
-    code = code_ref[...].astype(F32)
-    off_x = jnp.floor((code + 0.5) * (1.0 / (cube * cube)))
-    rest = code - off_x * (cube * cube)
-    off_y = jnp.floor((rest + 0.5) * (1.0 / cube))
-    off_z = rest - off_y * cube
-    for a in range(2):
-        packed[a * 8 : a * 8 + 8] = w_ref[a]
-        cell_x, cell_y, cell_z = (
-            cell[a : a + 1, k : k + 1] - n * jnp.floor(cell[a : a + 1, k : k + 1] * (1.0 / n))
-            for k, n in enumerate((SLAB, SIDE, SIDE))
-        )
-        y = off_y[a : a + 1] + (cell_y + float(SIDE - REACH))
-        z = off_z[a : a + 1] + (cell_z + float(SIDE - REACH))
-        y = y - SIDE * jnp.floor(y * (1.0 / SIDE))
-        z = z - SIDE * jnp.floor(z * (1.0 / SIDE))
-        packed[16 + a : 17 + a] = off_x[a : a + 1] + cell_x
-        packed[18 + a : 19 + a] = y * SIDE + z
-    packed[20:24] = jnp.zeros((4, LAT), F32)
-    packed[24:32] = jnp.concatenate([v_ref[:, y, :] for y in range(SIDE)], axis=1)
-    copies[0].wait()
     for q in range(SLAB):
         scratch[q] = x_ref[q].T
     for j in range(nd):
         start = (i ^ j) * nb
         for q in range(SLAB):
             outs[j][q * nb : (q + 1) * nb] = scratch[q, pl.ds(pl.multiple_of(start, nb), nb)]
-        outs[j][SLAB * nb :] = packed[...]
+        outs[j][SLAB * nb :] = packed_ref[...]
 
 
 def build_projectors(nd, scratch, wh_ref, wl_ref, v_ref):
@@ -163,7 +132,7 @@
 
 
 def arrival_order(nd):
-    return [*range(nd // 2, nd), *range(1, nd // 2), 0]
+    return [1, 2, *range(nd // 2, nd), *range(3, nd // 2), 0]
 
 
 def filter_kernel(nd, nb, total, pos_ref, kb_ref, lh_ref, ll_ref, fold_ref, *refs):
@@ -279,23 +248,28 @@
             out[...] = (y * scale[None]).reshape(half * nb, LAT)
 
 
-def join_kernel(nd, nb, pos_ref, *refs):
-    pieces, z_ref = refs[:nd], refs[-1]
+def join_kernel(nd, nb, outs, pos_ref, *refs):
+    pieces, (z_ref, *parts) = refs[:nd], refs[-outs:]
     i = pos_ref[0]
     for j in range(nd):
         rows = pl.ds(pl.multiple_of((i ^ j) * nb, nb), nb)
         for q in range(SLAB // 2):
             z_ref[q, rows] = pieces[j][q * nb : (q + 1) * nb]
-
-
-def blocks_kernel(pos_ref, za, zb, ca, cb, far, far_core, keep, send, back, back_send, g_ref, back_ref):
+    for k, part in enumerate(parts):
+        part[...] = z_ref[k * part.shape[0] : (k + 1) * part.shape[0]]
+
+
+def blocks_kernel(parts, pos_ref, za, zb, ca, cb, *refs):
+    far, far_core = refs[:parts], refs[parts : 2 * parts]
+    keep, send, back, back_send, g_ref, back_ref = refs[2 * parts :]
     i, c = pos_ref[0], pos_ref[1] & 1
+    per = SLAB // 2 // parts
     totals = None
     for q in range(SLAB // 2):
         zh, zl = halves(zb[q])
         ch, cl = halves(cb[q])
-        fh, fl = halves(far[q])
-        gh, gl = halves(far_core[q])
+        fh, fl = halves(far[q // per][q % per])
+        gh, gl = halves(far_core[q // per][q % per])
         wh, wl = halves(za[q])
         xh, xl = halves(ca[q])
         now = (
@@ -378,11 +352,10 @@
     far_ref[(b & 1) ^ 1] = totals["back_core"]
 
 
-def call(kernel, out_shape, operands, scratch=(), name=None, ties=(), hbm=()):
+def call(kernel, out_shape, operands, scratch=(), name=None, ties=()):
     specs = [
         pl.BlockSpec(memory_space=pltpu.SMEM if o.dtype == jnp.int32 and o.size < 128 else pltpu.VMEM) for o in operands
-    ]
-    specs = [pl.BlockSpec(memory_space=pltpu.HBM) for _ in hbm] + specs + [pl.BlockSpec(memory_space=pl.ANY) for _ in ties]
+    ] + [pl.BlockSpec(memory_space=pl.ANY) for _ in ties]
     single = not isinstance(out_shape, (list, tuple))
     return pl.pallas_call(
         kernel,
@@ -396,7 +369,7 @@
         scratch_shapes=list(scratch),
         compiler_params=pltpu.CompilerParams(vmem_limit_bytes=VMEM_LIMIT),
         name=name,
-    )(*hbm, *operands, *ties)
+    )(*operands, *ties)
 
 
 def shape(*dims, dtype=F32):
@@ -459,26 +432,16 @@
     R = SLAB * nb
 
     waves = trial_waves.reshape(SLAB, LAT, bands)
+    packed = packed_atoms(potential, proj_weights, atom_cell, point_codes)
     if direct:
         cut = call(
             functools.partial(split_kernel, nd, nb),
             [shape(R + 32, LAT)] * nd,
-            [],
-            [
-                pltpu.VMEM(atom_cell.shape, jnp.int32),
-                pltpu.VMEM(waves.shape, F32),
-                pltpu.VMEM(potential.shape, F32),
-                pltpu.VMEM(proj_weights.shape, F32),
-                pltpu.VMEM(point_codes.shape, jnp.int32),
-                pltpu.VMEM((SLAB, bands, LAT), F32),
-                pltpu.VMEM((32, 256), F32),
-                pltpu.SemaphoreType.DMA((5,)),
-            ],
+            [waves, packed],
+            [pltpu.VMEM((SLAB, bands, LAT), F32)],
             "split",
-            hbm=[atom_cell, waves, potential, proj_weights, point_codes],
         )
     else:
-        packed = packed_atoms(potential, proj_weights, atom_cell, point_codes)
         gathered = lax.all_gather(packed, "dom", axis=0)
         turned = waves.transpose(0, 2, 1).reshape(SLAB, nd, real, LAT).transpose(1, 0, 2, 3)
         cut = [turned[j] for j in range(nd)]
@@ -526,22 +489,27 @@
     nd, half = len(first), SLAB // 2
     nb = bands // nd
 
-    def join(pieces, ties):
+    def join(pieces, outs, ties):
         return call(
-            functools.partial(join_kernel, nd, nb), shape(half, bands, LAT), [pos] + pieces, (), "join", ties
+            functools.partial(join_kernel, nd, nb, len(outs) + 1),
+            [shape(half, bands, LAT)] + outs,
+            [pos] + pieces,
+            (),
+            "join",
+            ties,
         )
 
-    za = join(first, [])
-    far = xor_permute(za, "band", 2)
+    za, *sends = join(first, [shape(half // PARTS, bands, LAT)] * PARTS, [])
+    far = [xor_permute(p, "band", 2) for p in sends]
     core_a = xor_permute(za, "band", 1)
-    zb = join(second, [far])
+    (zb,) = join(second, [], far)
     core_b = xor_permute(zb, "band", 1)
-    far_core = xor_permute(far, "band", 1)
+    far_core = [xor_permute(p, "band", 1) for p in far]
     part, share = shape(4, bands // 2, bands), shape(2, bands // 2, bands)
     keep, send, back, back_send = call(
-        blocks_kernel,
+        functools.partial(blocks_kernel, PARTS),
         [part, part, share, share],
-        [pos, za, zb, core_a, core_b, far, far_core],
+        [pos, za, zb, core_a, core_b] + far + far_core,
         [pltpu.VMEM((4, bands, bands), F32), pltpu.VMEM((2, bands, bands), F32)],
         "blocks",
     )

time: 118 us -> 117 us (level)
  waiting for transfers between devices: 46.5 us -> 41.4 us
  starting transfers between devices: 48.5 us -> 53 us
  local copies, waits for them, and re-layouts: 4.8 us -> 3.45 us
    ppermute x32 -> x38, starting transfers between devices: 45.8 us -> 52.1 us  [xor_permute(): return lax.ppermute(value, axis, [(k, k ^ step) for k in range(count)])]
    ppermute x32 -> x38, waiting for transfers between devices: 44.1 us -> 39 us  [xor_permute(): return lax.ppermute(value, axis, [(k, k ^ step) for k in range(count)])]
    unnamed x18 -> x14, local copies, waits for them, and re-layouts: 4.79 us -> 2.49 us
    ppermute x1, starting transfers between devices: 2.74 us -> 0.91 us  [both_permute(): return lax.ppermute(value, ('band', 'dom'), pairs)]
  transfers between devices with their start and end apart: 33 -> 39, of which waited for: 17 -> 13; matrix products, arithmetic and copies ran while one was open for 0% -> 0% of each run, Pallas kernels for 2% -> 3%
where the time goes in v9:
time: 117 us
  starting transfers between devices  53 us (45%)
  waiting for transfers between devices  41.4 us (35%)
  Pallas kernels  17.1 us (15%)
  local copies, waits for them, and re-layouts  3.45 us (3%)
  other arithmetic  1.25 us (1%)
    ppermute x38, starting transfers between devices, xor_permute(): return lax.ppermute(value, axis, [(k, k ^ step) for k in range(count)])  52.1 us
    ppermute x38, waiting for transfers between devices, xor_permute(): return lax.ppermute(value, axis, [(k, k ^ step) for k in range(count)])  39 us
    pallas_call x9, Pallas kernels, call(): pl.pallas_call(kernel, out_shape=out_shape, in_specs=specs, out_specs=pl....  17.1 us
    unnamed x14, local copies, waits for them, and re-layouts  2.49 us
    ppermute x1, waiting for transfers between devices, both_permute(): return lax.ppermute(value, ('band', 'dom'), pairs)  2.45 us
  transfers between devices with their start and end apart: 39, of which 13 were waited for; matrix products, arithmetic and copies ran while one was open for 0% of the time, Pallas kernels for 3%

profile of v9, /device:TPU:0, one launch (start us, length us, event | category | flops | bytes accessed | tf_op | source)
XLA Modules:
  0.0 117.0 jit_solution(4308701837972072948)
XLA Ops:
  5.0 3.0 %collective-permute-start = (f32[160,256]{1,0:T(8,128)S(1)}, f32[160,256]{1,0:T(8,128)S(1)}, u32[]{:S(2)}, u32[]{:S(2)}) collective-permute-start(f32[160,256]{1,0:T(8,128)S(1)} %get-tuple-element.37), channel_id=1, source_target_pairs={{0,1},{1,0},{2,3},{3,2},{4,5},{5,4},{6,7},{7,6},{8,9},{9,8},{10,11... | collective-permute-start | bytes 491528 | tf_op jit(solution)/shard_map/ppermute | solution.py:381
  8.0 1.6 %collective-permute-start.1 = (f32[160,256]{1,0:T(8,128)S(1)}, f32[160,256]{1,0:T(8,128)S(1)}, u32[]{:S(2)}, u32[]{:S(2)}) collective-permute-start(f32[160,256]{1,0:T(8,128)S(1)} %get-tuple-element.38), channel_id=1, source_target_pairs={{0,2},{1,3},{2,0},{3,1},{4,6},{5,7},{6,4},{7,5},{8,10},{9,11},{10,... | collective-permute-start | bytes 491528 | tf_op jit(solution)/shard_map/ppermute | solution.py:381
  9.6 2.6 %collective-permute-start.2 = (f32[160,256]{1,0:T(8,128)S(1)}, f32[160,256]{1,0:T(8,128)S(1)}, u32[]{:S(2)}, u32[]{:S(2)}) collective-permute-start(f32[160,256]{1,0:T(8,128)S(1)} %get-tuple-element.39), channel_id=1, source_target_pairs={{0,4},{1,5},{2,6},{3,7},{4,0},{5,1},{6,2},{7,3},{8,12},{9,13},{10,... | collective-permute-start | bytes 491528 | tf_op jit(solution)/shard_map/ppermute | solution.py:381
  12.4 2.5 %collective-permute-start.4 = (f32[160,256]{1,0:T(8,128)S(1)}, f32[160,256]{1,0:T(8,128)S(1)}, u32[]{:S(2)}, u32[]{:S(2)}) collective-permute-start(f32[160,256]{1,0:T(8,128)S(1)} %get-tuple-element.41), channel_id=1, source_target_pairs={{0,6},{1,7},{2,4},{3,5},{4,2},{5,3},{6,0},{7,1},{8,14},{9,15},{10,... | collective-permute-start | bytes 491528 | tf_op jit(solution)/shard_map/ppermute | solution.py:381
  14.9 2.3 %collective-permute-start.5 = (f32[160,256]{1,0:T(8,128)S(1)}, f32[160,256]{1,0:T(8,128)S(1)}, u32[]{:S(2)}, u32[]{:S(2)}) collective-permute-start(f32[160,256]{1,0:T(8,128)S(1)} %get-tuple-element.42), channel_id=1, source_target_pairs={{0,7},{1,6},{2,5},{3,4},{4,3},{5,2},{6,1},{7,0},{8,15},{9,14},{10,... | collective-permute-start | bytes 491528 | tf_op jit(solution)/shard_map/ppermute | solution.py:381
  18.0 13.4 %collective-permute-done.2.refs_2_ = f32[160,256]{1,0:T(8,128)S(1)} collective-permute-done((f32[160,256]{1,0:T(8,128)S(1)}, f32[160,256]{1,0:T(8,128)S(1)}, u32[]{:S(2)}, u32[]{:S(2)}) %collective-permute-start.2) | collective-permute-done | bytes 163872 | tf_op jit(solution)/shard_map/ppermute | solution.py:381
  31.4 3.0 %collective-permute-done.3.refs_3_ = f32[160,256]{1,0:T(8,128)S(1)} collective-permute-done((f32[160,256]{1,0:T(8,128)S(1)}, f32[160,256]{1,0:T(8,128)S(1)}, u32[]{:S(2)}, u32[]{:S(2)}) %collective-permute-start.3) | collective-permute-done | bytes 163872 | tf_op jit(solution)/shard_map/ppermute | solution.py:381
  34.4 8.9 %filter.1 = (f32[64,256]{1,0:T(8,128)S(1)}, f32[64,256]{1,0:T(8,128)S(1)}, f32[64,256]{1,0:T(8,128)S(1)}, f32[64,256]{1,0:T(8,128)S(1)}, f32[64,256]{1,0:T(8,128...) custom-call(s32[3]{0:T(128)S(1)} %pad_add_fusion.pos_ref, ...), custom_call_target="tpu_custom_call" | custom-call | tf_op jit(solution)/shard_map/filter/pallas_call | solution.py:360
  43.3 2.1 %collective-permute-start.7 = (f32[64,256]{1,0:T(8,128)S(1)}, f32[64,256]{1,0:T(8,128)S(1)}, u32[]{:S(2)}, u32[]{:S(2)}) collective-permute-start(f32[64,256]{1,0:T(8,128)S(1)} %get-tuple-element.46), channel_id=1, source_target_pairs={{0,1},{1,0},{2,3},{3,2},{4,5},{5,4},{6,7},{7,6},{8,9},{9,8},{10,11... | collective-permute-start | bytes 196616 | tf_op jit(solution)/shard_map/ppermute | solution.py:381
  45.4 6.1 %collective-permute-start.8 = (f32[64,256]{1,0:T(8,128)S(1)}, f32[64,256]{1,0:T(8,128)S(1)}, u32[]{:S(2)}, u32[]{:S(2)}) collective-permute-start(f32[64,256]{1,0:T(8,128)S(1)} %get-tuple-element.47), channel_id=1, source_target_pairs={{0,2},{1,3},{2,0},{3,1},{4,6},{5,7},{6,4},{7,5},{8,10},{9,11},{10,... | collective-permute-start | bytes 196616 | tf_op jit(solution)/shard_map/ppermute | solution.py:381
  51.5 3.0 %collective-permute-start.10 = (f32[64,256]{1,0:T(8,128)S(1)}, f32[64,256]{1,0:T(8,128)S(1)}, u32[]{:S(2)}, u32[]{:S(2)}) collective-permute-start(f32[64,256]{1,0:T(8,128)S(1)} %get-tuple-element.49), channel_id=1, source_target_pairs={{0,4},{1,5},{2,6},{3,7},{4,0},{5,1},{6,2},{7,3},{8,12},{9,13},{10,... | collective-permute-start | bytes 196616 | tf_op jit(solution)/shard_map/ppermute | solution.py:381
  55.4 2.4 %collective-permute-start.12 = (f32[64,256]{1,0:T(8,128)S(1)}, f32[64,256]{1,0:T(8,128)S(1)}, u32[]{:S(2)}, u32[]{:S(2)}) collective-permute-start(f32[64,256]{1,0:T(8,128)S(1)} %get-tuple-element.51), channel_id=1, source_target_pairs={{0,6},{1,7},{2,4},{3,5},{4,2},{5,3},{6,0},{7,1},{8,14},{9,15},{10,... | collective-permute-start | bytes 196616 | tf_op jit(solution)/shard_map/ppermute | solution.py:381
  57.8 1.5 %collective-permute-start.13 = (f32[64,256]{1,0:T(8,128)S(1)}, f32[64,256]{1,0:T(8,128)S(1)}, u32[]{:S(2)}, u32[]{:S(2)}) collective-permute-start(f32[64,256]{1,0:T(8,128)S(1)} %get-tuple-element.52), channel_id=1, source_target_pairs={{0,7},{1,6},{2,5},{3,4},{4,3},{5,2},{6,1},{7,0},{8,15},{9,14},{10,... | collective-permute-start | bytes 196616 | tf_op jit(solution)/shard_map/ppermute | solution.py:381
  59.3 1.5 %collective-permute-start.14 = (f32[64,256]{1,0:T(8,128)S(1)}, f32[64,256]{1,0:T(8,128)S(1)}, u32[]{:S(2)}, u32[]{:S(2)}) collective-permute-start(f32[64,256]{1,0:T(8,128)S(1)} %get-tuple-element.55), channel_id=1, source_target_pairs={{0,1},{1,0},{2,3},{3,2},{4,5},{5,4},{6,7},{7,6},{8,9},{9,8},{10,11... | collective-permute-start | bytes 196616 | tf_op jit(solution)/shard_map/ppermute | solution.py:381
  60.8 2.9 %collective-permute-done.11.refs_5_ = f32[64,256]{1,0:T(8,128)S(1)} collective-permute-done((f32[64,256]{1,0:T(8,128)S(1)}, f32[64,256]{1,0:T(8,128)S(1)}, u32[]{:S(2)}, u32[]{:S(2)}) %collective-permute-start.11) | collective-permute-done | bytes 65568 | tf_op jit(solution)/shard_map/ppermute | solution.py:381
  64.3 3.3 %collective-permute-start.17 = (f32[64,256]{1,0:T(8,128)S(1)}, f32[64,256]{1,0:T(8,128)S(1)}, u32[]{:S(2)}, u32[]{:S(2)}) collective-permute-start(f32[64,256]{1,0:T(8,128)S(1)} %get-tuple-element.58), channel_id=1, source_target_pairs={{0,4},{1,5},{2,6},{3,7},{4,0},{5,1},{6,2},{7,3},{8,12},{9,13},{10,... | collective-permute-start | bytes 196616 | tf_op jit(solution)/shard_map/ppermute | solution.py:381
  67.6 1.3 %collective-permute-start.18 = (f32[64,256]{1,0:T(8,128)S(1)}, f32[64,256]{1,0:T(8,128)S(1)}, u32[]{:S(2)}, u32[]{:S(2)}) collective-permute-start(f32[64,256]{1,0:T(8,128)S(1)} %get-tuple-element.59), channel_id=1, source_target_pairs={{0,5},{1,4},{2,7},{3,6},{4,1},{5,0},{6,3},{7,2},{8,13},{9,12},{10,... | collective-permute-start | bytes 196616 | tf_op jit(solution)/shard_map/ppermute | solution.py:381
  69.5 1.4 %collective-permute-start.19 = (f32[64,256]{1,0:T(8,128)S(1)}, f32[64,256]{1,0:T(8,128)S(1)}, u32[]{:S(2)}, u32[]{:S(2)}) collective-permute-start(f32[64,256]{1,0:T(8,128)S(1)} %get-tuple-element.60), channel_id=1, source_target_pairs={{0,6},{1,7},{2,4},{3,5},{4,2},{5,3},{6,0},{7,1},{8,14},{9,15},{10,... | collective-permute-start | bytes 196616 | tf_op jit(solution)/shard_map/ppermute | solution.py:381
  70.9 1.5 %collective-permute-start.21 = (f32[1,128,256]{2,1,0:T(8,128)S(1)}, f32[1,128,256]{2,1,0:T(8,128)S(1)}, u32[]{:S(2)}, u32[]{:S(2)}) collective-permute-start(f32[1,128,256]{2,1,0:T(8,128)S(1)} %get-tuple-element.62), channel_id=1, source_target_pairs={{0,16},{8,24},{16,0},{24,8},{1,17},{9,25},{17,1},{25,9},{2,18},{10... | collective-permute-start | bytes 393224 | tf_op jit(solution)/shard_map/ppermute | solution.py:381
  73.0 1.5 %collective-permute-start.23 = (f32[1,128,256]{2,1,0:T(8,128)S(1)}, f32[1,128,256]{2,1,0:T(8,128)S(1)}, u32[]{:S(2)}, u32[]{:S(2)}) collective-permute-start(f32[1,128,256]{2,1,0:T(8,128)S(1)} %get-tuple-element.64), channel_id=1, source_target_pairs={{0,16},{8,24},{16,0},{24,8},{1,17},{9,25},{17,1},{25,9},{2,18},{10... | collective-permute-start | bytes 393224 | tf_op jit(solution)/shard_map/ppermute | solution.py:381
  74.6 1.6 %collective-permute-start.24 = (f32[1,128,256]{2,1,0:T(8,128)S(1)}, f32[1,128,256]{2,1,0:T(8,128)S(1)}, u32[]{:S(2)}, u32[]{:S(2)}) collective-permute-start(f32[1,128,256]{2,1,0:T(8,128)S(1)} %get-tuple-element.65), channel_id=1, source_target_pairs={{0,16},{8,24},{16,0},{24,8},{1,17},{9,25},{17,1},{25,9},{2,18},{10... | collective-permute-start | bytes 393224 | tf_op jit(solution)/shard_map/ppermute | solution.py:381
  76.2 2.3 %collective-permute-start.20 = (f32[64,256]{1,0:T(8,128)S(1)}, f32[64,256]{1,0:T(8,128)S(1)}, u32[]{:S(2)}, u32[]{:S(2)}) collective-permute-start(f32[64,256]{1,0:T(8,128)S(1)} %get-tuple-element.61), channel_id=1, source_target_pairs={{0,7},{1,6},{2,5},{3,4},{4,3},{5,2},{6,1},{7,0},{8,15},{9,14},{10,... | collective-permute-start | bytes 196616 | tf_op jit(solution)/shard_map/ppermute | solution.py:381
  78.5 4.6 %collective-permute-done.20.refs_7_ = f32[64,256]{1,0:T(8,128)S(1)} collective-permute-done((f32[64,256]{1,0:T(8,128)S(1)}, f32[64,256]{1,0:T(8,128)S(1)}, u32[]{:S(2)}, u32[]{:S(2)}) %collective-permute-start.20) | collective-permute-done | bytes 65568 | tf_op jit(solution)/shard_map/ppermute | solution.py:381
  87.5 2.3 %blocks.1 = (f32[4,64,128]{2,1,0:T(8,128)S(1)}, f32[4,64,128]{2,1,0:T(8,128)S(1)}, f32[2,64,128]{2,1,0:T(8,128)S(1)}, f32[2,64,128]{2,1,0:T(8,128)S(1)}) custom-call(s32[3]{0:T(128)S(1)} %pad_add_fusion.pos_ref, f32[4,128,256]{2,1,0:T(8,128)S(1)} %get-tuple-element.53.za, f32[4,128,256]{2,1,0:T(8,128)S(1)} %join.3.zb, ...), custom_call_target="tpu_custom_call" | custom-call | tf_op jit(solution)/shard_map/blocks/pallas_call | solution.py:360
  91.0 1.5 %collective-permute-start.32 = (f32[2,64,128]{2,1,0:T(8,128)S(1)}, f32[2,64,128]{2,1,0:T(8,128)S(1)}, u32[]{:S(2)}, u32[]{:S(2)}) collective-permute-start(f32[2,64,128]{2,1,0:T(8,128)S(1)} %get-tuple-element.68), channel_id=1, source_target_pairs={{0,16},{8,24},{16,0},{24,8},{1,17},{9,25},{17,1},{25,9},{2,18},{10... | collective-permute-start | bytes 196616 | tf_op jit(solution)/shard_map/ppermute | solution.py:381
  93.4 1.8 %collective-permute-done.32.back = f32[2,64,128]{2,1,0:T(8,128)S(1)} collective-permute-done((f32[2,64,128]{2,1,0:T(8,128)S(1)}, f32[2,64,128]{2,1,0:T(8,128)S(1)}, u32[]{:S(2)}, u32[]{:S(2)}) %collective-permute-start.32) | collective-permute-done | bytes 65568 | tf_op jit(solution)/shard_map/ppermute | solution.py:381
  95.2 2.4 %collective-permute-done.33.back_other = f32[2,64,128]{2,1,0:T(8,128)S(1)} collective-permute-done((f32[2,64,128]{2,1,0:T(8,128)S(1)}, f32[2,64,128]{2,1,0:T(8,128)S(1)}, u32[]{:S(2)}, u32[]{:S(2)}) %collective-permute-start.33) | collective-permute-done | bytes 65568 | tf_op jit(solution)/shard_map/ppermute | solution.py:387
  98.3 4.3 %collective-permute-done.34 = f32[4,32,128]{2,1,0:T(8,128)S(1)} collective-permute-done((f32[4,32,128]{2,1,0:T(8,128)S(1)}, f32[4,32,128]{2,1,0:T(8,128)S(1)}, u32[]{:S(2)}, u32[]{:S(2)}) %collective-permute-start.34) | collective-permute-done | bytes 65568 | tf_op jit(solution)/shard_map/ppermute | solution.py:381
  103.0 5.0 %collective-permute-done.35.other = f32[4,32,128]{2,1,0:T(8,128)S(1)} collective-permute-done((f32[4,32,128]{2,1,0:T(8,128)S(1)}, f32[4,32,128]{2,1,0:T(8,128)S(1)}, u32[]{:S(2)}, u32[]{:S(2)}) %collective-permute-start.35) | collective-permute-done | bytes 65568 | tf_op jit(solution)/shard_map/ppermute | solution.py:381
  109.3 2.2 %collective-permute-start.37 = (f32[4,32,128]{2,1,0:T(8,128)S(1)}, f32[4,32,128]{2,1,0:T(8,128)S(1)}, u32[]{:S(2)}, u32[]{:S(2)}) collective-permute-start(f32[4,32,128]{2,1,0:T(8,128)S(1)} %pair.1.refs_0_), channel_id=1, source_target_pairs={{0,2},{1,3},{2,0},{3,1},{4,6},{5,7},{6,4},{7,5},{8,10},{9,11},{10,... | collective-permute-start | bytes 196616 | tf_op jit(solution)/shard_map/ppermute | solution.py:381
  112.1 1.8 %output.1 = f32[8,256,128]{2,1,0:T(8,128)} custom-call(s32[3]{0:T(128)S(1)} %pad_add_fusion.pos_ref, f32[4,128,256]{2,1,0:T(8,128)S(1)} %get-tuple-element.53.za, f32[4,128,256]{2,1,0:T(8,128)S(1)} %join.3.zb), custom_call_target="tpu_custom_call" | custom-call | tf_op jit(solution)/shard_map/output/pallas_call | solution.py:360
  114.4 1.3 %collective-permute-done.36.refs_1_ = f32[4,32,128]{2,1,0:T(8,128)S(1)} collective-permute-done((f32[4,32,128]{2,1,0:T(8,128)S(1)}, f32[4,32,128]{2,1,0:T(8,128)S(1)}, u32[]{:S(2)}, u32[]{:S(2)}) %collective-permute-start.36) | collective-permute-done | bytes 65568 | tf_op jit(solution)/shard_map/ppermute | solution.py:381
  (78 shorter events, 19.3 us)
Async XLA Ops:
  5.0 10.0 %collective-permute-start = (f32[160,256]{1,0:T(8,128)S(1)}, f32[160,256]{1,0:T(8,128)S(1)}, u32[]{:S(2)}, u32[]{:S(2)}) collective-permute-start(f32[160,256]{1,0:T(8,128)S(1)} %get-tuple-element.37), channel_id=1, source_target_pairs={{0,1},{1,0},{2,3},{3,2},{4,5},{5,4},{6,7},{7,6},{8,9},{9,8},{10,11... | collective-permute-start | bytes 491528 | tf_op jit(solution)/shard_map/ppermute | solution.py:381
  8.0 9.2 %collective-permute-start.1 = (f32[160,256]{1,0:T(8,128)S(1)}, f32[160,256]{1,0:T(8,128)S(1)}, u32[]{:S(2)}, u32[]{:S(2)}) collective-permute-start(f32[160,256]{1,0:T(8,128)S(1)} %get-tuple-element.38), channel_id=1, source_target_pairs={{0,2},{1,3},{2,0},{3,1},{4,6},{5,7},{6,4},{7,5},{8,10},{9,11},{10,... | collective-permute-start | bytes 491528 | tf_op jit(solution)/shard_map/ppermute | solution.py:381
  9.6 21.8 %collective-permute-start.2 = (f32[160,256]{1,0:T(8,128)S(1)}, f32[160,256]{1,0:T(8,128)S(1)}, u32[]{:S(2)}, u32[]{:S(2)}) collective-permute-start(f32[160,256]{1,0:T(8,128)S(1)} %get-tuple-element.39), channel_id=1, source_target_pairs={{0,4},{1,5},{2,6},{3,7},{4,0},{5,1},{6,2},{7,3},{8,12},{9,13},{10,... | collective-permute-start | bytes 491528 | tf_op jit(solution)/shard_map/ppermute | solution.py:381
  12.1 22.2 %collective-permute-start.3 = (f32[160,256]{1,0:T(8,128)S(1)}, f32[160,256]{1,0:T(8,128)S(1)}, u32[]{:S(2)}, u32[]{:S(2)}) collective-permute-start(f32[160,256]{1,0:T(8,128)S(1)} %get-tuple-element.40), channel_id=1, source_target_pairs={{0,5},{1,4},{2,7},{3,6},{4,1},{5,0},{6,3},{7,2},{8,13},{9,12},{10,... | collective-permute-start | bytes 491528 | tf_op jit(solution)/shard_map/ppermute | solution.py:381
  12.4 21.9 %collective-permute-start.4 = (f32[160,256]{1,0:T(8,128)S(1)}, f32[160,256]{1,0:T(8,128)S(1)}, u32[]{:S(2)}, u32[]{:S(2)}) collective-permute-start(f32[160,256]{1,0:T(8,128)S(1)} %get-tuple-element.41), channel_id=1, source_target_pairs={{0,6},{1,7},{2,4},{3,5},{4,2},{5,3},{6,0},{7,1},{8,14},{9,15},{10,... | collective-permute-start | bytes 491528 | tf_op jit(solution)/shard_map/ppermute | solution.py:381
  14.9 19.5 %collective-permute-start.5 = (f32[160,256]{1,0:T(8,128)S(1)}, f32[160,256]{1,0:T(8,128)S(1)}, u32[]{:S(2)}, u32[]{:S(2)}) collective-permute-start(f32[160,256]{1,0:T(8,128)S(1)} %get-tuple-element.42), channel_id=1, source_target_pairs={{0,7},{1,6},{2,5},{3,4},{4,3},{5,2},{6,1},{7,0},{8,15},{9,14},{10,... | collective-permute-start | bytes 491528 | tf_op jit(solution)/shard_map/ppermute | solution.py:381
  17.2 17.2 %collective-permute-start.6 = (f32[160,256]{1,0:T(8,128)S(1)}, f32[160,256]{1,0:T(8,128)S(1)}, u32[]{:S(2)}, u32[]{:S(2)}) collective-permute-start(f32[160,256]{1,0:T(8,128)S(1)} %get-tuple-element.43), channel_id=1, source_target_pairs={{0,3},{1,2},{2,1},{3,0},{4,7},{5,6},{6,5},{7,4},{8,11},{9,10},{10,... | collective-permute-start | bytes 491528 | tf_op jit(solution)/shard_map/ppermute | solution.py:381
  43.3 12.1 %collective-permute-start.7 = (f32[64,256]{1,0:T(8,128)S(1)}, f32[64,256]{1,0:T(8,128)S(1)}, u32[]{:S(2)}, u32[]{:S(2)}) collective-permute-start(f32[64,256]{1,0:T(8,128)S(1)} %get-tuple-element.46), channel_id=1, source_target_pairs={{0,1},{1,0},{2,3},{3,2},{4,5},{5,4},{6,7},{7,6},{8,9},{9,8},{10,11... | collective-permute-start | bytes 196616 | tf_op jit(solution)/shard_map/ppermute | solution.py:381
  45.4 12.4 %collective-permute-start.8 = (f32[64,256]{1,0:T(8,128)S(1)}, f32[64,256]{1,0:T(8,128)S(1)}, u32[]{:S(2)}, u32[]{:S(2)}) collective-permute-start(f32[64,256]{1,0:T(8,128)S(1)} %get-tuple-element.47), channel_id=1, source_target_pairs={{0,2},{1,3},{2,0},{3,1},{4,6},{5,7},{6,4},{7,5},{8,10},{9,11},{10,... | collective-permute-start | bytes 196616 | tf_op jit(solution)/shard_map/ppermute | solution.py:381
  51.5 7.8 %collective-permute-start.9 = (f32[64,256]{1,0:T(8,128)S(1)}, f32[64,256]{1,0:T(8,128)S(1)}, u32[]{:S(2)}, u32[]{:S(2)}) collective-permute-start(f32[64,256]{1,0:T(8,128)S(1)} %get-tuple-element.48), channel_id=1, source_target_pairs={{0,3},{1,2},{2,1},{3,0},{4,7},{5,6},{6,5},{7,4},{8,11},{9,10},{10,... | collective-permute-start | bytes 196616 | tf_op jit(solution)/shard_map/ppermute | solution.py:381
  51.5 9.3 %collective-permute-start.10 = (f32[64,256]{1,0:T(8,128)S(1)}, f32[64,256]{1,0:T(8,128)S(1)}, u32[]{:S(2)}, u32[]{:S(2)}) collective-permute-start(f32[64,256]{1,0:T(8,128)S(1)} %get-tuple-element.49), channel_id=1, source_target_pairs={{0,4},{1,5},{2,6},{3,7},{4,0},{5,1},{6,2},{7,3},{8,12},{9,13},{10,... | collective-permute-start | bytes 196616 | tf_op jit(solution)/shard_map/ppermute | solution.py:381
  54.5 9.2 %collective-permute-start.11 = (f32[64,256]{1,0:T(8,128)S(1)}, f32[64,256]{1,0:T(8,128)S(1)}, u32[]{:S(2)}, u32[]{:S(2)}) collective-permute-start(f32[64,256]{1,0:T(8,128)S(1)} %get-tuple-element.50), channel_id=1, source_target_pairs={{0,5},{1,4},{2,7},{3,6},{4,1},{5,0},{6,3},{7,2},{8,13},{9,12},{10,... | collective-permute-start | bytes 196616 | tf_op jit(solution)/shard_map/ppermute | solution.py:381
  55.4 8.9 %collective-permute-start.12 = (f32[64,256]{1,0:T(8,128)S(1)}, f32[64,256]{1,0:T(8,128)S(1)}, u32[]{:S(2)}, u32[]{:S(2)}) collective-permute-start(f32[64,256]{1,0:T(8,128)S(1)} %get-tuple-element.51), channel_id=1, source_target_pairs={{0,6},{1,7},{2,4},{3,5},{4,2},{5,3},{6,0},{7,1},{8,14},{9,15},{10,... | collective-permute-start | bytes 196616 | tf_op jit(solution)/shard_map/ppermute | solution.py:381
  57.8 9.8 %collective-permute-start.13 = (f32[64,256]{1,0:T(8,128)S(1)}, f32[64,256]{1,0:T(8,128)S(1)}, u32[]{:S(2)}, u32[]{:S(2)}) collective-permute-start(f32[64,256]{1,0:T(8,128)S(1)} %get-tuple-element.52), channel_id=1, source_target_pairs={{0,7},{1,6},{2,5},{3,4},{4,3},{5,2},{6,1},{7,0},{8,15},{9,14},{10,... | collective-permute-start | bytes 196616 | tf_op jit(solution)/shard_map/ppermute | solution.py:381
  59.3 10.2 %collective-permute-start.14 = (f32[64,256]{1,0:T(8,128)S(1)}, f32[64,256]{1,0:T(8,128)S(1)}, u32[]{:S(2)}, u32[]{:S(2)}) collective-permute-start(f32[64,256]{1,0:T(8,128)S(1)} %get-tuple-element.55), channel_id=1, source_target_pairs={{0,1},{1,0},{2,3},{3,2},{4,5},{5,4},{6,7},{7,6},{8,9},{9,8},{10,11... | collective-permute-start | bytes 196616 | tf_op jit(solution)/shard_map/ppermute | solution.py:381
  60.7 10.2 %collective-permute-start.15 = (f32[64,256]{1,0:T(8,128)S(1)}, f32[64,256]{1,0:T(8,128)S(1)}, u32[]{:S(2)}, u32[]{:S(2)}) collective-permute-start(f32[64,256]{1,0:T(8,128)S(1)} %get-tuple-element.56), channel_id=1, source_target_pairs={{0,2},{1,3},{2,0},{3,1},{4,6},{5,7},{6,4},{7,5},{8,10},{9,11},{10,... | collective-permute-start | bytes 196616 | tf_op jit(solution)/shard_map/ppermute | solution.py:381
  63.7 8.8 %collective-permute-start.16 = (f32[64,256]{1,0:T(8,128)S(1)}, f32[64,256]{1,0:T(8,128)S(1)}, u32[]{:S(2)}, u32[]{:S(2)}) collective-permute-start(f32[64,256]{1,0:T(8,128)S(1)} %get-tuple-element.57), channel_id=1, source_target_pairs={{0,3},{1,2},{2,1},{3,0},{4,7},{5,6},{6,5},{7,4},{8,11},{9,10},{10,... | collective-permute-start | bytes 196616 | tf_op jit(solution)/shard_map/ppermute | solution.py:381
  64.3 8.7 %collective-permute-start.17 = (f32[64,256]{1,0:T(8,128)S(1)}, f32[64,256]{1,0:T(8,128)S(1)}, u32[]{:S(2)}, u32[]{:S(2)}) collective-permute-start(f32[64,256]{1,0:T(8,128)S(1)} %get-tuple-element.58), channel_id=1, source_target_pairs={{0,4},{1,5},{2,6},{3,7},{4,0},{5,1},{6,2},{7,3},{8,12},{9,13},{10,... | collective-permute-start | bytes 196616 | tf_op jit(solution)/shard_map/ppermute | solution.py:381
  67.6 7.0 %collective-permute-start.18 = (f32[64,256]{1,0:T(8,128)S(1)}, f32[64,256]{1,0:T(8,128)S(1)}, u32[]{:S(2)}, u32[]{:S(2)}) collective-permute-start(f32[64,256]{1,0:T(8,128)S(1)} %get-tuple-element.59), channel_id=1, source_target_pairs={{0,5},{1,4},{2,7},{3,6},{4,1},{5,0},{6,3},{7,2},{8,13},{9,12},{10,... | collective-permute-start | bytes 196616 | tf_op jit(solution)/shard_map/ppermute | solution.py:381
  69.5 6.7 %collective-permute-start.19 = (f32[64,256]{1,0:T(8,128)S(1)}, f32[64,256]{1,0:T(8,128)S(1)}, u32[]{:S(2)}, u32[]{:S(2)}) collective-permute-start(f32[64,256]{1,0:T(8,128)S(1)} %get-tuple-element.60), channel_id=1, source_target_pairs={{0,6},{1,7},{2,4},{3,5},{4,2},{5,3},{6,0},{7,1},{8,14},{9,15},{10,... | collective-permute-start | bytes 196616 | tf_op jit(solution)/shard_map/ppermute | solution.py:381
  70.9 12.2 %collective-permute-start.21 = (f32[1,128,256]{2,1,0:T(8,128)S(1)}, f32[1,128,256]{2,1,0:T(8,128)S(1)}, u32[]{:S(2)}, u32[]{:S(2)}) collective-permute-start(f32[1,128,256]{2,1,0:T(8,128)S(1)} %get-tuple-element.62), channel_id=1, source_target_pairs={{0,16},{8,24},{16,0},{24,8},{1,17},{9,25},{17,1},{25,9},{2,18},{10... | collective-permute-start | bytes 393224 | tf_op jit(solution)/shard_map/ppermute | solution.py:381
  72.5 10.7 %collective-permute-start.22 = (f32[1,128,256]{2,1,0:T(8,128)S(1)}, f32[1,128,256]{2,1,0:T(8,128)S(1)}, u32[]{:S(2)}, u32[]{:S(2)}) collective-permute-start(f32[1,128,256]{2,1,0:T(8,128)S(1)} %get-tuple-element.63), channel_id=1, source_target_pairs={{0,16},{8,24},{16,0},{24,8},{1,17},{9,25},{17,1},{25,9},{2,18},{10... | collective-permute-start | bytes 393224 | tf_op jit(solution)/shard_map/ppermute | solution.py:381
  73.0 10.2 %collective-permute-start.23 = (f32[1,128,256]{2,1,0:T(8,128)S(1)}, f32[1,128,256]{2,1,0:T(8,128)S(1)}, u32[]{:S(2)}, u32[]{:S(2)}) collective-permute-start(f32[1,128,256]{2,1,0:T(8,128)S(1)} %get-tuple-element.64), channel_id=1, source_target_pairs={{0,16},{8,24},{16,0},{24,8},{1,17},{9,25},{17,1},{25,9},{2,18},{10... | collective-permute-start | bytes 393224 | tf_op jit(solution)/shard_map/ppermute | solution.py:381
  74.6 8.7 %collective-permute-start.24 = (f32[1,128,256]{2,1,0:T(8,128)S(1)}, f32[1,128,256]{2,1,0:T(8,128)S(1)}, u32[]{:S(2)}, u32[]{:S(2)}) collective-permute-start(f32[1,128,256]{2,1,0:T(8,128)S(1)} %get-tuple-element.65), channel_id=1, source_target_pairs={{0,16},{8,24},{16,0},{24,8},{1,17},{9,25},{17,1},{25,9},{2,18},{10... | collective-permute-start | bytes 393224 | tf_op jit(solution)/shard_map/ppermute | solution.py:381
  76.2 7.0 %collective-permute-start.20 = (f32[64,256]{1,0:T(8,128)S(1)}, f32[64,256]{1,0:T(8,128)S(1)}, u32[]{:S(2)}, u32[]{:S(2)}) collective-permute-start(f32[64,256]{1,0:T(8,128)S(1)} %get-tuple-element.61), channel_id=1, source_target_pairs={{0,7},{1,6},{2,5},{3,4},{4,3},{5,2},{6,1},{7,0},{8,15},{9,14},{10,... | collective-permute-start | bytes 196616 | tf_op jit(solution)/shard_map/ppermute | solution.py:381
  83.2 4.3 %collective-permute-start.25 = (f32[4,128,256]{2,1,0:T(8,128)S(1)}, f32[4,128,256]{2,1,0:T(8,128)S(1)}, u32[]{:S(2)}, u32[]{:S(2)}) collective-permute-start(f32[4,128,256]{2,1,0:T(8,128)S(1)} %get-tuple-element.53.za), channel_id=1, source_target_pairs={{0,8},{8,0},{16,24},{24,16},{1,9},{9,1},{17,25},{25,17},{2,10},{10... | collective-permute-start | bytes 1572872 | tf_op jit(solution)/shard_map/ppermute | solution.py:381
  89.8 7.9 %collective-permute-start.31 = (f32[4,64,128]{2,1,0:T(8,128)S(1)}, f32[4,64,128]{2,1,0:T(8,128)S(1)}, u32[]{:S(2)}, u32[]{:S(2)}) collective-permute-start(f32[4,64,128]{2,1,0:T(8,128)S(1)} %get-tuple-element.67), channel_id=1, source_target_pairs={{0,1},{1,0},{2,3},{3,2},{4,5},{5,4},{6,7},{7,6},{8,9},{9,8},{10,11... | collective-permute-start | bytes 393224 | tf_op jit(solution)/shard_map/ppermute | solution.py:381
  92.5 5.2 %collective-permute-start.33 = (f32[2,64,128]{2,1,0:T(8,128)S(1)}, f32[2,64,128]{2,1,0:T(8,128)S(1)}, u32[]{:S(2)}, u32[]{:S(2)}) collective-permute-start(f32[2,64,128]{2,1,0:T(8,128)S(1)} %get-tuple-element.69), channel_id=1, source_target_pairs={{0,17},{1,16},{2,19},{3,18},{4,21},{5,20},{6,23},{7,22},{8,25},{9,... | collective-permute-start | bytes 196616 | tf_op jit(solution)/shard_map/ppermute | solution.py:387
  98.3 4.3 %collective-permute-start.34 = (f32[4,32,128]{2,1,0:T(8,128)S(1)}, f32[4,32,128]{2,1,0:T(8,128)S(1)}, u32[]{:S(2)}, u32[]{:S(2)}) collective-permute-start(f32[4,32,128]{2,1,0:T(8,128)S(1)} %get-tuple-element.71), channel_id=1, source_target_pairs={{0,2},{1,3},{2,0},{3,1},{4,6},{5,7},{6,4},{7,5},{8,10},{9,11},{10,... | collective-permute-start | bytes 196616 | tf_op jit(solution)/shard_map/ppermute | solution.py:381
  102.6 5.4 %collective-permute-start.35 = (f32[4,32,128]{2,1,0:T(8,128)S(1)}, f32[4,32,128]{2,1,0:T(8,128)S(1)}, u32[]{:S(2)}, u32[]{:S(2)}) collective-permute-start(f32[4,32,128]{2,1,0:T(8,128)S(1)} %add.80.mine), channel_id=1, source_target_pairs={{0,4},{1,5},{2,6},{3,7},{4,0},{5,1},{6,2},{7,3},{8,12},{9,13},{10,... | collective-permute-start | bytes 196616 | tf_op jit(solution)/shard_map/ppermute | solution.py:381
  108.5 5.4 %collective-permute-start.38 = (f32[4,32,128]{2,1,0:T(8,128)S(1)}, f32[4,32,128]{2,1,0:T(8,128)S(1)}, u32[]{:S(2)}, u32[]{:S(2)}) collective-permute-start(f32[4,32,128]{2,1,0:T(8,128)S(1)} %pair.1.refs_0_), channel_id=1, source_target_pairs={{0,3},{1,2},{2,1},{3,0},{4,7},{5,6},{6,5},{7,4},{8,11},{9,10},{10,... | collective-permute-start | bytes 196616 | tf_op jit(solution)/shard_map/ppermute | solution.py:381
  109.3 5.1 %collective-permute-start.37 = (f32[4,32,128]{2,1,0:T(8,128)S(1)}, f32[4,32,128]{2,1,0:T(8,128)S(1)}, u32[]{:S(2)}, u32[]{:S(2)}) collective-permute-start(f32[4,32,128]{2,1,0:T(8,128)S(1)} %pair.1.refs_0_), channel_id=1, source_target_pairs={{0,2},{1,3},{2,0},{3,1},{4,6},{5,7},{6,4},{7,5},{8,10},{9,11},{10,... | collective-permute-start | bytes 196616 | tf_op jit(solution)/shard_map/ppermute | solution.py:381
  (14 other events, 112.0 us)

commit v10 on v9

--- a/solution.py
+++ b/solution.py
@@ -51,7 +51,9 @@
 
 
 def dot3(ah, al, bh, bl, dims=NN):
-    return dot(ah, bh, dims) + dot(al, bh, dims) + dot(ah, bl, dims)
+    rows = ah.shape[0]
+    both = dot(jnp.concatenate([ah, al], axis=0), bh, dims)
+    return both[:rows] + both[rows:] + dot(ah, bl, dims)
 
 
 def lateral_matrix():
@@ -248,13 +250,13 @@
             out[...] = (y * scale[None]).reshape(half * nb, LAT)
 
 
-def join_kernel(nd, nb, outs, pos_ref, *refs):
-    pieces, (z_ref, *parts) = refs[:nd], refs[-outs:]
+def join_kernel(order, nb, outs, pos_ref, *refs):
+    pieces, (z_ref, *parts) = refs[: len(order)], refs[-outs:]
     i = pos_ref[0]
-    for j in range(nd):
+    for piece, j in zip(pieces, order):
         rows = pl.ds(pl.multiple_of((i ^ j) * nb, nb), nb)
         for q in range(SLAB // 2):
-            z_ref[q, rows] = pieces[j][q * nb : (q + 1) * nb]
+            z_ref[q, rows] = piece[q * nb : (q + 1) * nb]
     for k, part in enumerate(parts):
         part[...] = z_ref[k * part.shape[0] : (k + 1) * part.shape[0]]
 
@@ -489,20 +491,20 @@
     nd, half = len(first), SLAB // 2
     nb = bands // nd
 
-    def join(pieces, outs, ties):
+    def join(pieces, order, outs, ties):
         return call(
-            functools.partial(join_kernel, nd, nb, len(outs) + 1),
+            functools.partial(join_kernel, order, nb, len(outs) + 1),
             [shape(half, bands, LAT)] + outs,
-            [pos] + pieces,
+            [pos] + [pieces[j] for j in order],
             (),
             "join",
             ties,
         )
 
-    za, *sends = join(first, [shape(half // PARTS, bands, LAT)] * PARTS, [])
+    za, *sends = join(first, (0, 1, 2, 4, 5, 6, 7, 3), [shape(half // PARTS, bands, LAT)] * PARTS, [])
     far = [xor_permute(p, "band", 2) for p in sends]
     core_a = xor_permute(za, "band", 1)
-    (zb,) = join(second, [], far)
+    (zb,) = join(second, range(nd), [], far)
     core_b = xor_permute(zb, "band", 1)
     far_core = [xor_permute(p, "band", 1) for p in far]
     part, share = shape(4, bands // 2, bands), shape(2, bands // 2, bands)

time: 117 us -> 116 us (level)
    ppermute x38, starting transfers between devices: 52.1 us -> 50.6 us  [xor_permute(): return lax.ppermute(value, axis, [(k, k ^ step) for k in range(count)])]
where the time goes in v10:
time: 116 us; the launch traced here: 115 us
  starting transfers between devices  51.9 us (45%)
  waiting for transfers between devices  41.9 us (36%)
  Pallas kernels  16.1 us (14%)
  local copies, waits for them, and re-layouts  3.45 us (3%)
  other arithmetic  1.25 us (1%)
    ppermute x38, starting transfers between devices, xor_permute(): return lax.ppermute(value, axis, [(k, k ^ step) for k in range(count)])  50.6 us
    ppermute x38, waiting for transfers between devices, xor_permute(): return lax.ppermute(value, axis, [(k, k ^ step) for k in range(count)])  38.7 us
    pallas_call x9, Pallas kernels, call(): pl.pallas_call(kernel, out_shape=out_shape, in_specs=specs, out_specs=pl....  16.1 us
    ppermute x1, waiting for transfers between devices, both_permute(): return lax.ppermute(value, ('band', 'dom'), pairs)  3.17 us
    unnamed x14, local copies, waits for them, and re-layouts  2.49 us
  transfers between devices with their start and end apart: 39, of which 13 were waited for; matrix products, arithmetic and copies ran while one was open for 0% of the time, Pallas kernels for 3%

profile of v10, /device:TPU:0, one launch (start us, length us, event | category | flops | bytes accessed | tf_op | source)
XLA Modules:
  0.0 115.5 jit_solution(6307043344518975253)
XLA Ops:
  5.0 3.0 %collective-permute-start = (f32[160,256]{1,0:T(8,128)S(1)}, f32[160,256]{1,0:T(8,128)S(1)}, u32[]{:S(2)}, u32[]{:S(2)}) collective-permute-start(f32[160,256]{1,0:T(8,128)S(1)} %get-tuple-element.37), channel_id=1, source_target_pairs={{0,1},{1,0},{2,3},{3,2},{4,5},{5,4},{6,7},{7,6},{8,9},{9,8},{10,11... | collective-permute-start | bytes 491528 | tf_op jit(solution)/shard_map/ppermute | solution.py:383
  8.0 1.6 %collective-permute-start.1 = (f32[160,256]{1,0:T(8,128)S(1)}, f32[160,256]{1,0:T(8,128)S(1)}, u32[]{:S(2)}, u32[]{:S(2)}) collective-permute-start(f32[160,256]{1,0:T(8,128)S(1)} %get-tuple-element.38), channel_id=1, source_target_pairs={{0,2},{1,3},{2,0},{3,1},{4,6},{5,7},{6,4},{7,5},{8,10},{9,11},{10,... | collective-permute-start | bytes 491528 | tf_op jit(solution)/shard_map/ppermute | solution.py:383
  9.6 2.6 %collective-permute-start.2 = (f32[160,256]{1,0:T(8,128)S(1)}, f32[160,256]{1,0:T(8,128)S(1)}, u32[]{:S(2)}, u32[]{:S(2)}) collective-permute-start(f32[160,256]{1,0:T(8,128)S(1)} %get-tuple-element.39), channel_id=1, source_target_pairs={{0,4},{1,5},{2,6},{3,7},{4,0},{5,1},{6,2},{7,3},{8,12},{9,13},{10,... | collective-permute-start | bytes 491528 | tf_op jit(solution)/shard_map/ppermute | solution.py:383
  12.4 2.5 %collective-permute-start.4 = (f32[160,256]{1,0:T(8,128)S(1)}, f32[160,256]{1,0:T(8,128)S(1)}, u32[]{:S(2)}, u32[]{:S(2)}) collective-permute-start(f32[160,256]{1,0:T(8,128)S(1)} %get-tuple-element.41), channel_id=1, source_target_pairs={{0,6},{1,7},{2,4},{3,5},{4,2},{5,3},{6,0},{7,1},{8,14},{9,15},{10,... | collective-permute-start | bytes 491528 | tf_op jit(solution)/shard_map/ppermute | solution.py:383
  14.9 2.3 %collective-permute-start.5 = (f32[160,256]{1,0:T(8,128)S(1)}, f32[160,256]{1,0:T(8,128)S(1)}, u32[]{:S(2)}, u32[]{:S(2)}) collective-permute-start(f32[160,256]{1,0:T(8,128)S(1)} %get-tuple-element.42), channel_id=1, source_target_pairs={{0,7},{1,6},{2,5},{3,4},{4,3},{5,2},{6,1},{7,0},{8,15},{9,14},{10,... | collective-permute-start | bytes 491528 | tf_op jit(solution)/shard_map/ppermute | solution.py:383
  18.0 13.4 %collective-permute-done.2.refs_2_ = f32[160,256]{1,0:T(8,128)S(1)} collective-permute-done((f32[160,256]{1,0:T(8,128)S(1)}, f32[160,256]{1,0:T(8,128)S(1)}, u32[]{:S(2)}, u32[]{:S(2)}) %collective-permute-start.2) | collective-permute-done | bytes 163872 | tf_op jit(solution)/shard_map/ppermute | solution.py:383
  31.4 3.0 %collective-permute-done.3.refs_3_ = f32[160,256]{1,0:T(8,128)S(1)} collective-permute-done((f32[160,256]{1,0:T(8,128)S(1)}, f32[160,256]{1,0:T(8,128)S(1)}, u32[]{:S(2)}, u32[]{:S(2)}) %collective-permute-start.3) | collective-permute-done | bytes 163872 | tf_op jit(solution)/shard_map/ppermute | solution.py:383
  34.4 7.9 %filter.1 = (f32[64,256]{1,0:T(8,128)S(1)}, f32[64,256]{1,0:T(8,128)S(1)}, f32[64,256]{1,0:T(8,128)S(1)}, f32[64,256]{1,0:T(8,128)S(1)}, f32[64,256]{1,0:T(8,128...) custom-call(s32[3]{0:T(128)S(1)} %pad_add_fusion.pos_ref, ...), custom_call_target="tpu_custom_call" | custom-call | tf_op jit(solution)/shard_map/filter/pallas_call | solution.py:362
  42.3 2.1 %collective-permute-start.7 = (f32[64,256]{1,0:T(8,128)S(1)}, f32[64,256]{1,0:T(8,128)S(1)}, u32[]{:S(2)}, u32[]{:S(2)}) collective-permute-start(f32[64,256]{1,0:T(8,128)S(1)} %get-tuple-element.46), channel_id=1, source_target_pairs={{0,1},{1,0},{2,3},{3,2},{4,5},{5,4},{6,7},{7,6},{8,9},{9,8},{10,11... | collective-permute-start | bytes 196616 | tf_op jit(solution)/shard_map/ppermute | solution.py:383
  44.4 6.1 %collective-permute-start.8 = (f32[64,256]{1,0:T(8,128)S(1)}, f32[64,256]{1,0:T(8,128)S(1)}, u32[]{:S(2)}, u32[]{:S(2)}) collective-permute-start(f32[64,256]{1,0:T(8,128)S(1)} %get-tuple-element.47), channel_id=1, source_target_pairs={{0,2},{1,3},{2,0},{3,1},{4,6},{5,7},{6,4},{7,5},{8,10},{9,11},{10,... | collective-permute-start | bytes 196616 | tf_op jit(solution)/shard_map/ppermute | solution.py:383
  51.5 1.9 %collective-permute-start.10 = (f32[64,256]{1,0:T(8,128)S(1)}, f32[64,256]{1,0:T(8,128)S(1)}, u32[]{:S(2)}, u32[]{:S(2)}) collective-permute-start(f32[64,256]{1,0:T(8,128)S(1)} %get-tuple-element.49), channel_id=1, source_target_pairs={{0,5},{1,4},{2,7},{3,6},{4,1},{5,0},{6,3},{7,2},{8,13},{9,12},{10,... | collective-permute-start | bytes 196616 | tf_op jit(solution)/shard_map/ppermute | solution.py:383
  53.4 2.5 %collective-permute-start.11 = (f32[64,256]{1,0:T(8,128)S(1)}, f32[64,256]{1,0:T(8,128)S(1)}, u32[]{:S(2)}, u32[]{:S(2)}) collective-permute-start(f32[64,256]{1,0:T(8,128)S(1)} %get-tuple-element.50), channel_id=1, source_target_pairs={{0,6},{1,7},{2,4},{3,5},{4,2},{5,3},{6,0},{7,1},{8,14},{9,15},{10,... | collective-permute-start | bytes 196616 | tf_op jit(solution)/shard_map/ppermute | solution.py:383
  55.9 2.2 %collective-permute-start.12 = (f32[64,256]{1,0:T(8,128)S(1)}, f32[64,256]{1,0:T(8,128)S(1)}, u32[]{:S(2)}, u32[]{:S(2)}) collective-permute-start(f32[64,256]{1,0:T(8,128)S(1)} %get-tuple-element.51), channel_id=1, source_target_pairs={{0,7},{1,6},{2,5},{3,4},{4,3},{5,2},{6,1},{7,0},{8,15},{9,14},{10,... | collective-permute-start | bytes 196616 | tf_op jit(solution)/shard_map/ppermute | solution.py:383
  58.2 2.1 %collective-permute-done.9.refs_3_ = f32[64,256]{1,0:T(8,128)S(1)} collective-permute-done((f32[64,256]{1,0:T(8,128)S(1)}, f32[64,256]{1,0:T(8,128)S(1)}, u32[]{:S(2)}, u32[]{:S(2)}) %collective-permute-start.9) | collective-permute-done | bytes 65568 | tf_op jit(solution)/shard_map/ppermute | solution.py:383
  60.3 1.6 %collective-permute-done.10.refs_4_ = f32[64,256]{1,0:T(8,128)S(1)} collective-permute-done((f32[64,256]{1,0:T(8,128)S(1)}, f32[64,256]{1,0:T(8,128)S(1)}, u32[]{:S(2)}, u32[]{:S(2)}) %collective-permute-start.10) | collective-permute-done | bytes 65568 | tf_op jit(solution)/shard_map/ppermute | solution.py:383
  61.9 2.3 %collective-permute-start.16 = (f32[64,256]{1,0:T(8,128)S(1)}, f32[64,256]{1,0:T(8,128)S(1)}, u32[]{:S(2)}, u32[]{:S(2)}) collective-permute-start(f32[64,256]{1,0:T(8,128)S(1)} %get-tuple-element.57), channel_id=1, source_target_pairs={{0,3},{1,2},{2,1},{3,0},{4,7},{5,6},{6,5},{7,4},{8,11},{9,10},{10,... | collective-permute-start | bytes 196616 | tf_op jit(solution)/shard_map/ppermute | solution.py:383
  64.2 1.5 %collective-permute-start.17 = (f32[64,256]{1,0:T(8,128)S(1)}, f32[64,256]{1,0:T(8,128)S(1)}, u32[]{:S(2)}, u32[]{:S(2)}) collective-permute-start(f32[64,256]{1,0:T(8,128)S(1)} %get-tuple-element.58), channel_id=1, source_target_pairs={{0,4},{1,5},{2,6},{3,7},{4,0},{5,1},{6,2},{7,3},{8,12},{9,13},{10,... | collective-permute-start | bytes 196616 | tf_op jit(solution)/shard_map/ppermute | solution.py:383
  65.6 2.1 %collective-permute-start.18 = (f32[64,256]{1,0:T(8,128)S(1)}, f32[64,256]{1,0:T(8,128)S(1)}, u32[]{:S(2)}, u32[]{:S(2)}) collective-permute-start(f32[64,256]{1,0:T(8,128)S(1)} %get-tuple-element.59), channel_id=1, source_target_pairs={{0,5},{1,4},{2,7},{3,6},{4,1},{5,0},{6,3},{7,2},{8,13},{9,12},{10,... | collective-permute-start | bytes 196616 | tf_op jit(solution)/shard_map/ppermute | solution.py:383
  68.3 2.0 %collective-permute-start.19 = (f32[64,256]{1,0:T(8,128)S(1)}, f32[64,256]{1,0:T(8,128)S(1)}, u32[]{:S(2)}, u32[]{:S(2)}) collective-permute-start(f32[64,256]{1,0:T(8,128)S(1)} %get-tuple-element.60), channel_id=1, source_target_pairs={{0,6},{1,7},{2,4},{3,5},{4,2},{5,3},{6,0},{7,1},{8,14},{9,15},{10,... | collective-permute-start | bytes 196616 | tf_op jit(solution)/shard_map/ppermute | solution.py:383
  70.4 1.5 %collective-permute-start.21 = (f32[1,128,256]{2,1,0:T(8,128)S(1)}, f32[1,128,256]{2,1,0:T(8,128)S(1)}, u32[]{:S(2)}, u32[]{:S(2)}) collective-permute-start(f32[1,128,256]{2,1,0:T(8,128)S(1)} %get-tuple-element.62), channel_id=1, source_target_pairs={{0,16},{8,24},{16,0},{24,8},{1,17},{9,25},{17,1},{25,9},{2,18},{10... | collective-permute-start | bytes 393224 | tf_op jit(solution)/shard_map/ppermute | solution.py:383
  72.4 1.5 %collective-permute-start.23 = (f32[1,128,256]{2,1,0:T(8,128)S(1)}, f32[1,128,256]{2,1,0:T(8,128)S(1)}, u32[]{:S(2)}, u32[]{:S(2)}) collective-permute-start(f32[1,128,256]{2,1,0:T(8,128)S(1)} %get-tuple-element.64), channel_id=1, source_target_pairs={{0,16},{8,24},{16,0},{24,8},{1,17},{9,25},{17,1},{25,9},{2,18},{10... | collective-permute-start | bytes 393224 | tf_op jit(solution)/shard_map/ppermute | solution.py:383
  75.1 2.6 %collective-permute-start.20 = (f32[64,256]{1,0:T(8,128)S(1)}, f32[64,256]{1,0:T(8,128)S(1)}, u32[]{:S(2)}, u32[]{:S(2)}) collective-permute-start(f32[64,256]{1,0:T(8,128)S(1)} %get-tuple-element.61), channel_id=1, source_target_pairs={{0,7},{1,6},{2,5},{3,4},{4,3},{5,2},{6,1},{7,0},{8,15},{9,14},{10,... | collective-permute-start | bytes 196616 | tf_op jit(solution)/shard_map/ppermute | solution.py:383
  77.7 4.3 %collective-permute-done.20.refs_7_ = f32[64,256]{1,0:T(8,128)S(1)} collective-permute-done((f32[64,256]{1,0:T(8,128)S(1)}, f32[64,256]{1,0:T(8,128)S(1)}, u32[]{:S(2)}, u32[]{:S(2)}) %collective-permute-start.20) | collective-permute-done | bytes 65568 | tf_op jit(solution)/shard_map/ppermute | solution.py:383
  86.4 2.3 %blocks.1 = (f32[4,64,128]{2,1,0:T(8,128)S(1)}, f32[4,64,128]{2,1,0:T(8,128)S(1)}, f32[2,64,128]{2,1,0:T(8,128)S(1)}, f32[2,64,128]{2,1,0:T(8,128)S(1)}) custom-call(s32[3]{0:T(128)S(1)} %pad_add_fusion.pos_ref, f32[4,128,256]{2,1,0:T(8,128)S(1)} %get-tuple-element.53.za, f32[4,128,256]{2,1,0:T(8,128)S(1)} %join.3.zb, ...), custom_call_target="tpu_custom_call" | custom-call | tf_op jit(solution)/shard_map/blocks/pallas_call | solution.py:362
  89.5 1.5 %collective-permute-start.32 = (f32[2,64,128]{2,1,0:T(8,128)S(1)}, f32[2,64,128]{2,1,0:T(8,128)S(1)}, u32[]{:S(2)}, u32[]{:S(2)}) collective-permute-start(f32[2,64,128]{2,1,0:T(8,128)S(1)} %get-tuple-element.68), channel_id=1, source_target_pairs={{0,16},{8,24},{16,0},{24,8},{1,17},{9,25},{17,1},{25,9},{2,18},{10... | collective-permute-start | bytes 196616 | tf_op jit(solution)/shard_map/ppermute | solution.py:383
  92.3 1.5 %collective-permute-done.32.back = f32[2,64,128]{2,1,0:T(8,128)S(1)} collective-permute-done((f32[2,64,128]{2,1,0:T(8,128)S(1)}, f32[2,64,128]{2,1,0:T(8,128)S(1)}, u32[]{:S(2)}, u32[]{:S(2)}) %collective-permute-start.32) | collective-permute-done | bytes 65568 | tf_op jit(solution)/shard_map/ppermute | solution.py:383
  93.7 3.2 %collective-permute-done.33.back_other = f32[2,64,128]{2,1,0:T(8,128)S(1)} collective-permute-done((f32[2,64,128]{2,1,0:T(8,128)S(1)}, f32[2,64,128]{2,1,0:T(8,128)S(1)}, u32[]{:S(2)}, u32[]{:S(2)}) %collective-permute-start.33) | collective-permute-done | bytes 65568 | tf_op jit(solution)/shard_map/ppermute | solution.py:389
  97.6 4.3 %collective-permute-done.34 = f32[4,32,128]{2,1,0:T(8,128)S(1)} collective-permute-done((f32[4,32,128]{2,1,0:T(8,128)S(1)}, f32[4,32,128]{2,1,0:T(8,128)S(1)}, u32[]{:S(2)}, u32[]{:S(2)}) %collective-permute-start.34) | collective-permute-done | bytes 65568 | tf_op jit(solution)/shard_map/ppermute | solution.py:383
  102.5 4.7 %collective-permute-done.35.other = f32[4,32,128]{2,1,0:T(8,128)S(1)} collective-permute-done((f32[4,32,128]{2,1,0:T(8,128)S(1)}, f32[4,32,128]{2,1,0:T(8,128)S(1)}, u32[]{:S(2)}, u32[]{:S(2)}) %collective-permute-start.35) | collective-permute-done | bytes 65568 | tf_op jit(solution)/shard_map/ppermute | solution.py:383
  107.8 2.1 %collective-permute-start.37 = (f32[4,32,128]{2,1,0:T(8,128)S(1)}, f32[4,32,128]{2,1,0:T(8,128)S(1)}, u32[]{:S(2)}, u32[]{:S(2)}) collective-permute-start(f32[4,32,128]{2,1,0:T(8,128)S(1)} %pair.1.refs_0_), channel_id=1, source_target_pairs={{0,2},{1,3},{2,0},{3,1},{4,6},{5,7},{6,4},{7,5},{8,10},{9,11},{10,... | collective-permute-start | bytes 196616 | tf_op jit(solution)/shard_map/ppermute | solution.py:383
  109.9 1.4 %collective-permute-start.36 = (f32[4,32,128]{2,1,0:T(8,128)S(1)}, f32[4,32,128]{2,1,0:T(8,128)S(1)}, u32[]{:S(2)}, u32[]{:S(2)}) collective-permute-start(f32[4,32,128]{2,1,0:T(8,128)S(1)} %pair.1.refs_0_), channel_id=1, source_target_pairs={{0,1},{1,0},{2,3},{3,2},{4,5},{5,4},{6,7},{7,6},{8,9},{9,8},{10,11... | collective-permute-start | bytes 196616 | tf_op jit(solution)/shard_map/ppermute | solution.py:383
  111.3 1.8 %output.1 = f32[8,256,128]{2,1,0:T(8,128)} custom-call(s32[3]{0:T(128)S(1)} %pad_add_fusion.pos_ref, f32[4,128,256]{2,1,0:T(8,128)S(1)} %get-tuple-element.53.za, f32[4,128,256]{2,1,0:T(8,128)S(1)} %join.3.zb), custom_call_target="tpu_custom_call" | custom-call | tf_op jit(solution)/shard_map/output/pallas_call | solution.py:362
  (78 shorter events, 19.3 us)
Async XLA Ops:
  5.0 10.0 %collective-permute-start = (f32[160,256]{1,0:T(8,128)S(1)}, f32[160,256]{1,0:T(8,128)S(1)}, u32[]{:S(2)}, u32[]{:S(2)}) collective-permute-start(f32[160,256]{1,0:T(8,128)S(1)} %get-tuple-element.37), channel_id=1, source_target_pairs={{0,1},{1,0},{2,3},{3,2},{4,5},{5,4},{6,7},{7,6},{8,9},{9,8},{10,11... | collective-permute-start | bytes 491528 | tf_op jit(solution)/shard_map/ppermute | solution.py:383
  8.0 9.2 %collective-permute-start.1 = (f32[160,256]{1,0:T(8,128)S(1)}, f32[160,256]{1,0:T(8,128)S(1)}, u32[]{:S(2)}, u32[]{:S(2)}) collective-permute-start(f32[160,256]{1,0:T(8,128)S(1)} %get-tuple-element.38), channel_id=1, source_target_pairs={{0,2},{1,3},{2,0},{3,1},{4,6},{5,7},{6,4},{7,5},{8,10},{9,11},{10,... | collective-permute-start | bytes 491528 | tf_op jit(solution)/shard_map/ppermute | solution.py:383
  9.6 21.8 %collective-permute-start.2 = (f32[160,256]{1,0:T(8,128)S(1)}, f32[160,256]{1,0:T(8,128)S(1)}, u32[]{:S(2)}, u32[]{:S(2)}) collective-permute-start(f32[160,256]{1,0:T(8,128)S(1)} %get-tuple-element.39), channel_id=1, source_target_pairs={{0,4},{1,5},{2,6},{3,7},{4,0},{5,1},{6,2},{7,3},{8,12},{9,13},{10,... | collective-permute-start | bytes 491528 | tf_op jit(solution)/shard_map/ppermute | solution.py:383
  12.1 22.2 %collective-permute-start.3 = (f32[160,256]{1,0:T(8,128)S(1)}, f32[160,256]{1,0:T(8,128)S(1)}, u32[]{:S(2)}, u32[]{:S(2)}) collective-permute-start(f32[160,256]{1,0:T(8,128)S(1)} %get-tuple-element.40), channel_id=1, source_target_pairs={{0,5},{1,4},{2,7},{3,6},{4,1},{5,0},{6,3},{7,2},{8,13},{9,12},{10,... | collective-permute-start | bytes 491528 | tf_op jit(solution)/shard_map/ppermute | solution.py:383
  12.4 21.9 %collective-permute-start.4 = (f32[160,256]{1,0:T(8,128)S(1)}, f32[160,256]{1,0:T(8,128)S(1)}, u32[]{:S(2)}, u32[]{:S(2)}) collective-permute-start(f32[160,256]{1,0:T(8,128)S(1)} %get-tuple-element.41), channel_id=1, source_target_pairs={{0,6},{1,7},{2,4},{3,5},{4,2},{5,3},{6,0},{7,1},{8,14},{9,15},{10,... | collective-permute-start | bytes 491528 | tf_op jit(solution)/shard_map/ppermute | solution.py:383
  14.9 19.5 %collective-permute-start.5 = (f32[160,256]{1,0:T(8,128)S(1)}, f32[160,256]{1,0:T(8,128)S(1)}, u32[]{:S(2)}, u32[]{:S(2)}) collective-permute-start(f32[160,256]{1,0:T(8,128)S(1)} %get-tuple-element.42), channel_id=1, source_target_pairs={{0,7},{1,6},{2,5},{3,4},{4,3},{5,2},{6,1},{7,0},{8,15},{9,14},{10,... | collective-permute-start | bytes 491528 | tf_op jit(solution)/shard_map/ppermute | solution.py:383
  17.2 17.2 %collective-permute-start.6 = (f32[160,256]{1,0:T(8,128)S(1)}, f32[160,256]{1,0:T(8,128)S(1)}, u32[]{:S(2)}, u32[]{:S(2)}) collective-permute-start(f32[160,256]{1,0:T(8,128)S(1)} %get-tuple-element.43), channel_id=1, source_target_pairs={{0,3},{1,2},{2,1},{3,0},{4,7},{5,6},{6,5},{7,4},{8,11},{9,10},{10,... | collective-permute-start | bytes 491528 | tf_op jit(solution)/shard_map/ppermute | solution.py:383
  42.3 13.6 %collective-permute-start.7 = (f32[64,256]{1,0:T(8,128)S(1)}, f32[64,256]{1,0:T(8,128)S(1)}, u32[]{:S(2)}, u32[]{:S(2)}) collective-permute-start(f32[64,256]{1,0:T(8,128)S(1)} %get-tuple-element.46), channel_id=1, source_target_pairs={{0,1},{1,0},{2,3},{3,2},{4,5},{5,4},{6,7},{7,6},{8,9},{9,8},{10,11... | collective-permute-start | bytes 196616 | tf_op jit(solution)/shard_map/ppermute | solution.py:383
  44.4 13.7 %collective-permute-start.8 = (f32[64,256]{1,0:T(8,128)S(1)}, f32[64,256]{1,0:T(8,128)S(1)}, u32[]{:S(2)}, u32[]{:S(2)}) collective-permute-start(f32[64,256]{1,0:T(8,128)S(1)} %get-tuple-element.47), channel_id=1, source_target_pairs={{0,2},{1,3},{2,0},{3,1},{4,6},{5,7},{6,4},{7,5},{8,10},{9,11},{10,... | collective-permute-start | bytes 196616 | tf_op jit(solution)/shard_map/ppermute | solution.py:383
  50.5 9.8 %collective-permute-start.9 = (f32[64,256]{1,0:T(8,128)S(1)}, f32[64,256]{1,0:T(8,128)S(1)}, u32[]{:S(2)}, u32[]{:S(2)}) collective-permute-start(f32[64,256]{1,0:T(8,128)S(1)} %get-tuple-element.48), channel_id=1, source_target_pairs={{0,4},{1,5},{2,6},{3,7},{4,0},{5,1},{6,2},{7,3},{8,12},{9,13},{10,... | collective-permute-start | bytes 196616 | tf_op jit(solution)/shard_map/ppermute | solution.py:383
  51.5 10.3 %collective-permute-start.10 = (f32[64,256]{1,0:T(8,128)S(1)}, f32[64,256]{1,0:T(8,128)S(1)}, u32[]{:S(2)}, u32[]{:S(2)}) collective-permute-start(f32[64,256]{1,0:T(8,128)S(1)} %get-tuple-element.49), channel_id=1, source_target_pairs={{0,5},{1,4},{2,7},{3,6},{4,1},{5,0},{6,3},{7,2},{8,13},{9,12},{10,... | collective-permute-start | bytes 196616 | tf_op jit(solution)/shard_map/ppermute | solution.py:383
  53.4 8.4 %collective-permute-start.11 = (f32[64,256]{1,0:T(8,128)S(1)}, f32[64,256]{1,0:T(8,128)S(1)}, u32[]{:S(2)}, u32[]{:S(2)}) collective-permute-start(f32[64,256]{1,0:T(8,128)S(1)} %get-tuple-element.50), channel_id=1, source_target_pairs={{0,6},{1,7},{2,4},{3,5},{4,2},{5,3},{6,0},{7,1},{8,14},{9,15},{10,... | collective-permute-start | bytes 196616 | tf_op jit(solution)/shard_map/ppermute | solution.py:383
  55.9 8.3 %collective-permute-start.12 = (f32[64,256]{1,0:T(8,128)S(1)}, f32[64,256]{1,0:T(8,128)S(1)}, u32[]{:S(2)}, u32[]{:S(2)}) collective-permute-start(f32[64,256]{1,0:T(8,128)S(1)} %get-tuple-element.51), channel_id=1, source_target_pairs={{0,7},{1,6},{2,5},{3,4},{4,3},{5,2},{6,1},{7,0},{8,15},{9,14},{10,... | collective-permute-start | bytes 196616 | tf_op jit(solution)/shard_map/ppermute | solution.py:383
  58.1 7.5 %collective-permute-start.13 = (f32[64,256]{1,0:T(8,128)S(1)}, f32[64,256]{1,0:T(8,128)S(1)}, u32[]{:S(2)}, u32[]{:S(2)}) collective-permute-start(f32[64,256]{1,0:T(8,128)S(1)} %get-tuple-element.52), channel_id=1, source_target_pairs={{0,3},{1,2},{2,1},{3,0},{4,7},{5,6},{6,5},{7,4},{8,11},{9,10},{10,... | collective-permute-start | bytes 196616 | tf_op jit(solution)/shard_map/ppermute | solution.py:383
  60.3 8.1 %collective-permute-start.14 = (f32[64,256]{1,0:T(8,128)S(1)}, f32[64,256]{1,0:T(8,128)S(1)}, u32[]{:S(2)}, u32[]{:S(2)}) collective-permute-start(f32[64,256]{1,0:T(8,128)S(1)} %get-tuple-element.55), channel_id=1, source_target_pairs={{0,1},{1,0},{2,3},{3,2},{4,5},{5,4},{6,7},{7,6},{8,9},{9,8},{10,11... | collective-permute-start | bytes 196616 | tf_op jit(solution)/shard_map/ppermute | solution.py:383
  61.9 8.5 %collective-permute-start.15 = (f32[64,256]{1,0:T(8,128)S(1)}, f32[64,256]{1,0:T(8,128)S(1)}, u32[]{:S(2)}, u32[]{:S(2)}) collective-permute-start(f32[64,256]{1,0:T(8,128)S(1)} %get-tuple-element.56), channel_id=1, source_target_pairs={{0,2},{1,3},{2,0},{3,1},{4,6},{5,7},{6,4},{7,5},{8,10},{9,11},{10,... | collective-permute-start | bytes 196616 | tf_op jit(solution)/shard_map/ppermute | solution.py:383
  61.9 10.1 %collective-permute-start.16 = (f32[64,256]{1,0:T(8,128)S(1)}, f32[64,256]{1,0:T(8,128)S(1)}, u32[]{:S(2)}, u32[]{:S(2)}) collective-permute-start(f32[64,256]{1,0:T(8,128)S(1)} %get-tuple-element.57), channel_id=1, source_target_pairs={{0,3},{1,2},{2,1},{3,0},{4,7},{5,6},{6,5},{7,4},{8,11},{9,10},{10,... | collective-permute-start | bytes 196616 | tf_op jit(solution)/shard_map/ppermute | solution.py:383
  64.2 8.3 %collective-permute-start.17 = (f32[64,256]{1,0:T(8,128)S(1)}, f32[64,256]{1,0:T(8,128)S(1)}, u32[]{:S(2)}, u32[]{:S(2)}) collective-permute-start(f32[64,256]{1,0:T(8,128)S(1)} %get-tuple-element.58), channel_id=1, source_target_pairs={{0,4},{1,5},{2,6},{3,7},{4,0},{5,1},{6,2},{7,3},{8,12},{9,13},{10,... | collective-permute-start | bytes 196616 | tf_op jit(solution)/shard_map/ppermute | solution.py:383
  65.6 8.3 %collective-permute-start.18 = (f32[64,256]{1,0:T(8,128)S(1)}, f32[64,256]{1,0:T(8,128)S(1)}, u32[]{:S(2)}, u32[]{:S(2)}) collective-permute-start(f32[64,256]{1,0:T(8,128)S(1)} %get-tuple-element.59), channel_id=1, source_target_pairs={{0,5},{1,4},{2,7},{3,6},{4,1},{5,0},{6,3},{7,2},{8,13},{9,12},{10,... | collective-permute-start | bytes 196616 | tf_op jit(solution)/shard_map/ppermute | solution.py:383
  68.3 6.8 %collective-permute-start.19 = (f32[64,256]{1,0:T(8,128)S(1)}, f32[64,256]{1,0:T(8,128)S(1)}, u32[]{:S(2)}, u32[]{:S(2)}) collective-permute-start(f32[64,256]{1,0:T(8,128)S(1)} %get-tuple-element.60), channel_id=1, source_target_pairs={{0,6},{1,7},{2,4},{3,5},{4,2},{5,3},{6,0},{7,1},{8,14},{9,15},{10,... | collective-permute-start | bytes 196616 | tf_op jit(solution)/shard_map/ppermute | solution.py:383
  70.4 11.7 %collective-permute-start.21 = (f32[1,128,256]{2,1,0:T(8,128)S(1)}, f32[1,128,256]{2,1,0:T(8,128)S(1)}, u32[]{:S(2)}, u32[]{:S(2)}) collective-permute-start(f32[1,128,256]{2,1,0:T(8,128)S(1)} %get-tuple-element.62), channel_id=1, source_target_pairs={{0,16},{8,24},{16,0},{24,8},{1,17},{9,25},{17,1},{25,9},{2,18},{10... | collective-permute-start | bytes 393224 | tf_op jit(solution)/shard_map/ppermute | solution.py:383
  71.9 10.2 %collective-permute-start.22 = (f32[1,128,256]{2,1,0:T(8,128)S(1)}, f32[1,128,256]{2,1,0:T(8,128)S(1)}, u32[]{:S(2)}, u32[]{:S(2)}) collective-permute-start(f32[1,128,256]{2,1,0:T(8,128)S(1)} %get-tuple-element.63), channel_id=1, source_target_pairs={{0,16},{8,24},{16,0},{24,8},{1,17},{9,25},{17,1},{25,9},{2,18},{10... | collective-permute-start | bytes 393224 | tf_op jit(solution)/shard_map/ppermute | solution.py:383
  72.4 9.7 %collective-permute-start.23 = (f32[1,128,256]{2,1,0:T(8,128)S(1)}, f32[1,128,256]{2,1,0:T(8,128)S(1)}, u32[]{:S(2)}, u32[]{:S(2)}) collective-permute-start(f32[1,128,256]{2,1,0:T(8,128)S(1)} %get-tuple-element.64), channel_id=1, source_target_pairs={{0,16},{8,24},{16,0},{24,8},{1,17},{9,25},{17,1},{25,9},{2,18},{10... | collective-permute-start | bytes 393224 | tf_op jit(solution)/shard_map/ppermute | solution.py:383
  74.0 8.1 %collective-permute-start.24 = (f32[1,128,256]{2,1,0:T(8,128)S(1)}, f32[1,128,256]{2,1,0:T(8,128)S(1)}, u32[]{:S(2)}, u32[]{:S(2)}) collective-permute-start(f32[1,128,256]{2,1,0:T(8,128)S(1)} %get-tuple-element.65), channel_id=1, source_target_pairs={{0,16},{8,24},{16,0},{24,8},{1,17},{9,25},{17,1},{25,9},{2,18},{10... | collective-permute-start | bytes 393224 | tf_op jit(solution)/shard_map/ppermute | solution.py:383
  75.1 7.0 %collective-permute-start.20 = (f32[64,256]{1,0:T(8,128)S(1)}, f32[64,256]{1,0:T(8,128)S(1)}, u32[]{:S(2)}, u32[]{:S(2)}) collective-permute-start(f32[64,256]{1,0:T(8,128)S(1)} %get-tuple-element.61), channel_id=1, source_target_pairs={{0,7},{1,6},{2,5},{3,4},{4,3},{5,2},{6,1},{7,0},{8,15},{9,14},{10,... | collective-permute-start | bytes 196616 | tf_op jit(solution)/shard_map/ppermute | solution.py:383
  82.1 4.3 %collective-permute-start.25 = (f32[4,128,256]{2,1,0:T(8,128)S(1)}, f32[4,128,256]{2,1,0:T(8,128)S(1)}, u32[]{:S(2)}, u32[]{:S(2)}) collective-permute-start(f32[4,128,256]{2,1,0:T(8,128)S(1)} %get-tuple-element.53.za), channel_id=1, source_target_pairs={{0,8},{8,0},{16,24},{24,16},{1,9},{9,1},{17,25},{25,17},{2,10},{10... | collective-permute-start | bytes 1572872 | tf_op jit(solution)/shard_map/ppermute | solution.py:383
  88.7 8.2 %collective-permute-start.31 = (f32[4,64,128]{2,1,0:T(8,128)S(1)}, f32[4,64,128]{2,1,0:T(8,128)S(1)}, u32[]{:S(2)}, u32[]{:S(2)}) collective-permute-start(f32[4,64,128]{2,1,0:T(8,128)S(1)} %get-tuple-element.67), channel_id=1, source_target_pairs={{0,1},{1,0},{2,3},{3,2},{4,5},{5,4},{6,7},{7,6},{8,9},{9,8},{10,11... | collective-permute-start | bytes 393224 | tf_op jit(solution)/shard_map/ppermute | solution.py:383
  90.9 6.0 %collective-permute-start.33 = (f32[2,64,128]{2,1,0:T(8,128)S(1)}, f32[2,64,128]{2,1,0:T(8,128)S(1)}, u32[]{:S(2)}, u32[]{:S(2)}) collective-permute-start(f32[2,64,128]{2,1,0:T(8,128)S(1)} %get-tuple-element.69), channel_id=1, source_target_pairs={{0,17},{1,16},{2,19},{3,18},{4,21},{5,20},{6,23},{7,22},{8,25},{9,... | collective-permute-start | bytes 196616 | tf_op jit(solution)/shard_map/ppermute | solution.py:389
  97.5 4.3 %collective-permute-start.34 = (f32[4,32,128]{2,1,0:T(8,128)S(1)}, f32[4,32,128]{2,1,0:T(8,128)S(1)}, u32[]{:S(2)}, u32[]{:S(2)}) collective-permute-start(f32[4,32,128]{2,1,0:T(8,128)S(1)} %get-tuple-element.71), channel_id=1, source_target_pairs={{0,2},{1,3},{2,0},{3,1},{4,6},{5,7},{6,4},{7,5},{8,10},{9,11},{10,... | collective-permute-start | bytes 196616 | tf_op jit(solution)/shard_map/ppermute | solution.py:383
  101.8 5.4 %collective-permute-start.35 = (f32[4,32,128]{2,1,0:T(8,128)S(1)}, f32[4,32,128]{2,1,0:T(8,128)S(1)}, u32[]{:S(2)}, u32[]{:S(2)}) collective-permute-start(f32[4,32,128]{2,1,0:T(8,128)S(1)} %add.80.mine), channel_id=1, source_target_pairs={{0,4},{1,5},{2,6},{3,7},{4,0},{5,1},{6,2},{7,3},{8,12},{9,13},{10,... | collective-permute-start | bytes 196616 | tf_op jit(solution)/shard_map/ppermute | solution.py:383
  107.8 5.4 %collective-permute-start.38 = (f32[4,32,128]{2,1,0:T(8,128)S(1)}, f32[4,32,128]{2,1,0:T(8,128)S(1)}, u32[]{:S(2)}, u32[]{:S(2)}) collective-permute-start(f32[4,32,128]{2,1,0:T(8,128)S(1)} %pair.1.refs_0_), channel_id=1, source_target_pairs={{0,3},{1,2},{2,1},{3,0},{4,7},{5,6},{6,5},{7,4},{8,11},{9,10},{10,... | collective-permute-start | bytes 196616 | tf_op jit(solution)/shard_map/ppermute | solution.py:383
  107.8 5.3 %collective-permute-start.37 = (f32[4,32,128]{2,1,0:T(8,128)S(1)}, f32[4,32,128]{2,1,0:T(8,128)S(1)}, u32[]{:S(2)}, u32[]{:S(2)}) collective-permute-start(f32[4,32,128]{2,1,0:T(8,128)S(1)} %pair.1.refs_0_), channel_id=1, source_target_pairs={{0,2},{1,3},{2,0},{3,1},{4,6},{5,7},{6,4},{7,5},{8,10},{9,11},{10,... | collective-permute-start | bytes 196616 | tf_op jit(solution)/shard_map/ppermute | solution.py:383
  (14 other events, 112.0 us)

commit v11 on v10

--- a/solution.py
+++ b/solution.py
@@ -86,16 +86,35 @@
     return hi, lo
 
 
-def split_kernel(nd, nb, x_ref, packed_ref, *refs):
-    outs, scratch = refs[:-1], refs[-1]
+def split_kernel(nd, nb, cell_ref, x_ref, v_ref, w_ref, code_ref, *refs):
+    outs, (scratch, packed) = refs[:-2], refs[-2:]
     i = lax.axis_index("dom")
+    cube = 2 * REACH + 1
+    code = code_ref[...].astype(F32)
+    off_x = jnp.floor((code + 0.5) * (1.0 / (cube * cube)))
+    rest = code - off_x * (cube * cube)
+    off_y = jnp.floor((rest + 0.5) * (1.0 / cube))
+    off_z = rest - off_y * cube
+    for a in range(2):
+        packed[a * 8 : a * 8 + 8] = w_ref[a]
+        cell_x, cell_y, cell_z = (
+            lax.rem(cell_ref[a, k], n).astype(F32) for k, n in enumerate((SLAB, SIDE, SIDE))
+        )
+        y = off_y[a : a + 1] + (cell_y + float(SIDE - REACH))
+        z = off_z[a : a + 1] + (cell_z + float(SIDE - REACH))
+        y = y - SIDE * jnp.floor(y * (1.0 / SIDE))
+        z = z - SIDE * jnp.floor(z * (1.0 / SIDE))
+        packed[16 + a : 17 + a] = off_x[a : a + 1] + cell_x
+        packed[18 + a : 19 + a] = y * SIDE + z
+    packed[20:24] = jnp.zeros((4, LAT), F32)
+    packed[24:32] = jnp.concatenate([v_ref[:, y, :] for y in range(SIDE)], axis=1)
     for q in range(SLAB):
         scratch[q] = x_ref[q].T
     for j in range(nd):
         start = (i ^ j) * nb
         for q in range(SLAB):
             outs[j][q * nb : (q + 1) * nb] = scratch[q, pl.ds(pl.multiple_of(start, nb), nb)]
-        outs[j][SLAB * nb :] = packed_ref[...]
+        outs[j][SLAB * nb :] = packed[...]
 
 
 def build_projectors(nd, scratch, wh_ref, wl_ref, v_ref):
@@ -112,8 +131,9 @@
             hot = jnp.where(lat == place, 1.0, 0.0).astype(BF16)
             masked = jnp.where(px[None] == plane, w[None], 0.0).reshape(128, 256)
             mh, ml = halves(masked)
-            his.append(dot(mh, hot, NT).reshape(16, 8, LAT))
-            los.append(dot(ml, hot, NT).reshape(16, 8, LAT))
+            both = dot(jnp.concatenate([mh, ml], axis=0), hot, NT).reshape(2, 16, 8, LAT)
+            his.append(both[0])
+            los.append(both[1])
         hi = jnp.concatenate(his, axis=1).astype(BF16)
         lo = jnp.concatenate(los, axis=1).astype(BF16)
         for t in range(16):
@@ -434,16 +454,16 @@
     R = SLAB * nb
 
     waves = trial_waves.reshape(SLAB, LAT, bands)
-    packed = packed_atoms(potential, proj_weights, atom_cell, point_codes)
     if direct:
         cut = call(
             functools.partial(split_kernel, nd, nb),
             [shape(R + 32, LAT)] * nd,
-            [waves, packed],
-            [pltpu.VMEM((SLAB, bands, LAT), F32)],
+            [atom_cell, waves, potential, proj_weights, point_codes],
+            [pltpu.VMEM((SLAB, bands, LAT), F32), pltpu.VMEM((32, 256), F32)],
             "split",
         )
     else:
+        packed = packed_atoms(potential, proj_weights, atom_cell, point_codes)
         gathered = lax.all_gather(packed, "dom", axis=0)
         turned = waves.transpose(0, 2, 1).reshape(SLAB, nd, real, LAT).transpose(1, 0, 2, 3)
         cut = [turned[j] for j in range(nd)]

time: 116 us -> 116 us (level)
  local copies, waits for them, and re-layouts: 3.45 us -> 4.79 us
    unnamed x14 -> x18, local copies, waits for them, and re-layouts: 2.49 us -> 4.78 us
where the time goes in v11:
time: 116 us
  starting transfers between devices  51.6 us (44%)
  waiting for transfers between devices  42.2 us (36%)
  Pallas kernels  16.3 us (14%)
  local copies, waits for them, and re-layouts  4.79 us (4%)
    ppermute x38, starting transfers between devices, xor_permute(): return lax.ppermute(value, axis, [(k, k ^ step) for k in range(count)])  50.5 us
    ppermute x38, waiting for transfers between devices, xor_permute(): return lax.ppermute(value, axis, [(k, k ^ step) for k in range(count)])  39.1 us
    pallas_call x9, Pallas kernels, call(): pl.pallas_call(kernel, out_shape=out_shape, in_specs=specs, out_specs=pl....  16.3 us
    unnamed x18, local copies, waits for them, and re-layouts  4.78 us
    ppermute x1, waiting for transfers between devices, both_permute(): return lax.ppermute(value, ('band', 'dom'), pairs)  3.08 us
  transfers between devices with their start and end apart: 39, of which 13 were waited for; matrix products, arithmetic and copies ran while one was open for 0% of the time, Pallas kernels for 3%

profile of v11, /device:TPU:0, one launch (start us, length us, event | category | flops | bytes accessed | tf_op | source)
XLA Modules:
  0.0 115.9 jit_solution(14715943302205223168)
XLA Ops:
  5.8 3.0 %collective-permute-start = (f32[160,256]{1,0:T(8,128)S(1)}, f32[160,256]{1,0:T(8,128)S(1)}, u32[]{:S(2)}, u32[]{:S(2)}) collective-permute-start(f32[160,256]{1,0:T(8,128)S(1)} %get-tuple-element.37), channel_id=1, source_target_pairs={{0,1},{1,0},{2,3},{3,2},{4,5},{5,4},{6,7},{7,6},{8,9},{9,8},{10,11... | collective-permute-start | bytes 491528 | tf_op jit(solution)/shard_map/ppermute | solution.py:403
  8.8 1.6 %collective-permute-start.1 = (f32[160,256]{1,0:T(8,128)S(1)}, f32[160,256]{1,0:T(8,128)S(1)}, u32[]{:S(2)}, u32[]{:S(2)}) collective-permute-start(f32[160,256]{1,0:T(8,128)S(1)} %get-tuple-element.38), channel_id=1, source_target_pairs={{0,2},{1,3},{2,0},{3,1},{4,6},{5,7},{6,4},{7,5},{8,10},{9,11},{10,... | collective-permute-start | bytes 491528 | tf_op jit(solution)/shard_map/ppermute | solution.py:403
  10.4 2.6 %collective-permute-start.2 = (f32[160,256]{1,0:T(8,128)S(1)}, f32[160,256]{1,0:T(8,128)S(1)}, u32[]{:S(2)}, u32[]{:S(2)}) collective-permute-start(f32[160,256]{1,0:T(8,128)S(1)} %get-tuple-element.39), channel_id=1, source_target_pairs={{0,4},{1,5},{2,6},{3,7},{4,0},{5,1},{6,2},{7,3},{8,12},{9,13},{10,... | collective-permute-start | bytes 491528 | tf_op jit(solution)/shard_map/ppermute | solution.py:403
  13.3 2.5 %collective-permute-start.4 = (f32[160,256]{1,0:T(8,128)S(1)}, f32[160,256]{1,0:T(8,128)S(1)}, u32[]{:S(2)}, u32[]{:S(2)}) collective-permute-start(f32[160,256]{1,0:T(8,128)S(1)} %get-tuple-element.41), channel_id=1, source_target_pairs={{0,6},{1,7},{2,4},{3,5},{4,2},{5,3},{6,0},{7,1},{8,14},{9,15},{10,... | collective-permute-start | bytes 491528 | tf_op jit(solution)/shard_map/ppermute | solution.py:403
  15.7 2.3 %collective-permute-start.5 = (f32[160,256]{1,0:T(8,128)S(1)}, f32[160,256]{1,0:T(8,128)S(1)}, u32[]{:S(2)}, u32[]{:S(2)}) collective-permute-start(f32[160,256]{1,0:T(8,128)S(1)} %get-tuple-element.42), channel_id=1, source_target_pairs={{0,7},{1,6},{2,5},{3,4},{4,3},{5,2},{6,1},{7,0},{8,15},{9,14},{10,... | collective-permute-start | bytes 491528 | tf_op jit(solution)/shard_map/ppermute | solution.py:403
  18.8 13.4 %collective-permute-done.2.refs_2_ = f32[160,256]{1,0:T(8,128)S(1)} collective-permute-done((f32[160,256]{1,0:T(8,128)S(1)}, f32[160,256]{1,0:T(8,128)S(1)}, u32[]{:S(2)}, u32[]{:S(2)}) %collective-permute-start.2) | collective-permute-done | bytes 163872 | tf_op jit(solution)/shard_map/ppermute | solution.py:403
  32.2 3.0 %collective-permute-done.3.refs_3_ = f32[160,256]{1,0:T(8,128)S(1)} collective-permute-done((f32[160,256]{1,0:T(8,128)S(1)}, f32[160,256]{1,0:T(8,128)S(1)}, u32[]{:S(2)}, u32[]{:S(2)}) %collective-permute-start.3) | collective-permute-done | bytes 163872 | tf_op jit(solution)/shard_map/ppermute | solution.py:403
  35.2 7.5 %filter.1 = (f32[64,256]{1,0:T(8,128)S(1)}, f32[64,256]{1,0:T(8,128)S(1)}, f32[64,256]{1,0:T(8,128)S(1)}, f32[64,256]{1,0:T(8,128)S(1)}, f32[64,256]{1,0:T(8,128...) custom-call(s32[3]{0:T(128)S(1)} %pad_add_fusion.pos_ref, ...), custom_call_target="tpu_custom_call" | custom-call | tf_op jit(solution)/shard_map/filter/pallas_call | solution.py:382
  42.8 2.1 %collective-permute-start.7 = (f32[64,256]{1,0:T(8,128)S(1)}, f32[64,256]{1,0:T(8,128)S(1)}, u32[]{:S(2)}, u32[]{:S(2)}) collective-permute-start(f32[64,256]{1,0:T(8,128)S(1)} %get-tuple-element.46), channel_id=1, source_target_pairs={{0,1},{1,0},{2,3},{3,2},{4,5},{5,4},{6,7},{7,6},{8,9},{9,8},{10,11... | collective-permute-start | bytes 196616 | tf_op jit(solution)/shard_map/ppermute | solution.py:403
  44.8 6.1 %collective-permute-start.8 = (f32[64,256]{1,0:T(8,128)S(1)}, f32[64,256]{1,0:T(8,128)S(1)}, u32[]{:S(2)}, u32[]{:S(2)}) collective-permute-start(f32[64,256]{1,0:T(8,128)S(1)} %get-tuple-element.47), channel_id=1, source_target_pairs={{0,2},{1,3},{2,0},{3,1},{4,6},{5,7},{6,4},{7,5},{8,10},{9,11},{10,... | collective-permute-start | bytes 196616 | tf_op jit(solution)/shard_map/ppermute | solution.py:403
  52.0 1.9 %collective-permute-start.10 = (f32[64,256]{1,0:T(8,128)S(1)}, f32[64,256]{1,0:T(8,128)S(1)}, u32[]{:S(2)}, u32[]{:S(2)}) collective-permute-start(f32[64,256]{1,0:T(8,128)S(1)} %get-tuple-element.49), channel_id=1, source_target_pairs={{0,5},{1,4},{2,7},{3,6},{4,1},{5,0},{6,3},{7,2},{8,13},{9,12},{10,... | collective-permute-start | bytes 196616 | tf_op jit(solution)/shard_map/ppermute | solution.py:403
  53.9 2.5 %collective-permute-start.11 = (f32[64,256]{1,0:T(8,128)S(1)}, f32[64,256]{1,0:T(8,128)S(1)}, u32[]{:S(2)}, u32[]{:S(2)}) collective-permute-start(f32[64,256]{1,0:T(8,128)S(1)} %get-tuple-element.50), channel_id=1, source_target_pairs={{0,6},{1,7},{2,4},{3,5},{4,2},{5,3},{6,0},{7,1},{8,14},{9,15},{10,... | collective-permute-start | bytes 196616 | tf_op jit(solution)/shard_map/ppermute | solution.py:403
  56.3 2.2 %collective-permute-start.12 = (f32[64,256]{1,0:T(8,128)S(1)}, f32[64,256]{1,0:T(8,128)S(1)}, u32[]{:S(2)}, u32[]{:S(2)}) collective-permute-start(f32[64,256]{1,0:T(8,128)S(1)} %get-tuple-element.51), channel_id=1, source_target_pairs={{0,7},{1,6},{2,5},{3,4},{4,3},{5,2},{6,1},{7,0},{8,15},{9,14},{10,... | collective-permute-start | bytes 196616 | tf_op jit(solution)/shard_map/ppermute | solution.py:403
  58.6 2.1 %collective-permute-done.9.refs_3_ = f32[64,256]{1,0:T(8,128)S(1)} collective-permute-done((f32[64,256]{1,0:T(8,128)S(1)}, f32[64,256]{1,0:T(8,128)S(1)}, u32[]{:S(2)}, u32[]{:S(2)}) %collective-permute-start.9) | collective-permute-done | bytes 65568 | tf_op jit(solution)/shard_map/ppermute | solution.py:403
  60.7 1.6 %collective-permute-done.10.refs_4_ = f32[64,256]{1,0:T(8,128)S(1)} collective-permute-done((f32[64,256]{1,0:T(8,128)S(1)}, f32[64,256]{1,0:T(8,128)S(1)}, u32[]{:S(2)}, u32[]{:S(2)}) %collective-permute-start.10) | collective-permute-done | bytes 65568 | tf_op jit(solution)/shard_map/ppermute | solution.py:403
  62.3 2.3 %collective-permute-start.16 = (f32[64,256]{1,0:T(8,128)S(1)}, f32[64,256]{1,0:T(8,128)S(1)}, u32[]{:S(2)}, u32[]{:S(2)}) collective-permute-start(f32[64,256]{1,0:T(8,128)S(1)} %get-tuple-element.57), channel_id=1, source_target_pairs={{0,3},{1,2},{2,1},{3,0},{4,7},{5,6},{6,5},{7,4},{8,11},{9,10},{10,... | collective-permute-start | bytes 196616 | tf_op jit(solution)/shard_map/ppermute | solution.py:403
  64.6 1.5 %collective-permute-start.17 = (f32[64,256]{1,0:T(8,128)S(1)}, f32[64,256]{1,0:T(8,128)S(1)}, u32[]{:S(2)}, u32[]{:S(2)}) collective-permute-start(f32[64,256]{1,0:T(8,128)S(1)} %get-tuple-element.58), channel_id=1, source_target_pairs={{0,4},{1,5},{2,6},{3,7},{4,0},{5,1},{6,2},{7,3},{8,12},{9,13},{10,... | collective-permute-start | bytes 196616 | tf_op jit(solution)/shard_map/ppermute | solution.py:403
  66.0 2.1 %collective-permute-start.18 = (f32[64,256]{1,0:T(8,128)S(1)}, f32[64,256]{1,0:T(8,128)S(1)}, u32[]{:S(2)}, u32[]{:S(2)}) collective-permute-start(f32[64,256]{1,0:T(8,128)S(1)} %get-tuple-element.59), channel_id=1, source_target_pairs={{0,5},{1,4},{2,7},{3,6},{4,1},{5,0},{6,3},{7,2},{8,13},{9,12},{10,... | collective-permute-start | bytes 196616 | tf_op jit(solution)/shard_map/ppermute | solution.py:403
  68.8 1.8 %collective-permute-start.19 = (f32[64,256]{1,0:T(8,128)S(1)}, f32[64,256]{1,0:T(8,128)S(1)}, u32[]{:S(2)}, u32[]{:S(2)}) collective-permute-start(f32[64,256]{1,0:T(8,128)S(1)} %get-tuple-element.60), channel_id=1, source_target_pairs={{0,6},{1,7},{2,4},{3,5},{4,2},{5,3},{6,0},{7,1},{8,14},{9,15},{10,... | collective-permute-start | bytes 196616 | tf_op jit(solution)/shard_map/ppermute | solution.py:403
  70.6 1.5 %collective-permute-start.21 = (f32[1,128,256]{2,1,0:T(8,128)S(1)}, f32[1,128,256]{2,1,0:T(8,128)S(1)}, u32[]{:S(2)}, u32[]{:S(2)}) collective-permute-start(f32[1,128,256]{2,1,0:T(8,128)S(1)} %get-tuple-element.62), channel_id=1, source_target_pairs={{0,16},{8,24},{16,0},{24,8},{1,17},{9,25},{17,1},{25,9},{2,18},{10... | collective-permute-start | bytes 393224 | tf_op jit(solution)/shard_map/ppermute | solution.py:403
  72.7 1.5 %collective-permute-start.23 = (f32[1,128,256]{2,1,0:T(8,128)S(1)}, f32[1,128,256]{2,1,0:T(8,128)S(1)}, u32[]{:S(2)}, u32[]{:S(2)}) collective-permute-start(f32[1,128,256]{2,1,0:T(8,128)S(1)} %get-tuple-element.64), channel_id=1, source_target_pairs={{0,16},{8,24},{16,0},{24,8},{1,17},{9,25},{17,1},{25,9},{2,18},{10... | collective-permute-start | bytes 393224 | tf_op jit(solution)/shard_map/ppermute | solution.py:403
  75.3 2.8 %collective-permute-start.20 = (f32[64,256]{1,0:T(8,128)S(1)}, f32[64,256]{1,0:T(8,128)S(1)}, u32[]{:S(2)}, u32[]{:S(2)}) collective-permute-start(f32[64,256]{1,0:T(8,128)S(1)} %get-tuple-element.61), channel_id=1, source_target_pairs={{0,7},{1,6},{2,5},{3,4},{4,3},{5,2},{6,1},{7,0},{8,15},{9,14},{10,... | collective-permute-start | bytes 196616 | tf_op jit(solution)/shard_map/ppermute | solution.py:403
  78.1 4.2 %collective-permute-done.20.refs_7_ = f32[64,256]{1,0:T(8,128)S(1)} collective-permute-done((f32[64,256]{1,0:T(8,128)S(1)}, f32[64,256]{1,0:T(8,128)S(1)}, u32[]{:S(2)}, u32[]{:S(2)}) %collective-permute-start.20) | collective-permute-done | bytes 65568 | tf_op jit(solution)/shard_map/ppermute | solution.py:403
  86.6 2.3 %blocks.1 = (f32[4,64,128]{2,1,0:T(8,128)S(1)}, f32[4,64,128]{2,1,0:T(8,128)S(1)}, f32[2,64,128]{2,1,0:T(8,128)S(1)}, f32[2,64,128]{2,1,0:T(8,128)S(1)}) custom-call(s32[3]{0:T(128)S(1)} %pad_add_fusion.pos_ref, f32[4,128,256]{2,1,0:T(8,128)S(1)} %get-tuple-element.53.za, f32[4,128,256]{2,1,0:T(8,128)S(1)} %join.3.zb, ...), custom_call_target="tpu_custom_call" | custom-call | tf_op jit(solution)/shard_map/blocks/pallas_call | solution.py:382
  89.8 1.5 %collective-permute-start.32 = (f32[2,64,128]{2,1,0:T(8,128)S(1)}, f32[2,64,128]{2,1,0:T(8,128)S(1)}, u32[]{:S(2)}, u32[]{:S(2)}) collective-permute-start(f32[2,64,128]{2,1,0:T(8,128)S(1)} %get-tuple-element.68), channel_id=1, source_target_pairs={{0,16},{8,24},{16,0},{24,8},{1,17},{9,25},{17,1},{25,9},{2,18},{10... | collective-permute-start | bytes 196616 | tf_op jit(solution)/shard_map/ppermute | solution.py:403
  92.5 1.6 %collective-permute-done.32.back = f32[2,64,128]{2,1,0:T(8,128)S(1)} collective-permute-done((f32[2,64,128]{2,1,0:T(8,128)S(1)}, f32[2,64,128]{2,1,0:T(8,128)S(1)}, u32[]{:S(2)}, u32[]{:S(2)}) %collective-permute-start.32) | collective-permute-done | bytes 65568 | tf_op jit(solution)/shard_map/ppermute | solution.py:403
  94.1 3.1 %collective-permute-done.33.back_other = f32[2,64,128]{2,1,0:T(8,128)S(1)} collective-permute-done((f32[2,64,128]{2,1,0:T(8,128)S(1)}, f32[2,64,128]{2,1,0:T(8,128)S(1)}, u32[]{:S(2)}, u32[]{:S(2)}) %collective-permute-start.33) | collective-permute-done | bytes 65568 | tf_op jit(solution)/shard_map/ppermute | solution.py:409
  97.9 4.3 %collective-permute-done.34 = f32[4,32,128]{2,1,0:T(8,128)S(1)} collective-permute-done((f32[4,32,128]{2,1,0:T(8,128)S(1)}, f32[4,32,128]{2,1,0:T(8,128)S(1)}, u32[]{:S(2)}, u32[]{:S(2)}) %collective-permute-start.34) | collective-permute-done | bytes 65568 | tf_op jit(solution)/shard_map/ppermute | solution.py:403
  102.5 5.0 %collective-permute-done.35.other = f32[4,32,128]{2,1,0:T(8,128)S(1)} collective-permute-done((f32[4,32,128]{2,1,0:T(8,128)S(1)}, f32[4,32,128]{2,1,0:T(8,128)S(1)}, u32[]{:S(2)}, u32[]{:S(2)}) %collective-permute-start.35) | collective-permute-done | bytes 65568 | tf_op jit(solution)/shard_map/ppermute | solution.py:403
  108.2 2.2 %collective-permute-start.37 = (f32[4,32,128]{2,1,0:T(8,128)S(1)}, f32[4,32,128]{2,1,0:T(8,128)S(1)}, u32[]{:S(2)}, u32[]{:S(2)}) collective-permute-start(f32[4,32,128]{2,1,0:T(8,128)S(1)} %pair.1.refs_0_), channel_id=1, source_target_pairs={{0,2},{1,3},{2,0},{3,1},{4,6},{5,7},{6,4},{7,5},{8,10},{9,11},{10,... | collective-permute-start | bytes 196616 | tf_op jit(solution)/shard_map/ppermute | solution.py:403
  111.6 1.8 %output.1 = f32[8,256,128]{2,1,0:T(8,128)} custom-call(s32[3]{0:T(128)S(1)} %pad_add_fusion.pos_ref, f32[4,128,256]{2,1,0:T(8,128)S(1)} %get-tuple-element.53.za, f32[4,128,256]{2,1,0:T(8,128)S(1)} %join.3.zb), custom_call_target="tpu_custom_call" | custom-call | tf_op jit(solution)/shard_map/output/pallas_call | solution.py:382
  114.6 1.3 %place.1 = f32[128,512]{1,0:T(8,128)} custom-call(s32[3]{0:T(128)S(1)} %pad_add_fusion.pos_ref, f32[4,32,128]{2,1,0:T(8,128)S(1)} %pair.1.refs_0_, f32[4,32,128]{2,1,0:T(8,128)S(1)} %collective-permute-done.36.refs_1_, f32[4,32,128]{2,1,0:T(8,128)S(1)} %collective-permute-done.37.refs_2_, f32[4,32,128]{2,1,0:T(8,128)S(1)} %collective-permute-done.38.refs_3_), custom_call_target="tpu_custom_call" | custom-call | tf_op jit(solution)/shard_map/place/pallas_call | solution.py:382
  (77 shorter events, 20.0 us)
Async XLA Ops:
  5.8 10.0 %collective-permute-start = (f32[160,256]{1,0:T(8,128)S(1)}, f32[160,256]{1,0:T(8,128)S(1)}, u32[]{:S(2)}, u32[]{:S(2)}) collective-permute-start(f32[160,256]{1,0:T(8,128)S(1)} %get-tuple-element.37), channel_id=1, source_target_pairs={{0,1},{1,0},{2,3},{3,2},{4,5},{5,4},{6,7},{7,6},{8,9},{9,8},{10,11... | collective-permute-start | bytes 491528 | tf_op jit(solution)/shard_map/ppermute | solution.py:403
  8.8 9.2 %collective-permute-start.1 = (f32[160,256]{1,0:T(8,128)S(1)}, f32[160,256]{1,0:T(8,128)S(1)}, u32[]{:S(2)}, u32[]{:S(2)}) collective-permute-start(f32[160,256]{1,0:T(8,128)S(1)} %get-tuple-element.38), channel_id=1, source_target_pairs={{0,2},{1,3},{2,0},{3,1},{4,6},{5,7},{6,4},{7,5},{8,10},{9,11},{10,... | collective-permute-start | bytes 491528 | tf_op jit(solution)/shard_map/ppermute | solution.py:403
  10.4 21.8 %collective-permute-start.2 = (f32[160,256]{1,0:T(8,128)S(1)}, f32[160,256]{1,0:T(8,128)S(1)}, u32[]{:S(2)}, u32[]{:S(2)}) collective-permute-start(f32[160,256]{1,0:T(8,128)S(1)} %get-tuple-element.39), channel_id=1, source_target_pairs={{0,4},{1,5},{2,6},{3,7},{4,0},{5,1},{6,2},{7,3},{8,12},{9,13},{10,... | collective-permute-start | bytes 491528 | tf_op jit(solution)/shard_map/ppermute | solution.py:403
  13.0 22.2 %collective-permute-start.3 = (f32[160,256]{1,0:T(8,128)S(1)}, f32[160,256]{1,0:T(8,128)S(1)}, u32[]{:S(2)}, u32[]{:S(2)}) collective-permute-start(f32[160,256]{1,0:T(8,128)S(1)} %get-tuple-element.40), channel_id=1, source_target_pairs={{0,5},{1,4},{2,7},{3,6},{4,1},{5,0},{6,3},{7,2},{8,13},{9,12},{10,... | collective-permute-start | bytes 491528 | tf_op jit(solution)/shard_map/ppermute | solution.py:403
  13.3 21.9 %collective-permute-start.4 = (f32[160,256]{1,0:T(8,128)S(1)}, f32[160,256]{1,0:T(8,128)S(1)}, u32[]{:S(2)}, u32[]{:S(2)}) collective-permute-start(f32[160,256]{1,0:T(8,128)S(1)} %get-tuple-element.41), channel_id=1, source_target_pairs={{0,6},{1,7},{2,4},{3,5},{4,2},{5,3},{6,0},{7,1},{8,14},{9,15},{10,... | collective-permute-start | bytes 491528 | tf_op jit(solution)/shard_map/ppermute | solution.py:403
  15.7 19.5 %collective-permute-start.5 = (f32[160,256]{1,0:T(8,128)S(1)}, f32[160,256]{1,0:T(8,128)S(1)}, u32[]{:S(2)}, u32[]{:S(2)}) collective-permute-start(f32[160,256]{1,0:T(8,128)S(1)} %get-tuple-element.42), channel_id=1, source_target_pairs={{0,7},{1,6},{2,5},{3,4},{4,3},{5,2},{6,1},{7,0},{8,15},{9,14},{10,... | collective-permute-start | bytes 491528 | tf_op jit(solution)/shard_map/ppermute | solution.py:403
  18.0 17.2 %collective-permute-start.6 = (f32[160,256]{1,0:T(8,128)S(1)}, f32[160,256]{1,0:T(8,128)S(1)}, u32[]{:S(2)}, u32[]{:S(2)}) collective-permute-start(f32[160,256]{1,0:T(8,128)S(1)} %get-tuple-element.43), channel_id=1, source_target_pairs={{0,3},{1,2},{2,1},{3,0},{4,7},{5,6},{6,5},{7,4},{8,11},{9,10},{10,... | collective-permute-start | bytes 491528 | tf_op jit(solution)/shard_map/ppermute | solution.py:403
  42.8 13.6 %collective-permute-start.7 = (f32[64,256]{1,0:T(8,128)S(1)}, f32[64,256]{1,0:T(8,128)S(1)}, u32[]{:S(2)}, u32[]{:S(2)}) collective-permute-start(f32[64,256]{1,0:T(8,128)S(1)} %get-tuple-element.46), channel_id=1, source_target_pairs={{0,1},{1,0},{2,3},{3,2},{4,5},{5,4},{6,7},{7,6},{8,9},{9,8},{10,11... | collective-permute-start | bytes 196616 | tf_op jit(solution)/shard_map/ppermute | solution.py:403
  44.8 13.7 %collective-permute-start.8 = (f32[64,256]{1,0:T(8,128)S(1)}, f32[64,256]{1,0:T(8,128)S(1)}, u32[]{:S(2)}, u32[]{:S(2)}) collective-permute-start(f32[64,256]{1,0:T(8,128)S(1)} %get-tuple-element.47), channel_id=1, source_target_pairs={{0,2},{1,3},{2,0},{3,1},{4,6},{5,7},{6,4},{7,5},{8,10},{9,11},{10,... | collective-permute-start | bytes 196616 | tf_op jit(solution)/shard_map/ppermute | solution.py:403
  50.9 9.8 %collective-permute-start.9 = (f32[64,256]{1,0:T(8,128)S(1)}, f32[64,256]{1,0:T(8,128)S(1)}, u32[]{:S(2)}, u32[]{:S(2)}) collective-permute-start(f32[64,256]{1,0:T(8,128)S(1)} %get-tuple-element.48), channel_id=1, source_target_pairs={{0,4},{1,5},{2,6},{3,7},{4,0},{5,1},{6,2},{7,3},{8,12},{9,13},{10,... | collective-permute-start | bytes 196616 | tf_op jit(solution)/shard_map/ppermute | solution.py:403
  52.0 10.3 %collective-permute-start.10 = (f32[64,256]{1,0:T(8,128)S(1)}, f32[64,256]{1,0:T(8,128)S(1)}, u32[]{:S(2)}, u32[]{:S(2)}) collective-permute-start(f32[64,256]{1,0:T(8,128)S(1)} %get-tuple-element.49), channel_id=1, source_target_pairs={{0,5},{1,4},{2,7},{3,6},{4,1},{5,0},{6,3},{7,2},{8,13},{9,12},{10,... | collective-permute-start | bytes 196616 | tf_op jit(solution)/shard_map/ppermute | solution.py:403
  53.9 8.4 %collective-permute-start.11 = (f32[64,256]{1,0:T(8,128)S(1)}, f32[64,256]{1,0:T(8,128)S(1)}, u32[]{:S(2)}, u32[]{:S(2)}) collective-permute-start(f32[64,256]{1,0:T(8,128)S(1)} %get-tuple-element.50), channel_id=1, source_target_pairs={{0,6},{1,7},{2,4},{3,5},{4,2},{5,3},{6,0},{7,1},{8,14},{9,15},{10,... | collective-permute-start | bytes 196616 | tf_op jit(solution)/shard_map/ppermute | solution.py:403
  56.3 8.2 %collective-permute-start.12 = (f32[64,256]{1,0:T(8,128)S(1)}, f32[64,256]{1,0:T(8,128)S(1)}, u32[]{:S(2)}, u32[]{:S(2)}) collective-permute-start(f32[64,256]{1,0:T(8,128)S(1)} %get-tuple-element.51), channel_id=1, source_target_pairs={{0,7},{1,6},{2,5},{3,4},{4,3},{5,2},{6,1},{7,0},{8,15},{9,14},{10,... | collective-permute-start | bytes 196616 | tf_op jit(solution)/shard_map/ppermute | solution.py:403
  58.6 7.5 %collective-permute-start.13 = (f32[64,256]{1,0:T(8,128)S(1)}, f32[64,256]{1,0:T(8,128)S(1)}, u32[]{:S(2)}, u32[]{:S(2)}) collective-permute-start(f32[64,256]{1,0:T(8,128)S(1)} %get-tuple-element.52), channel_id=1, source_target_pairs={{0,3},{1,2},{2,1},{3,0},{4,7},{5,6},{6,5},{7,4},{8,11},{9,10},{10,... | collective-permute-start | bytes 196616 | tf_op jit(solution)/shard_map/ppermute | solution.py:403
  60.7 8.1 %collective-permute-start.14 = (f32[64,256]{1,0:T(8,128)S(1)}, f32[64,256]{1,0:T(8,128)S(1)}, u32[]{:S(2)}, u32[]{:S(2)}) collective-permute-start(f32[64,256]{1,0:T(8,128)S(1)} %get-tuple-element.55), channel_id=1, source_target_pairs={{0,1},{1,0},{2,3},{3,2},{4,5},{5,4},{6,7},{7,6},{8,9},{9,8},{10,11... | collective-permute-start | bytes 196616 | tf_op jit(solution)/shard_map/ppermute | solution.py:403
  62.3 8.3 %collective-permute-start.15 = (f32[64,256]{1,0:T(8,128)S(1)}, f32[64,256]{1,0:T(8,128)S(1)}, u32[]{:S(2)}, u32[]{:S(2)}) collective-permute-start(f32[64,256]{1,0:T(8,128)S(1)} %get-tuple-element.56), channel_id=1, source_target_pairs={{0,2},{1,3},{2,0},{3,1},{4,6},{5,7},{6,4},{7,5},{8,10},{9,11},{10,... | collective-permute-start | bytes 196616 | tf_op jit(solution)/shard_map/ppermute | solution.py:403
  62.3 9.8 %collective-permute-start.16 = (f32[64,256]{1,0:T(8,128)S(1)}, f32[64,256]{1,0:T(8,128)S(1)}, u32[]{:S(2)}, u32[]{:S(2)}) collective-permute-start(f32[64,256]{1,0:T(8,128)S(1)} %get-tuple-element.57), channel_id=1, source_target_pairs={{0,3},{1,2},{2,1},{3,0},{4,7},{5,6},{6,5},{7,4},{8,11},{9,10},{10,... | collective-permute-start | bytes 196616 | tf_op jit(solution)/shard_map/ppermute | solution.py:403
  64.6 8.1 %collective-permute-start.17 = (f32[64,256]{1,0:T(8,128)S(1)}, f32[64,256]{1,0:T(8,128)S(1)}, u32[]{:S(2)}, u32[]{:S(2)}) collective-permute-start(f32[64,256]{1,0:T(8,128)S(1)} %get-tuple-element.58), channel_id=1, source_target_pairs={{0,4},{1,5},{2,6},{3,7},{4,0},{5,1},{6,2},{7,3},{8,12},{9,13},{10,... | collective-permute-start | bytes 196616 | tf_op jit(solution)/shard_map/ppermute | solution.py:403
  66.0 8.1 %collective-permute-start.18 = (f32[64,256]{1,0:T(8,128)S(1)}, f32[64,256]{1,0:T(8,128)S(1)}, u32[]{:S(2)}, u32[]{:S(2)}) collective-permute-start(f32[64,256]{1,0:T(8,128)S(1)} %get-tuple-element.59), channel_id=1, source_target_pairs={{0,5},{1,4},{2,7},{3,6},{4,1},{5,0},{6,3},{7,2},{8,13},{9,12},{10,... | collective-permute-start | bytes 196616 | tf_op jit(solution)/shard_map/ppermute | solution.py:403
  68.8 6.5 %collective-permute-start.19 = (f32[64,256]{1,0:T(8,128)S(1)}, f32[64,256]{1,0:T(8,128)S(1)}, u32[]{:S(2)}, u32[]{:S(2)}) collective-permute-start(f32[64,256]{1,0:T(8,128)S(1)} %get-tuple-element.60), channel_id=1, source_target_pairs={{0,6},{1,7},{2,4},{3,5},{4,2},{5,3},{6,0},{7,1},{8,14},{9,15},{10,... | collective-permute-start | bytes 196616 | tf_op jit(solution)/shard_map/ppermute | solution.py:403
  70.6 11.7 %collective-permute-start.21 = (f32[1,128,256]{2,1,0:T(8,128)S(1)}, f32[1,128,256]{2,1,0:T(8,128)S(1)}, u32[]{:S(2)}, u32[]{:S(2)}) collective-permute-start(f32[1,128,256]{2,1,0:T(8,128)S(1)} %get-tuple-element.62), channel_id=1, source_target_pairs={{0,16},{8,24},{16,0},{24,8},{1,17},{9,25},{17,1},{25,9},{2,18},{10... | collective-permute-start | bytes 393224 | tf_op jit(solution)/shard_map/ppermute | solution.py:403
  72.1 10.1 %collective-permute-start.22 = (f32[1,128,256]{2,1,0:T(8,128)S(1)}, f32[1,128,256]{2,1,0:T(8,128)S(1)}, u32[]{:S(2)}, u32[]{:S(2)}) collective-permute-start(f32[1,128,256]{2,1,0:T(8,128)S(1)} %get-tuple-element.63), channel_id=1, source_target_pairs={{0,16},{8,24},{16,0},{24,8},{1,17},{9,25},{17,1},{25,9},{2,18},{10... | collective-permute-start | bytes 393224 | tf_op jit(solution)/shard_map/ppermute | solution.py:403
  72.7 9.6 %collective-permute-start.23 = (f32[1,128,256]{2,1,0:T(8,128)S(1)}, f32[1,128,256]{2,1,0:T(8,128)S(1)}, u32[]{:S(2)}, u32[]{:S(2)}) collective-permute-start(f32[1,128,256]{2,1,0:T(8,128)S(1)} %get-tuple-element.64), channel_id=1, source_target_pairs={{0,16},{8,24},{16,0},{24,8},{1,17},{9,25},{17,1},{25,9},{2,18},{10... | collective-permute-start | bytes 393224 | tf_op jit(solution)/shard_map/ppermute | solution.py:403
  74.2 8.1 %collective-permute-start.24 = (f32[1,128,256]{2,1,0:T(8,128)S(1)}, f32[1,128,256]{2,1,0:T(8,128)S(1)}, u32[]{:S(2)}, u32[]{:S(2)}) collective-permute-start(f32[1,128,256]{2,1,0:T(8,128)S(1)} %get-tuple-element.65), channel_id=1, source_target_pairs={{0,16},{8,24},{16,0},{24,8},{1,17},{9,25},{17,1},{25,9},{2,18},{10... | collective-permute-start | bytes 393224 | tf_op jit(solution)/shard_map/ppermute | solution.py:403
  75.3 7.0 %collective-permute-start.20 = (f32[64,256]{1,0:T(8,128)S(1)}, f32[64,256]{1,0:T(8,128)S(1)}, u32[]{:S(2)}, u32[]{:S(2)}) collective-permute-start(f32[64,256]{1,0:T(8,128)S(1)} %get-tuple-element.61), channel_id=1, source_target_pairs={{0,7},{1,6},{2,5},{3,4},{4,3},{5,2},{6,1},{7,0},{8,15},{9,14},{10,... | collective-permute-start | bytes 196616 | tf_op jit(solution)/shard_map/ppermute | solution.py:403
  82.3 4.3 %collective-permute-start.25 = (f32[4,128,256]{2,1,0:T(8,128)S(1)}, f32[4,128,256]{2,1,0:T(8,128)S(1)}, u32[]{:S(2)}, u32[]{:S(2)}) collective-permute-start(f32[4,128,256]{2,1,0:T(8,128)S(1)} %get-tuple-element.53.za), channel_id=1, source_target_pairs={{0,8},{8,0},{16,24},{24,16},{1,9},{9,1},{17,25},{25,17},{2,10},{10... | collective-permute-start | bytes 1572872 | tf_op jit(solution)/shard_map/ppermute | solution.py:403
  88.9 8.3 %collective-permute-start.31 = (f32[4,64,128]{2,1,0:T(8,128)S(1)}, f32[4,64,128]{2,1,0:T(8,128)S(1)}, u32[]{:S(2)}, u32[]{:S(2)}) collective-permute-start(f32[4,64,128]{2,1,0:T(8,128)S(1)} %get-tuple-element.67), channel_id=1, source_target_pairs={{0,1},{1,0},{2,3},{3,2},{4,5},{5,4},{6,7},{7,6},{8,9},{9,8},{10,11... | collective-permute-start | bytes 393224 | tf_op jit(solution)/shard_map/ppermute | solution.py:403
  91.4 5.8 %collective-permute-start.33 = (f32[2,64,128]{2,1,0:T(8,128)S(1)}, f32[2,64,128]{2,1,0:T(8,128)S(1)}, u32[]{:S(2)}, u32[]{:S(2)}) collective-permute-start(f32[2,64,128]{2,1,0:T(8,128)S(1)} %get-tuple-element.69), channel_id=1, source_target_pairs={{0,17},{1,16},{2,19},{3,18},{4,21},{5,20},{6,23},{7,22},{8,25},{9,... | collective-permute-start | bytes 196616 | tf_op jit(solution)/shard_map/ppermute | solution.py:409
  97.8 4.3 %collective-permute-start.34 = (f32[4,32,128]{2,1,0:T(8,128)S(1)}, f32[4,32,128]{2,1,0:T(8,128)S(1)}, u32[]{:S(2)}, u32[]{:S(2)}) collective-permute-start(f32[4,32,128]{2,1,0:T(8,128)S(1)} %get-tuple-element.71), channel_id=1, source_target_pairs={{0,2},{1,3},{2,0},{3,1},{4,6},{5,7},{6,4},{7,5},{8,10},{9,11},{10,... | collective-permute-start | bytes 196616 | tf_op jit(solution)/shard_map/ppermute | solution.py:403
  102.1 5.4 %collective-permute-start.35 = (f32[4,32,128]{2,1,0:T(8,128)S(1)}, f32[4,32,128]{2,1,0:T(8,128)S(1)}, u32[]{:S(2)}, u32[]{:S(2)}) collective-permute-start(f32[4,32,128]{2,1,0:T(8,128)S(1)} %add.4.mine), channel_id=1, source_target_pairs={{0,4},{1,5},{2,6},{3,7},{4,0},{5,1},{6,2},{7,3},{8,12},{9,13},{10,... | collective-permute-start | bytes 196616 | tf_op jit(solution)/shard_map/ppermute | solution.py:403
  108.1 5.4 %collective-permute-start.38 = (f32[4,32,128]{2,1,0:T(8,128)S(1)}, f32[4,32,128]{2,1,0:T(8,128)S(1)}, u32[]{:S(2)}, u32[]{:S(2)}) collective-permute-start(f32[4,32,128]{2,1,0:T(8,128)S(1)} %pair.1.refs_0_), channel_id=1, source_target_pairs={{0,3},{1,2},{2,1},{3,0},{4,7},{5,6},{6,5},{7,4},{8,11},{9,10},{10,... | collective-permute-start | bytes 196616 | tf_op jit(solution)/shard_map/ppermute | solution.py:403
  108.2 5.3 %collective-permute-start.37 = (f32[4,32,128]{2,1,0:T(8,128)S(1)}, f32[4,32,128]{2,1,0:T(8,128)S(1)}, u32[]{:S(2)}, u32[]{:S(2)}) collective-permute-start(f32[4,32,128]{2,1,0:T(8,128)S(1)} %pair.1.refs_0_), channel_id=1, source_target_pairs={{0,2},{1,3},{2,0},{3,1},{4,6},{5,7},{6,4},{7,5},{8,10},{9,11},{10,... | collective-permute-start | bytes 196616 | tf_op jit(solution)/shard_map/ppermute | solution.py:403
  (16 other events, 115.0 us)

commit v12 on v10

--- a/solution.py
+++ b/solution.py
@@ -504,7 +504,7 @@
     za, *sends = join(first, (0, 1, 2, 4, 5, 6, 7, 3), [shape(half // PARTS, bands, LAT)] * PARTS, [])
     far = [xor_permute(p, "band", 2) for p in sends]
     core_a = xor_permute(za, "band", 1)
-    (zb,) = join(second, range(nd), [], far)
+    (zb,) = join(second, (0, 1, 2, 4, 5, 6, 7, 3), [], far)
     core_b = xor_permute(zb, "band", 1)
     far_core = [xor_permute(p, "band", 1) for p in far]
     part, share = shape(4, bands // 2, bands), shape(2, bands // 2, bands)

time: 116 us -> 116 us (level)
  waiting for transfers between devices: 41.9 us -> 43.5 us
    ppermute x38, waiting for transfers between devices: 38.7 us -> 40.3 us  [xor_permute(): return lax.ppermute(value, axis, [(k, k ^ step) for k in range(count)])]
    ppermute x38, starting transfers between devices: 50.6 us -> 49.4 us  [xor_permute(): return lax.ppermute(value, axis, [(k, k ^ step) for k in range(count)])]
where the time goes in v12:
time: 116 us
  starting transfers between devices  50.9 us (44%)
  waiting for transfers between devices  43.5 us (38%)
  Pallas kernels  16.1 us (14%)
  local copies, waits for them, and re-layouts  3.45 us (3%)
  other arithmetic  1.25 us (1%)
    ppermute x38, starting transfers between devices, xor_permute(): return lax.ppermute(value, axis, [(k, k ^ step) for k in range(count)])  49.4 us
    ppermute x38, waiting for transfers between devices, xor_permute(): return lax.ppermute(value, axis, [(k, k ^ step) for k in range(count)])  40.3 us
    pallas_call x9, Pallas kernels, call(): pl.pallas_call(kernel, out_shape=out_shape, in_specs=specs, out_specs=pl....  16.1 us
    ppermute x1, waiting for transfers between devices, both_permute(): return lax.ppermute(value, ('band', 'dom'), pairs)  3.29 us
    unnamed x14, local copies, waits for them, and re-layouts  2.49 us
  transfers between devices with their start and end apart: 39, of which 13 were waited for; matrix products, arithmetic and copies ran while one was open for 0% of the time, Pallas kernels for 3%

profile of v12, /device:TPU:0, one launch (start us, length us, event | category | flops | bytes accessed | tf_op | source)
XLA Modules:
  0.0 116.0 jit_solution(10292214859714935783)
XLA Ops:
  5.0 3.0 %collective-permute-start = (f32[160,256]{1,0:T(8,128)S(1)}, f32[160,256]{1,0:T(8,128)S(1)}, u32[]{:S(2)}, u32[]{:S(2)}) collective-permute-start(f32[160,256]{1,0:T(8,128)S(1)} %get-tuple-element.37), channel_id=1, source_target_pairs={{0,1},{1,0},{2,3},{3,2},{4,5},{5,4},{6,7},{7,6},{8,9},{9,8},{10,11... | collective-permute-start | bytes 491528 | tf_op jit(solution)/shard_map/ppermute | solution.py:383
  8.0 1.6 %collective-permute-start.1 = (f32[160,256]{1,0:T(8,128)S(1)}, f32[160,256]{1,0:T(8,128)S(1)}, u32[]{:S(2)}, u32[]{:S(2)}) collective-permute-start(f32[160,256]{1,0:T(8,128)S(1)} %get-tuple-element.38), channel_id=1, source_target_pairs={{0,2},{1,3},{2,0},{3,1},{4,6},{5,7},{6,4},{7,5},{8,10},{9,11},{10,... | collective-permute-start | bytes 491528 | tf_op jit(solution)/shard_map/ppermute | solution.py:383
  9.6 2.6 %collective-permute-start.2 = (f32[160,256]{1,0:T(8,128)S(1)}, f32[160,256]{1,0:T(8,128)S(1)}, u32[]{:S(2)}, u32[]{:S(2)}) collective-permute-start(f32[160,256]{1,0:T(8,128)S(1)} %get-tuple-element.39), channel_id=1, source_target_pairs={{0,4},{1,5},{2,6},{3,7},{4,0},{5,1},{6,2},{7,3},{8,12},{9,13},{10,... | collective-permute-start | bytes 491528 | tf_op jit(solution)/shard_map/ppermute | solution.py:383
  12.4 2.5 %collective-permute-start.4 = (f32[160,256]{1,0:T(8,128)S(1)}, f32[160,256]{1,0:T(8,128)S(1)}, u32[]{:S(2)}, u32[]{:S(2)}) collective-permute-start(f32[160,256]{1,0:T(8,128)S(1)} %get-tuple-element.41), channel_id=1, source_target_pairs={{0,6},{1,7},{2,4},{3,5},{4,2},{5,3},{6,0},{7,1},{8,14},{9,15},{10,... | collective-permute-start | bytes 491528 | tf_op jit(solution)/shard_map/ppermute | solution.py:383
  14.9 2.3 %collective-permute-start.5 = (f32[160,256]{1,0:T(8,128)S(1)}, f32[160,256]{1,0:T(8,128)S(1)}, u32[]{:S(2)}, u32[]{:S(2)}) collective-permute-start(f32[160,256]{1,0:T(8,128)S(1)} %get-tuple-element.42), channel_id=1, source_target_pairs={{0,7},{1,6},{2,5},{3,4},{4,3},{5,2},{6,1},{7,0},{8,15},{9,14},{10,... | collective-permute-start | bytes 491528 | tf_op jit(solution)/shard_map/ppermute | solution.py:383
  18.0 13.4 %collective-permute-done.2.refs_2_ = f32[160,256]{1,0:T(8,128)S(1)} collective-permute-done((f32[160,256]{1,0:T(8,128)S(1)}, f32[160,256]{1,0:T(8,128)S(1)}, u32[]{:S(2)}, u32[]{:S(2)}) %collective-permute-start.2) | collective-permute-done | bytes 163872 | tf_op jit(solution)/shard_map/ppermute | solution.py:383
  31.4 3.0 %collective-permute-done.3.refs_3_ = f32[160,256]{1,0:T(8,128)S(1)} collective-permute-done((f32[160,256]{1,0:T(8,128)S(1)}, f32[160,256]{1,0:T(8,128)S(1)}, u32[]{:S(2)}, u32[]{:S(2)}) %collective-permute-start.3) | collective-permute-done | bytes 163872 | tf_op jit(solution)/shard_map/ppermute | solution.py:383
  34.4 7.9 %filter.1 = (f32[64,256]{1,0:T(8,128)S(1)}, f32[64,256]{1,0:T(8,128)S(1)}, f32[64,256]{1,0:T(8,128)S(1)}, f32[64,256]{1,0:T(8,128)S(1)}, f32[64,256]{1,0:T(8,128...) custom-call(s32[3]{0:T(128)S(1)} %pad_add_fusion.pos_ref, ...), custom_call_target="tpu_custom_call" | custom-call | tf_op jit(solution)/shard_map/filter/pallas_call | solution.py:362
  42.3 2.1 %collective-permute-start.7 = (f32[64,256]{1,0:T(8,128)S(1)}, f32[64,256]{1,0:T(8,128)S(1)}, u32[]{:S(2)}, u32[]{:S(2)}) collective-permute-start(f32[64,256]{1,0:T(8,128)S(1)} %get-tuple-element.46), channel_id=1, source_target_pairs={{0,1},{1,0},{2,3},{3,2},{4,5},{5,4},{6,7},{7,6},{8,9},{9,8},{10,11... | collective-permute-start | bytes 196616 | tf_op jit(solution)/shard_map/ppermute | solution.py:383
  44.4 6.1 %collective-permute-start.8 = (f32[64,256]{1,0:T(8,128)S(1)}, f32[64,256]{1,0:T(8,128)S(1)}, u32[]{:S(2)}, u32[]{:S(2)}) collective-permute-start(f32[64,256]{1,0:T(8,128)S(1)} %get-tuple-element.47), channel_id=1, source_target_pairs={{0,2},{1,3},{2,0},{3,1},{4,6},{5,7},{6,4},{7,5},{8,10},{9,11},{10,... | collective-permute-start | bytes 196616 | tf_op jit(solution)/shard_map/ppermute | solution.py:383
  51.5 1.9 %collective-permute-start.10 = (f32[64,256]{1,0:T(8,128)S(1)}, f32[64,256]{1,0:T(8,128)S(1)}, u32[]{:S(2)}, u32[]{:S(2)}) collective-permute-start(f32[64,256]{1,0:T(8,128)S(1)} %get-tuple-element.49), channel_id=1, source_target_pairs={{0,5},{1,4},{2,7},{3,6},{4,1},{5,0},{6,3},{7,2},{8,13},{9,12},{10,... | collective-permute-start | bytes 196616 | tf_op jit(solution)/shard_map/ppermute | solution.py:383
  53.4 2.5 %collective-permute-start.11 = (f32[64,256]{1,0:T(8,128)S(1)}, f32[64,256]{1,0:T(8,128)S(1)}, u32[]{:S(2)}, u32[]{:S(2)}) collective-permute-start(f32[64,256]{1,0:T(8,128)S(1)} %get-tuple-element.50), channel_id=1, source_target_pairs={{0,6},{1,7},{2,4},{3,5},{4,2},{5,3},{6,0},{7,1},{8,14},{9,15},{10,... | collective-permute-start | bytes 196616 | tf_op jit(solution)/shard_map/ppermute | solution.py:383
  55.9 2.2 %collective-permute-start.12 = (f32[64,256]{1,0:T(8,128)S(1)}, f32[64,256]{1,0:T(8,128)S(1)}, u32[]{:S(2)}, u32[]{:S(2)}) collective-permute-start(f32[64,256]{1,0:T(8,128)S(1)} %get-tuple-element.51), channel_id=1, source_target_pairs={{0,7},{1,6},{2,5},{3,4},{4,3},{5,2},{6,1},{7,0},{8,15},{9,14},{10,... | collective-permute-start | bytes 196616 | tf_op jit(solution)/shard_map/ppermute | solution.py:383
  58.2 2.1 %collective-permute-done.9.refs_3_ = f32[64,256]{1,0:T(8,128)S(1)} collective-permute-done((f32[64,256]{1,0:T(8,128)S(1)}, f32[64,256]{1,0:T(8,128)S(1)}, u32[]{:S(2)}, u32[]{:S(2)}) %collective-permute-start.9) | collective-permute-done | bytes 65568 | tf_op jit(solution)/shard_map/ppermute | solution.py:383
  60.3 1.6 %collective-permute-done.10.refs_4_ = f32[64,256]{1,0:T(8,128)S(1)} collective-permute-done((f32[64,256]{1,0:T(8,128)S(1)}, f32[64,256]{1,0:T(8,128)S(1)}, u32[]{:S(2)}, u32[]{:S(2)}) %collective-permute-start.10) | collective-permute-done | bytes 65568 | tf_op jit(solution)/shard_map/ppermute | solution.py:383
  61.9 3.5 %collective-permute-start.16 = (f32[64,256]{1,0:T(8,128)S(1)}, f32[64,256]{1,0:T(8,128)S(1)}, u32[]{:S(2)}, u32[]{:S(2)}) collective-permute-start(f32[64,256]{1,0:T(8,128)S(1)} %get-tuple-element.57), channel_id=1, source_target_pairs={{0,4},{1,5},{2,6},{3,7},{4,0},{5,1},{6,2},{7,3},{8,12},{9,13},{10,... | collective-permute-start | bytes 196616 | tf_op jit(solution)/shard_map/ppermute | solution.py:383
  65.4 2.3 %collective-permute-start.17 = (f32[64,256]{1,0:T(8,128)S(1)}, f32[64,256]{1,0:T(8,128)S(1)}, u32[]{:S(2)}, u32[]{:S(2)}) collective-permute-start(f32[64,256]{1,0:T(8,128)S(1)} %get-tuple-element.58), channel_id=1, source_target_pairs={{0,5},{1,4},{2,7},{3,6},{4,1},{5,0},{6,3},{7,2},{8,13},{9,12},{10,... | collective-permute-start | bytes 196616 | tf_op jit(solution)/shard_map/ppermute | solution.py:383
  67.7 2.2 %collective-permute-start.18 = (f32[64,256]{1,0:T(8,128)S(1)}, f32[64,256]{1,0:T(8,128)S(1)}, u32[]{:S(2)}, u32[]{:S(2)}) collective-permute-start(f32[64,256]{1,0:T(8,128)S(1)} %get-tuple-element.59), channel_id=1, source_target_pairs={{0,6},{1,7},{2,4},{3,5},{4,2},{5,3},{6,0},{7,1},{8,14},{9,15},{10,... | collective-permute-start | bytes 196616 | tf_op jit(solution)/shard_map/ppermute | solution.py:383
  70.5 1.8 %collective-permute-start.19 = (f32[64,256]{1,0:T(8,128)S(1)}, f32[64,256]{1,0:T(8,128)S(1)}, u32[]{:S(2)}, u32[]{:S(2)}) collective-permute-start(f32[64,256]{1,0:T(8,128)S(1)} %get-tuple-element.60), channel_id=1, source_target_pairs={{0,7},{1,6},{2,5},{3,4},{4,3},{5,2},{6,1},{7,0},{8,15},{9,14},{10,... | collective-permute-start | bytes 196616 | tf_op jit(solution)/shard_map/ppermute | solution.py:383
  72.3 1.5 %collective-permute-start.21 = (f32[1,128,256]{2,1,0:T(8,128)S(1)}, f32[1,128,256]{2,1,0:T(8,128)S(1)}, u32[]{:S(2)}, u32[]{:S(2)}) collective-permute-start(f32[1,128,256]{2,1,0:T(8,128)S(1)} %get-tuple-element.62), channel_id=1, source_target_pairs={{0,16},{8,24},{16,0},{24,8},{1,17},{9,25},{17,1},{25,9},{2,18},{10... | collective-permute-start | bytes 393224 | tf_op jit(solution)/shard_map/ppermute | solution.py:383
  74.3 1.5 %collective-permute-start.23 = (f32[1,128,256]{2,1,0:T(8,128)S(1)}, f32[1,128,256]{2,1,0:T(8,128)S(1)}, u32[]{:S(2)}, u32[]{:S(2)}) collective-permute-start(f32[1,128,256]{2,1,0:T(8,128)S(1)} %get-tuple-element.64), channel_id=1, source_target_pairs={{0,16},{8,24},{16,0},{24,8},{1,17},{9,25},{17,1},{25,9},{2,18},{10... | collective-permute-start | bytes 393224 | tf_op jit(solution)/shard_map/ppermute | solution.py:383
  77.5 5.2 %collective-permute-done.20.refs_7_ = f32[64,256]{1,0:T(8,128)S(1)} collective-permute-done((f32[64,256]{1,0:T(8,128)S(1)}, f32[64,256]{1,0:T(8,128)S(1)}, u32[]{:S(2)}, u32[]{:S(2)}) %collective-permute-start.20) | collective-permute-done | bytes 65568 | tf_op jit(solution)/shard_map/ppermute | solution.py:383
  87.0 2.3 %blocks.1 = (f32[4,64,128]{2,1,0:T(8,128)S(1)}, f32[4,64,128]{2,1,0:T(8,128)S(1)}, f32[2,64,128]{2,1,0:T(8,128)S(1)}, f32[2,64,128]{2,1,0:T(8,128)S(1)}) custom-call(s32[3]{0:T(128)S(1)} %pad_add_fusion.pos_ref, f32[4,128,256]{2,1,0:T(8,128)S(1)} %get-tuple-element.53.za, f32[4,128,256]{2,1,0:T(8,128)S(1)} %join.3.zb, ...), custom_call_target="tpu_custom_call" | custom-call | tf_op jit(solution)/shard_map/blocks/pallas_call | solution.py:362
  90.0 1.5 %collective-permute-start.32 = (f32[2,64,128]{2,1,0:T(8,128)S(1)}, f32[2,64,128]{2,1,0:T(8,128)S(1)}, u32[]{:S(2)}, u32[]{:S(2)}) collective-permute-start(f32[2,64,128]{2,1,0:T(8,128)S(1)} %get-tuple-element.68), channel_id=1, source_target_pairs={{0,16},{8,24},{16,0},{24,8},{1,17},{9,25},{17,1},{25,9},{2,18},{10... | collective-permute-start | bytes 196616 | tf_op jit(solution)/shard_map/ppermute | solution.py:383
  91.5 1.4 %collective-permute-start.33 = (f32[2,64,128]{2,1,0:T(8,128)S(1)}, f32[2,64,128]{2,1,0:T(8,128)S(1)}, u32[]{:S(2)}, u32[]{:S(2)}) collective-permute-start(f32[2,64,128]{2,1,0:T(8,128)S(1)} %get-tuple-element.69), channel_id=1, source_target_pairs={{0,17},{1,16},{2,19},{3,18},{4,21},{5,20},{6,23},{7,22},{8,25},{9,... | collective-permute-start | bytes 196616 | tf_op jit(solution)/shard_map/ppermute | solution.py:389
  92.9 1.3 %collective-permute-done.32.back = f32[2,64,128]{2,1,0:T(8,128)S(1)} collective-permute-done((f32[2,64,128]{2,1,0:T(8,128)S(1)}, f32[2,64,128]{2,1,0:T(8,128)S(1)}, u32[]{:S(2)}, u32[]{:S(2)}) %collective-permute-start.32) | collective-permute-done | bytes 65568 | tf_op jit(solution)/shard_map/ppermute | solution.py:383
  94.2 3.3 %collective-permute-done.33.back_other = f32[2,64,128]{2,1,0:T(8,128)S(1)} collective-permute-done((f32[2,64,128]{2,1,0:T(8,128)S(1)}, f32[2,64,128]{2,1,0:T(8,128)S(1)}, u32[]{:S(2)}, u32[]{:S(2)}) %collective-permute-start.33) | collective-permute-done | bytes 65568 | tf_op jit(solution)/shard_map/ppermute | solution.py:389
  98.2 4.3 %collective-permute-done.34 = f32[4,32,128]{2,1,0:T(8,128)S(1)} collective-permute-done((f32[4,32,128]{2,1,0:T(8,128)S(1)}, f32[4,32,128]{2,1,0:T(8,128)S(1)}, u32[]{:S(2)}, u32[]{:S(2)}) %collective-permute-start.34) | collective-permute-done | bytes 65568 | tf_op jit(solution)/shard_map/ppermute | solution.py:383
  102.7 5.1 %collective-permute-done.35.other = f32[4,32,128]{2,1,0:T(8,128)S(1)} collective-permute-done((f32[4,32,128]{2,1,0:T(8,128)S(1)}, f32[4,32,128]{2,1,0:T(8,128)S(1)}, u32[]{:S(2)}, u32[]{:S(2)}) %collective-permute-start.35) | collective-permute-done | bytes 65568 | tf_op jit(solution)/shard_map/ppermute | solution.py:383
  108.5 2.1 %collective-permute-start.37 = (f32[4,32,128]{2,1,0:T(8,128)S(1)}, f32[4,32,128]{2,1,0:T(8,128)S(1)}, u32[]{:S(2)}, u32[]{:S(2)}) collective-permute-start(f32[4,32,128]{2,1,0:T(8,128)S(1)} %pair.1.refs_0_), channel_id=1, source_target_pairs={{0,2},{1,3},{2,0},{3,1},{4,6},{5,7},{6,4},{7,5},{8,10},{9,11},{10,... | collective-permute-start | bytes 196616 | tf_op jit(solution)/shard_map/ppermute | solution.py:383
  110.5 1.4 %collective-permute-start.36 = (f32[4,32,128]{2,1,0:T(8,128)S(1)}, f32[4,32,128]{2,1,0:T(8,128)S(1)}, u32[]{:S(2)}, u32[]{:S(2)}) collective-permute-start(f32[4,32,128]{2,1,0:T(8,128)S(1)} %pair.1.refs_0_), channel_id=1, source_target_pairs={{0,1},{1,0},{2,3},{3,2},{4,5},{5,4},{6,7},{7,6},{8,9},{9,8},{10,11... | collective-permute-start | bytes 196616 | tf_op jit(solution)/shard_map/ppermute | solution.py:383
  111.9 1.8 %output.1 = f32[8,256,128]{2,1,0:T(8,128)} custom-call(s32[3]{0:T(128)S(1)} %pad_add_fusion.pos_ref, f32[4,128,256]{2,1,0:T(8,128)S(1)} %get-tuple-element.53.za, f32[4,128,256]{2,1,0:T(8,128)S(1)} %join.3.zb), custom_call_target="tpu_custom_call" | custom-call | tf_op jit(solution)/shard_map/output/pallas_call | solution.py:362
  (78 shorter events, 18.0 us)
Async XLA Ops:
  5.0 10.0 %collective-permute-start = (f32[160,256]{1,0:T(8,128)S(1)}, f32[160,256]{1,0:T(8,128)S(1)}, u32[]{:S(2)}, u32[]{:S(2)}) collective-permute-start(f32[160,256]{1,0:T(8,128)S(1)} %get-tuple-element.37), channel_id=1, source_target_pairs={{0,1},{1,0},{2,3},{3,2},{4,5},{5,4},{6,7},{7,6},{8,9},{9,8},{10,11... | collective-permute-start | bytes 491528 | tf_op jit(solution)/shard_map/ppermute | solution.py:383
  8.0 9.2 %collective-permute-start.1 = (f32[160,256]{1,0:T(8,128)S(1)}, f32[160,256]{1,0:T(8,128)S(1)}, u32[]{:S(2)}, u32[]{:S(2)}) collective-permute-start(f32[160,256]{1,0:T(8,128)S(1)} %get-tuple-element.38), channel_id=1, source_target_pairs={{0,2},{1,3},{2,0},{3,1},{4,6},{5,7},{6,4},{7,5},{8,10},{9,11},{10,... | collective-permute-start | bytes 491528 | tf_op jit(solution)/shard_map/ppermute | solution.py:383
  9.6 21.8 %collective-permute-start.2 = (f32[160,256]{1,0:T(8,128)S(1)}, f32[160,256]{1,0:T(8,128)S(1)}, u32[]{:S(2)}, u32[]{:S(2)}) collective-permute-start(f32[160,256]{1,0:T(8,128)S(1)} %get-tuple-element.39), channel_id=1, source_target_pairs={{0,4},{1,5},{2,6},{3,7},{4,0},{5,1},{6,2},{7,3},{8,12},{9,13},{10,... | collective-permute-start | bytes 491528 | tf_op jit(solution)/shard_map/ppermute | solution.py:383
  12.1 22.2 %collective-permute-start.3 = (f32[160,256]{1,0:T(8,128)S(1)}, f32[160,256]{1,0:T(8,128)S(1)}, u32[]{:S(2)}, u32[]{:S(2)}) collective-permute-start(f32[160,256]{1,0:T(8,128)S(1)} %get-tuple-element.40), channel_id=1, source_target_pairs={{0,5},{1,4},{2,7},{3,6},{4,1},{5,0},{6,3},{7,2},{8,13},{9,12},{10,... | collective-permute-start | bytes 491528 | tf_op jit(solution)/shard_map/ppermute | solution.py:383
  12.4 21.9 %collective-permute-start.4 = (f32[160,256]{1,0:T(8,128)S(1)}, f32[160,256]{1,0:T(8,128)S(1)}, u32[]{:S(2)}, u32[]{:S(2)}) collective-permute-start(f32[160,256]{1,0:T(8,128)S(1)} %get-tuple-element.41), channel_id=1, source_target_pairs={{0,6},{1,7},{2,4},{3,5},{4,2},{5,3},{6,0},{7,1},{8,14},{9,15},{10,... | collective-permute-start | bytes 491528 | tf_op jit(solution)/shard_map/ppermute | solution.py:383
  14.9 19.5 %collective-permute-start.5 = (f32[160,256]{1,0:T(8,128)S(1)}, f32[160,256]{1,0:T(8,128)S(1)}, u32[]{:S(2)}, u32[]{:S(2)}) collective-permute-start(f32[160,256]{1,0:T(8,128)S(1)} %get-tuple-element.42), channel_id=1, source_target_pairs={{0,7},{1,6},{2,5},{3,4},{4,3},{5,2},{6,1},{7,0},{8,15},{9,14},{10,... | collective-permute-start | bytes 491528 | tf_op jit(solution)/shard_map/ppermute | solution.py:383
  17.2 17.2 %collective-permute-start.6 = (f32[160,256]{1,0:T(8,128)S(1)}, f32[160,256]{1,0:T(8,128)S(1)}, u32[]{:S(2)}, u32[]{:S(2)}) collective-permute-start(f32[160,256]{1,0:T(8,128)S(1)} %get-tuple-element.43), channel_id=1, source_target_pairs={{0,3},{1,2},{2,1},{3,0},{4,7},{5,6},{6,5},{7,4},{8,11},{9,10},{10,... | collective-permute-start | bytes 491528 | tf_op jit(solution)/shard_map/ppermute | solution.py:383
  42.3 13.6 %collective-permute-start.7 = (f32[64,256]{1,0:T(8,128)S(1)}, f32[64,256]{1,0:T(8,128)S(1)}, u32[]{:S(2)}, u32[]{:S(2)}) collective-permute-start(f32[64,256]{1,0:T(8,128)S(1)} %get-tuple-element.46), channel_id=1, source_target_pairs={{0,1},{1,0},{2,3},{3,2},{4,5},{5,4},{6,7},{7,6},{8,9},{9,8},{10,11... | collective-permute-start | bytes 196616 | tf_op jit(solution)/shard_map/ppermute | solution.py:383
  44.4 13.7 %collective-permute-start.8 = (f32[64,256]{1,0:T(8,128)S(1)}, f32[64,256]{1,0:T(8,128)S(1)}, u32[]{:S(2)}, u32[]{:S(2)}) collective-permute-start(f32[64,256]{1,0:T(8,128)S(1)} %get-tuple-element.47), channel_id=1, source_target_pairs={{0,2},{1,3},{2,0},{3,1},{4,6},{5,7},{6,4},{7,5},{8,10},{9,11},{10,... | collective-permute-start | bytes 196616 | tf_op jit(solution)/shard_map/ppermute | solution.py:383
  50.5 9.8 %collective-permute-start.9 = (f32[64,256]{1,0:T(8,128)S(1)}, f32[64,256]{1,0:T(8,128)S(1)}, u32[]{:S(2)}, u32[]{:S(2)}) collective-permute-start(f32[64,256]{1,0:T(8,128)S(1)} %get-tuple-element.48), channel_id=1, source_target_pairs={{0,4},{1,5},{2,6},{3,7},{4,0},{5,1},{6,2},{7,3},{8,12},{9,13},{10,... | collective-permute-start | bytes 196616 | tf_op jit(solution)/shard_map/ppermute | solution.py:383
  51.5 10.3 %collective-permute-start.10 = (f32[64,256]{1,0:T(8,128)S(1)}, f32[64,256]{1,0:T(8,128)S(1)}, u32[]{:S(2)}, u32[]{:S(2)}) collective-permute-start(f32[64,256]{1,0:T(8,128)S(1)} %get-tuple-element.49), channel_id=1, source_target_pairs={{0,5},{1,4},{2,7},{3,6},{4,1},{5,0},{6,3},{7,2},{8,13},{9,12},{10,... | collective-permute-start | bytes 196616 | tf_op jit(solution)/shard_map/ppermute | solution.py:383
  53.4 8.4 %collective-permute-start.11 = (f32[64,256]{1,0:T(8,128)S(1)}, f32[64,256]{1,0:T(8,128)S(1)}, u32[]{:S(2)}, u32[]{:S(2)}) collective-permute-start(f32[64,256]{1,0:T(8,128)S(1)} %get-tuple-element.50), channel_id=1, source_target_pairs={{0,6},{1,7},{2,4},{3,5},{4,2},{5,3},{6,0},{7,1},{8,14},{9,15},{10,... | collective-permute-start | bytes 196616 | tf_op jit(solution)/shard_map/ppermute | solution.py:383
  55.9 9.5 %collective-permute-start.12 = (f32[64,256]{1,0:T(8,128)S(1)}, f32[64,256]{1,0:T(8,128)S(1)}, u32[]{:S(2)}, u32[]{:S(2)}) collective-permute-start(f32[64,256]{1,0:T(8,128)S(1)} %get-tuple-element.51), channel_id=1, source_target_pairs={{0,7},{1,6},{2,5},{3,4},{4,3},{5,2},{6,1},{7,0},{8,15},{9,14},{10,... | collective-permute-start | bytes 196616 | tf_op jit(solution)/shard_map/ppermute | solution.py:383
  58.1 9.5 %collective-permute-start.13 = (f32[64,256]{1,0:T(8,128)S(1)}, f32[64,256]{1,0:T(8,128)S(1)}, u32[]{:S(2)}, u32[]{:S(2)}) collective-permute-start(f32[64,256]{1,0:T(8,128)S(1)} %get-tuple-element.52), channel_id=1, source_target_pairs={{0,3},{1,2},{2,1},{3,0},{4,7},{5,6},{6,5},{7,4},{8,11},{9,10},{10,... | collective-permute-start | bytes 196616 | tf_op jit(solution)/shard_map/ppermute | solution.py:383
  60.3 10.2 %collective-permute-start.14 = (f32[64,256]{1,0:T(8,128)S(1)}, f32[64,256]{1,0:T(8,128)S(1)}, u32[]{:S(2)}, u32[]{:S(2)}) collective-permute-start(f32[64,256]{1,0:T(8,128)S(1)} %get-tuple-element.55), channel_id=1, source_target_pairs={{0,1},{1,0},{2,3},{3,2},{4,5},{5,4},{6,7},{7,6},{8,9},{9,8},{10,11... | collective-permute-start | bytes 196616 | tf_op jit(solution)/shard_map/ppermute | solution.py:383
  61.9 10.4 %collective-permute-start.15 = (f32[64,256]{1,0:T(8,128)S(1)}, f32[64,256]{1,0:T(8,128)S(1)}, u32[]{:S(2)}, u32[]{:S(2)}) collective-permute-start(f32[64,256]{1,0:T(8,128)S(1)} %get-tuple-element.56), channel_id=1, source_target_pairs={{0,2},{1,3},{2,0},{3,1},{4,6},{5,7},{6,4},{7,5},{8,10},{9,11},{10,... | collective-permute-start | bytes 196616 | tf_op jit(solution)/shard_map/ppermute | solution.py:383
  61.9 12.0 %collective-permute-start.16 = (f32[64,256]{1,0:T(8,128)S(1)}, f32[64,256]{1,0:T(8,128)S(1)}, u32[]{:S(2)}, u32[]{:S(2)}) collective-permute-start(f32[64,256]{1,0:T(8,128)S(1)} %get-tuple-element.57), channel_id=1, source_target_pairs={{0,4},{1,5},{2,6},{3,7},{4,0},{5,1},{6,2},{7,3},{8,12},{9,13},{10,... | collective-permute-start | bytes 196616 | tf_op jit(solution)/shard_map/ppermute | solution.py:383
  65.4 8.9 %collective-permute-start.17 = (f32[64,256]{1,0:T(8,128)S(1)}, f32[64,256]{1,0:T(8,128)S(1)}, u32[]{:S(2)}, u32[]{:S(2)}) collective-permute-start(f32[64,256]{1,0:T(8,128)S(1)} %get-tuple-element.58), channel_id=1, source_target_pairs={{0,5},{1,4},{2,7},{3,6},{4,1},{5,0},{6,3},{7,2},{8,13},{9,12},{10,... | collective-permute-start | bytes 196616 | tf_op jit(solution)/shard_map/ppermute | solution.py:383
  67.7 8.2 %collective-permute-start.18 = (f32[64,256]{1,0:T(8,128)S(1)}, f32[64,256]{1,0:T(8,128)S(1)}, u32[]{:S(2)}, u32[]{:S(2)}) collective-permute-start(f32[64,256]{1,0:T(8,128)S(1)} %get-tuple-element.59), channel_id=1, source_target_pairs={{0,6},{1,7},{2,4},{3,5},{4,2},{5,3},{6,0},{7,1},{8,14},{9,15},{10,... | collective-permute-start | bytes 196616 | tf_op jit(solution)/shard_map/ppermute | solution.py:383
  70.5 7.0 %collective-permute-start.19 = (f32[64,256]{1,0:T(8,128)S(1)}, f32[64,256]{1,0:T(8,128)S(1)}, u32[]{:S(2)}, u32[]{:S(2)}) collective-permute-start(f32[64,256]{1,0:T(8,128)S(1)} %get-tuple-element.60), channel_id=1, source_target_pairs={{0,7},{1,6},{2,5},{3,4},{4,3},{5,2},{6,1},{7,0},{8,15},{9,14},{10,... | collective-permute-start | bytes 196616 | tf_op jit(solution)/shard_map/ppermute | solution.py:383
  72.3 10.4 %collective-permute-start.21 = (f32[1,128,256]{2,1,0:T(8,128)S(1)}, f32[1,128,256]{2,1,0:T(8,128)S(1)}, u32[]{:S(2)}, u32[]{:S(2)}) collective-permute-start(f32[1,128,256]{2,1,0:T(8,128)S(1)} %get-tuple-element.62), channel_id=1, source_target_pairs={{0,16},{8,24},{16,0},{24,8},{1,17},{9,25},{17,1},{25,9},{2,18},{10... | collective-permute-start | bytes 393224 | tf_op jit(solution)/shard_map/ppermute | solution.py:383
  73.8 8.9 %collective-permute-start.22 = (f32[1,128,256]{2,1,0:T(8,128)S(1)}, f32[1,128,256]{2,1,0:T(8,128)S(1)}, u32[]{:S(2)}, u32[]{:S(2)}) collective-permute-start(f32[1,128,256]{2,1,0:T(8,128)S(1)} %get-tuple-element.63), channel_id=1, source_target_pairs={{0,16},{8,24},{16,0},{24,8},{1,17},{9,25},{17,1},{25,9},{2,18},{10... | collective-permute-start | bytes 393224 | tf_op jit(solution)/shard_map/ppermute | solution.py:383
  74.3 8.4 %collective-permute-start.23 = (f32[1,128,256]{2,1,0:T(8,128)S(1)}, f32[1,128,256]{2,1,0:T(8,128)S(1)}, u32[]{:S(2)}, u32[]{:S(2)}) collective-permute-start(f32[1,128,256]{2,1,0:T(8,128)S(1)} %get-tuple-element.64), channel_id=1, source_target_pairs={{0,16},{8,24},{16,0},{24,8},{1,17},{9,25},{17,1},{25,9},{2,18},{10... | collective-permute-start | bytes 393224 | tf_op jit(solution)/shard_map/ppermute | solution.py:383
  75.8 6.9 %collective-permute-start.24 = (f32[1,128,256]{2,1,0:T(8,128)S(1)}, f32[1,128,256]{2,1,0:T(8,128)S(1)}, u32[]{:S(2)}, u32[]{:S(2)}) collective-permute-start(f32[1,128,256]{2,1,0:T(8,128)S(1)} %get-tuple-element.65), channel_id=1, source_target_pairs={{0,16},{8,24},{16,0},{24,8},{1,17},{9,25},{17,1},{25,9},{2,18},{10... | collective-permute-start | bytes 393224 | tf_op jit(solution)/shard_map/ppermute | solution.py:383
  77.5 5.2 %collective-permute-start.20 = (f32[64,256]{1,0:T(8,128)S(1)}, f32[64,256]{1,0:T(8,128)S(1)}, u32[]{:S(2)}, u32[]{:S(2)}) collective-permute-start(f32[64,256]{1,0:T(8,128)S(1)} %get-tuple-element.61), channel_id=1, source_target_pairs={{0,3},{1,2},{2,1},{3,0},{4,7},{5,6},{6,5},{7,4},{8,11},{9,10},{10,... | collective-permute-start | bytes 196616 | tf_op jit(solution)/shard_map/ppermute | solution.py:383
  82.7 4.3 %collective-permute-start.25 = (f32[4,128,256]{2,1,0:T(8,128)S(1)}, f32[4,128,256]{2,1,0:T(8,128)S(1)}, u32[]{:S(2)}, u32[]{:S(2)}) collective-permute-start(f32[4,128,256]{2,1,0:T(8,128)S(1)} %get-tuple-element.53.za), channel_id=1, source_target_pairs={{0,8},{8,0},{16,24},{24,16},{1,9},{9,1},{17,25},{25,17},{2,10},{10... | collective-permute-start | bytes 1572872 | tf_op jit(solution)/shard_map/ppermute | solution.py:383
  89.3 8.2 %collective-permute-start.31 = (f32[4,64,128]{2,1,0:T(8,128)S(1)}, f32[4,64,128]{2,1,0:T(8,128)S(1)}, u32[]{:S(2)}, u32[]{:S(2)}) collective-permute-start(f32[4,64,128]{2,1,0:T(8,128)S(1)} %get-tuple-element.67), channel_id=1, source_target_pairs={{0,1},{1,0},{2,3},{3,2},{4,5},{5,4},{6,7},{7,6},{8,9},{9,8},{10,11... | collective-permute-start | bytes 393224 | tf_op jit(solution)/shard_map/ppermute | solution.py:383
  91.5 6.0 %collective-permute-start.33 = (f32[2,64,128]{2,1,0:T(8,128)S(1)}, f32[2,64,128]{2,1,0:T(8,128)S(1)}, u32[]{:S(2)}, u32[]{:S(2)}) collective-permute-start(f32[2,64,128]{2,1,0:T(8,128)S(1)} %get-tuple-element.69), channel_id=1, source_target_pairs={{0,17},{1,16},{2,19},{3,18},{4,21},{5,20},{6,23},{7,22},{8,25},{9,... | collective-permute-start | bytes 196616 | tf_op jit(solution)/shard_map/ppermute | solution.py:389
  98.1 4.3 %collective-permute-start.34 = (f32[4,32,128]{2,1,0:T(8,128)S(1)}, f32[4,32,128]{2,1,0:T(8,128)S(1)}, u32[]{:S(2)}, u32[]{:S(2)}) collective-permute-start(f32[4,32,128]{2,1,0:T(8,128)S(1)} %get-tuple-element.71), channel_id=1, source_target_pairs={{0,2},{1,3},{2,0},{3,1},{4,6},{5,7},{6,4},{7,5},{8,10},{9,11},{10,... | collective-permute-start | bytes 196616 | tf_op jit(solution)/shard_map/ppermute | solution.py:383
  102.4 5.4 %collective-permute-start.35 = (f32[4,32,128]{2,1,0:T(8,128)S(1)}, f32[4,32,128]{2,1,0:T(8,128)S(1)}, u32[]{:S(2)}, u32[]{:S(2)}) collective-permute-start(f32[4,32,128]{2,1,0:T(8,128)S(1)} %add.80.mine), channel_id=1, source_target_pairs={{0,4},{1,5},{2,6},{3,7},{4,0},{5,1},{6,2},{7,3},{8,12},{9,13},{10,... | collective-permute-start | bytes 196616 | tf_op jit(solution)/shard_map/ppermute | solution.py:383
  108.4 5.4 %collective-permute-start.38 = (f32[4,32,128]{2,1,0:T(8,128)S(1)}, f32[4,32,128]{2,1,0:T(8,128)S(1)}, u32[]{:S(2)}, u32[]{:S(2)}) collective-permute-start(f32[4,32,128]{2,1,0:T(8,128)S(1)} %pair.1.refs_0_), channel_id=1, source_target_pairs={{0,3},{1,2},{2,1},{3,0},{4,7},{5,6},{6,5},{7,4},{8,11},{9,10},{10,... | collective-permute-start | bytes 196616 | tf_op jit(solution)/shard_map/ppermute | solution.py:383
  108.5 5.3 %collective-permute-start.37 = (f32[4,32,128]{2,1,0:T(8,128)S(1)}, f32[4,32,128]{2,1,0:T(8,128)S(1)}, u32[]{:S(2)}, u32[]{:S(2)}) collective-permute-start(f32[4,32,128]{2,1,0:T(8,128)S(1)} %pair.1.refs_0_), channel_id=1, source_target_pairs={{0,2},{1,3},{2,0},{3,1},{4,6},{5,7},{6,4},{7,5},{8,10},{9,11},{10,... | collective-permute-start | bytes 196616 | tf_op jit(solution)/shard_map/ppermute | solution.py:383
  (14 other events, 112.0 us)
